TPU v7x, 128 devices: a whole 4x4x4 slice. The times are simulated.
128 devices in a mesh: row: 16 (over y, x), col: 8 (over z, core).
Axes of the slice: x: 4, y: 4, z: 4, core: 2. Of those that a mesh axis runs over, the one named last changes fastest.
Arguments:
- right_sides: float32 [32, 262144], P(None, ('row', 'col')), may hold values from -60 to 60
- diag_blocks: float32 [1024, 256, 256], P(('row', 'col')), may hold values from -1 to 3, as said below
- couplings: float32 [8192, 256, 256], P(('row', 'col')), may hold values from -0.125 to 0.125
- pair_index: int32 [2, 8192], P(None, ('row', 'col')), may hold values from 0 to 1023, as said below
Outputs:
- solution_field: float32 [32, 262144], P(None, ('row', 'col'))
- residual: float32 [32, 262144], P(None, ('row', 'col'))
Inputs may be any that keep to these rules, and one draw needn't show every extreme that they name: `diag_blocks`: each block is symmetric; each of its diagonal entries is at least 1 and exceeds the sum of the magnitudes of the other entries of its row. Device i along row+col owns block rows i * 8 to (i + 1) * 8 - 1, and pair_index[0, k] of every block in its part of pair_index is one of them. pair_index[1, k] is a block row of the same device or of a device whose row index and col index each differ from its own by at most one.
All inputs are finite; a program needn't handle non-finite values.
Results may differ from a plain program's by a relative error of at most 0.0003.
Values sent between devices are 32-bit elements; how exact they have to be, the bound alone decides.
No kernel may reach another device: no remote copies, remote signals or barrier semaphores. Data moves between devices by JAX's collectives and lax.ppermute only.
A program may use at most 128 MiB of HBM per device.

v0:
```python
import jax
import jax.numpy as jnp
from jax import lax
from jax.experimental import pallas as pl
from jax.experimental.pallas import tpu as pltpu
from jax.sharding import PartitionSpec as P

F32 = jnp.float32
BF16 = jnp.bfloat16
HIGHEST = lax.Precision.HIGHEST
VMEM_SPEC = pl.BlockSpec(memory_space=pltpu.VMEM)
SMEM_SPEC = pl.BlockSpec(memory_space=pltpu.SMEM)
CHUNK = 8


def in_vmem(value):
    return pltpu.with_memory_space_constraint(value, pltpu.VMEM)


def pairs_of(count, shift):
    found = []
    for place in range(count):
        partner = ((place + shift) ^ 1) - shift
        if 0 <= partner < count:
            found.append((place, partner))
    return found


def swapped(value, axis, shift):
    return lax.ppermute(value, axis, pairs_of(lax.axis_size(axis), shift))


def slot_of(target, mine):
    return jnp.where(target == mine, 0, jnp.where(target == (mine ^ 1), 1, 2))


def split(value):
    high = value.astype(BF16)
    return high, (value - high.astype(F32)).astype(BF16)


def dot_nt(left, right):
    return lax.dot_general(left, right, (((1,), (1,)), ((), ())), preferred_element_type=F32)


def dot_nn(left, right):
    return lax.dot_general(left, right, (((1,), (0,)), ((), ())), preferred_element_type=F32)


def full_nn(left, right):
    return lax.dot_general(left, right, (((1,), (0,)), ((), ())), precision=HIGHEST, preferred_element_type=F32)


def full_tn(left, right):
    return lax.dot_general(left, right, (((0,), (0,)), ((), ())), precision=HIGHEST, preferred_element_type=F32)


def gram(left, right):
    both = dot_nt(left, right)
    half = both.shape[0] // 2
    return both[:half, :half] + both[:half, half:] + both[half:, :half] + both[half:, half:]


def times(dot, stacked, high, low):
    half = stacked.shape[0] // 2
    first = dot(stacked, high)
    return first[:half] + first[half:] + dot(stacked[:half], low)


def stacked_split(value):
    return jnp.concatenate(split(value), axis=0)


def call(body, out_shape, n_smem, args, scratch=(), limit=24 << 20):
    return pl.pallas_call(
        body,
        out_shape=out_shape,
        in_specs=[SMEM_SPEC] * n_smem + [VMEM_SPEC] * (len(args) - n_smem),
        out_specs=jax.tree.map(lambda _: VMEM_SPEC, out_shape),
        scratch_shapes=list(scratch),
        compiler_params=pltpu.CompilerParams(vmem_limit_bytes=limit),
    )(*args[:n_smem], *[in_vmem(a) for a in args[n_smem:]])


def prepare_body(couplings, diag, right, c_high, c_low, d_high, d_low, own, grams):
    step = pl.program_id(0)
    per = couplings.shape[0]
    for place in range(per):
        high, low = split(couplings[place])
        c_high[step * per + place] = high
        c_low[step * per + place] = low
    high, low = split(diag[0])
    d_high[step] = high
    d_low[step] = low
    vector = stacked_split(right[...])
    term = times(dot_nt, vector, high, low)
    own[step] = term

    @pl.when(step == 0)
    def _():
        grams[...] = jnp.zeros_like(grams)

    grams[0] += gram(vector, vector)
    grams[1] += gram(stacked_split(term), vector)


def prepare(couplings, diag, right):
    count, width = couplings.shape[0], couplings.shape[1]
    blocks, rows = diag.shape[0], right.shape[0]
    per = count // blocks
    return pl.pallas_call(
        prepare_body,
        grid=(blocks,),
        in_specs=[
            pl.BlockSpec((per, width, width), lambda i: (i, 0, 0)),
            pl.BlockSpec((1, width, width), lambda i: (i, 0, 0)),
            pl.BlockSpec((rows, width), lambda i: (0, i)),
        ],
        out_specs=[VMEM_SPEC] * 6,
        out_shape=[
            pltpu.VMEM((count, width, width), BF16),
            pltpu.VMEM((count, width, width), BF16),
            pltpu.VMEM((blocks, width, width), BF16),
            pltpu.VMEM((blocks, width, width), BF16),
            pltpu.VMEM((blocks, rows, width), F32),
            pltpu.VMEM((2, rows, rows), F32),
        ],
        compiler_params=pltpu.CompilerParams(vmem_limit_bytes=24 << 20),
    )(couplings, diag, right)


def stack_flat_body(own, first, second, out):
    blocks, width = out.shape[1], out.shape[3]
    for slot, source in enumerate((own, first, second)):
        for q in range(blocks):
            out[slot, q] = source[:, q * width:(q + 1) * width]


def stack_body(own, first, second, out):
    for slot, source in enumerate((own, first, second)):
        out[slot] = source[...]


def operator_body(table_row, local_row, t0, t1, t2, c_high, c_low, p0, p1, p2, g_out, table, strain, strain_hl, pieces):
    blocks, rows, width = t0.shape[1], t0.shape[2], t0.shape[3]
    count = c_high.shape[0]
    for group, source in enumerate((t0, t1, t2)):
        for slot in range(3):
            def fill(q, carry, group=group, slot=slot, source=source):
                table[(group * 3 + slot) * blocks + q] = stacked_split(source[slot, q])
                return carry
            lax.fori_loop(0, blocks, fill, 0, unroll=True)
    strain[...] = jnp.zeros_like(strain)
    pieces[...] = jnp.zeros_like(pieces)

    def pull(chunk, carry):
        terms = []
        for place in range(CHUNK):
            k = chunk * CHUNK + place
            terms.append((local_row[k], times(dot_nt, table[table_row[k]], c_high[k], c_low[k])))
        for row, term in terms:
            strain[row] += term
        return carry

    lax.fori_loop(0, count // CHUNK, pull, 0)
    total = jnp.zeros((rows, rows), F32)
    for q in range(blocks):
        both = stacked_split(strain[q])
        strain_hl[q] = both
        total += gram(both, both)
    g_out[...] = total

    def push(chunk, carry):
        terms = []
        for place in range(CHUNK):
            k = chunk * CHUNK + place
            terms.append((table_row[k], times(dot_nn, strain_hl[local_row[k]], c_high[k], c_low[k])))
        for row, term in terms:
            pieces[row] += term
        return carry

    lax.fori_loop(0, count // CHUNK, push, 0)
    for group, target in enumerate((p0, p1, p2)):
        for slot in range(3):
            for q in range(blocks):
                target[slot, q] = pieces[(group * 3 + slot) * blocks + q]


def apply_couplings(tables, c_high, c_low, table_row, local_row):
    _, blocks, rows, width = tables[0].shape
    piece = pltpu.VMEM((3, blocks, rows, width), F32)
    return call(
        operator_body,
        [piece, piece, piece, pltpu.VMEM((rows, rows), F32)],
        2,
        (table_row, local_row, *tables, c_high, c_low),
        [
            pltpu.VMEM((9 * blocks, 2 * rows, width), BF16),
            pltpu.VMEM((blocks, rows, width), F32),
            pltpu.VMEM((blocks, 2 * rows, width), BF16),
            pltpu.VMEM((9 * blocks, rows, width), F32),
        ],
    )


def middle_body(p0, q1, q2, own, m0, m1, m2):
    m1[...] = p0[1] + q1[1] + q2[1]
    m2[...] = p0[2] + q1[2] + q2[2]
    m0[...] = p0[0] + q1[0] + q2[0] + own[...]


def returned(p0, p1, p2, own):
    q1 = swapped(p1, "col", 0)
    q2 = swapped(p2, "col", 1)
    shape = pltpu.VMEM(own.shape, F32)
    m0, m1, m2 = call(middle_body, [shape] * 3, 0, (p0, q1, q2, own))
    return m0, swapped(m1, "row", 0), swapped(m2, "row", 1)


def sum_body(m0, a, b, out):
    out[...] = m0[...] + a[...] + b[...]


def diag_body(vector, d_high, d_low, own, grams):
    g2 = jnp.zeros(grams.shape[1:], F32)
    g3 = jnp.zeros(grams.shape[1:], F32)
    for q in range(vector.shape[0]):
        both = stacked_split(vector[q])
        term = times(dot_nt, both, d_high[q], d_low[q])
        own[q] = term
        g2 += gram(both, both)
        g3 += gram(stacked_split(term), both)
    grams[0] = g2
    grams[1] = g3


def eliminated(matrix, right):
    size = matrix.shape[0]
    work = jnp.concatenate([matrix, right], axis=1)
    rows = lax.broadcasted_iota(jnp.int32, work.shape, 0)
    for k in range(size):
        pivot_row = work[k:k + 1, :] / work[k:k + 1, k:k + 1]
        work = jnp.where(rows == k, pivot_row, work - work[:, k:k + 1] * pivot_row)
    return work[:, size:]


def finish_body(grams, right, u, m0, a, b, x_out, r_out):
    size = grams.shape[0]
    g0, g1, g2, g3 = (grams[:, i * size:(i + 1) * size] for i in range(4))
    eye = (lax.broadcasted_iota(jnp.int32, (size, size), 0) == lax.broadcasted_iota(jnp.int32, (size, size), 1)).astype(F32)
    alpha = eliminated(g1, g0)
    inverse = eliminated(g0, eye)
    fresh = (g0 - full_nn(g1, alpha)) - full_tn(alpha, g1 - full_nn(g2, alpha))
    mix = eye + full_nn(inverse, fresh)
    e1 = full_nn(g1, mix) - full_nn(g2, alpha)
    e2 = full_nn(g2, mix) - full_nn(g3, alpha)
    curvature = full_tn(mix, e1) - full_tn(alpha, e2)
    second = eliminated(curvature, fresh)
    p = alpha + full_nn(mix, second)
    q = full_nn(alpha, second)
    width = u.shape[2]
    for block in range(u.shape[0]):
        lanes = slice(block * width, (block + 1) * width)
        w = m0[block] + a[block] + b[block]
        x_out[:, lanes] = full_tn(p, right[:, lanes]) - full_tn(q, u[block])
        r_out[:, lanes] = right[:, lanes] - full_tn(p, u[block]) + full_tn(q, w)


def total_over_devices(value):
    count = lax.axis_size("row") * lax.axis_size("col")
    for mask in (1, 2, 6, 8, 24, 32, 96):
        moved = lax.ppermute(value, ("row", "col"), [(i, i ^ mask) for i in range(count)])
        value = value + moved
    return value


def per_device(right_sides, diag_blocks, couplings, pair_index):
    blocks, width = diag_blocks.shape[0], diag_blocks.shape[1]
    rows = right_sides.shape[0]
    col_size = lax.axis_size("col")
    my_row, my_col = lax.axis_index("row"), lax.axis_index("col")
    local_row = pair_index[0] - (my_row * col_size + my_col) * blocks
    owner = pair_index[1] // blocks
    slot = slot_of(owner % col_size, my_col) * 3 + slot_of(owner // col_size, my_row)
    table_row = slot * blocks + pair_index[1] % blocks

    block_shape = pltpu.VMEM((blocks, rows, width), F32)
    stack_shape = pltpu.VMEM((3, blocks, rows, width), F32)
    gram_shape = pltpu.VMEM((2, rows, rows), F32)

    first = swapped(right_sides, "row", 0)
    second = swapped(right_sides, "row", 1)
    c_high, c_low, d_high, d_low, own, g01 = prepare(couplings, diag_blocks, right_sides)
    t0 = call(stack_flat_body, stack_shape, 0, (right_sides, first, second))
    tables = (t0, swapped(t0, "col", 0), swapped(t0, "col", 1))
    p0, p1, p2, g1s = apply_couplings(tables, c_high, c_low, table_row, local_row)
    m0, a, b = returned(p0, p1, p2, own)
    u = call(sum_body, block_shape, 0, (m0, a, b))

    first = swapped(u, "row", 0)
    second = swapped(u, "row", 1)
    own, g23 = call(diag_body, [block_shape, gram_shape], 0, (u, d_high, d_low))
    t0 = call(stack_body, stack_shape, 0, (u, first, second))
    tables = (t0, swapped(t0, "col", 0), swapped(t0, "col", 1))
    p0, p1, p2, g3s = apply_couplings(tables, c_high, c_low, table_row, local_row)
    grams = jnp.concatenate([g01[0], g01[1] + g1s, g23[0], g23[1] + g3s], axis=1)
    grams = total_over_devices(grams)
    m0, a, b = returned(p0, p1, p2, own)
    flat = jax.ShapeDtypeStruct(right_sides.shape, F32)
    return tuple(call(finish_body, [flat, flat], 0, (grams, right_sides, u, m0, a, b)))


def solution(mesh):
    return jax.shard_map(
        per_device,
        mesh=mesh,
        in_specs=(
            P(None, ("row", "col")),
            P(("row", "col"), None, None),
            P(("row", "col"), None, None),
            P(None, ("row", "col")),
        ),
        out_specs=(P(None, ("row", "col")), P(None, ("row", "col"))),
        check_vma=False,
    )
```

profile of v0, /device:TPU:0, one launch (start us, length us, event | category | flops | bytes accessed | tf_op | source)
XLA Modules:
  0.0 160.1 jit_solution(12930962207569437885)
XLA Ops:
  1.3 4.4 %collective-permute-start = (f32[32,2048]{1,0:T(8,128)}, f32[32,2048]{1,0:T(8,128)S(1)}, u32[]{:S(2)}, u32[]{:S(2)}) collective-permute-start(f32[32,2048]{1,0:T(8,128)} %right.3), channel_id=1, source_target_pairs={{0,8},{8,0},{16,24},{24,16},{32,40},{40,32},{48,56},{56,48},{64,72... | collective-permute-start | bytes 786440 | tf_op jit(solution)/shard_map/ppermute | solution.py:30
  5.7 6.2 %collective-permute-done.first = f32[32,2048]{1,0:T(8,128)S(1)} collective-permute-done((f32[32,2048]{1,0:T(8,128)}, f32[32,2048]{1,0:T(8,128)S(1)}, u32[]{:S(2)}, u32[]{:S(2)}) %collective-permute-start) | collective-permute-done | bytes 262176 | tf_op jit(solution)/shard_map/ppermute | solution.py:30
  13.7 3.3 %collective-permute-start.2 = (f32[3,8,32,256]{3,2,1,0:T(8,128)S(1)}, f32[3,8,32,256]{3,2,1,0:T(8,128)S(1)}, u32[]{:S(2)}, u32[]{:S(2)}) collective-permute-start(f32[3,8,32,256]{3,2,1,0:T(8,128)S(1)} %shard_map.60.t0), channel_id=1, source_target_pairs={{0,1},{1,0},{2,3},{3,2},{4,5},{5,4},{6,7},{7,6},{8,9},{9,8},{10,11... | collective-permute-start | bytes 2359304 | tf_op jit(solution)/shard_map/ppermute | solution.py:30
  19.5 11.2 %shard_map.59 = (bf16[64,256,256]{2,1,0:T(8,128)(2,1)S(1)}, bf16[64,256,256]{2,1,0:T(8,128)(2,1)S(1)}, bf16[8,256,256]{2,1,0:T(8,128)(2,1)S(1)}, bf16[8,256,256]...) custom-call(f32[64,256,256]{2,1,0:T(8,128)} %couplings.1, f32[8,256,256]{2,1,0:T(8,128)S(1)} %copy-done.3, ...), custom_call_target="tpu_custom_call" | custom-call | tf_op jit(solution)/shard_map/pallas_call | solution.py:111
  30.8 10.9 %shard_map.61 = (f32[3,8,32,256]{3,2,1,0:T(8,128)S(1)}, f32[3,8,32,256]{3,2,1,0:T(8,128)S(1)}, f32[3,8,32,256]{3,2,1,0:T(8,128)S(1)}, f32[32,32]{1,0:T(8,128)S(1)}) custom-call(s32[64]{0:T(128)S(1)} %fusion.table_row, s32[64]{0:T(128)S(1)} %subtract_bitcast_fusion.local_row, f32[3,8,32,256]{3,2,1,0:T(8,128)S(1)} %shard_map.60.t0, ...), custom_call_target="tpu_custom_call" | custom-call | tf_op jit(solution)/shard_map/pallas_call | solution.py:75
  44.2 1.8 %collective-permute-start.6 = (f32[8,32,256]{2,1,0:T(8,128)S(1)}, f32[8,32,256]{2,1,0:T(8,128)S(1)}, u32[]{:S(2)}, u32[]{:S(2)}) collective-permute-start(f32[8,32,256]{2,1,0:T(8,128)S(1)} %get-tuple-element.33), channel_id=1, source_target_pairs={{0,8},{8,0},{16,24},{24,16},{32,40},{40,32},{48,56},{56,48},{64,72... | collective-permute-start | bytes 786440 | tf_op jit(solution)/shard_map/ppermute | solution.py:30
  46.7 4.0 %collective-permute-done.6.a = f32[8,32,256]{2,1,0:T(8,128)S(1)} collective-permute-done((f32[8,32,256]{2,1,0:T(8,128)S(1)}, f32[8,32,256]{2,1,0:T(8,128)S(1)}, u32[]{:S(2)}, u32[]{:S(2)}) %collective-permute-start.6) | collective-permute-done | bytes 262176 | tf_op jit(solution)/shard_map/ppermute | solution.py:30
  51.4 8.4 %collective-permute-start.8 = (f32[8,32,256]{2,1,0:T(8,128)S(1)}, f32[8,32,256]{2,1,0:T(8,128)S(1)}, u32[]{:S(2)}, u32[]{:S(2)}) collective-permute-start(f32[8,32,256]{2,1,0:T(8,128)S(1)} %shard_map.63.vector.own.u), channel_id=1, source_target_pairs={{0,8},{8,0},{16,24},{24,16},{32,40},{40,32},{48,56},{56,48},{64,72... | collective-permute-start | bytes 786440 | tf_op jit(solution)/shard_map/ppermute | solution.py:30
  59.8 4.3 %collective-permute-done.8.first = f32[8,32,256]{2,1,0:T(8,128)S(1)} collective-permute-done((f32[8,32,256]{2,1,0:T(8,128)S(1)}, f32[8,32,256]{2,1,0:T(8,128)S(1)}, u32[]{:S(2)}, u32[]{:S(2)}) %collective-permute-start.8) | collective-permute-done | bytes 262176 | tf_op jit(solution)/shard_map/ppermute | solution.py:30
  65.1 17.6 %collective-permute-start.10 = (f32[3,8,32,256]{3,2,1,0:T(8,128)S(1)}, f32[3,8,32,256]{3,2,1,0:T(8,128)S(1)}, u32[]{:S(2)}, u32[]{:S(2)}) collective-permute-start(f32[3,8,32,256]{3,2,1,0:T(8,128)S(1)} %shard_map.65.t0), channel_id=1, source_target_pairs={{0,1},{1,0},{2,3},{3,2},{4,5},{5,4},{6,7},{7,6},{8,9},{9,8},{10,11... | collective-permute-start | bytes 2359304 | tf_op jit(solution)/shard_map/ppermute | solution.py:30
  82.7 1.9 %collective-permute-done.10.t1 = f32[3,8,32,256]{3,2,1,0:T(8,128)S(1)} collective-permute-done((f32[3,8,32,256]{3,2,1,0:T(8,128)S(1)}, f32[3,8,32,256]{3,2,1,0:T(8,128)S(1)}, u32[]{:S(2)}, u32[]{:S(2)}) %collective-permute-start.10) | collective-permute-done | bytes 786464 | tf_op jit(solution)/shard_map/ppermute | solution.py:30
  84.6 10.9 %shard_map.66 = (f32[3,8,32,256]{3,2,1,0:T(8,128)S(1)}, f32[3,8,32,256]{3,2,1,0:T(8,128)S(1)}, f32[3,8,32,256]{3,2,1,0:T(8,128)S(1)}, f32[32,32]{1,0:T(8,128)S(1)}) custom-call(s32[64]{0:T(128)S(1)} %fusion.table_row, s32[64]{0:T(128)S(1)} %subtract_bitcast_fusion.local_row, f32[3,8,32,256]{3,2,1,0:T(8,128)S(1)} %shard_map.65.t0, ...), custom_call_target="tpu_custom_call" | custom-call | tf_op jit(solution)/shard_map/pallas_call | solution.py:75
  95.5 7.8 %collective-permute-start.19 = (f32[3,8,32,256]{3,2,1,0:T(8,128)S(1)}, f32[3,8,32,256]{3,2,1,0:T(8,128)S(1)}, u32[]{:S(2)}, u32[]{:S(2)}) collective-permute-start(f32[3,8,32,256]{3,2,1,0:T(8,128)S(1)} %get-tuple-element.40), channel_id=1, source_target_pairs={{0,1},{1,0},{2,3},{3,2},{4,5},{5,4},{6,7},{7,6},{8,9},{9,8},{10,11... | collective-permute-start | bytes 2359304 | tf_op jit(solution)/shard_map/ppermute | solution.py:30
  104.0 2.2 %shard_map.64 = (f32[8,32,256]{2,1,0:T(8,128)S(1)}, f32[2,32,32]{2,1,0:T(8,128)S(1)}) custom-call(f32[8,32,256]{2,1,0:T(8,128)S(1)} %shard_map.63.vector.own.u, bf16[8,256,256]{2,1,0:T(8,128)(2,1)S(1)} %get-tuple-element.35.d_high, bf16[8,256,256]{2,1,0:T(8,128)(2,1)S(1)} %get-tuple-element.36.d_low), custom_call_target="tpu_custom_call" | custom-call | tf_op jit(solution)/shard_map/pallas_call | solution.py:75
  109.0 10.5 %collective-permute-start.12 = (f32[32,128]{1,0:T(8,128)S(1)}, f32[32,128]{1,0:T(8,128)S(1)}, u32[]{:S(2)}, u32[]{:S(2)}) collective-permute-start(f32[32,128]{1,0:T(8,128)S(1)} %pad_maximum_fusion), channel_id=1, source_target_pairs={{0,1},{1,0},{2,3},{3,2},{4,5},{5,4},{6,7},{7,6},{8,9},{9,8},{10,11... | collective-permute-start | bytes 49160 | tf_op jit(solution)/shard_map/ppermute | solution.py:272
  120.3 2.0 %collective-permute-start.13 = (f32[32,128]{1,0:T(8,128)S(1)}, f32[32,128]{1,0:T(8,128)S(1)}, u32[]{:S(2)}, u32[]{:S(2)}) collective-permute-start(f32[32,128]{1,0:T(8,128)S(1)} %add.55), channel_id=1, source_target_pairs={{0,2},{1,3},{2,0},{3,1},{4,6},{5,7},{6,4},{7,5},{8,10},{9,11},{10,... | collective-permute-start | bytes 49160 | tf_op jit(solution)/shard_map/ppermute | solution.py:272
  124.0 2.5 %collective-permute-start.14 = (f32[32,128]{1,0:T(8,128)S(1)}, f32[32,128]{1,0:T(8,128)S(1)}, u32[]{:S(2)}, u32[]{:S(2)}) collective-permute-start(f32[32,128]{1,0:T(8,128)S(1)} %add.56), channel_id=1, source_target_pairs={{0,6},{1,7},{2,4},{3,5},{4,2},{5,3},{6,0},{7,1},{8,14},{9,15},{10,... | collective-permute-start | bytes 49160 | tf_op jit(solution)/shard_map/ppermute | solution.py:272
  126.5 2.5 %collective-permute-done.14 = f32[32,128]{1,0:T(8,128)S(1)} collective-permute-done((f32[32,128]{1,0:T(8,128)S(1)}, f32[32,128]{1,0:T(8,128)S(1)}, u32[]{:S(2)}, u32[]{:S(2)}) %collective-permute-start.14) | collective-permute-done | bytes 16416 | tf_op jit(solution)/shard_map/ppermute | solution.py:272
  129.0 6.2 %collective-permute-start.15 = (f32[32,128]{1,0:T(8,128)S(1)}, f32[32,128]{1,0:T(8,128)S(1)}, u32[]{:S(2)}, u32[]{:S(2)}) collective-permute-start(f32[32,128]{1,0:T(8,128)S(1)} %add.57), channel_id=1, source_target_pairs={{0,8},{1,9},{2,10},{3,11},{4,12},{5,13},{6,14},{7,15},{8,0},{9,1},... | collective-permute-start | bytes 49160 | tf_op jit(solution)/shard_map/ppermute | solution.py:272
  136.9 2.7 %collective-permute-start.16 = (f32[32,128]{1,0:T(8,128)S(1)}, f32[32,128]{1,0:T(8,128)S(1)}, u32[]{:S(2)}, u32[]{:S(2)}) collective-permute-start(f32[32,128]{1,0:T(8,128)S(1)} %add.58), channel_id=1, source_target_pairs={{0,24},{1,25},{2,26},{3,27},{4,28},{5,29},{6,30},{7,31},{8,16},{9,... | collective-permute-start | bytes 49160 | tf_op jit(solution)/shard_map/ppermute | solution.py:272
  139.6 2.2 %collective-permute-done.16 = f32[32,128]{1,0:T(8,128)S(1)} collective-permute-done((f32[32,128]{1,0:T(8,128)S(1)}, f32[32,128]{1,0:T(8,128)S(1)}, u32[]{:S(2)}, u32[]{:S(2)}) %collective-permute-start.16) | collective-permute-done | bytes 16416 | tf_op jit(solution)/shard_map/ppermute | solution.py:272
  141.8 2.2 %collective-permute-start.17 = (f32[32,128]{1,0:T(8,128)S(1)}, f32[32,128]{1,0:T(8,128)S(1)}, u32[]{:S(2)}, u32[]{:S(2)}) collective-permute-start(f32[32,128]{1,0:T(8,128)S(1)} %add.59), channel_id=1, source_target_pairs={{0,32},{1,33},{2,34},{3,35},{4,36},{5,37},{6,38},{7,39},{8,40},{9,... | collective-permute-start | bytes 49160 | tf_op jit(solution)/shard_map/ppermute | solution.py:272
  145.7 3.8 %collective-permute-start.18 = (f32[32,128]{1,0:T(8,128)S(1)}, f32[32,128]{1,0:T(8,128)S(1)}, u32[]{:S(2)}, u32[]{:S(2)}) collective-permute-start(f32[32,128]{1,0:T(8,128)S(1)} %add.60), channel_id=1, source_target_pairs={{0,96},{1,97},{2,98},{3,99},{4,100},{5,101},{6,102},{7,103},{8,104... | collective-permute-start | bytes 49160 | tf_op jit(solution)/shard_map/ppermute | solution.py:272
  151.2 8.8 %shard_map.68 = (f32[32,2048]{1,0:T(8,128)}, f32[32,2048]{1,0:T(8,128)}) custom-call(f32[32,128]{1,0:T(8,128)S(1)} %add.61.grams, f32[32,2048]{1,0:T(8,128)S(1)} %copy-done.2, f32[8,32,256]{2,1,0:T(8,128)S(1)} %shard_map.63.vector.own.u, f32[8,32,256]{2,1,0:T(8,128)S(1)} %get-tuple-element.43.m0, f32[8,32,256]{2,1,0:T(8,128)S(1)} %collective-permute-done.21.a, ...), custom_call_target="tpu_custom_call" | custom-call | tf_op jit(solution)/shard_map/pallas_call | solution.py:75
  (56 shorter events, 21.0 us)
Async XLA Ops:
  0.6 5.1 %collective-permute-start.1 = (f32[32,2048]{1,0:T(8,128)}, f32[32,2048]{1,0:T(8,128)S(1)}, u32[]{:S(2)}, u32[]{:S(2)}) collective-permute-start(f32[32,2048]{1,0:T(8,128)} %right.3), channel_id=1, source_target_pairs={{8,16},{16,8},{24,32},{32,24},{40,48},{48,40},{56,64},{64,56},{72,... | collective-permute-start | bytes 786440 | tf_op jit(solution)/shard_map/ppermute | solution.py:30
  1.3 10.6 %collective-permute-start = (f32[32,2048]{1,0:T(8,128)}, f32[32,2048]{1,0:T(8,128)S(1)}, u32[]{:S(2)}, u32[]{:S(2)}) collective-permute-start(f32[32,2048]{1,0:T(8,128)} %right.3), channel_id=1, source_target_pairs={{0,8},{8,0},{16,24},{24,16},{32,40},{40,32},{48,56},{56,48},{64,72... | collective-permute-start | bytes 786440 | tf_op jit(solution)/shard_map/ppermute | solution.py:30
  12.9 17.8 %collective-permute-start.3 = (f32[3,8,32,256]{3,2,1,0:T(8,128)S(1)}, f32[3,8,32,256]{3,2,1,0:T(8,128)S(1)}, u32[]{:S(2)}, u32[]{:S(2)}) collective-permute-start(f32[3,8,32,256]{3,2,1,0:T(8,128)S(1)} %shard_map.60.t0), channel_id=1, source_target_pairs={{1,2},{2,1},{3,4},{4,3},{5,6},{6,5},{9,10},{10,9},{11,12},{12,11},... | collective-permute-start | bytes 2359304 | tf_op jit(solution)/shard_map/ppermute | solution.py:30
  13.7 17.1 %collective-permute-start.2 = (f32[3,8,32,256]{3,2,1,0:T(8,128)S(1)}, f32[3,8,32,256]{3,2,1,0:T(8,128)S(1)}, u32[]{:S(2)}, u32[]{:S(2)}) collective-permute-start(f32[3,8,32,256]{3,2,1,0:T(8,128)S(1)} %shard_map.60.t0), channel_id=1, source_target_pairs={{0,1},{1,0},{2,3},{3,2},{4,5},{5,4},{6,7},{7,6},{8,9},{9,8},{10,11... | collective-permute-start | bytes 2359304 | tf_op jit(solution)/shard_map/ppermute | solution.py:30
  41.7 2.4 %collective-permute-start.4 = (f32[3,8,32,256]{3,2,1,0:T(8,128)S(1)}, f32[3,8,32,256]{3,2,1,0:T(8,128)S(1)}, u32[]{:S(2)}, u32[]{:S(2)}) collective-permute-start(f32[3,8,32,256]{3,2,1,0:T(8,128)S(1)} %get-tuple-element.29), channel_id=1, source_target_pairs={{0,1},{1,0},{2,3},{3,2},{4,5},{5,4},{6,7},{7,6},{8,9},{9,8},{10,11... | collective-permute-start | bytes 2359304 | tf_op jit(solution)/shard_map/ppermute | solution.py:30
  41.8 2.2 %collective-permute-start.5 = (f32[3,8,32,256]{3,2,1,0:T(8,128)S(1)}, f32[3,8,32,256]{3,2,1,0:T(8,128)S(1)}, u32[]{:S(2)}, u32[]{:S(2)}) collective-permute-start(f32[3,8,32,256]{3,2,1,0:T(8,128)S(1)} %get-tuple-element.30), channel_id=1, source_target_pairs={{1,2},{2,1},{3,4},{4,3},{5,6},{6,5},{9,10},{10,9},{11,12},{12,11},... | collective-permute-start | bytes 2359304 | tf_op jit(solution)/shard_map/ppermute | solution.py:30
  44.2 6.5 %collective-permute-start.6 = (f32[8,32,256]{2,1,0:T(8,128)S(1)}, f32[8,32,256]{2,1,0:T(8,128)S(1)}, u32[]{:S(2)}, u32[]{:S(2)}) collective-permute-start(f32[8,32,256]{2,1,0:T(8,128)S(1)} %get-tuple-element.33), channel_id=1, source_target_pairs={{0,8},{8,0},{16,24},{24,16},{32,40},{40,32},{48,56},{56,48},{64,72... | collective-permute-start | bytes 786440 | tf_op jit(solution)/shard_map/ppermute | solution.py:30
  46.0 4.6 %collective-permute-start.7 = (f32[8,32,256]{2,1,0:T(8,128)S(1)}, f32[8,32,256]{2,1,0:T(8,128)S(1)}, u32[]{:S(2)}, u32[]{:S(2)}) collective-permute-start(f32[8,32,256]{2,1,0:T(8,128)S(1)} %get-tuple-element.34), channel_id=1, source_target_pairs={{8,16},{16,8},{24,32},{32,24},{40,48},{48,40},{56,64},{64,56},{72,... | collective-permute-start | bytes 786440 | tf_op jit(solution)/shard_map/ppermute | solution.py:30
  50.7 9.1 %collective-permute-start.9 = (f32[8,32,256]{2,1,0:T(8,128)S(1)}, f32[8,32,256]{2,1,0:T(8,128)S(1)}, u32[]{:S(2)}, u32[]{:S(2)}) collective-permute-start(f32[8,32,256]{2,1,0:T(8,128)S(1)} %shard_map.63.vector.own.u), channel_id=1, source_target_pairs={{8,16},{16,8},{24,32},{32,24},{40,48},{48,40},{56,64},{64,56},{72,... | collective-permute-start | bytes 786440 | tf_op jit(solution)/shard_map/ppermute | solution.py:30
  51.4 12.8 %collective-permute-start.8 = (f32[8,32,256]{2,1,0:T(8,128)S(1)}, f32[8,32,256]{2,1,0:T(8,128)S(1)}, u32[]{:S(2)}, u32[]{:S(2)}) collective-permute-start(f32[8,32,256]{2,1,0:T(8,128)S(1)} %shard_map.63.vector.own.u), channel_id=1, source_target_pairs={{0,8},{8,0},{16,24},{24,16},{32,40},{40,32},{48,56},{56,48},{64,72... | collective-permute-start | bytes 786440 | tf_op jit(solution)/shard_map/ppermute | solution.py:30
  64.2 87.0 %copy-start.2 = (f32[32,2048]{1,0:T(8,128)S(1)}, f32[32,2048]{1,0:T(8,128)}, u32[]{:S(2)}) copy-start(f32[32,2048]{1,0:T(8,128)} %right.3) | copy-start | bytes 786436
  64.2 18.5 %collective-permute-start.11 = (f32[3,8,32,256]{3,2,1,0:T(8,128)S(1)}, f32[3,8,32,256]{3,2,1,0:T(8,128)S(1)}, u32[]{:S(2)}, u32[]{:S(2)}) collective-permute-start(f32[3,8,32,256]{3,2,1,0:T(8,128)S(1)} %shard_map.65.t0), channel_id=1, source_target_pairs={{1,2},{2,1},{3,4},{4,3},{5,6},{6,5},{9,10},{10,9},{11,12},{12,11},... | collective-permute-start | bytes 2359304 | tf_op jit(solution)/shard_map/ppermute | solution.py:30
  65.1 19.5 %collective-permute-start.10 = (f32[3,8,32,256]{3,2,1,0:T(8,128)S(1)}, f32[3,8,32,256]{3,2,1,0:T(8,128)S(1)}, u32[]{:S(2)}, u32[]{:S(2)}) collective-permute-start(f32[3,8,32,256]{3,2,1,0:T(8,128)S(1)} %shard_map.65.t0), channel_id=1, source_target_pairs={{0,1},{1,0},{2,3},{3,2},{4,5},{5,4},{6,7},{7,6},{8,9},{9,8},{10,11... | collective-permute-start | bytes 2359304 | tf_op jit(solution)/shard_map/ppermute | solution.py:30
  95.5 10.8 %collective-permute-start.19 = (f32[3,8,32,256]{3,2,1,0:T(8,128)S(1)}, f32[3,8,32,256]{3,2,1,0:T(8,128)S(1)}, u32[]{:S(2)}, u32[]{:S(2)}) collective-permute-start(f32[3,8,32,256]{3,2,1,0:T(8,128)S(1)} %get-tuple-element.40), channel_id=1, source_target_pairs={{0,1},{1,0},{2,3},{3,2},{4,5},{5,4},{6,7},{7,6},{8,9},{9,8},{10,11... | collective-permute-start | bytes 2359304 | tf_op jit(solution)/shard_map/ppermute | solution.py:30
  103.2 3.0 %collective-permute-start.20 = (f32[3,8,32,256]{3,2,1,0:T(8,128)S(1)}, f32[3,8,32,256]{3,2,1,0:T(8,128)S(1)}, u32[]{:S(2)}, u32[]{:S(2)}) collective-permute-start(f32[3,8,32,256]{3,2,1,0:T(8,128)S(1)} %get-tuple-element.41), channel_id=1, source_target_pairs={{1,2},{2,1},{3,4},{4,3},{5,6},{6,5},{9,10},{10,9},{11,12},{12,11},... | collective-permute-start | bytes 2359304 | tf_op jit(solution)/shard_map/ppermute | solution.py:30
  106.4 44.8 %collective-permute-start.21 = (f32[8,32,256]{2,1,0:T(8,128)S(1)}, f32[8,32,256]{2,1,0:T(8,128)S(1)}, u32[]{:S(2)}, u32[]{:S(2)}) collective-permute-start(f32[8,32,256]{2,1,0:T(8,128)S(1)} %get-tuple-element.44), channel_id=1, source_target_pairs={{0,8},{8,0},{16,24},{24,16},{32,40},{40,32},{48,56},{56,48},{64,72... | collective-permute-start | bytes 786440 | tf_op jit(solution)/shard_map/ppermute | solution.py:30
  108.2 43.0 %collective-permute-start.22 = (f32[8,32,256]{2,1,0:T(8,128)S(1)}, f32[8,32,256]{2,1,0:T(8,128)S(1)}, u32[]{:S(2)}, u32[]{:S(2)}) collective-permute-start(f32[8,32,256]{2,1,0:T(8,128)S(1)} %get-tuple-element.45), channel_id=1, source_target_pairs={{8,16},{16,8},{24,32},{32,24},{40,48},{48,40},{56,64},{64,56},{72,... | collective-permute-start | bytes 786440 | tf_op jit(solution)/shard_map/ppermute | solution.py:30
  109.0 11.3 %collective-permute-start.12 = (f32[32,128]{1,0:T(8,128)S(1)}, f32[32,128]{1,0:T(8,128)S(1)}, u32[]{:S(2)}, u32[]{:S(2)}) collective-permute-start(f32[32,128]{1,0:T(8,128)S(1)} %pad_maximum_fusion), channel_id=1, source_target_pairs={{0,1},{1,0},{2,3},{3,2},{4,5},{5,4},{6,7},{7,6},{8,9},{9,8},{10,11... | collective-permute-start | bytes 49160 | tf_op jit(solution)/shard_map/ppermute | solution.py:272
  120.3 3.7 %collective-permute-start.13 = (f32[32,128]{1,0:T(8,128)S(1)}, f32[32,128]{1,0:T(8,128)S(1)}, u32[]{:S(2)}, u32[]{:S(2)}) collective-permute-start(f32[32,128]{1,0:T(8,128)S(1)} %add.55), channel_id=1, source_target_pairs={{0,2},{1,3},{2,0},{3,1},{4,6},{5,7},{6,4},{7,5},{8,10},{9,11},{10,... | collective-permute-start | bytes 49160 | tf_op jit(solution)/shard_map/ppermute | solution.py:272
  124.0 4.9 %collective-permute-start.14 = (f32[32,128]{1,0:T(8,128)S(1)}, f32[32,128]{1,0:T(8,128)S(1)}, u32[]{:S(2)}, u32[]{:S(2)}) collective-permute-start(f32[32,128]{1,0:T(8,128)S(1)} %add.56), channel_id=1, source_target_pairs={{0,6},{1,7},{2,4},{3,5},{4,2},{5,3},{6,0},{7,1},{8,14},{9,15},{10,... | collective-permute-start | bytes 49160 | tf_op jit(solution)/shard_map/ppermute | solution.py:272
  129.0 7.9 %collective-permute-start.15 = (f32[32,128]{1,0:T(8,128)S(1)}, f32[32,128]{1,0:T(8,128)S(1)}, u32[]{:S(2)}, u32[]{:S(2)}) collective-permute-start(f32[32,128]{1,0:T(8,128)S(1)} %add.57), channel_id=1, source_target_pairs={{0,8},{1,9},{2,10},{3,11},{4,12},{5,13},{6,14},{7,15},{8,0},{9,1},... | collective-permute-start | bytes 49160 | tf_op jit(solution)/shard_map/ppermute | solution.py:272
  136.9 4.9 %collective-permute-start.16 = (f32[32,128]{1,0:T(8,128)S(1)}, f32[32,128]{1,0:T(8,128)S(1)}, u32[]{:S(2)}, u32[]{:S(2)}) collective-permute-start(f32[32,128]{1,0:T(8,128)S(1)} %add.58), channel_id=1, source_target_pairs={{0,24},{1,25},{2,26},{3,27},{4,28},{5,29},{6,30},{7,31},{8,16},{9,... | collective-permute-start | bytes 49160 | tf_op jit(solution)/shard_map/ppermute | solution.py:272
  141.8 3.9 %collective-permute-start.17 = (f32[32,128]{1,0:T(8,128)S(1)}, f32[32,128]{1,0:T(8,128)S(1)}, u32[]{:S(2)}, u32[]{:S(2)}) collective-permute-start(f32[32,128]{1,0:T(8,128)S(1)} %add.59), channel_id=1, source_target_pairs={{0,32},{1,33},{2,34},{3,35},{4,36},{5,37},{6,38},{7,39},{8,40},{9,... | collective-permute-start | bytes 49160 | tf_op jit(solution)/shard_map/ppermute | solution.py:272
  145.7 5.5 %collective-permute-start.18 = (f32[32,128]{1,0:T(8,128)S(1)}, f32[32,128]{1,0:T(8,128)S(1)}, u32[]{:S(2)}, u32[]{:S(2)}) collective-permute-start(f32[32,128]{1,0:T(8,128)S(1)} %add.60), channel_id=1, source_target_pairs={{0,96},{1,97},{2,98},{3,99},{4,100},{5,101},{6,102},{7,103},{8,104... | collective-permute-start | bytes 49160 | tf_op jit(solution)/shard_map/ppermute | solution.py:272
  (4 other events, 14.7 us)
where the time goes:
time: 161 us; the launch traced here: 160 us
  starting transfers between devices  80.6 us (50%)
  Pallas kernels  44.5 us (28%)
  waiting for transfers between devices  30.5 us (19%)
  local copies, waits for them, and re-layouts  3.51 us (2%)
    ppermute x16, starting transfers between devices, swapped(): return lax.ppermute(value, axis, pairs_of(lax.axis_size(axis), shift))  50.9 us
    pallas_call x9, Pallas kernels, call(): pl.pallas_call(body, out_shape=out_shape, in_specs=[SMEM_SPEC] * n_smem +...  33.3 us
    ppermute x7, starting transfers between devices, total_over_devices(): lax.ppermute(value, ('row', 'col'), [(i, i ^ mask) for i in range(count)])  29.7 us
    ppermute x16, waiting for transfers between devices, swapped(): return lax.ppermute(value, axis, pairs_of(lax.axis_size(axis), shift))  18 us
    ppermute x7, waiting for transfers between devices, total_over_devices(): lax.ppermute(value, ('row', 'col'), [(i, i ^ mask) for i in range(count)])  12.5 us
    pallas_call x1, Pallas kernels, prepare(): pl.pallas_call(prepare_body, grid=(blocks,), in_specs=[pl.BlockSpec((per,...  11.2 us
    unnamed x10, local copies, waits for them, and re-layouts  3.5 us
  transfers between devices with their start and end apart: 23, of which 12 were waited for; matrix products, arithmetic and copies ran while one was open for 0% of the time, Pallas kernels for 8%

commit v1 on v0

v1 whole, which is shorter than its diff:
```python
import jax
import jax.numpy as jnp
from jax import lax
from jax.experimental import pallas as pl
from jax.experimental.pallas import tpu as pltpu
from jax.sharding import PartitionSpec as P

F32 = jnp.float32
BF16 = jnp.bfloat16
HIGHEST = lax.Precision.HIGHEST
VMEM_SPEC = pl.BlockSpec(memory_space=pltpu.VMEM)
SMEM_SPEC = pl.BlockSpec(memory_space=pltpu.SMEM)
CHUNK = 8
HALVES = 2
TOKEN = pltpu.VMEM((8, 128), F32)


def in_vmem(value):
    return pltpu.with_memory_space_constraint(value, pltpu.VMEM)


def in_hbm(value):
    return pltpu.with_memory_space_constraint(value, pltpu.HBM)


def pairs_of(count, shift):
    found = []
    for place in range(count):
        partner = ((place + shift) ^ 1) - shift
        if 0 <= partner < count:
            found.append((place, partner))
    return found


def swapped(value, axis, shift):
    return lax.ppermute(value, axis, pairs_of(lax.axis_size(axis), shift))


def slot_of(target, mine):
    return jnp.where(target == mine, 0, jnp.where(target == (mine ^ 1), 1, 2))


def split(value):
    high = value.astype(BF16)
    return high, (value - high.astype(F32)).astype(BF16)


def dot_nt(left, right):
    return lax.dot_general(left, right, (((1,), (1,)), ((), ())), preferred_element_type=F32)


def dot_nn(left, right):
    return lax.dot_general(left, right, (((1,), (0,)), ((), ())), preferred_element_type=F32)


def full_nn(left, right):
    return lax.dot_general(left, right, (((1,), (0,)), ((), ())), precision=HIGHEST, preferred_element_type=F32)


def full_tn(left, right):
    return lax.dot_general(left, right, (((0,), (0,)), ((), ())), precision=HIGHEST, preferred_element_type=F32)


def gram(left, right):
    both = dot_nt(left, right)
    half = both.shape[0] // 2
    return both[:half, :half] + both[:half, half:] + both[half:, :half] + both[half:, half:]


def times(dot, stacked, high, low):
    half = stacked.shape[0] // 2
    first = dot(stacked, high)
    return first[:half] + first[half:] + dot(stacked[:half], low)


def stacked_split(value):
    return jnp.concatenate(split(value), axis=0)


def call(body, out_shape, n_smem, args, scratch=(), aliases=None, limit=12 << 20):
    return pl.pallas_call(
        body,
        out_shape=out_shape,
        in_specs=[SMEM_SPEC] * n_smem + [VMEM_SPEC] * (len(args) - n_smem),
        out_specs=jax.tree.map(lambda _: VMEM_SPEC, out_shape),
        scratch_shapes=list(scratch),
        name=body.__name__,
        input_output_aliases=aliases or {},
        compiler_params=pltpu.CompilerParams(vmem_limit_bytes=limit),
    )(*args[:n_smem], *[in_vmem(a) for a in args[n_smem:]])


def prepare_body(couplings, c_high, c_low, token):
    per = couplings.shape[0]
    first = pl.program_id(0) * per
    token[...] = jnp.zeros_like(token)
    for place in range(per):
        high, low = split(couplings[place])
        c_high[first + place] = high
        c_low[first + place] = low


def prepare(couplings, part):
    count, width = couplings.shape[0] // HALVES, couplings.shape[1]
    steps = count // CHUNK
    half = pltpu.VMEM((count, width, width), BF16)
    return pl.pallas_call(
        prepare_body,
        grid=(steps,),
        in_specs=[pl.BlockSpec((CHUNK, width, width), lambda i: (i + part * steps, 0, 0))],
        out_specs=[VMEM_SPEC] * 3,
        out_shape=[half, half, TOKEN],
        name="prepare",
        compiler_params=pltpu.CompilerParams(vmem_limit_bytes=12 << 20),
    )(in_hbm(couplings))


def block_of(source, q, width):
    return source[q] if len(source.shape) == 3 else source[:, q * width:(q + 1) * width]


def stack_body(first, second, *rest):
    out = rest[-1]
    blocks, width = out.shape[1], out.shape[3]
    for slot, source in enumerate((first, second)):
        for q in range(blocks):
            out[slot, q] = block_of(source, q, width)


def accumulate(dot, far, routes, near, source_row, target_row, source, target, halves):
    for half in range(HALVES):
        c_high, c_low = halves[2 * half], halves[2 * half + 1]

        def step(chunk, carry):
            terms = []
            for place in range(CHUNK):
                i = chunk * CHUNK + place
                k = routes[half, 0, i]
                terms.append((routes[half, target_row, i], times(dot, source[routes[half, source_row, i]], c_high[k], c_low[k])))
            for row, term in terms:
                target[row] += term
            return carry

        edge = near[half] // CHUNK
        first, last = (edge, routes.shape[2] // CHUNK) if far else (0, edge)
        lax.fori_loop(first, last, step, 0)


def pull_near_body(routes, near, own, ra, rb, ca, cb, *refs):
    *halves, table, strain = refs
    blocks, width = strain.shape[0], strain.shape[2]
    for slot, source in enumerate((own, ra, rb, ca, cb)):
        for q in range(blocks):
            table[slot * blocks + q] = stacked_split(block_of(source, q, width))
    strain[...] = jnp.zeros_like(strain)
    accumulate(dot_nt, False, routes, near, 1, 2, table, strain, halves)


def pull_far_body(routes, near, table_in, strain_in, da, db, *refs):
    halves, refs = refs[:2 * HALVES], refs[2 * HALVES:]
    *grams, table, strain_hl, g_out, strain = refs
    blocks = strain.shape[0]
    for group, source in enumerate((da, db)):
        for slot in range(2):
            for q in range(blocks):
                table[(5 + 2 * group + slot) * blocks + q] = stacked_split(source[slot, q])
    strain[...] = strain_in[...]
    accumulate(dot_nt, True, routes, near, 1, 2, table, strain, halves)
    total = jnp.zeros((strain.shape[1],) * 2, F32)
    for q in range(blocks):
        both = stacked_split(strain[q])
        strain_hl[q] = both
        total += gram(both, both)
    if not grams:
        g_out[...] = total
    else:
        g01, g1, g23 = grams
        size = total.shape[0]
        for i, part in enumerate((g01[0], g01[1] + g1[...], g23[0], g23[1] + total)):
            g_out[:, i * size:(i + 1) * size] = part


def push_far_body(routes, near, strain_hl, *refs):
    *halves, pieces, da, db = refs
    blocks = strain_hl.shape[0]
    pieces[...] = jnp.zeros_like(pieces)
    accumulate(dot_nn, True, routes, near, 2, 1, strain_hl, pieces, halves)
    for group, target in enumerate((da, db)):
        for slot in range(2):
            for q in range(blocks):
                target[slot, q] = pieces[(5 + 2 * group + slot) * blocks + q]


def push_near_body(routes, near, strain_hl, *refs):
    halves, pieces_in = refs[:2 * HALVES], refs[2 * HALVES]
    own, ra, rb, ca, cb, pieces = refs[-6:]
    blocks = strain_hl.shape[0]
    pieces[...] = pieces_in[:pieces.shape[0]]
    accumulate(dot_nn, False, routes, near, 2, 1, strain_hl, pieces, halves)
    for slot, target in enumerate((own, ra, rb, ca, cb)):
        for q in range(blocks):
            target[q] = pieces[slot * blocks + q]


def diag_body(vector, diag, own, grams):
    size = grams.shape[1]
    first = jnp.zeros((size, size), F32)
    second = jnp.zeros((size, size), F32)
    width = diag.shape[1]
    for q in range(diag.shape[0]):
        both = stacked_split(block_of(vector, q, width))
        term = times(dot_nn, both, *split(diag[q]))
        own[q] = term
        first += gram(both, both)
        second += gram(stacked_split(term), both)
    grams[0] = first
    grams[1] = second


def middle_body(ra, rb, qa, qb, ma, mb):
    ma[...] = ra[...] + qa[0] + qb[0]
    mb[...] = rb[...] + qa[1] + qb[1]


def middle_gram_body(ra, rb, qa, qb, g, moved, ma, mb, g_out):
    middle_body(ra, rb, qa, qb, ma, mb)
    g_out[...] = g[...] + moved[...]


def sum_body(own, diag, ca, cb, ra, rb, out):
    out[...] = (own[...] + diag[...]) + (ca[...] + cb[...]) + (ra[...] + rb[...])


def eliminated(matrix, right):
    size = matrix.shape[0]
    work = jnp.concatenate([matrix, right], axis=1)
    rows = lax.broadcasted_iota(jnp.int32, work.shape, 0)
    for k in range(0, size, 2):
        upper, lower = work[k:k + 1, :], work[k + 1:k + 2, :]
        upper = upper / upper[:, k:k + 1]
        lower = lower - lower[:, k:k + 1] * upper
        lower = lower / lower[:, k + 1:k + 2]
        upper = upper - upper[:, k + 1:k + 2] * lower
        rest = work - work[:, k:k + 1] * upper - work[:, k + 1:k + 2] * lower
        work = jnp.where(rows == k, upper, jnp.where(rows == k + 1, lower, rest))
    return work[:, size:]


def finish_body(grams, moved, right, u, own, diag, ca, cb, ra, rb, x_out, r_out):
    size = grams.shape[0]
    total = grams[...] + moved[...]
    g0, g1, g2, g3 = (total[:, i * size:(i + 1) * size] for i in range(4))
    eye = (lax.broadcasted_iota(jnp.int32, (size, size), 0) == lax.broadcasted_iota(jnp.int32, (size, size), 1)).astype(F32)
    alpha = eliminated(g1, g0)
    inverse = eliminated(g0, eye)
    fresh = (g0 - full_nn(g1, alpha)) - full_tn(alpha, g1 - full_nn(g2, alpha))
    mix = eye + full_nn(inverse, fresh)
    e1 = full_nn(g1, mix) - full_nn(g2, alpha)
    e2 = full_nn(g2, mix) - full_nn(g3, alpha)
    curvature = full_tn(mix, e1) - full_tn(alpha, e2)
    second = eliminated(curvature, fresh)
    p = alpha + full_nn(mix, second)
    q = full_nn(alpha, second)
    width = u.shape[2]
    for block in range(u.shape[0]):
        lanes = slice(block * width, (block + 1) * width)
        w = (own[block] + diag[block]) + (ca[block] + cb[block]) + (ra[block] + rb[block])
        x_out[:, lanes] = full_tn(p, right[:, lanes]) - full_tn(q, u[block])
        r_out[:, lanes] = right[:, lanes] - full_tn(p, u[block]) + full_tn(q, w)


MASKS = (1, 2, 6, 8, 24, 32, 96)


def exchanged(value, mask):
    count = lax.axis_size("row") * lax.axis_size("col")
    return lax.ppermute(value, ("row", "col"), [(i, i ^ mask) for i in range(count)])


def routing(pair_index, blocks):
    count = pair_index.shape[1]
    col_size = lax.axis_size("col")
    my_row, my_col = lax.axis_index("row"), lax.axis_index("col")
    local_row = pair_index[0] - (my_row * col_size + my_col) * blocks
    owner = pair_index[1] // blocks
    row_slot = slot_of(owner // col_size, my_row)
    col_slot = slot_of(owner % col_size, my_col)
    far = (row_slot > 0) & (col_slot > 0)
    slot = jnp.where(far, 2 + 2 * col_slot + row_slot, jnp.where(col_slot > 0, 2 + col_slot, row_slot))
    table_row = slot * blocks + pair_index[1] % blocks
    count = count // HALVES
    number = jnp.arange(count, dtype=jnp.int32)
    far = far.reshape(HALVES, count)
    key = jnp.where(far, count, 0) + number
    rank = jnp.sum((key[:, None, :] < key[:, :, None]).astype(jnp.int32), axis=2)
    placed = rank[:, None, :] == number[:, None]
    columns = [jnp.broadcast_to(number, far.shape), table_row.reshape(far.shape), local_row.reshape(far.shape)]
    routes = jnp.stack([jnp.sum(jnp.where(placed, c[:, None, :], 0), axis=2) for c in columns], axis=1)
    near = count - jnp.sum(far.astype(jnp.int32), axis=1)
    return routes, near


def per_device(right_sides, diag_blocks, couplings, pair_index):
    blocks, width = diag_blocks.shape[0], diag_blocks.shape[1]
    rows = right_sides.shape[0]
    block_shape = pltpu.VMEM((blocks, rows, width), F32)
    pair_shape = pltpu.VMEM((2, blocks, rows, width), F32)
    table_shape = pltpu.VMEM((9 * blocks, 2 * rows, width), BF16)
    split_shape = pltpu.VMEM((blocks, 2 * rows, width), BF16)
    pieces_shape = pltpu.VMEM((9 * blocks, rows, width), F32)
    near_pieces_shape = pltpu.VMEM((5 * blocks, rows, width), F32)
    gram_shape = pltpu.VMEM((rows, rows), F32)
    grams_shape = pltpu.VMEM((2, rows, rows), F32)
    all_grams_shape = pltpu.VMEM((rows, 4 * rows), F32)

    def spread(vector, *after):
        ra, rb = swapped(vector, "row", 0), swapped(vector, "row", 1)
        ca, cb = swapped(vector, "col", 0), swapped(vector, "col", 1)
        both = call(stack_body, pair_shape, 0, (ra, rb) + (after or (ca, cb)))
        return (vector, ra, rb, ca, cb), swapped(both, "col", 0), swapped(both, "col", 1)

    def pulled(near_tables, da, db, split_couplings, *grams):
        table, strain = call(pull_near_body, [table_shape, block_shape], 2, (routes, near, *near_tables, *split_couplings))
        _, strain_hl, g = call(
            pull_far_body, [table_shape, split_shape, all_grams_shape if grams else gram_shape], 2,
            (routes, near, table, strain, da, db, *split_couplings, *grams), [block_shape], aliases={2: 0})
        return strain_hl, g

    def pushed(strain_hl, split_couplings, *after):
        pieces, da, db = call(push_far_body, [pieces_shape, pair_shape, pair_shape], 2, (routes, near, strain_hl, *split_couplings))
        da, db = swapped(da, "col", 0), swapped(db, "col", 1)
        own, ra, rb, ca, cb = call(
            push_near_body, [block_shape] * 5, 2, (routes, near, strain_hl, *split_couplings, pieces, *after), [near_pieces_shape])
        return own, ra, rb, swapped(ca, "col", 0), swapped(cb, "col", 1), da, db

    routes, near = routing(pair_index, blocks)
    *early, token = prepare(couplings, 0)
    near_tables, da, db = spread(right_sides, token)
    *late, _ = prepare(couplings, 1)
    split_couplings = early + late
    strain_hl, g1s = pulled(near_tables, da, db, split_couplings)
    own, ra, rb, ca, cb, da, db = pushed(strain_hl, split_couplings)
    diag, g01 = call(diag_body, [block_shape, grams_shape], 0, (right_sides, diag_blocks))
    ra, rb = call(middle_body, [block_shape] * 2, 0, (ra, rb, da, db))
    ra, rb = swapped(ra, "row", 0), swapped(rb, "row", 1)
    u = call(sum_body, block_shape, 0, (own, diag, ca, cb, ra, rb))

    near_tables, da, db = spread(u)
    diag, g23 = call(diag_body, [block_shape, grams_shape], 0, (u, diag_blocks))
    strain_hl, grams = pulled(near_tables, da, db, split_couplings, g01, g1s, g23)
    grams = grams + exchanged(grams, MASKS[0])
    own, ra, rb, ca, cb, da, db = pushed(strain_hl, split_couplings, grams)
    for mask in MASKS[1:3]:
        grams = grams + exchanged(grams, mask)
    ra, rb, grams = call(
        middle_gram_body, [block_shape] * 2 + [all_grams_shape], 0,
        (ra, rb, da, db, grams, exchanged(grams, MASKS[3])))
    ra, rb = swapped(ra, "row", 0), swapped(rb, "row", 1)
    for mask in MASKS[4:6]:
        grams = grams + exchanged(grams, mask)
    flat = jax.ShapeDtypeStruct(right_sides.shape, F32)
    return tuple(call(
        finish_body, [flat, flat], 0,
        (grams, exchanged(grams, MASKS[6]), right_sides, u, own, diag, ca, cb, ra, rb)))


def solution(mesh):
    return jax.shard_map(
        per_device,
        mesh=mesh,
        in_specs=(
            P(None, ("row", "col")),
            P(("row", "col"), None, None),
            P(("row", "col"), None, None),
            P(None, ("row", "col")),
        ),
        out_specs=(P(None, ("row", "col")), P(None, ("row", "col"))),
        check_vma=False,
    )
```

time: 161 us -> 151 us (0.938)
  starting transfers between devices: 80.6 us -> 69.6 us
  Pallas kernels: 44.5 us -> 48.6 us
  local copies, waits for them, and re-layouts: 3.51 us -> 0.18 us
    ppermute x16 -> x24, waiting for transfers between devices: 18 us -> 9.91 us  [swapped(): return lax.ppermute(value, axis, pairs_of(lax.axis_size(axis), shift))]
    ppermute x7, waiting for transfers between devices: 12.5 us -> 19.7 us  [exchanged(): lax.ppermute(value, ('row', 'col'), [(i, i ^ mask) for i in range(count)])]
    ppermute x16 -> x24, starting transfers between devices: 50.9 us -> 44 us  [swapped(): return lax.ppermute(value, axis, pairs_of(lax.axis_size(axis), shift))]
    pallas_call x9 -> x16, Pallas kernels: 33.3 us -> 39.1 us  [call(): pl.pallas_call(body, out_shape=out_shape, in_specs=[SMEM_SPEC] * n_smem +...]
    ppermute x7, starting transfers between devices: 29.7 us -> 25.6 us  [exchanged(): lax.ppermute(value, ('row', 'col'), [(i, i ^ mask) for i in range(count)])]
    unnamed x10 -> x4, local copies, waits for them, and re-layouts: 3.5 us -> 0.01 us
    pallas_call x1 -> x2, Pallas kernels: 11.2 us -> 9.54 us  [prepare(): pl.pallas_call(prepare_body, grid=(steps,), in_specs=[pl.BlockSpec((CHUNK...]
  transfers between devices with their start and end apart: 23 -> 31, of which waited for: 12 -> 9; matrix products, arithmetic and copies ran while one was open for 0% -> 1% of each run, Pallas kernels for 8% -> 20%
where the time goes in v1:
time: 151 us; the launch traced here: 150 us
  starting transfers between devices  69.6 us (46%)
  Pallas kernels  48.6 us (32%)
  waiting for transfers between devices  29.6 us (20%)
    ppermute x24, starting transfers between devices, swapped(): return lax.ppermute(value, axis, pairs_of(lax.axis_size(axis), shift))  44 us
    pallas_call x16, Pallas kernels, call(): pl.pallas_call(body, out_shape=out_shape, in_specs=[SMEM_SPEC] * n_smem +...  39.1 us
    ppermute x7, starting transfers between devices, exchanged(): lax.ppermute(value, ('row', 'col'), [(i, i ^ mask) for i in range(count)])  25.6 us
    ppermute x7, waiting for transfers between devices, exchanged(): lax.ppermute(value, ('row', 'col'), [(i, i ^ mask) for i in range(count)])  19.7 us
    ppermute x24, waiting for transfers between devices, swapped(): return lax.ppermute(value, axis, pairs_of(lax.axis_size(axis), shift))  9.91 us
    pallas_call x2, Pallas kernels, prepare(): pl.pallas_call(prepare_body, grid=(steps,), in_specs=[pl.BlockSpec((CHUNK...  9.54 us
  transfers between devices with their start and end apart: 31, of which 9 were waited for; matrix products, arithmetic and copies ran while one was open for 1% of the time, Pallas kernels for 20%

profile of v1, /device:TPU:0, one launch (start us, length us, event | category | flops | bytes accessed | tf_op | source)
XLA Modules:
  0.0 150.3 jit_solution(13985207337398945822)
XLA Ops:
  1.3 3.4 %collective-permute-start.2 = (f32[32,2048]{1,0:T(8,128)}, f32[32,2048]{1,0:T(8,128)S(1)}, u32[]{:S(2)}, u32[]{:S(2)}) collective-permute-start(f32[32,2048]{1,0:T(8,128)} %right.1), channel_id=1, source_target_pairs={{0,1},{1,0},{2,3},{3,2},{4,5},{5,4},{6,7},{7,6},{8,9},{9,8},{10,11... | collective-permute-start | bytes 786440 | tf_op jit(solution)/shard_map/ppermute | solution.py:36
  5.4 4.3 %collective-permute-start = (f32[32,2048]{1,0:T(8,128)}, f32[32,2048]{1,0:T(8,128)S(1)}, u32[]{:S(2)}, u32[]{:S(2)}) collective-permute-start(f32[32,2048]{1,0:T(8,128)} %right.1), channel_id=1, source_target_pairs={{0,8},{8,0},{16,24},{24,16},{32,40},{40,32},{48,56},{56,48},{64,72... | collective-permute-start | bytes 786440 | tf_op jit(solution)/shard_map/ppermute | solution.py:36
  10.8 4.6 %prepare.2 = (bf16[32,256,256]{2,1,0:T(8,128)(2,1)S(1)}, bf16[32,256,256]{2,1,0:T(8,128)(2,1)S(1)}, f32[8,128]{1,0:T(8,128)S(1)}) custom-call(f32[64,256,256]{2,1,0:T(8,128)} %couplings.3), custom_call_target="tpu_custom_call" | custom-call | tf_op jit(solution)/shard_map/prepare/pallas_call | solution.py:107
  16.9 3.3 %collective-permute-start.4 = (f32[2,8,32,256]{3,2,1,0:T(8,128)S(1)}, f32[2,8,32,256]{3,2,1,0:T(8,128)S(1)}, u32[]{:S(2)}, u32[]{:S(2)}) collective-permute-start(f32[2,8,32,256]{3,2,1,0:T(8,128)S(1)} %stack_body.2), channel_id=1, source_target_pairs={{0,1},{1,0},{2,3},{3,2},{4,5},{5,4},{6,7},{7,6},{8,9},{9,8},{10,11... | collective-permute-start | bytes 1572872 | tf_op jit(solution)/shard_map/ppermute | solution.py:36
  20.6 4.9 %prepare.3 = (bf16[32,256,256]{2,1,0:T(8,128)(2,1)S(1)}, bf16[32,256,256]{2,1,0:T(8,128)(2,1)S(1)}, f32[8,128]{1,0:T(8,128)}) custom-call(f32[64,256,256]{2,1,0:T(8,128)} %couplings.3), custom_call_target="tpu_custom_call" | custom-call | tf_op jit(solution)/shard_map/prepare/pallas_call | solution.py:107
  25.6 5.2 %pull_near_body.2 = (bf16[72,64,256]{2,1,0:T(8,128)(2,1)S(1)}, f32[8,32,256]{2,1,0:T(8,128)S(1)}) custom-call(s32[2,3,32]{2,1,0:T(4,128)S(1)} %pad_add_fusion.routes, s32[2]{0:T(128)S(1)} %broadcast_subtract_fusion.near, f32[32,2048]{1,0:T(8,128)S(1)} %copy-done.1, f32[32,2048]{1,0:T(8,128)S(1)} %collective-permute-done.ra.first, ...), custom_call_target="tpu_custom_call" | custom-call | tf_op jit(solution)/shard_map/pull_near_body/pallas_call | solution.py:81
  35.9 3.5 %push_near_body.2 = (f32[8,32,256]{2,1,0:T(8,128)S(1)}, f32[8,32,256]{2,1,0:T(8,128)S(1)}, f32[8,32,256]{2,1,0:T(8,128)S(1)}, f32[8,32,256]{2,1,0:T(8,128)S(1)}, f32[8,32,256]{2,1,0:T(8,128)S(1)}) custom-call(s32[2,3,32]{2,1,0:T(4,128)S(1)} %pad_add_fusion.routes, s32[2]{0:T(128)S(1)} %broadcast_subtract_fusion.near, ...), custom_call_target="tpu_custom_call" | custom-call | tf_op jit(solution)/shard_map/push_near_body/pallas_call | solution.py:81
  39.4 3.5 %collective-permute-start.6 = (f32[8,32,256]{2,1,0:T(8,128)S(1)}, f32[8,32,256]{2,1,0:T(8,128)S(1)}, u32[]{:S(2)}, u32[]{:S(2)}) collective-permute-start(f32[8,32,256]{2,1,0:T(8,128)S(1)} %get-tuple-element.51), channel_id=1, source_target_pairs={{0,1},{1,0},{2,3},{3,2},{4,5},{5,4},{6,7},{7,6},{8,9},{9,8},{10,11... | collective-permute-start | bytes 786440 | tf_op jit(solution)/shard_map/ppermute | solution.py:36
  48.0 2.9 %collective-permute-done.10.ra = f32[8,32,256]{2,1,0:T(8,128)S(1)} collective-permute-done((f32[8,32,256]{2,1,0:T(8,128)S(1)}, f32[8,32,256]{2,1,0:T(8,128)S(1)}, u32[]{:S(2)}, u32[]{:S(2)}) %collective-permute-start.10) | collective-permute-done | bytes 262176 | tf_op jit(solution)/shard_map/ppermute | solution.py:36
  51.7 7.7 %collective-permute-start.14 = (f32[8,32,256]{2,1,0:T(8,128)S(1)}, f32[8,32,256]{2,1,0:T(8,128)S(1)}, u32[]{:S(2)}, u32[]{:S(2)}) collective-permute-start(f32[8,32,256]{2,1,0:T(8,128)S(1)} %sum_body.1.own.vector.u), channel_id=1, source_target_pairs={{0,1},{1,0},{2,3},{3,2},{4,5},{5,4},{6,7},{7,6},{8,9},{9,8},{10,11... | collective-permute-start | bytes 786440 | tf_op jit(solution)/shard_map/ppermute | solution.py:36
  60.1 8.3 %collective-permute-start.12 = (f32[8,32,256]{2,1,0:T(8,128)S(1)}, f32[8,32,256]{2,1,0:T(8,128)S(1)}, u32[]{:S(2)}, u32[]{:S(2)}) collective-permute-start(f32[8,32,256]{2,1,0:T(8,128)S(1)} %sum_body.1.own.vector.u), channel_id=1, source_target_pairs={{0,8},{8,0},{16,24},{24,16},{32,40},{40,32},{48,56},{56,48},{64,72... | collective-permute-start | bytes 786440 | tf_op jit(solution)/shard_map/ppermute | solution.py:36
  68.4 6.2 %collective-permute-done.12.ra.first = f32[8,32,256]{2,1,0:T(8,128)S(1)} collective-permute-done((f32[8,32,256]{2,1,0:T(8,128)S(1)}, f32[8,32,256]{2,1,0:T(8,128)S(1)}, u32[]{:S(2)}, u32[]{:S(2)}) %collective-permute-start.12) | collective-permute-done | bytes 262176 | tf_op jit(solution)/shard_map/ppermute | solution.py:36
  75.3 3.1 %collective-permute-start.16 = (f32[2,8,32,256]{3,2,1,0:T(8,128)S(1)}, f32[2,8,32,256]{3,2,1,0:T(8,128)S(1)}, u32[]{:S(2)}, u32[]{:S(2)}) collective-permute-start(f32[2,8,32,256]{3,2,1,0:T(8,128)S(1)} %stack_body.3), channel_id=1, source_target_pairs={{0,1},{1,0},{2,3},{3,2},{4,5},{5,4},{6,7},{7,6},{8,9},{9,8},{10,11... | collective-permute-start | bytes 1572872 | tf_op jit(solution)/shard_map/ppermute | solution.py:36
  80.2 5.2 %pull_near_body.3 = (bf16[72,64,256]{2,1,0:T(8,128)(2,1)S(1)}, f32[8,32,256]{2,1,0:T(8,128)S(1)}) custom-call(s32[2,3,32]{2,1,0:T(4,128)S(1)} %pad_add_fusion.routes, s32[2]{0:T(128)S(1)} %broadcast_subtract_fusion.near, f32[8,32,256]{2,1,0:T(8,128)S(1)} %sum_body.1.own.vector.u, f32[8,32,256]{2,1,0:T(8,128)S(1)} %collective-permute-done.12.ra.first, ...), custom_call_target="tpu_custom_call" | custom-call | tf_op jit(solution)/shard_map/pull_near_body/pallas_call | solution.py:81
  85.4 2.8 %pull_far_body.3 = (bf16[72,64,256]{2,1,0:T(8,128)(2,1)S(1)}, bf16[8,64,256]{2,1,0:T(8,128)(2,1)S(1)}, f32[32,128]{1,0:T(8,128)S(1)}) custom-call(s32[2,3,32]{2,1,0:T(4,128)S(1)} %pad_add_fusion.routes, s32[2]{0:T(128)S(1)} %broadcast_subtract_fusion.near, bf16[72,64,256]{2,1,0:T(8,128)(2,1)S(1)} %get-tuple-element.59.table_in, ...), custom_call_target="tpu_custom_call", output_to_operand_aliasing={{0}: (2, {})} | custom-call | tf_op jit(solution)/shard_map/pull_far_body/pallas_call | solution.py:81
  90.7 3.5 %collective-permute-start.18 = (f32[32,128]{1,0:T(8,128)S(1)}, f32[32,128]{1,0:T(8,128)S(1)}, u32[]{:S(2)}, u32[]{:S(2)}) collective-permute-start(f32[32,128]{1,0:T(8,128)S(1)} %get-tuple-element.66), channel_id=1, source_target_pairs={{0,1},{1,0},{2,3},{3,2},{4,5},{5,4},{6,7},{7,6},{8,9},{9,8},{10,11... | collective-permute-start | bytes 49160 | tf_op jit(solution)/shard_map/ppermute | solution.py:277
  97.2 4.4 %collective-permute-done.21 = f32[32,128]{1,0:T(8,128)S(1)} collective-permute-done((f32[32,128]{1,0:T(8,128)S(1)}, f32[32,128]{1,0:T(8,128)S(1)}, u32[]{:S(2)}, u32[]{:S(2)}) %collective-permute-start.21) | collective-permute-done | bytes 16416 | tf_op jit(solution)/shard_map/ppermute | solution.py:277
  101.5 2.7 %collective-permute-start.22 = (f32[32,128]{1,0:T(8,128)S(1)}, f32[32,128]{1,0:T(8,128)S(1)}, u32[]{:S(2)}, u32[]{:S(2)}) collective-permute-start(f32[32,128]{1,0:T(8,128)S(1)} %add.136), channel_id=1, source_target_pairs={{0,6},{1,7},{2,4},{3,5},{4,2},{5,3},{6,0},{7,1},{8,14},{9,15},{10,... | collective-permute-start | bytes 49160 | tf_op jit(solution)/shard_map/ppermute | solution.py:277
  106.5 3.4 %collective-permute-start.23 = (f32[32,128]{1,0:T(8,128)S(1)}, f32[32,128]{1,0:T(8,128)S(1)}, u32[]{:S(2)}, u32[]{:S(2)}) collective-permute-start(f32[32,128]{1,0:T(8,128)S(1)} %add.137.g), channel_id=1, source_target_pairs={{0,8},{1,9},{2,10},{3,11},{4,12},{5,13},{6,14},{7,15},{8,0},{9,1},... | collective-permute-start | bytes 49160 | tf_op jit(solution)/shard_map/ppermute | solution.py:277
  109.9 3.5 %push_near_body.3 = (f32[8,32,256]{2,1,0:T(8,128)S(1)}, f32[8,32,256]{2,1,0:T(8,128)S(1)}, f32[8,32,256]{2,1,0:T(8,128)S(1)}, f32[8,32,256]{2,1,0:T(8,128)S(1)}, f32[8,32,256]{2,1,0:T(8,128)S(1)}) custom-call(s32[2,3,32]{2,1,0:T(4,128)S(1)} %pad_add_fusion.routes, s32[2]{0:T(128)S(1)} %broadcast_subtract_fusion.near, ...), custom_call_target="tpu_custom_call" | custom-call | tf_op jit(solution)/shard_map/push_near_body/pallas_call | solution.py:81
  115.1 10.4 %collective-permute-start.24 = (f32[32,128]{1,0:T(8,128)S(1)}, f32[32,128]{1,0:T(8,128)S(1)}, u32[]{:S(2)}, u32[]{:S(2)}) collective-permute-start(f32[32,128]{1,0:T(8,128)S(1)} %get-tuple-element.71), channel_id=1, source_target_pairs={{0,24},{1,25},{2,26},{3,27},{4,28},{5,29},{6,30},{7,31},{8,16},{9,... | collective-permute-start | bytes 49160 | tf_op jit(solution)/shard_map/ppermute | solution.py:277
  125.5 7.0 %collective-permute-done.24 = f32[32,128]{1,0:T(8,128)S(1)} collective-permute-done((f32[32,128]{1,0:T(8,128)S(1)}, f32[32,128]{1,0:T(8,128)S(1)}, u32[]{:S(2)}, u32[]{:S(2)}) %collective-permute-start.24) | collective-permute-done | bytes 16416 | tf_op jit(solution)/shard_map/ppermute | solution.py:277
  137.7 3.5 %collective-permute-done.26.moved = f32[32,128]{1,0:T(8,128)S(1)} collective-permute-done((f32[32,128]{1,0:T(8,128)S(1)}, f32[32,128]{1,0:T(8,128)S(1)}, u32[]{:S(2)}, u32[]{:S(2)}) %collective-permute-start.26) | collective-permute-done | bytes 16416 | tf_op jit(solution)/shard_map/ppermute | solution.py:277
  141.3 9.0 %finish_body.1 = (f32[32,2048]{1,0:T(8,128)}, f32[32,2048]{1,0:T(8,128)}) custom-call(f32[32,128]{1,0:T(8,128)S(1)} %add.139.grams, f32[32,128]{1,0:T(8,128)S(1)} %collective-permute-done.26.moved, f32[32,2048]{1,0:T(8,128)S(1)} %copy-done.1, f32[8,32,256]{2,1,0:T(8,128)S(1)} %sum_body.1.own.vector.u, f32[8,32,256]{2,1,0:T(8,128)S(1)} %get-tuple-element.72.own, ...), custom_call_target="tpu_custom_call" | custom-call | tf_op jit(solution)/shard_map/finish_body/pallas_call | solution.py:81
  (74 shorter events, 32.8 us)
Async XLA Ops:
  0.6 24.9 %collective-permute-start.3 = (f32[32,2048]{1,0:T(8,128)}, f32[32,2048]{1,0:T(8,128)S(1)}, u32[]{:S(2)}, u32[]{:S(2)}) collective-permute-start(f32[32,2048]{1,0:T(8,128)} %right.1), channel_id=1, source_target_pairs={{1,2},{2,1},{3,4},{4,3},{5,6},{6,5},{9,10},{10,9},{11,12},{12,11},... | collective-permute-start | bytes 786440 | tf_op jit(solution)/shard_map/ppermute | solution.py:36
  1.3 24.2 %collective-permute-start.2 = (f32[32,2048]{1,0:T(8,128)}, f32[32,2048]{1,0:T(8,128)S(1)}, u32[]{:S(2)}, u32[]{:S(2)}) collective-permute-start(f32[32,2048]{1,0:T(8,128)} %right.1), channel_id=1, source_target_pairs={{0,1},{1,0},{2,3},{3,2},{4,5},{5,4},{6,7},{7,6},{8,9},{9,8},{10,11... | collective-permute-start | bytes 786440 | tf_op jit(solution)/shard_map/ppermute | solution.py:36
  4.7 10.7 %collective-permute-start.1 = (f32[32,2048]{1,0:T(8,128)}, f32[32,2048]{1,0:T(8,128)S(1)}, u32[]{:S(2)}, u32[]{:S(2)}) collective-permute-start(f32[32,2048]{1,0:T(8,128)} %right.1), channel_id=1, source_target_pairs={{8,16},{16,8},{24,32},{32,24},{40,48},{48,40},{56,64},{64,56},{72,... | collective-permute-start | bytes 786440 | tf_op jit(solution)/shard_map/ppermute | solution.py:36
  5.4 10.7 %collective-permute-start = (f32[32,2048]{1,0:T(8,128)}, f32[32,2048]{1,0:T(8,128)S(1)}, u32[]{:S(2)}, u32[]{:S(2)}) collective-permute-start(f32[32,2048]{1,0:T(8,128)} %right.1), channel_id=1, source_target_pairs={{0,8},{8,0},{16,24},{24,16},{32,40},{40,32},{48,56},{56,48},{64,72... | collective-permute-start | bytes 786440 | tf_op jit(solution)/shard_map/ppermute | solution.py:36
  16.2 14.6 %collective-permute-start.5 = (f32[2,8,32,256]{3,2,1,0:T(8,128)S(1)}, f32[2,8,32,256]{3,2,1,0:T(8,128)S(1)}, u32[]{:S(2)}, u32[]{:S(2)}) collective-permute-start(f32[2,8,32,256]{3,2,1,0:T(8,128)S(1)} %stack_body.2), channel_id=1, source_target_pairs={{1,2},{2,1},{3,4},{4,3},{5,6},{6,5},{9,10},{10,9},{11,12},{12,11},... | collective-permute-start | bytes 1572872 | tf_op jit(solution)/shard_map/ppermute | solution.py:36
  16.9 13.9 %collective-permute-start.4 = (f32[2,8,32,256]{3,2,1,0:T(8,128)S(1)}, f32[2,8,32,256]{3,2,1,0:T(8,128)S(1)}, u32[]{:S(2)}, u32[]{:S(2)}) collective-permute-start(f32[2,8,32,256]{3,2,1,0:T(8,128)S(1)} %stack_body.2), channel_id=1, source_target_pairs={{0,1},{1,0},{2,3},{3,2},{4,5},{5,4},{6,7},{7,6},{8,9},{9,8},{10,11... | collective-permute-start | bytes 1572872 | tf_op jit(solution)/shard_map/ppermute | solution.py:36
  35.1 8.5 %collective-permute-start.8 = (f32[2,8,32,256]{3,2,1,0:T(8,128)S(1)}, f32[2,8,32,256]{3,2,1,0:T(8,128)S(1)}, u32[]{:S(2)}, u32[]{:S(2)}) collective-permute-start(f32[2,8,32,256]{3,2,1,0:T(8,128)S(1)} %get-tuple-element.55), channel_id=1, source_target_pairs={{0,1},{1,0},{2,3},{3,2},{4,5},{5,4},{6,7},{7,6},{8,9},{9,8},{10,11... | collective-permute-start | bytes 1572872 | tf_op jit(solution)/shard_map/ppermute | solution.py:36
  35.2 8.4 %collective-permute-start.9 = (f32[2,8,32,256]{3,2,1,0:T(8,128)S(1)}, f32[2,8,32,256]{3,2,1,0:T(8,128)S(1)}, u32[]{:S(2)}, u32[]{:S(2)}) collective-permute-start(f32[2,8,32,256]{3,2,1,0:T(8,128)S(1)} %get-tuple-element.56), channel_id=1, source_target_pairs={{1,2},{2,1},{3,4},{4,3},{5,6},{6,5},{9,10},{10,9},{11,12},{12,11},... | collective-permute-start | bytes 1572872 | tf_op jit(solution)/shard_map/ppermute | solution.py:36
  39.4 8.5 %collective-permute-start.6 = (f32[8,32,256]{2,1,0:T(8,128)S(1)}, f32[8,32,256]{2,1,0:T(8,128)S(1)}, u32[]{:S(2)}, u32[]{:S(2)}) collective-permute-start(f32[8,32,256]{2,1,0:T(8,128)S(1)} %get-tuple-element.51), channel_id=1, source_target_pairs={{0,1},{1,0},{2,3},{3,2},{4,5},{5,4},{6,7},{7,6},{8,9},{9,8},{10,11... | collective-permute-start | bytes 786440 | tf_op jit(solution)/shard_map/ppermute | solution.py:36
  43.7 7.2 %collective-permute-start.10 = (f32[8,32,256]{2,1,0:T(8,128)S(1)}, f32[8,32,256]{2,1,0:T(8,128)S(1)}, u32[]{:S(2)}, u32[]{:S(2)}) collective-permute-start(f32[8,32,256]{2,1,0:T(8,128)S(1)} %get-tuple-element.57), channel_id=1, source_target_pairs={{0,8},{8,0},{16,24},{24,16},{32,40},{40,32},{48,56},{56,48},{64,72... | collective-permute-start | bytes 786440 | tf_op jit(solution)/shard_map/ppermute | solution.py:36
  51.0 17.4 %collective-permute-start.15 = (f32[8,32,256]{2,1,0:T(8,128)S(1)}, f32[8,32,256]{2,1,0:T(8,128)S(1)}, u32[]{:S(2)}, u32[]{:S(2)}) collective-permute-start(f32[8,32,256]{2,1,0:T(8,128)S(1)} %sum_body.1.own.vector.u), channel_id=1, source_target_pairs={{1,2},{2,1},{3,4},{4,3},{5,6},{6,5},{9,10},{10,9},{11,12},{12,11},... | collective-permute-start | bytes 786440 | tf_op jit(solution)/shard_map/ppermute | solution.py:36
  51.7 16.7 %collective-permute-start.14 = (f32[8,32,256]{2,1,0:T(8,128)S(1)}, f32[8,32,256]{2,1,0:T(8,128)S(1)}, u32[]{:S(2)}, u32[]{:S(2)}) collective-permute-start(f32[8,32,256]{2,1,0:T(8,128)S(1)} %sum_body.1.own.vector.u), channel_id=1, source_target_pairs={{0,1},{1,0},{2,3},{3,2},{4,5},{5,4},{6,7},{7,6},{8,9},{9,8},{10,11... | collective-permute-start | bytes 786440 | tf_op jit(solution)/shard_map/ppermute | solution.py:36
  59.4 9.0 %collective-permute-start.13 = (f32[8,32,256]{2,1,0:T(8,128)S(1)}, f32[8,32,256]{2,1,0:T(8,128)S(1)}, u32[]{:S(2)}, u32[]{:S(2)}) collective-permute-start(f32[8,32,256]{2,1,0:T(8,128)S(1)} %sum_body.1.own.vector.u), channel_id=1, source_target_pairs={{8,16},{16,8},{24,32},{32,24},{40,48},{48,40},{56,64},{64,56},{72,... | collective-permute-start | bytes 786440 | tf_op jit(solution)/shard_map/ppermute | solution.py:36
  60.1 14.5 %collective-permute-start.12 = (f32[8,32,256]{2,1,0:T(8,128)S(1)}, f32[8,32,256]{2,1,0:T(8,128)S(1)}, u32[]{:S(2)}, u32[]{:S(2)}) collective-permute-start(f32[8,32,256]{2,1,0:T(8,128)S(1)} %sum_body.1.own.vector.u), channel_id=1, source_target_pairs={{0,8},{8,0},{16,24},{24,16},{32,40},{40,32},{48,56},{56,48},{64,72... | collective-permute-start | bytes 786440 | tf_op jit(solution)/shard_map/ppermute | solution.py:36
  74.6 10.8 %collective-permute-start.17 = (f32[2,8,32,256]{3,2,1,0:T(8,128)S(1)}, f32[2,8,32,256]{3,2,1,0:T(8,128)S(1)}, u32[]{:S(2)}, u32[]{:S(2)}) collective-permute-start(f32[2,8,32,256]{3,2,1,0:T(8,128)S(1)} %stack_body.3), channel_id=1, source_target_pairs={{1,2},{2,1},{3,4},{4,3},{5,6},{6,5},{9,10},{10,9},{11,12},{12,11},... | collective-permute-start | bytes 1572872 | tf_op jit(solution)/shard_map/ppermute | solution.py:36
  75.3 10.1 %collective-permute-start.16 = (f32[2,8,32,256]{3,2,1,0:T(8,128)S(1)}, f32[2,8,32,256]{3,2,1,0:T(8,128)S(1)}, u32[]{:S(2)}, u32[]{:S(2)}) collective-permute-start(f32[2,8,32,256]{3,2,1,0:T(8,128)S(1)} %stack_body.3), channel_id=1, source_target_pairs={{0,1},{1,0},{2,3},{3,2},{4,5},{5,4},{6,7},{7,6},{8,9},{9,8},{10,11... | collective-permute-start | bytes 1572872 | tf_op jit(solution)/shard_map/ppermute | solution.py:36
  89.9 24.3 %collective-permute-start.19 = (f32[2,8,32,256]{3,2,1,0:T(8,128)S(1)}, f32[2,8,32,256]{3,2,1,0:T(8,128)S(1)}, u32[]{:S(2)}, u32[]{:S(2)}) collective-permute-start(f32[2,8,32,256]{3,2,1,0:T(8,128)S(1)} %get-tuple-element.69), channel_id=1, source_target_pairs={{0,1},{1,0},{2,3},{3,2},{4,5},{5,4},{6,7},{7,6},{8,9},{9,8},{10,11... | collective-permute-start | bytes 1572872 | tf_op jit(solution)/shard_map/ppermute | solution.py:36
  90.0 24.2 %collective-permute-start.20 = (f32[2,8,32,256]{3,2,1,0:T(8,128)S(1)}, f32[2,8,32,256]{3,2,1,0:T(8,128)S(1)}, u32[]{:S(2)}, u32[]{:S(2)}) collective-permute-start(f32[2,8,32,256]{3,2,1,0:T(8,128)S(1)} %get-tuple-element.70), channel_id=1, source_target_pairs={{1,2},{2,1},{3,4},{4,3},{5,6},{6,5},{9,10},{10,9},{11,12},{12,11},... | collective-permute-start | bytes 1572872 | tf_op jit(solution)/shard_map/ppermute | solution.py:36
  106.5 7.7 %collective-permute-start.23 = (f32[32,128]{1,0:T(8,128)S(1)}, f32[32,128]{1,0:T(8,128)S(1)}, u32[]{:S(2)}, u32[]{:S(2)}) collective-permute-start(f32[32,128]{1,0:T(8,128)S(1)} %add.137.g), channel_id=1, source_target_pairs={{0,8},{1,9},{2,10},{3,11},{4,12},{5,13},{6,14},{7,15},{8,0},{9,1},... | collective-permute-start | bytes 49160 | tf_op jit(solution)/shard_map/ppermute | solution.py:277
  113.5 24.3 %collective-permute-start.27 = (f32[8,32,256]{2,1,0:T(8,128)S(1)}, f32[8,32,256]{2,1,0:T(8,128)S(1)}, u32[]{:S(2)}, u32[]{:S(2)}) collective-permute-start(f32[8,32,256]{2,1,0:T(8,128)S(1)} %get-tuple-element.74), channel_id=1, source_target_pairs={{0,1},{1,0},{2,3},{3,2},{4,5},{5,4},{6,7},{7,6},{8,9},{9,8},{10,11... | collective-permute-start | bytes 786440 | tf_op jit(solution)/shard_map/ppermute | solution.py:36
  113.6 24.2 %collective-permute-start.28 = (f32[8,32,256]{2,1,0:T(8,128)S(1)}, f32[8,32,256]{2,1,0:T(8,128)S(1)}, u32[]{:S(2)}, u32[]{:S(2)}) collective-permute-start(f32[8,32,256]{2,1,0:T(8,128)S(1)} %get-tuple-element.75), channel_id=1, source_target_pairs={{1,2},{2,1},{3,4},{4,3},{5,6},{6,5},{9,10},{10,9},{11,12},{12,11},... | collective-permute-start | bytes 786440 | tf_op jit(solution)/shard_map/ppermute | solution.py:36
  114.4 26.9 %collective-permute-start.29 = (f32[8,32,256]{2,1,0:T(8,128)S(1)}, f32[8,32,256]{2,1,0:T(8,128)S(1)}, u32[]{:S(2)}, u32[]{:S(2)}) collective-permute-start(f32[8,32,256]{2,1,0:T(8,128)S(1)} %get-tuple-element.76), channel_id=1, source_target_pairs={{0,8},{8,0},{16,24},{24,16},{32,40},{40,32},{48,56},{56,48},{64,72... | collective-permute-start | bytes 786440 | tf_op jit(solution)/shard_map/ppermute | solution.py:36
  114.5 26.8 %collective-permute-start.30 = (f32[8,32,256]{2,1,0:T(8,128)S(1)}, f32[8,32,256]{2,1,0:T(8,128)S(1)}, u32[]{:S(2)}, u32[]{:S(2)}) collective-permute-start(f32[8,32,256]{2,1,0:T(8,128)S(1)} %get-tuple-element.77), channel_id=1, source_target_pairs={{8,16},{16,8},{24,32},{32,24},{40,48},{48,40},{56,64},{64,56},{72,... | collective-permute-start | bytes 786440 | tf_op jit(solution)/shard_map/ppermute | solution.py:36
  115.1 17.4 %collective-permute-start.24 = (f32[32,128]{1,0:T(8,128)S(1)}, f32[32,128]{1,0:T(8,128)S(1)}, u32[]{:S(2)}, u32[]{:S(2)}) collective-permute-start(f32[32,128]{1,0:T(8,128)S(1)} %get-tuple-element.71), channel_id=1, source_target_pairs={{0,24},{1,25},{2,26},{3,27},{4,28},{5,29},{6,30},{7,31},{8,16},{9,... | collective-permute-start | bytes 49160 | tf_op jit(solution)/shard_map/ppermute | solution.py:277
  (9 other events, 50.2 us)

commit v2 on v1

--- a/solution.py
+++ b/solution.py
@@ -24,12 +24,7 @@
 
 
 def pairs_of(count, shift):
-    found = []
-    for place in range(count):
-        partner = ((place + shift) ^ 1) - shift
-        if 0 <= partner < count:
-            found.append((place, partner))
-    return found
+    return [(place, (((place + shift) ^ 1) - shift) % count) for place in range(count)]
 
 
 def swapped(value, axis, shift):
@@ -119,8 +114,8 @@
     return source[q] if len(source.shape) == 3 else source[:, q * width:(q + 1) * width]
 
 
-def stack_body(first, second, *rest):
-    out = rest[-1]
+def stack_body(*refs):
+    first, second, out = refs[-3:]
     blocks, width = out.shape[1], out.shape[3]
     for slot, source in enumerate((first, second)):
         for q in range(blocks):
@@ -181,14 +176,29 @@
 
 
 def push_far_body(routes, near, strain_hl, *refs):
-    *halves, pieces, da, db = refs
+    halves, (pieces, *targets) = refs[:2 * HALVES], refs[2 * HALVES:]
     blocks = strain_hl.shape[0]
     pieces[...] = jnp.zeros_like(pieces)
     accumulate(dot_nn, True, routes, near, 2, 1, strain_hl, pieces, halves)
-    for group, target in enumerate((da, db)):
+    for group, target in enumerate(targets):
         for slot in range(2):
             for q in range(blocks):
                 target[slot, q] = pieces[(5 + 2 * group + slot) * blocks + q]
+
+
+def push_all_body(routes, near, strain_hl, *refs):
+    halves, pieces_in = refs[:2 * HALVES], refs[2 * HALVES]
+    own, ra, rb, qa, qb, pieces = refs[-6:]
+    blocks = strain_hl.shape[0]
+    pieces[...] = pieces_in[...]
+    accumulate(dot_nn, False, routes, near, 2, 1, strain_hl, pieces, halves)
+    for slot, target in enumerate((own, ra, rb)):
+        for q in range(blocks):
+            target[q] = pieces[slot * blocks + q]
+    for group, target in enumerate((qa, qb)):
+        for slot, place in enumerate((3 + group, 5 + 2 * group, 6 + 2 * group)):
+            for q in range(blocks):
+                target[slot, q] = pieces[place * blocks + q]
 
 
 def push_near_body(routes, near, strain_hl, *refs):
@@ -222,9 +232,10 @@
     mb[...] = rb[...] + qa[1] + qb[1]
 
 
-def middle_gram_body(ra, rb, qa, qb, g, moved, ma, mb, g_out):
-    middle_body(ra, rb, qa, qb, ma, mb)
-    g_out[...] = g[...] + moved[...]
+def middle_last_body(own, ra, rb, qa, qb, diag, grams, rest, ma, mb):
+    rest[...] = (own[...] + diag[...]) + (qa[0] + qb[0])
+    ma[...] = ra[...] + qa[1] + qb[1]
+    mb[...] = rb[...] + qa[2] + qb[2]
 
 
 def sum_body(own, diag, ca, cb, ra, rb, out):
@@ -246,7 +257,7 @@
     return work[:, size:]
 
 
-def finish_body(grams, moved, right, u, own, diag, ca, cb, ra, rb, x_out, r_out):
+def solve_body(grams, moved, p, q):
     size = grams.shape[0]
     total = grams[...] + moved[...]
     g0, g1, g2, g3 = (total[:, i * size:(i + 1) * size] for i in range(4))
@@ -259,17 +270,20 @@
     e2 = full_nn(g2, mix) - full_nn(g3, alpha)
     curvature = full_tn(mix, e1) - full_tn(alpha, e2)
     second = eliminated(curvature, fresh)
-    p = alpha + full_nn(mix, second)
-    q = full_nn(alpha, second)
+    p[...] = alpha + full_nn(mix, second)
+    q[...] = full_nn(alpha, second)
+
+
+def finish_body(p, q, right, u, rest, ra, rb, x_out, r_out):
     width = u.shape[2]
     for block in range(u.shape[0]):
         lanes = slice(block * width, (block + 1) * width)
-        w = (own[block] + diag[block]) + (ca[block] + cb[block]) + (ra[block] + rb[block])
-        x_out[:, lanes] = full_tn(p, right[:, lanes]) - full_tn(q, u[block])
-        r_out[:, lanes] = right[:, lanes] - full_tn(p, u[block]) + full_tn(q, w)
-
-
-MASKS = (1, 2, 6, 8, 24, 32, 96)
+        w = rest[block] + ra[block] + rb[block]
+        x_out[:, lanes] = full_tn(p[...], right[:, lanes]) - full_tn(q[...], u[block])
+        r_out[:, lanes] = right[:, lanes] - full_tn(p[...], u[block]) + full_tn(q[...], w)
+
+
+MASKS = (2, 8, 24, 32, 96, 1, 6)
 
 
 def exchanged(value, mask):
@@ -304,6 +318,7 @@
     blocks, width = diag_blocks.shape[0], diag_blocks.shape[1]
     rows = right_sides.shape[0]
     block_shape = pltpu.VMEM((blocks, rows, width), F32)
+    stack_shape = pltpu.VMEM((3, blocks, rows, width), F32)
     pair_shape = pltpu.VMEM((2, blocks, rows, width), F32)
     table_shape = pltpu.VMEM((9 * blocks, 2 * rows, width), BF16)
     split_shape = pltpu.VMEM((blocks, 2 * rows, width), BF16)
@@ -316,7 +331,7 @@
     def spread(vector, *after):
         ra, rb = swapped(vector, "row", 0), swapped(vector, "row", 1)
         ca, cb = swapped(vector, "col", 0), swapped(vector, "col", 1)
-        both = call(stack_body, pair_shape, 0, (ra, rb) + (after or (ca, cb)))
+        both = call(stack_body, pair_shape, 0, (after or (ca, cb)) + (ra, rb))
         return (vector, ra, rb, ca, cb), swapped(both, "col", 0), swapped(both, "col", 1)
 
     def pulled(near_tables, da, db, split_couplings, *grams):
@@ -326,11 +341,11 @@
             (routes, near, table, strain, da, db, *split_couplings, *grams), [block_shape], aliases={2: 0})
         return strain_hl, g
 
-    def pushed(strain_hl, split_couplings, *after):
+    def pushed(strain_hl, split_couplings):
         pieces, da, db = call(push_far_body, [pieces_shape, pair_shape, pair_shape], 2, (routes, near, strain_hl, *split_couplings))
         da, db = swapped(da, "col", 0), swapped(db, "col", 1)
         own, ra, rb, ca, cb = call(
-            push_near_body, [block_shape] * 5, 2, (routes, near, strain_hl, *split_couplings, pieces, *after), [near_pieces_shape])
+            push_near_body, [block_shape] * 5, 2, (routes, near, strain_hl, *split_couplings, pieces), [near_pieces_shape])
         return own, ra, rb, swapped(ca, "col", 0), swapped(cb, "col", 1), da, db
 
     routes, near = routing(pair_index, blocks)
@@ -348,20 +363,20 @@
     near_tables, da, db = spread(u)
     diag, g23 = call(diag_body, [block_shape, grams_shape], 0, (u, diag_blocks))
     strain_hl, grams = pulled(near_tables, da, db, split_couplings, g01, g1s, g23)
+    pieces, = call(push_far_body, [pieces_shape], 2, (routes, near, strain_hl, *split_couplings))
     grams = grams + exchanged(grams, MASKS[0])
-    own, ra, rb, ca, cb, da, db = pushed(strain_hl, split_couplings, grams)
-    for mask in MASKS[1:3]:
+    own, ra, rb, qa, qb = call(
+        push_all_body, [block_shape] * 3 + [stack_shape] * 2, 2,
+        (routes, near, strain_hl, *split_couplings, pieces, grams), [pieces_shape])
+    qa, qb = swapped(qa, "col", 0), swapped(qb, "col", 1)
+    for mask in MASKS[1:-1]:
         grams = grams + exchanged(grams, mask)
-    ra, rb, grams = call(
-        middle_gram_body, [block_shape] * 2 + [all_grams_shape], 0,
-        (ra, rb, da, db, grams, exchanged(grams, MASKS[3])))
+    moved = exchanged(grams, MASKS[-1])
+    rest, ra, rb = call(middle_last_body, [block_shape] * 3, 0, (own, ra, rb, qa, qb, diag, moved))
     ra, rb = swapped(ra, "row", 0), swapped(rb, "row", 1)
-    for mask in MASKS[4:6]:
-        grams = grams + exchanged(grams, mask)
+    p, q = call(solve_body, [gram_shape] * 2, 0, (grams, moved))
     flat = jax.ShapeDtypeStruct(right_sides.shape, F32)
-    return tuple(call(
-        finish_body, [flat, flat], 0,
-        (grams, exchanged(grams, MASKS[6]), right_sides, u, own, diag, ca, cb, ra, rb)))
+    return tuple(call(finish_body, [flat, flat], 0, (p, q, right_sides, u, rest, ra, rb)))
 
 
 def solution(mesh):

time: 151 us -> 129 us (0.85)
  starting transfers between devices: 69.6 us -> 26.3 us
  waiting for transfers between devices: 29.6 us -> 51.3 us
    ppermute x7, starting transfers between devices: 25.6 us -> 0.62 us  [exchanged(): lax.ppermute(value, ('row', 'col'), [(i, i ^ mask) for i in range(count)])]
    ppermute x24 -> x22, starting transfers between devices: 44 us -> 25.7 us  [swapped(): return lax.ppermute(value, axis, pairs_of(lax.axis_size(axis), shift))]
    ppermute x24 -> x22, waiting for transfers between devices: 9.91 us -> 26.3 us  [swapped(): return lax.ppermute(value, axis, pairs_of(lax.axis_size(axis), shift))]
    ppermute x7, waiting for transfers between devices: 19.7 us -> 24.9 us  [exchanged(): lax.ppermute(value, ('row', 'col'), [(i, i ^ mask) for i in range(count)])]
    pallas_call x16 -> x17, Pallas kernels: 39.1 us -> 39.2 us  [call(): pl.pallas_call(body, out_shape=out_shape, in_specs=[SMEM_SPEC] * n_smem +...]
  transfers between devices with their start and end apart: 31 -> 29, of which waited for: 9 -> 16; matrix products, arithmetic and copies ran while one was open for 1% -> 1% of each run, Pallas kernels for 20% -> 28%
where the time goes in v2:
time: 129 us
  waiting for transfers between devices  51.3 us (40%)
  Pallas kernels  48.7 us (38%)
  starting transfers between devices  26.3 us (20%)
  other arithmetic  1.33 us (1%)
    pallas_call x17, Pallas kernels, call(): pl.pallas_call(body, out_shape=out_shape, in_specs=[SMEM_SPEC] * n_smem +...  39.2 us
    ppermute x22, waiting for transfers between devices, swapped(): return lax.ppermute(value, axis, pairs_of(lax.axis_size(axis), shift))  26.3 us
    ppermute x22, starting transfers between devices, swapped(): return lax.ppermute(value, axis, pairs_of(lax.axis_size(axis), shift))  25.7 us
    ppermute x7, waiting for transfers between devices, exchanged(): lax.ppermute(value, ('row', 'col'), [(i, i ^ mask) for i in range(count)])  24.9 us
    pallas_call x2, Pallas kernels, prepare(): pl.pallas_call(prepare_body, grid=(steps,), in_specs=[pl.BlockSpec((CHUNK...  9.54 us
  transfers between devices with their start and end apart: 29, of which 16 were waited for; matrix products, arithmetic and copies ran while one was open for 1% of the time, Pallas kernels for 28%

profile of v2, /device:TPU:0, one launch (start us, length us, event | category | flops | bytes accessed | tf_op | source)
XLA Modules:
  0.0 128.7 jit_solution(1923794677543328473)
XLA Ops:
  0.6 3.6 %collective-permute-start.3 = (f32[32,2048]{1,0:T(8,128)}, f32[32,2048]{1,0:T(8,128)S(1)}, u32[]{:S(2)}, u32[]{:S(2)}) collective-permute-start(f32[32,2048]{1,0:T(8,128)} %right.1), channel_id=1, source_target_pairs={{0,7},{1,2},{2,1},{3,4},{4,3},{5,6},{6,5},{7,0},{8,15},{9,10},{10,... | collective-permute-start | bytes 786440 | tf_op jit(solution)/shard_map/ppermute | solution.py:31
  4.3 5.2 %collective-permute-start.1 = (f32[32,2048]{1,0:T(8,128)}, f32[32,2048]{1,0:T(8,128)S(1)}, u32[]{:S(2)}, u32[]{:S(2)}) collective-permute-start(f32[32,2048]{1,0:T(8,128)} %right.1), channel_id=1, source_target_pairs={{0,120},{8,16},{16,8},{24,32},{32,24},{40,48},{48,40},{56,64},{64,... | collective-permute-start | bytes 786440 | tf_op jit(solution)/shard_map/ppermute | solution.py:31
  10.6 4.6 %prepare.2 = (bf16[32,256,256]{2,1,0:T(8,128)(2,1)S(1)}, bf16[32,256,256]{2,1,0:T(8,128)(2,1)S(1)}, f32[8,128]{1,0:T(8,128)S(1)}) custom-call(f32[64,256,256]{2,1,0:T(8,128)} %couplings.3), custom_call_target="tpu_custom_call" | custom-call | tf_op jit(solution)/shard_map/prepare/pallas_call | solution.py:102
  18.8 4.9 %prepare.3 = (bf16[32,256,256]{2,1,0:T(8,128)(2,1)S(1)}, bf16[32,256,256]{2,1,0:T(8,128)(2,1)S(1)}, f32[8,128]{1,0:T(8,128)}) custom-call(f32[64,256,256]{2,1,0:T(8,128)} %couplings.3), custom_call_target="tpu_custom_call" | custom-call | tf_op jit(solution)/shard_map/prepare/pallas_call | solution.py:102
  23.7 5.2 %pull_near_body.2 = (bf16[72,64,256]{2,1,0:T(8,128)(2,1)S(1)}, f32[8,32,256]{2,1,0:T(8,128)S(1)}) custom-call(s32[2,3,32]{2,1,0:T(4,128)S(1)} %pad_add_fusion.routes, s32[2]{0:T(128)S(1)} %broadcast_subtract_fusion.near, f32[32,2048]{1,0:T(8,128)S(1)} %copy-done.1, f32[32,2048]{1,0:T(8,128)S(1)} %collective-permute-done.ra.refs_1_, ...), custom_call_target="tpu_custom_call" | custom-call | tf_op jit(solution)/shard_map/pull_near_body/pallas_call | solution.py:76
  28.9 2.5 %pull_far_body.2 = (bf16[72,64,256]{2,1,0:T(8,128)(2,1)S(1)}, bf16[8,64,256]{2,1,0:T(8,128)(2,1)S(1)}, f32[32,32]{1,0:T(8,128)S(1)}) custom-call(s32[2,3,32]{2,1,0:T(4,128)S(1)} %pad_add_fusion.routes, s32[2]{0:T(128)S(1)} %broadcast_subtract_fusion.near, bf16[72,64,256]{2,1,0:T(8,128)(2,1)S(1)} %get-tuple-element.43.table_in, ...), custom_call_target="tpu_custom_call", output_to_operand_aliasing={{0}: (2, {})} | custom-call | tf_op jit(solution)/shard_map/pull_far_body/pallas_call | solution.py:76
  33.8 2.9 %collective-permute-start.9 = (f32[2,8,32,256]{3,2,1,0:T(8,128)S(1)}, f32[2,8,32,256]{3,2,1,0:T(8,128)S(1)}, u32[]{:S(2)}, u32[]{:S(2)}) collective-permute-start(f32[2,8,32,256]{3,2,1,0:T(8,128)S(1)} %get-tuple-element.55), channel_id=1, source_target_pairs={{0,7},{1,2},{2,1},{3,4},{4,3},{5,6},{6,5},{7,0},{8,15},{9,10},{10,... | collective-permute-start | bytes 1572872 | tf_op jit(solution)/shard_map/ppermute | solution.py:31
  36.7 3.5 %push_near_body.1 = (f32[8,32,256]{2,1,0:T(8,128)S(1)}, f32[8,32,256]{2,1,0:T(8,128)S(1)}, f32[8,32,256]{2,1,0:T(8,128)S(1)}, f32[8,32,256]{2,1,0:T(8,128)S(1)}, f32[8,32,256]{2,1,0:T(8,128)S(1)}) custom-call(s32[2,3,32]{2,1,0:T(4,128)S(1)} %pad_add_fusion.routes, s32[2]{0:T(128)S(1)} %broadcast_subtract_fusion.near, ...), custom_call_target="tpu_custom_call" | custom-call | tf_op jit(solution)/shard_map/push_near_body/pallas_call | solution.py:76
  40.8 2.8 %collective-permute-done.9.qb = f32[2,8,32,256]{3,2,1,0:T(8,128)S(1)} collective-permute-done((f32[2,8,32,256]{3,2,1,0:T(8,128)S(1)}, f32[2,8,32,256]{3,2,1,0:T(8,128)S(1)}, u32[]{:S(2)}, u32[]{:S(2)}) %collective-permute-start.9) | collective-permute-done | bytes 524320 | tf_op jit(solution)/shard_map/ppermute | solution.py:31
  51.2 4.6 %collective-permute-done.11.rb = f32[8,32,256]{2,1,0:T(8,128)S(1)} collective-permute-done((f32[8,32,256]{2,1,0:T(8,128)S(1)}, f32[8,32,256]{2,1,0:T(8,128)S(1)}, u32[]{:S(2)}, u32[]{:S(2)}) %collective-permute-start.11) | collective-permute-done | bytes 262176 | tf_op jit(solution)/shard_map/ppermute | solution.py:31
  55.9 3.7 %collective-permute-start.15 = (f32[8,32,256]{2,1,0:T(8,128)S(1)}, f32[8,32,256]{2,1,0:T(8,128)S(1)}, u32[]{:S(2)}, u32[]{:S(2)}) collective-permute-start(f32[8,32,256]{2,1,0:T(8,128)S(1)} %sum_body.1.own.vector.u), channel_id=1, source_target_pairs={{0,7},{1,2},{2,1},{3,4},{4,3},{5,6},{6,5},{7,0},{8,15},{9,10},{10,... | collective-permute-start | bytes 786440 | tf_op jit(solution)/shard_map/ppermute | solution.py:31
  61.2 2.5 %collective-permute-done.15.cb.refs_1_ = f32[8,32,256]{2,1,0:T(8,128)S(1)} collective-permute-done((f32[8,32,256]{2,1,0:T(8,128)S(1)}, f32[8,32,256]{2,1,0:T(8,128)S(1)}, u32[]{:S(2)}, u32[]{:S(2)}) %collective-permute-start.15) | collective-permute-done | bytes 262176 | tf_op jit(solution)/shard_map/ppermute | solution.py:31
  63.7 8.0 %collective-permute-done.13.rb.refs_3_ = f32[8,32,256]{2,1,0:T(8,128)S(1)} collective-permute-done((f32[8,32,256]{2,1,0:T(8,128)S(1)}, f32[8,32,256]{2,1,0:T(8,128)S(1)}, u32[]{:S(2)}, u32[]{:S(2)}) %collective-permute-start.13) | collective-permute-done | bytes 262176 | tf_op jit(solution)/shard_map/ppermute | solution.py:31
  73.7 5.4 %pull_near_body.3 = (bf16[72,64,256]{2,1,0:T(8,128)(2,1)S(1)}, f32[8,32,256]{2,1,0:T(8,128)S(1)}) custom-call(s32[2,3,32]{2,1,0:T(4,128)S(1)} %pad_add_fusion.routes, s32[2]{0:T(128)S(1)} %broadcast_subtract_fusion.near, f32[8,32,256]{2,1,0:T(8,128)S(1)} %sum_body.1.own.vector.u, f32[8,32,256]{2,1,0:T(8,128)S(1)} %collective-permute-done.12.ra.refs_2_, ...), custom_call_target="tpu_custom_call" | custom-call | tf_op jit(solution)/shard_map/pull_near_body/pallas_call | solution.py:76
  79.1 2.6 %collective-permute-done.17.db = f32[2,8,32,256]{3,2,1,0:T(8,128)S(1)} collective-permute-done((f32[2,8,32,256]{3,2,1,0:T(8,128)S(1)}, f32[2,8,32,256]{3,2,1,0:T(8,128)S(1)}, u32[]{:S(2)}, u32[]{:S(2)}) %collective-permute-start.17) | collective-permute-done | bytes 524320 | tf_op jit(solution)/shard_map/ppermute | solution.py:31
  81.6 2.6 %pull_far_body.3 = (bf16[72,64,256]{2,1,0:T(8,128)(2,1)S(1)}, bf16[8,64,256]{2,1,0:T(8,128)(2,1)S(1)}, f32[32,128]{1,0:T(8,128)S(1)}) custom-call(s32[2,3,32]{2,1,0:T(4,128)S(1)} %pad_add_fusion.routes, s32[2]{0:T(128)S(1)} %broadcast_subtract_fusion.near, bf16[72,64,256]{2,1,0:T(8,128)(2,1)S(1)} %get-tuple-element.58.table_in, ...), custom_call_target="tpu_custom_call", output_to_operand_aliasing={{0}: (2, {})} | custom-call | tf_op jit(solution)/shard_map/pull_far_body/pallas_call | solution.py:76
  88.0 3.7 %push_all_body.1 = (f32[8,32,256]{2,1,0:T(8,128)S(1)}, f32[8,32,256]{2,1,0:T(8,128)S(1)}, f32[8,32,256]{2,1,0:T(8,128)S(1)}, f32[3,8,32,256]{3,2,1,0:T(8,128)S(1)}, f32[3,8,32,256]{3,2,1,0:T(8,128)S(1)}) custom-call(s32[2,3,32]{2,1,0:T(4,128)S(1)} %pad_add_fusion.routes, s32[2]{0:T(128)S(1)} %broadcast_subtract_fusion.near, ...), custom_call_target="tpu_custom_call" | custom-call | tf_op jit(solution)/shard_map/push_all_body/pallas_call | solution.py:76
  92.6 3.7 %collective-permute-done.19 = f32[32,128]{1,0:T(8,128)S(1)} collective-permute-done((f32[32,128]{1,0:T(8,128)S(1)}, f32[32,128]{1,0:T(8,128)S(1)}, u32[]{:S(2)}, u32[]{:S(2)}) %collective-permute-start.19) | collective-permute-done | bytes 16416 | tf_op jit(solution)/shard_map/ppermute | solution.py:291
  96.3 4.9 %collective-permute-done.20 = f32[32,128]{1,0:T(8,128)S(1)} collective-permute-done((f32[32,128]{1,0:T(8,128)S(1)}, f32[32,128]{1,0:T(8,128)S(1)}, u32[]{:S(2)}, u32[]{:S(2)}) %collective-permute-start.20) | collective-permute-done | bytes 16416 | tf_op jit(solution)/shard_map/ppermute | solution.py:291
  101.3 3.7 %collective-permute-done.21 = f32[32,128]{1,0:T(8,128)S(1)} collective-permute-done((f32[32,128]{1,0:T(8,128)S(1)}, f32[32,128]{1,0:T(8,128)S(1)}, u32[]{:S(2)}, u32[]{:S(2)}) %collective-permute-start.21) | collective-permute-done | bytes 16416 | tf_op jit(solution)/shard_map/ppermute | solution.py:291
  105.0 4.9 %collective-permute-done.22 = f32[32,128]{1,0:T(8,128)S(1)} collective-permute-done((f32[32,128]{1,0:T(8,128)S(1)}, f32[32,128]{1,0:T(8,128)S(1)}, u32[]{:S(2)}, u32[]{:S(2)}) %collective-permute-start.22) | collective-permute-done | bytes 16416 | tf_op jit(solution)/shard_map/ppermute | solution.py:291
  111.7 4.4 %collective-permute-done.24.moved.grams = f32[32,128]{1,0:T(8,128)S(1)} collective-permute-done((f32[32,128]{1,0:T(8,128)S(1)}, f32[32,128]{1,0:T(8,128)S(1)}, u32[]{:S(2)}, u32[]{:S(2)}) %collective-permute-start.24) | collective-permute-done | bytes 16416 | tf_op jit(solution)/shard_map/ppermute | solution.py:291
  116.3 2.5 %collective-permute-start.28 = (f32[8,32,256]{2,1,0:T(8,128)S(1)}, f32[8,32,256]{2,1,0:T(8,128)S(1)}, u32[]{:S(2)}, u32[]{:S(2)}) collective-permute-start(f32[8,32,256]{2,1,0:T(8,128)S(1)} %get-tuple-element.75), channel_id=1, source_target_pairs={{0,120},{8,16},{16,8},{24,32},{32,24},{40,48},{48,40},{56,64},{64,... | collective-permute-start | bytes 786440 | tf_op jit(solution)/shard_map/ppermute | solution.py:31
  118.8 7.2 %solve_body.1 = (f32[32,32]{1,0:T(8,128)S(1)}, f32[32,32]{1,0:T(8,128)S(1)}) custom-call(f32[32,128]{1,0:T(8,128)S(1)} %add.143.grams, f32[32,128]{1,0:T(8,128)S(1)} %collective-permute-done.24.moved.grams), custom_call_target="tpu_custom_call" | custom-call | tf_op jit(solution)/shard_map/solve_body/pallas_call | solution.py:76
  (72 shorter events, 28.0 us)
Async XLA Ops:
  0.6 23.1 %collective-permute-start.3 = (f32[32,2048]{1,0:T(8,128)}, f32[32,2048]{1,0:T(8,128)S(1)}, u32[]{:S(2)}, u32[]{:S(2)}) collective-permute-start(f32[32,2048]{1,0:T(8,128)} %right.1), channel_id=1, source_target_pairs={{0,7},{1,2},{2,1},{3,4},{4,3},{5,6},{6,5},{7,0},{8,15},{9,10},{10,... | collective-permute-start | bytes 786440 | tf_op jit(solution)/shard_map/ppermute | solution.py:31
  4.3 19.4 %collective-permute-start.2 = (f32[32,2048]{1,0:T(8,128)}, f32[32,2048]{1,0:T(8,128)S(1)}, u32[]{:S(2)}, u32[]{:S(2)}) collective-permute-start(f32[32,2048]{1,0:T(8,128)} %right.1), channel_id=1, source_target_pairs={{0,1},{1,0},{2,3},{3,2},{4,5},{5,4},{6,7},{7,6},{8,9},{9,8},{10,11... | collective-permute-start | bytes 786440 | tf_op jit(solution)/shard_map/ppermute | solution.py:31
  4.3 12.4 %collective-permute-start.1 = (f32[32,2048]{1,0:T(8,128)}, f32[32,2048]{1,0:T(8,128)S(1)}, u32[]{:S(2)}, u32[]{:S(2)}) collective-permute-start(f32[32,2048]{1,0:T(8,128)} %right.1), channel_id=1, source_target_pairs={{0,120},{8,16},{16,8},{24,32},{32,24},{40,48},{48,40},{56,64},{64,... | collective-permute-start | bytes 786440 | tf_op jit(solution)/shard_map/ppermute | solution.py:31
  9.5 8.6 %collective-permute-start = (f32[32,2048]{1,0:T(8,128)}, f32[32,2048]{1,0:T(8,128)S(1)}, u32[]{:S(2)}, u32[]{:S(2)}) collective-permute-start(f32[32,2048]{1,0:T(8,128)} %right.1), channel_id=1, source_target_pairs={{0,8},{8,0},{16,24},{24,16},{32,40},{40,32},{48,56},{56,48},{64,72... | collective-permute-start | bytes 786440 | tf_op jit(solution)/shard_map/ppermute | solution.py:31
  18.2 10.8 %collective-permute-start.5 = (f32[2,8,32,256]{3,2,1,0:T(8,128)S(1)}, f32[2,8,32,256]{3,2,1,0:T(8,128)S(1)}, u32[]{:S(2)}, u32[]{:S(2)}) collective-permute-start(f32[2,8,32,256]{3,2,1,0:T(8,128)S(1)} %stack_body.2), channel_id=1, source_target_pairs={{0,7},{1,2},{2,1},{3,4},{4,3},{5,6},{6,5},{7,0},{8,15},{9,10},{10,... | collective-permute-start | bytes 1572872 | tf_op jit(solution)/shard_map/ppermute | solution.py:31
  18.3 10.7 %collective-permute-start.4 = (f32[2,8,32,256]{3,2,1,0:T(8,128)S(1)}, f32[2,8,32,256]{3,2,1,0:T(8,128)S(1)}, u32[]{:S(2)}, u32[]{:S(2)}) collective-permute-start(f32[2,8,32,256]{3,2,1,0:T(8,128)S(1)} %stack_body.2), channel_id=1, source_target_pairs={{0,1},{1,0},{2,3},{3,2},{4,5},{5,4},{6,7},{7,6},{8,9},{9,8},{10,11... | collective-permute-start | bytes 1572872 | tf_op jit(solution)/shard_map/ppermute | solution.py:31
  33.2 7.6 %collective-permute-start.8 = (f32[2,8,32,256]{3,2,1,0:T(8,128)S(1)}, f32[2,8,32,256]{3,2,1,0:T(8,128)S(1)}, u32[]{:S(2)}, u32[]{:S(2)}) collective-permute-start(f32[2,8,32,256]{3,2,1,0:T(8,128)S(1)} %get-tuple-element.54), channel_id=1, source_target_pairs={{0,1},{1,0},{2,3},{3,2},{4,5},{5,4},{6,7},{7,6},{8,9},{9,8},{10,11... | collective-permute-start | bytes 1572872 | tf_op jit(solution)/shard_map/ppermute | solution.py:31
  33.8 9.8 %collective-permute-start.9 = (f32[2,8,32,256]{3,2,1,0:T(8,128)S(1)}, f32[2,8,32,256]{3,2,1,0:T(8,128)S(1)}, u32[]{:S(2)}, u32[]{:S(2)}) collective-permute-start(f32[2,8,32,256]{3,2,1,0:T(8,128)S(1)} %get-tuple-element.55), channel_id=1, source_target_pairs={{0,7},{1,2},{2,1},{3,4},{4,3},{5,6},{6,5},{7,0},{8,15},{9,10},{10,... | collective-permute-start | bytes 1572872 | tf_op jit(solution)/shard_map/ppermute | solution.py:31
  40.2 9.0 %collective-permute-start.6 = (f32[8,32,256]{2,1,0:T(8,128)S(1)}, f32[8,32,256]{2,1,0:T(8,128)S(1)}, u32[]{:S(2)}, u32[]{:S(2)}) collective-permute-start(f32[8,32,256]{2,1,0:T(8,128)S(1)} %get-tuple-element.50), channel_id=1, source_target_pairs={{0,1},{1,0},{2,3},{3,2},{4,5},{5,4},{6,7},{7,6},{8,9},{9,8},{10,11... | collective-permute-start | bytes 786440 | tf_op jit(solution)/shard_map/ppermute | solution.py:31
  40.3 8.9 %collective-permute-start.7 = (f32[8,32,256]{2,1,0:T(8,128)S(1)}, f32[8,32,256]{2,1,0:T(8,128)S(1)}, u32[]{:S(2)}, u32[]{:S(2)}) collective-permute-start(f32[8,32,256]{2,1,0:T(8,128)S(1)} %get-tuple-element.51), channel_id=1, source_target_pairs={{0,7},{1,2},{2,1},{3,4},{4,3},{5,6},{6,5},{7,0},{8,15},{9,10},{10,... | collective-permute-start | bytes 786440 | tf_op jit(solution)/shard_map/ppermute | solution.py:31
  43.7 7.5 %collective-permute-start.10 = (f32[8,32,256]{2,1,0:T(8,128)S(1)}, f32[8,32,256]{2,1,0:T(8,128)S(1)}, u32[]{:S(2)}, u32[]{:S(2)}) collective-permute-start(f32[8,32,256]{2,1,0:T(8,128)S(1)} %get-tuple-element.56), channel_id=1, source_target_pairs={{0,8},{8,0},{16,24},{24,16},{32,40},{40,32},{48,56},{56,48},{64,72... | collective-permute-start | bytes 786440 | tf_op jit(solution)/shard_map/ppermute | solution.py:31
  45.8 10.0 %collective-permute-start.11 = (f32[8,32,256]{2,1,0:T(8,128)S(1)}, f32[8,32,256]{2,1,0:T(8,128)S(1)}, u32[]{:S(2)}, u32[]{:S(2)}) collective-permute-start(f32[8,32,256]{2,1,0:T(8,128)S(1)} %get-tuple-element.57), channel_id=1, source_target_pairs={{0,120},{8,16},{16,8},{24,32},{32,24},{40,48},{48,40},{56,64},{64,... | collective-permute-start | bytes 786440 | tf_op jit(solution)/shard_map/ppermute | solution.py:31
  55.9 7.8 %collective-permute-start.15 = (f32[8,32,256]{2,1,0:T(8,128)S(1)}, f32[8,32,256]{2,1,0:T(8,128)S(1)}, u32[]{:S(2)}, u32[]{:S(2)}) collective-permute-start(f32[8,32,256]{2,1,0:T(8,128)S(1)} %sum_body.1.own.vector.u), channel_id=1, source_target_pairs={{0,7},{1,2},{2,1},{3,4},{4,3},{5,6},{6,5},{7,0},{8,15},{9,10},{10,... | collective-permute-start | bytes 786440 | tf_op jit(solution)/shard_map/ppermute | solution.py:31
  59.7 12.0 %collective-permute-start.13 = (f32[8,32,256]{2,1,0:T(8,128)S(1)}, f32[8,32,256]{2,1,0:T(8,128)S(1)}, u32[]{:S(2)}, u32[]{:S(2)}) collective-permute-start(f32[8,32,256]{2,1,0:T(8,128)S(1)} %sum_body.1.own.vector.u), channel_id=1, source_target_pairs={{0,120},{8,16},{16,8},{24,32},{32,24},{40,48},{48,40},{56,64},{64,... | collective-permute-start | bytes 786440 | tf_op jit(solution)/shard_map/ppermute | solution.py:31
  61.2 10.5 %collective-permute-start.12 = (f32[8,32,256]{2,1,0:T(8,128)S(1)}, f32[8,32,256]{2,1,0:T(8,128)S(1)}, u32[]{:S(2)}, u32[]{:S(2)}) collective-permute-start(f32[8,32,256]{2,1,0:T(8,128)S(1)} %sum_body.1.own.vector.u), channel_id=1, source_target_pairs={{0,8},{8,0},{16,24},{24,16},{32,40},{40,32},{48,56},{56,48},{64,72... | collective-permute-start | bytes 786440 | tf_op jit(solution)/shard_map/ppermute | solution.py:31
  71.7 9.9 %collective-permute-start.17 = (f32[2,8,32,256]{3,2,1,0:T(8,128)S(1)}, f32[2,8,32,256]{3,2,1,0:T(8,128)S(1)}, u32[]{:S(2)}, u32[]{:S(2)}) collective-permute-start(f32[2,8,32,256]{3,2,1,0:T(8,128)S(1)} %stack_body.3), channel_id=1, source_target_pairs={{0,7},{1,2},{2,1},{3,4},{4,3},{5,6},{6,5},{7,0},{8,15},{9,10},{10,... | collective-permute-start | bytes 1572872 | tf_op jit(solution)/shard_map/ppermute | solution.py:31
  71.8 9.8 %collective-permute-start.16 = (f32[2,8,32,256]{3,2,1,0:T(8,128)S(1)}, f32[2,8,32,256]{3,2,1,0:T(8,128)S(1)}, u32[]{:S(2)}, u32[]{:S(2)}) collective-permute-start(f32[2,8,32,256]{3,2,1,0:T(8,128)S(1)} %stack_body.3), channel_id=1, source_target_pairs={{0,1},{1,0},{2,3},{3,2},{4,5},{5,4},{6,7},{7,6},{8,9},{9,8},{10,11... | collective-permute-start | bytes 1572872 | tf_op jit(solution)/shard_map/ppermute | solution.py:31
  91.7 24.4 %collective-permute-start.25 = (f32[3,8,32,256]{3,2,1,0:T(8,128)S(1)}, f32[3,8,32,256]{3,2,1,0:T(8,128)S(1)}, u32[]{:S(2)}, u32[]{:S(2)}) collective-permute-start(f32[3,8,32,256]{3,2,1,0:T(8,128)S(1)} %get-tuple-element.70), channel_id=1, source_target_pairs={{0,1},{1,0},{2,3},{3,2},{4,5},{5,4},{6,7},{7,6},{8,9},{9,8},{10,11... | collective-permute-start | bytes 2359304 | tf_op jit(solution)/shard_map/ppermute | solution.py:31
  91.8 24.3 %collective-permute-start.26 = (f32[3,8,32,256]{3,2,1,0:T(8,128)S(1)}, f32[3,8,32,256]{3,2,1,0:T(8,128)S(1)}, u32[]{:S(2)}, u32[]{:S(2)}) collective-permute-start(f32[3,8,32,256]{3,2,1,0:T(8,128)S(1)} %get-tuple-element.71), channel_id=1, source_target_pairs={{0,7},{1,2},{2,1},{3,4},{4,3},{5,6},{6,5},{7,0},{8,15},{9,10},{10,... | collective-permute-start | bytes 2359304 | tf_op jit(solution)/shard_map/ppermute | solution.py:31
  96.3 4.9 %collective-permute-start.20 = (f32[32,128]{1,0:T(8,128)S(1)}, f32[32,128]{1,0:T(8,128)S(1)}, u32[]{:S(2)}, u32[]{:S(2)}) collective-permute-start(f32[32,128]{1,0:T(8,128)S(1)} %add.139), channel_id=1, source_target_pairs={{0,24},{1,25},{2,26},{3,27},{4,28},{5,29},{6,30},{7,31},{8,16},{9,... | collective-permute-start | bytes 49160 | tf_op jit(solution)/shard_map/ppermute | solution.py:291
  105.0 4.9 %collective-permute-start.22 = (f32[32,128]{1,0:T(8,128)S(1)}, f32[32,128]{1,0:T(8,128)S(1)}, u32[]{:S(2)}, u32[]{:S(2)}) collective-permute-start(f32[32,128]{1,0:T(8,128)S(1)} %add.141), channel_id=1, source_target_pairs={{0,96},{1,97},{2,98},{3,99},{4,100},{5,101},{6,102},{7,103},{8,104... | collective-permute-start | bytes 49160 | tf_op jit(solution)/shard_map/ppermute | solution.py:291
  111.1 4.9 %collective-permute-start.24 = (f32[32,128]{1,0:T(8,128)S(1)}, f32[32,128]{1,0:T(8,128)S(1)}, u32[]{:S(2)}, u32[]{:S(2)}) collective-permute-start(f32[32,128]{1,0:T(8,128)S(1)} %add.143.grams), channel_id=1, source_target_pairs={{0,6},{1,7},{2,4},{3,5},{4,2},{5,3},{6,0},{7,1},{8,14},{9,15},{10,... | collective-permute-start | bytes 49160 | tf_op jit(solution)/shard_map/ppermute | solution.py:291
  116.2 9.8 %collective-permute-start.27 = (f32[8,32,256]{2,1,0:T(8,128)S(1)}, f32[8,32,256]{2,1,0:T(8,128)S(1)}, u32[]{:S(2)}, u32[]{:S(2)}) collective-permute-start(f32[8,32,256]{2,1,0:T(8,128)S(1)} %get-tuple-element.74), channel_id=1, source_target_pairs={{0,8},{8,0},{16,24},{24,16},{32,40},{40,32},{48,56},{56,48},{64,72... | collective-permute-start | bytes 786440 | tf_op jit(solution)/shard_map/ppermute | solution.py:31
  116.3 10.6 %collective-permute-start.28 = (f32[8,32,256]{2,1,0:T(8,128)S(1)}, f32[8,32,256]{2,1,0:T(8,128)S(1)}, u32[]{:S(2)}, u32[]{:S(2)}) collective-permute-start(f32[8,32,256]{2,1,0:T(8,128)S(1)} %get-tuple-element.75), channel_id=1, source_target_pairs={{0,120},{8,16},{16,8},{24,32},{32,24},{40,48},{48,40},{56,64},{64,... | collective-permute-start | bytes 786440 | tf_op jit(solution)/shard_map/ppermute | solution.py:31
  (7 other events, 32.2 us)

commit v3 on v2

v3 whole, which is shorter than its diff:
```python
import jax
import jax.numpy as jnp
from jax import lax
from jax.experimental import pallas as pl
from jax.experimental.pallas import tpu as pltpu
from jax.sharding import PartitionSpec as P

F32 = jnp.float32
BF16 = jnp.bfloat16
HIGHEST = lax.Precision.HIGHEST
VMEM_SPEC = pl.BlockSpec(memory_space=pltpu.VMEM)
SMEM_SPEC = pl.BlockSpec(memory_space=pltpu.SMEM)
CHUNK = 8
PREPARED = 4
PARTS = 2
NEAR_TABLES = 7
TOKEN = pltpu.VMEM((8, 128), F32)


def in_vmem(value):
    return pltpu.with_memory_space_constraint(value, pltpu.VMEM)


def in_hbm(value):
    return pltpu.with_memory_space_constraint(value, pltpu.HBM)


def pairs_of(count, shift):
    return [(place, (((place + shift) ^ 1) - shift) % count) for place in range(count)]


def swapped(value, axis, shift):
    return lax.ppermute(value, axis, pairs_of(lax.axis_size(axis), shift))


def slot_of(target, mine):
    return jnp.where(target == mine, 0, jnp.where(target == (mine ^ 1), 1, 2))


def split(value):
    high = value.astype(BF16)
    return high, (value - high.astype(F32)).astype(BF16)


def dot_nt(left, right):
    return lax.dot_general(left, right, (((1,), (1,)), ((), ())), preferred_element_type=F32)


def dot_nn(left, right):
    return lax.dot_general(left, right, (((1,), (0,)), ((), ())), preferred_element_type=F32)


def full_nn(left, right):
    return lax.dot_general(left, right, (((1,), (0,)), ((), ())), precision=HIGHEST, preferred_element_type=F32)


def full_tn(left, right):
    return lax.dot_general(left, right, (((0,), (0,)), ((), ())), precision=HIGHEST, preferred_element_type=F32)


def gram(left, right):
    both = dot_nt(left, right)
    half = both.shape[0] // 2
    return both[:half, :half] + both[:half, half:] + both[half:, :half] + both[half:, half:]


def times(dot, stacked, high, low):
    half = stacked.shape[0] // 2
    first = dot(stacked, high)
    return first[:half] + first[half:] + dot(stacked[:half], low)


def stacked_split(value):
    return jnp.concatenate(split(value), axis=0)


def call(body, out_shape, n_smem, args, scratch=(), aliases=None, limit=12 << 20):
    return pl.pallas_call(
        body,
        out_shape=out_shape,
        in_specs=[SMEM_SPEC] * n_smem + [VMEM_SPEC] * (len(args) - n_smem),
        out_specs=jax.tree.map(lambda _: VMEM_SPEC, out_shape),
        scratch_shapes=list(scratch),
        name=body.__name__,
        input_output_aliases=aliases or {},
        compiler_params=pltpu.CompilerParams(vmem_limit_bytes=limit),
    )(*args[:n_smem], *[in_vmem(a) for a in args[n_smem:]])


def prepare_body(couplings, c_high, c_low, token):
    per = couplings.shape[0]
    first = pl.program_id(0) * per
    token[...] = jnp.zeros_like(token)
    for place in range(per):
        high, low = split(couplings[place])
        c_high[first + place] = high
        c_low[first + place] = low


def part_edges(count):
    return (0, count * 5 // (8 * CHUNK) * CHUNK, count)


def prepare(couplings, part):
    width = couplings.shape[1]
    first, last = part_edges(couplings.shape[0])[part:part + 2]
    skip = first // PREPARED
    shape = pltpu.VMEM((last - first, width, width), BF16)
    return pl.pallas_call(
        prepare_body,
        grid=((last - first) // PREPARED,),
        in_specs=[pl.BlockSpec((PREPARED, width, width), lambda i: (i + skip, 0, 0))],
        out_specs=[VMEM_SPEC] * 3,
        out_shape=[shape, shape, TOKEN],
        name="prepare",
        compiler_params=pltpu.CompilerParams(vmem_limit_bytes=12 << 20),
    )(in_hbm(couplings))


def block_of(source, q, width):
    return source[q] if len(source.shape) == 3 else source[:, q * width:(q + 1) * width]


def stack_body(*refs):
    vectors, whole, pair = refs[-5:-2], refs[-2], refs[-1]
    blocks, width = whole.shape[1], whole.shape[3]
    for slot, source in enumerate(vectors):
        for q in range(blocks):
            block = block_of(source, q, width)
            whole[slot, q] = block
            if slot:
                pair[slot - 1, q] = block


def accumulate(dot, late, routes, edges, source_row, target_row, source, target, parts):
    for part in range(PARTS):
        c_high, c_low = parts[2 * part], parts[2 * part + 1]

        def step(chunk, carry):
            terms = []
            for place in range(CHUNK):
                i = chunk * CHUNK + place
                k = routes[0, i]
                terms.append((routes[target_row, i], times(dot, source[routes[source_row, i]], c_high[k], c_low[k])))
            for row, term in terms:
                target[row] += term
            return carry

        low, high = part_edges(routes.shape[1])[part:part + 2]
        middle = edges[part] // CHUNK
        first, last = (middle, high // CHUNK) if late else (low // CHUNK, middle)
        lax.fori_loop(first, last, step, 0)


def pull_near_body(routes, edges, qa, whole, cb, *refs):
    parts, (table, strain) = refs[:2 * PARTS], refs[2 * PARTS:]
    blocks = strain.shape[0]
    for place, (source, slot) in enumerate(
            ((whole, 0), (whole, 1), (whole, 2), (qa, 0), (cb, None), (qa, 1), (qa, 2))):
        for q in range(blocks):
            block = block_of(source, q, strain.shape[2]) if slot is None else source[slot, q]
            table[place * blocks + q] = stacked_split(block)
    strain[...] = jnp.zeros_like(strain)
    accumulate(dot_nt, False, routes, edges, 1, 2, table, strain, parts)


def pull_late_body(routes, edges, table_in, strain_in, db, *refs):
    parts, refs = refs[:2 * PARTS], refs[2 * PARTS:]
    *grams, table, strain_hl, g_out, strain = refs
    blocks = strain.shape[0]
    for slot in range(2):
        for q in range(blocks):
            table[(NEAR_TABLES + slot) * blocks + q] = stacked_split(db[slot, q])
    strain[...] = strain_in[...]
    accumulate(dot_nt, True, routes, edges, 1, 2, table, strain, parts)
    total = jnp.zeros((strain.shape[1],) * 2, F32)
    for q in range(blocks):
        both = stacked_split(strain[q])
        strain_hl[q] = both
        total += gram(both, both)
    if not grams:
        g_out[...] = total
    else:
        g01, g1, g23 = grams
        size = total.shape[0]
        for i, part in enumerate((g01[0], g01[1] + g1[...], g23[0], g23[1] + total)):
            g_out[:, i * size:(i + 1) * size] = part


def push_late_body(routes, edges, strain_hl, *refs):
    parts, (pieces, *targets) = refs[:2 * PARTS], refs[2 * PARTS:]
    blocks = strain_hl.shape[0]
    pieces[...] = jnp.zeros_like(pieces)
    accumulate(dot_nn, True, routes, edges, 2, 1, strain_hl, pieces, parts)
    for db in targets:
        for slot in range(2):
            for q in range(blocks):
                db[slot, q] = pieces[(NEAR_TABLES + slot) * blocks + q]


def push_near(routes, edges, strain_hl, parts, pieces_in, pieces, targets):
    blocks = strain_hl.shape[0]
    pieces[...] = pieces_in[:pieces.shape[0]]
    accumulate(dot_nn, False, routes, edges, 2, 1, strain_hl, pieces, parts)
    for target, place in targets:
        for q in range(blocks):
            target[q] = pieces[place * blocks + q]


def push_near_body(routes, edges, strain_hl, *refs):
    parts, pieces_in, outs = refs[:2 * PARTS], refs[2 * PARTS], refs[2 * PARTS + 1:]
    *outs, pieces = outs
    push_near(routes, edges, strain_hl, parts, pieces_in, pieces, zip(outs, range(NEAR_TABLES)))


def push_last_body(routes, edges, strain_hl, *refs):
    parts, pieces_in, outs = refs[:2 * PARTS], refs[2 * PARTS], refs[2 * PARTS + 2:]
    *outs, qa, qb, pieces = outs
    outs += [qa.at[0], qa.at[1], qa.at[2], qb.at[0], qb.at[1], qb.at[2]]
    push_near(routes, edges, strain_hl, parts, pieces_in, pieces, zip(outs, (0, 1, 2, 3, 5, 6, 4, 7, 8)))


def diag_body(vector, diag, own, grams):
    size = grams.shape[1]
    first = jnp.zeros((size, size), F32)
    second = jnp.zeros((size, size), F32)
    width = diag.shape[1]
    for q in range(diag.shape[0]):
        both = stacked_split(block_of(vector, q, width))
        term = times(dot_nn, both, *split(diag[q]))
        own[q] = term
        first += gram(both, both)
        second += gram(stacked_split(term), both)
    grams[0] = first
    grams[1] = second


def middle_early_body(ra, rb, qa_first, qa_second, db, ma, mb):
    ma[...] = ra[...] + qa_first[...] + db[0]
    mb[...] = rb[...] + qa_second[...] + db[1]


def middle_last_body(own, diag, ra, rb, qa, qb, grams, rest, ma, mb):
    rest[...] = (own[...] + diag[...]) + (qa[0] + qb[0])
    ma[...] = ra[...] + qa[1] + qb[1]
    mb[...] = rb[...] + qa[2] + qb[2]


def sum_body(own, diag, ca, cb, ra, rb, out):
    out[...] = (own[...] + diag[...]) + (ca[...] + cb[...]) + (ra[...] + rb[...])


def eliminated(matrix, right):
    size = matrix.shape[0]
    on_diagonal = lax.broadcasted_iota(jnp.int32, (size, size), 0) == lax.broadcasted_iota(jnp.int32, (size, size), 1)
    diagonal = jnp.where(on_diagonal, matrix, 0.0)
    across = lax.rsqrt(jnp.sum(diagonal, axis=0, keepdims=True))
    down = lax.rsqrt(jnp.sum(diagonal, axis=1, keepdims=True))
    work = jnp.concatenate([matrix * down * across, right * down], axis=1)
    rows = lax.broadcasted_iota(jnp.int32, work.shape, 0)
    for k in range(0, size, 2):
        first = jnp.broadcast_to(work[:, k:k + 1], work.shape)
        second = jnp.broadcast_to(work[:, k + 1:k + 2], work.shape)
        upper, lower = work[k:k + 1, :], work[k + 1:k + 2, :]
        a, b, c, d = first[k:k + 1], second[k:k + 1], first[k + 1:k + 2], second[k + 1:k + 2]
        inverse = 1.0 / (a * d - b * c)
        new_upper = (d * upper - b * lower) * inverse
        new_lower = (a * lower - c * upper) * inverse
        rest = work - first * new_upper - second * new_lower
        work = jnp.where(rows == k, new_upper, jnp.where(rows == k + 1, new_lower, rest))
    return work[:, size:] * down


def solve_body(grams, moved, p, q):
    size = grams.shape[0]
    total = grams[...] + moved[...]
    g0, g1, g2, g3 = (total[:, i * size:(i + 1) * size] for i in range(4))
    eye = (lax.broadcasted_iota(jnp.int32, (size, size), 0) == lax.broadcasted_iota(jnp.int32, (size, size), 1)).astype(F32)
    alpha = eliminated(g1, g0)
    inverse = eliminated(g0, eye)
    fresh = (g0 - full_nn(g1, alpha)) - full_tn(alpha, g1 - full_nn(g2, alpha))
    mix = eye + full_nn(inverse, fresh)
    e1 = full_nn(g1, mix) - full_nn(g2, alpha)
    e2 = full_nn(g2, mix) - full_nn(g3, alpha)
    curvature = full_tn(mix, e1) - full_tn(alpha, e2)
    second = eliminated(curvature, fresh)
    p[...] = alpha + full_nn(mix, second)
    q[...] = full_nn(alpha, second)


def finish_body(p, q, right, u, rest, ra, rb, x_out, r_out):
    width = u.shape[2]
    for block in range(u.shape[0]):
        lanes = slice(block * width, (block + 1) * width)
        w = rest[block] + ra[block] + rb[block]
        x_out[:, lanes] = full_tn(p[...], right[:, lanes]) - full_tn(q[...], u[block])
        r_out[:, lanes] = right[:, lanes] - full_tn(p[...], u[block]) + full_tn(q[...], w)


MASKS = (2, 8, 24, 32, 96, 1, 6)


def exchanged(value, mask):
    count = lax.axis_size("row") * lax.axis_size("col")
    return lax.ppermute(value, ("row", "col"), [(i, i ^ mask) for i in range(count)])


def routing(pair_index, blocks):
    count = pair_index.shape[1]
    col_size = lax.axis_size("col")
    my_row, my_col = lax.axis_index("row"), lax.axis_index("col")
    local_row = pair_index[0] - (my_row * col_size + my_col) * blocks
    owner = pair_index[1] // blocks
    row_slot = slot_of(owner // col_size, my_row)
    col_slot = slot_of(owner % col_size, my_col)
    diagonal = (row_slot > 0) & (col_slot > 0)
    slot = jnp.where(diagonal, 2 + 2 * col_slot + row_slot, jnp.where(col_slot > 0, 2 + col_slot, row_slot))
    table_row = slot * blocks + pair_index[1] % blocks
    late = slot >= NEAR_TABLES
    number = jnp.arange(count, dtype=jnp.int32)
    split_at = part_edges(count)[1]
    part = (number >= split_at).astype(jnp.int32)
    key = (2 * part + late.astype(jnp.int32)) * count + number
    rank = jnp.sum((key[None, :] < key[:, None]).astype(jnp.int32), axis=1)
    placed = rank[None, :] == number[:, None]
    columns = (number - part * split_at, table_row, local_row)
    routes = jnp.stack([jnp.sum(jnp.where(placed, c[None, :], 0), axis=1) for c in columns])
    starts = jnp.arange(PARTS, dtype=jnp.int32)
    early = (part[None, :] == starts[:, None]) & ~late[None, :]
    edges = starts * split_at + jnp.sum(early.astype(jnp.int32), axis=1)
    return routes, edges


def per_device(right_sides, diag_blocks, couplings, pair_index):
    blocks, width = diag_blocks.shape[0], diag_blocks.shape[1]
    rows = right_sides.shape[0]
    block_shape = pltpu.VMEM((blocks, rows, width), F32)
    stack_shape = pltpu.VMEM((3, blocks, rows, width), F32)
    pair_shape = pltpu.VMEM((2, blocks, rows, width), F32)
    table_shape = pltpu.VMEM((9 * blocks, 2 * rows, width), BF16)
    split_shape = pltpu.VMEM((blocks, 2 * rows, width), BF16)
    pieces_shape = pltpu.VMEM((9 * blocks, rows, width), F32)
    near_pieces_shape = pltpu.VMEM((NEAR_TABLES * blocks, rows, width), F32)
    gram_shape = pltpu.VMEM((rows, rows), F32)
    grams_shape = pltpu.VMEM((2, rows, rows), F32)
    all_grams_shape = pltpu.VMEM((rows, 4 * rows), F32)

    def spread(vector, *after):
        cb = swapped(vector, "col", 1)
        ra, rb = swapped(vector, "row", 0), swapped(vector, "row", 1)
        whole, pair = call(stack_body, [stack_shape, pair_shape], 0, (after or (cb,)) + (vector, ra, rb))
        return (swapped(whole, "col", 0), whole, cb), swapped(pair, "col", 1)

    def pulled(near_tables, db, couplings, *grams):
        table, strain = call(pull_near_body, [table_shape, block_shape], 2, (routes, edges, *near_tables, *couplings))
        _, strain_hl, g = call(
            pull_late_body, [table_shape, split_shape, all_grams_shape if grams else gram_shape], 2,
            (routes, edges, table, strain, db, *couplings, *grams), [block_shape], aliases={2: 0})
        return strain_hl, g

    routes, edges = routing(pair_index, blocks)
    *larger, token = prepare(couplings, 0)
    near_tables, db = spread(right_sides, token)
    *smaller, _ = prepare(couplings, 1)
    couplings = larger + smaller
    strain_hl, g1s = pulled(near_tables, db, couplings)

    pieces, db = call(push_late_body, [pieces_shape, pair_shape], 2, (routes, edges, strain_hl, *couplings))
    db = swapped(db, "col", 1)
    own, ra, rb, ca, cb, qa_first, qa_second = call(
        push_near_body, [block_shape] * NEAR_TABLES, 2,
        (routes, edges, strain_hl, *couplings, pieces), [near_pieces_shape])
    ca, qa_first, qa_second = (swapped(a, "col", 0) for a in (ca, qa_first, qa_second))
    cb = swapped(cb, "col", 1)
    diag, g01 = call(diag_body, [block_shape, grams_shape], 0, (right_sides, diag_blocks))
    ra, rb = call(middle_early_body, [block_shape] * 2, 0, (ra, rb, qa_first, qa_second, db))
    ra, rb = swapped(ra, "row", 0), swapped(rb, "row", 1)
    u = call(sum_body, block_shape, 0, (own, diag, ca, cb, ra, rb))

    near_tables, db = spread(u)
    diag, g23 = call(diag_body, [block_shape, grams_shape], 0, (u, diag_blocks))
    strain_hl, grams = pulled(near_tables, db, couplings, g01, g1s, g23)
    pieces, = call(push_late_body, [pieces_shape], 2, (routes, edges, strain_hl, *couplings))
    grams = grams + exchanged(grams, MASKS[0])
    own, ra, rb, qa, qb = call(
        push_last_body, [block_shape] * 3 + [stack_shape] * 2, 2,
        (routes, edges, strain_hl, *couplings, pieces, grams), [pieces_shape])
    qa, qb = swapped(qa, "col", 0), swapped(qb, "col", 1)
    for mask in MASKS[1:4]:
        grams = grams + exchanged(grams, mask)
    rest, ra, rb = call(middle_last_body, [block_shape] * 3, 0, (own, diag, ra, rb, qa, qb, grams))
    ra, rb = swapped(ra, "row", 0), swapped(rb, "row", 1)
    for mask in MASKS[4:-1]:
        grams = grams + exchanged(grams, mask)
    p, q = call(solve_body, [gram_shape] * 2, 0, (grams, exchanged(grams, MASKS[-1])))
    flat = jax.ShapeDtypeStruct(right_sides.shape, F32)
    return tuple(call(finish_body, [flat, flat], 0, (p, q, right_sides, u, rest, ra, rb)))


def solution(mesh):
    return jax.shard_map(
        per_device,
        mesh=mesh,
        in_specs=(
            P(None, ("row", "col")),
            P(("row", "col"), None, None),
            P(("row", "col"), None, None),
            P(None, ("row", "col")),
        ),
        out_specs=(P(None, ("row", "col")), P(None, ("row", "col"))),
        check_vma=False,
    )
```

time: 129 us -> 127 us (0.984)
  starting transfers between devices: 26.3 us -> 22.7 us
    ppermute x7, waiting for transfers between devices: 24.9 us -> 30.1 us  [exchanged(): lax.ppermute(value, ('row', 'col'), [(i, i ^ mask) for i in range(count)])]
    ppermute x22 -> x21, waiting for transfers between devices: 26.3 us -> 21.4 us  [swapped(): return lax.ppermute(value, axis, pairs_of(lax.axis_size(axis), shift))]
    ppermute x22 -> x21, starting transfers between devices: 25.7 us -> 22.3 us  [swapped(): return lax.ppermute(value, axis, pairs_of(lax.axis_size(axis), shift))]
    pallas_call x2, Pallas kernels: 9.54 us -> 12.7 us  [prepare(): pl.pallas_call(prepare_body, grid=((last - first) // PREPARED,), in_specs...]
    pallas_call x17, Pallas kernels: 39.2 us -> 36.9 us  [call(): pl.pallas_call(body, out_shape=out_shape, in_specs=[SMEM_SPEC] * n_smem +...]
  transfers between devices with their start and end apart: 29 -> 28, of which waited for: 16 -> 14; matrix products, arithmetic and copies ran while one was open for 1% -> 2% of each run, Pallas kernels for 28% -> 32%
where the time goes in v3:
time: 127 us
  waiting for transfers between devices  51.6 us (41%)
  Pallas kernels  49.6 us (39%)
  starting transfers between devices  22.7 us (18%)
  other arithmetic  1.92 us (2%)
    pallas_call x17, Pallas kernels, call(): pl.pallas_call(body, out_shape=out_shape, in_specs=[SMEM_SPEC] * n_smem +...  36.9 us
    ppermute x7, waiting for transfers between devices, exchanged(): lax.ppermute(value, ('row', 'col'), [(i, i ^ mask) for i in range(count)])  30.1 us
    ppermute x21, starting transfers between devices, swapped(): return lax.ppermute(value, axis, pairs_of(lax.axis_size(axis), shift))  22.3 us
    ppermute x21, waiting for transfers between devices, swapped(): return lax.ppermute(value, axis, pairs_of(lax.axis_size(axis), shift))  21.4 us
    pallas_call x2, Pallas kernels, prepare(): pl.pallas_call(prepare_body, grid=((last - first) // PREPARED,), in_specs...  12.7 us
  transfers between devices with their start and end apart: 28, of which 14 were waited for; matrix products, arithmetic and copies ran while one was open for 2% of the time, Pallas kernels for 32%

profile of v3, /device:TPU:0, one launch (start us, length us, event | category | flops | bytes accessed | tf_op | source)
XLA Modules:
  0.0 126.7 jit_solution(1254226551357203744)
XLA Ops:
  0.6 3.6 %collective-permute-start.3 = (f32[32,2048]{1,0:T(8,128)}, f32[32,2048]{1,0:T(8,128)S(1)}, u32[]{:S(2)}, u32[]{:S(2)}) collective-permute-start(f32[32,2048]{1,0:T(8,128)} %right.1), channel_id=1, source_target_pairs={{0,7},{1,2},{2,1},{3,4},{4,3},{5,6},{6,5},{7,0},{8,15},{9,10},{10,... | collective-permute-start | bytes 786440 | tf_op jit(solution)/shard_map/ppermute | solution.py:33
  4.3 5.2 %collective-permute-start.1 = (f32[32,2048]{1,0:T(8,128)}, f32[32,2048]{1,0:T(8,128)S(1)}, u32[]{:S(2)}, u32[]{:S(2)}) collective-permute-start(f32[32,2048]{1,0:T(8,128)} %right.1), channel_id=1, source_target_pairs={{0,120},{8,16},{16,8},{24,32},{32,24},{40,48},{48,40},{56,64},{64,... | collective-permute-start | bytes 786440 | tf_op jit(solution)/shard_map/ppermute | solution.py:33
  10.9 7.6 %prepare.2 = (bf16[40,256,256]{2,1,0:T(8,128)(2,1)S(1)}, bf16[40,256,256]{2,1,0:T(8,128)(2,1)S(1)}, f32[8,128]{1,0:T(8,128)S(1)}) custom-call(f32[64,256,256]{2,1,0:T(8,128)} %couplings.3), custom_call_target="tpu_custom_call" | custom-call | tf_op jit(solution)/shard_map/prepare/pallas_call | solution.py:109
  20.1 5.1 %prepare.3 = (bf16[24,256,256]{2,1,0:T(8,128)(2,1)S(1)}, bf16[24,256,256]{2,1,0:T(8,128)(2,1)S(1)}, f32[8,128]{1,0:T(8,128)}) custom-call(f32[64,256,256]{2,1,0:T(8,128)} %couplings.3), custom_call_target="tpu_custom_call" | custom-call | tf_op jit(solution)/shard_map/prepare/pallas_call | solution.py:109
  25.2 6.7 %pull_near_body.2 = (bf16[72,64,256]{2,1,0:T(8,128)(2,1)S(1)}, f32[8,32,256]{2,1,0:T(8,128)S(1)}) custom-call(s32[3,64]{1,0:T(4,128)S(1)} %pad_add_fusion.routes, s32[2]{0:T(128)S(1)} %multiply_add_fusion.edges, f32[3,8,32,256]{3,2,1,0:T(8,128)S(1)} %collective-permute-done.2.qa, f32[3,8,32,256]{3,2,1,0:T(8,128)S(1)} %get-tuple-element.45.whole, ...), custom_call_target="tpu_custom_call" | custom-call | tf_op jit(solution)/shard_map/pull_near_body/pallas_call | solution.py:78
  33.7 2.3 %collective-permute-start.9 = (f32[2,8,32,256]{3,2,1,0:T(8,128)S(1)}, f32[2,8,32,256]{3,2,1,0:T(8,128)S(1)}, u32[]{:S(2)}, u32[]{:S(2)}) collective-permute-start(f32[2,8,32,256]{3,2,1,0:T(8,128)S(1)} %get-tuple-element.63), channel_id=1, source_target_pairs={{0,7},{1,2},{2,1},{3,4},{4,3},{5,6},{6,5},{7,0},{8,15},{9,10},{10,... | collective-permute-start | bytes 1572872 | tf_op jit(solution)/shard_map/ppermute | solution.py:33
  36.0 4.5 %push_near_body.1 = (f32[8,32,256]{2,1,0:T(8,128)S(1)}, f32[8,32,256]{2,1,0:T(8,128)S(1)}, f32[8,32,256]{2,1,0:T(8,128)S(1)}, f32[8,32,256]{2,1,0:T(8,128)S(1)},...) custom-call(s32[3,64]{1,0:T(4,128)S(1)} %pad_add_fusion.routes, ...), custom_call_target="tpu_custom_call" | custom-call | tf_op jit(solution)/shard_map/push_near_body/pallas_call | solution.py:78
  43.7 2.1 %collective-permute-start.10 = (f32[8,32,256]{2,1,0:T(8,128)S(1)}, f32[8,32,256]{2,1,0:T(8,128)S(1)}, u32[]{:S(2)}, u32[]{:S(2)}) collective-permute-start(f32[8,32,256]{2,1,0:T(8,128)S(1)} %get-tuple-element.64), channel_id=1, source_target_pairs={{0,8},{8,0},{16,24},{24,16},{32,40},{40,32},{48,56},{56,48},{64,72... | collective-permute-start | bytes 786440 | tf_op jit(solution)/shard_map/ppermute | solution.py:33
  46.3 1.7 %diag_body.2 = (f32[8,32,256]{2,1,0:T(8,128)S(1)}, f32[2,32,32]{2,1,0:T(8,128)S(1)}) custom-call(f32[32,2048]{1,0:T(8,128)S(1)} %copy-done.1, f32[8,256,256]{2,1,0:T(8,128)S(1)} %copy-done), custom_call_target="tpu_custom_call" | custom-call | tf_op jit(solution)/shard_map/diag_body/pallas_call | solution.py:78
  48.1 4.7 %collective-permute-done.10.ra = f32[8,32,256]{2,1,0:T(8,128)S(1)} collective-permute-done((f32[8,32,256]{2,1,0:T(8,128)S(1)}, f32[8,32,256]{2,1,0:T(8,128)S(1)}, u32[]{:S(2)}, u32[]{:S(2)}) %collective-permute-start.10) | collective-permute-done | bytes 262176 | tf_op jit(solution)/shard_map/ppermute | solution.py:33
  52.8 5.0 %collective-permute-done.11.rb = f32[8,32,256]{2,1,0:T(8,128)S(1)} collective-permute-done((f32[8,32,256]{2,1,0:T(8,128)S(1)}, f32[8,32,256]{2,1,0:T(8,128)S(1)}, u32[]{:S(2)}, u32[]{:S(2)}) %collective-permute-start.11) | collective-permute-done | bytes 262176 | tf_op jit(solution)/shard_map/ppermute | solution.py:33
  59.3 10.0 %collective-permute-done.14.refs_3_ = f32[8,32,256]{2,1,0:T(8,128)S(1)} collective-permute-done((f32[8,32,256]{2,1,0:T(8,128)S(1)}, f32[8,32,256]{2,1,0:T(8,128)S(1)}, u32[]{:S(2)}, u32[]{:S(2)}) %collective-permute-start.14) | collective-permute-done | bytes 262176 | tf_op jit(solution)/shard_map/ppermute | solution.py:33
  69.5 1.8 %collective-permute-start.16 = (f32[2,8,32,256]{3,2,1,0:T(8,128)S(1)}, f32[2,8,32,256]{3,2,1,0:T(8,128)S(1)}, u32[]{:S(2)}, u32[]{:S(2)}) collective-permute-start(f32[2,8,32,256]{3,2,1,0:T(8,128)S(1)} %get-tuple-element.69), channel_id=1, source_target_pairs={{0,7},{1,2},{2,1},{3,4},{4,3},{5,6},{6,5},{7,0},{8,15},{9,10},{10,... | collective-permute-start | bytes 1572872 | tf_op jit(solution)/shard_map/ppermute | solution.py:33
  71.3 1.7 %diag_body.3 = (f32[8,32,256]{2,1,0:T(8,128)S(1)}, f32[2,32,32]{2,1,0:T(8,128)S(1)}) custom-call(f32[8,32,256]{2,1,0:T(8,128)S(1)} %sum_body.1.refs_1_.vector.u, f32[8,256,256]{2,1,0:T(8,128)S(1)} %copy-done), custom_call_target="tpu_custom_call" | custom-call | tf_op jit(solution)/shard_map/diag_body/pallas_call | solution.py:78
  73.1 6.9 %pull_near_body.3 = (bf16[72,64,256]{2,1,0:T(8,128)(2,1)S(1)}, f32[8,32,256]{2,1,0:T(8,128)S(1)}) custom-call(s32[3,64]{1,0:T(4,128)S(1)} %pad_add_fusion.routes, s32[2]{0:T(128)S(1)} %multiply_add_fusion.edges, f32[3,8,32,256]{3,2,1,0:T(8,128)S(1)} %collective-permute-done.15.qa, f32[3,8,32,256]{3,2,1,0:T(8,128)S(1)} %get-tuple-element.66.whole, ...), custom_call_target="tpu_custom_call" | custom-call | tf_op jit(solution)/shard_map/pull_near_body/pallas_call | solution.py:78
  82.0 2.7 %collective-permute-done.17 = f32[32,128]{1,0:T(8,128)S(1)} collective-permute-done((f32[32,128]{1,0:T(8,128)S(1)}, f32[32,128]{1,0:T(8,128)S(1)}, u32[]{:S(2)}, u32[]{:S(2)}) %collective-permute-start.17) | collective-permute-done | bytes 16416 | tf_op jit(solution)/shard_map/ppermute | solution.py:305
  84.8 4.5 %push_last_body.1 = (f32[8,32,256]{2,1,0:T(8,128)S(1)}, f32[8,32,256]{2,1,0:T(8,128)S(1)}, f32[8,32,256]{2,1,0:T(8,128)S(1)}, f32[3,8,32,256]{3,2,1,0:T(8,128)S(1)}, f32[3,8,32,256]{3,2,1,0:T(8,128)S(1)}) custom-call(s32[3,64]{1,0:T(4,128)S(1)} %pad_add_fusion.routes, s32[2]{0:T(128)S(1)} %multiply_add_fusion.edges, ...), custom_call_target="tpu_custom_call" | custom-call | tf_op jit(solution)/shard_map/push_last_body/pallas_call | solution.py:78
  90.6 3.7 %collective-permute-done.18 = f32[32,128]{1,0:T(8,128)S(1)} collective-permute-done((f32[32,128]{1,0:T(8,128)S(1)}, f32[32,128]{1,0:T(8,128)S(1)}, u32[]{:S(2)}, u32[]{:S(2)}) %collective-permute-start.18) | collective-permute-done | bytes 16416 | tf_op jit(solution)/shard_map/ppermute | solution.py:305
  94.3 4.9 %collective-permute-done.19 = f32[32,128]{1,0:T(8,128)S(1)} collective-permute-done((f32[32,128]{1,0:T(8,128)S(1)}, f32[32,128]{1,0:T(8,128)S(1)}, u32[]{:S(2)}, u32[]{:S(2)}) %collective-permute-start.19) | collective-permute-done | bytes 16416 | tf_op jit(solution)/shard_map/ppermute | solution.py:305
  99.3 3.7 %collective-permute-done.20 = f32[32,128]{1,0:T(8,128)S(1)} collective-permute-done((f32[32,128]{1,0:T(8,128)S(1)}, f32[32,128]{1,0:T(8,128)S(1)}, u32[]{:S(2)}, u32[]{:S(2)}) %collective-permute-start.20) | collective-permute-done | bytes 16416 | tf_op jit(solution)/shard_map/ppermute | solution.py:305
  104.8 8.8 %collective-permute-done.21 = f32[32,128]{1,0:T(8,128)S(1)} collective-permute-done((f32[32,128]{1,0:T(8,128)S(1)}, f32[32,128]{1,0:T(8,128)S(1)}, u32[]{:S(2)}, u32[]{:S(2)}) %collective-permute-start.21) | collective-permute-done | bytes 16416 | tf_op jit(solution)/shard_map/ppermute | solution.py:305
  114.8 4.9 %collective-permute-done.23.moved = f32[32,128]{1,0:T(8,128)S(1)} collective-permute-done((f32[32,128]{1,0:T(8,128)S(1)}, f32[32,128]{1,0:T(8,128)S(1)}, u32[]{:S(2)}, u32[]{:S(2)}) %collective-permute-start.23) | collective-permute-done | bytes 16416 | tf_op jit(solution)/shard_map/ppermute | solution.py:305
  119.8 5.1 %solve_body.1 = (f32[32,32]{1,0:T(8,128)S(1)}, f32[32,32]{1,0:T(8,128)S(1)}) custom-call(f32[32,128]{1,0:T(8,128)S(1)} %add.141.grams, f32[32,128]{1,0:T(8,128)S(1)} %collective-permute-done.23.moved), custom_call_target="tpu_custom_call" | custom-call | tf_op jit(solution)/shard_map/solve_body/pallas_call | solution.py:78
  124.9 1.8 %finish_body.1 = (f32[32,2048]{1,0:T(8,128)}, f32[32,2048]{1,0:T(8,128)}) custom-call(f32[32,32]{1,0:T(8,128)S(1)} %get-tuple-element.74.p, f32[32,32]{1,0:T(8,128)S(1)} %get-tuple-element.75.q, f32[32,2048]{1,0:T(8,128)S(1)} %copy-done.1, f32[8,32,256]{2,1,0:T(8,128)S(1)} %sum_body.1.refs_1_.vector.u, f32[8,32,256]{2,1,0:T(8,128)S(1)} %get-tuple-element.83.rest, ...), custom_call_target="tpu_custom_call" | custom-call | tf_op jit(solution)/shard_map/finish_body/pallas_call | solution.py:78
  (73 shorter events, 16.4 us)
Async XLA Ops:
  0.6 24.6 %collective-permute-start.3 = (f32[32,2048]{1,0:T(8,128)}, f32[32,2048]{1,0:T(8,128)S(1)}, u32[]{:S(2)}, u32[]{:S(2)}) collective-permute-start(f32[32,2048]{1,0:T(8,128)} %right.1), channel_id=1, source_target_pairs={{0,7},{1,2},{2,1},{3,4},{4,3},{5,6},{6,5},{7,0},{8,15},{9,10},{10,... | collective-permute-start | bytes 786440 | tf_op jit(solution)/shard_map/ppermute | solution.py:33
  4.3 14.3 %collective-permute-start.1 = (f32[32,2048]{1,0:T(8,128)}, f32[32,2048]{1,0:T(8,128)S(1)}, u32[]{:S(2)}, u32[]{:S(2)}) collective-permute-start(f32[32,2048]{1,0:T(8,128)} %right.1), channel_id=1, source_target_pairs={{0,120},{8,16},{16,8},{24,32},{32,24},{40,48},{48,40},{56,64},{64,... | collective-permute-start | bytes 786440 | tf_op jit(solution)/shard_map/ppermute | solution.py:33
  9.5 9.1 %collective-permute-start = (f32[32,2048]{1,0:T(8,128)}, f32[32,2048]{1,0:T(8,128)S(1)}, u32[]{:S(2)}, u32[]{:S(2)}) collective-permute-start(f32[32,2048]{1,0:T(8,128)} %right.1), channel_id=1, source_target_pairs={{0,8},{8,0},{16,24},{24,16},{32,40},{40,32},{48,56},{56,48},{64,72... | collective-permute-start | bytes 786440 | tf_op jit(solution)/shard_map/ppermute | solution.py:33
  18.7 6.5 %collective-permute-start.2 = (f32[3,8,32,256]{3,2,1,0:T(8,128)S(1)}, f32[3,8,32,256]{3,2,1,0:T(8,128)S(1)}, u32[]{:S(2)}, u32[]{:S(2)}) collective-permute-start(f32[3,8,32,256]{3,2,1,0:T(8,128)S(1)} %get-tuple-element.45.whole), channel_id=1, source_target_pairs={{0,1},{1,0},{2,3},{3,2},{4,5},{5,4},{6,7},{7,6},{8,9},{9,8},{10,11... | collective-permute-start | bytes 2359304 | tf_op jit(solution)/shard_map/ppermute | solution.py:33
  19.1 12.8 %collective-permute-start.4 = (f32[2,8,32,256]{3,2,1,0:T(8,128)S(1)}, f32[2,8,32,256]{3,2,1,0:T(8,128)S(1)}, u32[]{:S(2)}, u32[]{:S(2)}) collective-permute-start(f32[2,8,32,256]{3,2,1,0:T(8,128)S(1)} %get-tuple-element.52), channel_id=1, source_target_pairs={{0,7},{1,2},{2,1},{3,4},{4,3},{5,6},{6,5},{7,0},{8,15},{9,10},{10,... | collective-permute-start | bytes 1572872 | tf_op jit(solution)/shard_map/ppermute | solution.py:33
  33.7 9.9 %collective-permute-start.9 = (f32[2,8,32,256]{3,2,1,0:T(8,128)S(1)}, f32[2,8,32,256]{3,2,1,0:T(8,128)S(1)}, u32[]{:S(2)}, u32[]{:S(2)}) collective-permute-start(f32[2,8,32,256]{3,2,1,0:T(8,128)S(1)} %get-tuple-element.63), channel_id=1, source_target_pairs={{0,7},{1,2},{2,1},{3,4},{4,3},{5,6},{6,5},{7,0},{8,15},{9,10},{10,... | collective-permute-start | bytes 1572872 | tf_op jit(solution)/shard_map/ppermute | solution.py:33
  41.0 7.0 %collective-permute-start.5 = (f32[8,32,256]{2,1,0:T(8,128)S(1)}, f32[8,32,256]{2,1,0:T(8,128)S(1)}, u32[]{:S(2)}, u32[]{:S(2)}) collective-permute-start(f32[8,32,256]{2,1,0:T(8,128)S(1)} %get-tuple-element.57), channel_id=1, source_target_pairs={{0,1},{1,0},{2,3},{3,2},{4,5},{5,4},{6,7},{7,6},{8,9},{9,8},{10,11... | collective-permute-start | bytes 786440 | tf_op jit(solution)/shard_map/ppermute | solution.py:33
  41.1 7.0 %collective-permute-start.6 = (f32[8,32,256]{2,1,0:T(8,128)S(1)}, f32[8,32,256]{2,1,0:T(8,128)S(1)}, u32[]{:S(2)}, u32[]{:S(2)}) collective-permute-start(f32[8,32,256]{2,1,0:T(8,128)S(1)} %get-tuple-element.58), channel_id=1, source_target_pairs={{0,7},{1,2},{2,1},{3,4},{4,3},{5,6},{6,5},{7,0},{8,15},{9,10},{10,... | collective-permute-start | bytes 786440 | tf_op jit(solution)/shard_map/ppermute | solution.py:33
  43.7 9.1 %collective-permute-start.10 = (f32[8,32,256]{2,1,0:T(8,128)S(1)}, f32[8,32,256]{2,1,0:T(8,128)S(1)}, u32[]{:S(2)}, u32[]{:S(2)}) collective-permute-start(f32[8,32,256]{2,1,0:T(8,128)S(1)} %get-tuple-element.64), channel_id=1, source_target_pairs={{0,8},{8,0},{16,24},{24,16},{32,40},{40,32},{48,56},{56,48},{64,72... | collective-permute-start | bytes 786440 | tf_op jit(solution)/shard_map/ppermute | solution.py:33
  45.8 12.1 %collective-permute-start.11 = (f32[8,32,256]{2,1,0:T(8,128)S(1)}, f32[8,32,256]{2,1,0:T(8,128)S(1)}, u32[]{:S(2)}, u32[]{:S(2)}) collective-permute-start(f32[8,32,256]{2,1,0:T(8,128)S(1)} %get-tuple-element.65), channel_id=1, source_target_pairs={{0,120},{8,16},{16,8},{24,32},{32,24},{40,48},{48,40},{56,64},{64,... | collective-permute-start | bytes 786440 | tf_op jit(solution)/shard_map/ppermute | solution.py:33
  57.9 11.4 %collective-permute-start.14 = (f32[8,32,256]{2,1,0:T(8,128)S(1)}, f32[8,32,256]{2,1,0:T(8,128)S(1)}, u32[]{:S(2)}, u32[]{:S(2)}) collective-permute-start(f32[8,32,256]{2,1,0:T(8,128)S(1)} %sum_body.1.refs_1_.vector.u), channel_id=1, source_target_pairs={{0,120},{8,16},{16,8},{24,32},{32,24},{40,48},{48,40},{56,64},{64,... | collective-permute-start | bytes 786440 | tf_op jit(solution)/shard_map/ppermute | solution.py:33
  58.3 11.0 %collective-permute-start.13 = (f32[8,32,256]{2,1,0:T(8,128)S(1)}, f32[8,32,256]{2,1,0:T(8,128)S(1)}, u32[]{:S(2)}, u32[]{:S(2)}) collective-permute-start(f32[8,32,256]{2,1,0:T(8,128)S(1)} %sum_body.1.refs_1_.vector.u), channel_id=1, source_target_pairs={{0,8},{8,0},{16,24},{24,16},{32,40},{40,32},{48,56},{56,48},{64,72... | collective-permute-start | bytes 786440 | tf_op jit(solution)/shard_map/ppermute | solution.py:33
  58.3 11.0 %collective-permute-start.12 = (f32[8,32,256]{2,1,0:T(8,128)S(1)}, f32[8,32,256]{2,1,0:T(8,128)S(1)}, u32[]{:S(2)}, u32[]{:S(2)}) collective-permute-start(f32[8,32,256]{2,1,0:T(8,128)S(1)} %sum_body.1.refs_1_.vector.u), channel_id=1, source_target_pairs={{0,7},{1,2},{2,1},{3,4},{4,3},{5,6},{6,5},{7,0},{8,15},{9,10},{10,... | collective-permute-start | bytes 786440 | tf_op jit(solution)/shard_map/ppermute | solution.py:33
  69.5 10.5 %collective-permute-start.16 = (f32[2,8,32,256]{3,2,1,0:T(8,128)S(1)}, f32[2,8,32,256]{3,2,1,0:T(8,128)S(1)}, u32[]{:S(2)}, u32[]{:S(2)}) collective-permute-start(f32[2,8,32,256]{3,2,1,0:T(8,128)S(1)} %get-tuple-element.69), channel_id=1, source_target_pairs={{0,7},{1,2},{2,1},{3,4},{4,3},{5,6},{6,5},{7,0},{8,15},{9,10},{10,... | collective-permute-start | bytes 1572872 | tf_op jit(solution)/shard_map/ppermute | solution.py:33
  81.0 3.8 %collective-permute-start.17 = (f32[32,128]{1,0:T(8,128)S(1)}, f32[32,128]{1,0:T(8,128)S(1)}, u32[]{:S(2)}, u32[]{:S(2)}) collective-permute-start(f32[32,128]{1,0:T(8,128)S(1)} %get-tuple-element.73), channel_id=1, source_target_pairs={{0,2},{1,3},{2,0},{3,1},{4,6},{5,7},{6,4},{7,5},{8,10},{9,11},{10,... | collective-permute-start | bytes 49160 | tf_op jit(solution)/shard_map/ppermute | solution.py:305
  89.3 13.7 %collective-permute-start.24 = (f32[3,8,32,256]{3,2,1,0:T(8,128)S(1)}, f32[3,8,32,256]{3,2,1,0:T(8,128)S(1)}, u32[]{:S(2)}, u32[]{:S(2)}) collective-permute-start(f32[3,8,32,256]{3,2,1,0:T(8,128)S(1)} %get-tuple-element.81), channel_id=1, source_target_pairs={{0,1},{1,0},{2,3},{3,2},{4,5},{5,4},{6,7},{7,6},{8,9},{9,8},{10,11... | collective-permute-start | bytes 2359304 | tf_op jit(solution)/shard_map/ppermute | solution.py:33
  89.4 13.6 %collective-permute-start.25 = (f32[3,8,32,256]{3,2,1,0:T(8,128)S(1)}, f32[3,8,32,256]{3,2,1,0:T(8,128)S(1)}, u32[]{:S(2)}, u32[]{:S(2)}) collective-permute-start(f32[3,8,32,256]{3,2,1,0:T(8,128)S(1)} %get-tuple-element.82), channel_id=1, source_target_pairs={{0,7},{1,2},{2,1},{3,4},{4,3},{5,6},{6,5},{7,0},{8,15},{9,10},{10,... | collective-permute-start | bytes 2359304 | tf_op jit(solution)/shard_map/ppermute | solution.py:33
  90.6 3.7 %collective-permute-start.18 = (f32[32,128]{1,0:T(8,128)S(1)}, f32[32,128]{1,0:T(8,128)S(1)}, u32[]{:S(2)}, u32[]{:S(2)}) collective-permute-start(f32[32,128]{1,0:T(8,128)S(1)} %add.136.refs_5_), channel_id=1, source_target_pairs={{0,8},{1,9},{2,10},{3,11},{4,12},{5,13},{6,14},{7,15},{8,0},{9,1},... | collective-permute-start | bytes 49160 | tf_op jit(solution)/shard_map/ppermute | solution.py:305
  94.3 4.9 %collective-permute-start.19 = (f32[32,128]{1,0:T(8,128)S(1)}, f32[32,128]{1,0:T(8,128)S(1)}, u32[]{:S(2)}, u32[]{:S(2)}) collective-permute-start(f32[32,128]{1,0:T(8,128)S(1)} %add.137), channel_id=1, source_target_pairs={{0,24},{1,25},{2,26},{3,27},{4,28},{5,29},{6,30},{7,31},{8,16},{9,... | collective-permute-start | bytes 49160 | tf_op jit(solution)/shard_map/ppermute | solution.py:305
  99.3 3.7 %collective-permute-start.20 = (f32[32,128]{1,0:T(8,128)S(1)}, f32[32,128]{1,0:T(8,128)S(1)}, u32[]{:S(2)}, u32[]{:S(2)}) collective-permute-start(f32[32,128]{1,0:T(8,128)S(1)} %add.138), channel_id=1, source_target_pairs={{0,32},{1,33},{2,34},{3,35},{4,36},{5,37},{6,38},{7,39},{8,40},{9,... | collective-permute-start | bytes 49160 | tf_op jit(solution)/shard_map/ppermute | solution.py:305
  103.2 21.7 %collective-permute-start.26 = (f32[8,32,256]{2,1,0:T(8,128)S(1)}, f32[8,32,256]{2,1,0:T(8,128)S(1)}, u32[]{:S(2)}, u32[]{:S(2)}) collective-permute-start(f32[8,32,256]{2,1,0:T(8,128)S(1)} %get-tuple-element.84), channel_id=1, source_target_pairs={{0,8},{8,0},{16,24},{24,16},{32,40},{40,32},{48,56},{56,48},{64,72... | collective-permute-start | bytes 786440 | tf_op jit(solution)/shard_map/ppermute | solution.py:33
  103.3 21.6 %collective-permute-start.27 = (f32[8,32,256]{2,1,0:T(8,128)S(1)}, f32[8,32,256]{2,1,0:T(8,128)S(1)}, u32[]{:S(2)}, u32[]{:S(2)}) collective-permute-start(f32[8,32,256]{2,1,0:T(8,128)S(1)} %get-tuple-element.85), channel_id=1, source_target_pairs={{0,120},{8,16},{16,8},{24,32},{32,24},{40,48},{48,40},{56,64},{64,... | collective-permute-start | bytes 786440 | tf_op jit(solution)/shard_map/ppermute | solution.py:33
  104.8 8.8 %collective-permute-start.21 = (f32[32,128]{1,0:T(8,128)S(1)}, f32[32,128]{1,0:T(8,128)S(1)}, u32[]{:S(2)}, u32[]{:S(2)}) collective-permute-start(f32[32,128]{1,0:T(8,128)S(1)} %add.139.grams), channel_id=1, source_target_pairs={{0,96},{1,97},{2,98},{3,99},{4,100},{5,101},{6,102},{7,103},{8,104... | collective-permute-start | bytes 49160 | tf_op jit(solution)/shard_map/ppermute | solution.py:305
  114.8 4.9 %collective-permute-start.23 = (f32[32,128]{1,0:T(8,128)S(1)}, f32[32,128]{1,0:T(8,128)S(1)}, u32[]{:S(2)}, u32[]{:S(2)}) collective-permute-start(f32[32,128]{1,0:T(8,128)S(1)} %add.141.grams), channel_id=1, source_target_pairs={{0,6},{1,7},{2,4},{3,5},{4,2},{5,3},{6,0},{7,1},{8,14},{9,15},{10,... | collective-permute-start | bytes 49160 | tf_op jit(solution)/shard_map/ppermute | solution.py:305
  (7 other events, 34.0 us)

commit v4 on v3

--- a/solution.py
+++ b/solution.py
@@ -11,8 +11,8 @@
 VMEM_SPEC = pl.BlockSpec(memory_space=pltpu.VMEM)
 SMEM_SPEC = pl.BlockSpec(memory_space=pltpu.SMEM)
 CHUNK = 8
-PREPARED = 4
-PARTS = 2
+HALF = 4
+PREPARED = 8
 NEAR_TABLES = 7
 TOKEN = pltpu.VMEM((8, 128), F32)
 
@@ -74,7 +74,7 @@
     return jnp.concatenate(split(value), axis=0)
 
 
-def call(body, out_shape, n_smem, args, scratch=(), aliases=None, limit=12 << 20):
+def call(body, out_shape, n_smem, args, scratch=(), aliases=None, limit=8 << 20):
     return pl.pallas_call(
         body,
         out_shape=out_shape,
@@ -87,34 +87,35 @@
     )(*args[:n_smem], *[in_vmem(a) for a in args[n_smem:]])
 
 
-def prepare_body(couplings, c_high, c_low, token):
-    per = couplings.shape[0]
-    first = pl.program_id(0) * per
+def prepare_body(routes, edge, couplings, c_high, c_low, token, buffer, arrived):
+    count = couplings.shape[0]
     token[...] = jnp.zeros_like(token)
-    for place in range(per):
-        high, low = split(couplings[place])
-        c_high[first + place] = high
-        c_low[first + place] = low
-
-
-def part_edges(count):
-    return (0, count * 5 // (8 * CHUNK) * CHUNK, count)
-
-
-def prepare(couplings, part):
-    width = couplings.shape[1]
-    first, last = part_edges(couplings.shape[0])[part:part + 2]
-    skip = first // PREPARED
-    shape = pltpu.VMEM((last - first, width, width), BF16)
+    copies = []
+    for i in range(count // PREPARED):
+        part = pl.ds(i * PREPARED, PREPARED)
+        copies.append(pltpu.make_async_copy(couplings.at[part], buffer.at[part], arrived.at[i]))
+    for copy in copies:
+        copy.start()
+    for i, copy in enumerate(copies):
+        copy.wait()
+        for k in range(i * PREPARED, (i + 1) * PREPARED):
+            c_high[k], c_low[k] = split(buffer[k])
+
+
+def prepare(couplings, routes, edge):
+    shape = pltpu.VMEM(couplings.shape, BF16)
     return pl.pallas_call(
         prepare_body,
-        grid=((last - first) // PREPARED,),
-        in_specs=[pl.BlockSpec((PREPARED, width, width), lambda i: (i + skip, 0, 0))],
+        in_specs=[SMEM_SPEC, SMEM_SPEC, pl.BlockSpec(memory_space=pltpu.HBM)],
         out_specs=[VMEM_SPEC] * 3,
         out_shape=[shape, shape, TOKEN],
+        scratch_shapes=[
+            pltpu.VMEM(couplings.shape, F32),
+            pltpu.SemaphoreType.DMA((couplings.shape[0] // PREPARED,)),
+        ],
         name="prepare",
-        compiler_params=pltpu.CompilerParams(vmem_limit_bytes=12 << 20),
-    )(in_hbm(couplings))
+        compiler_params=pltpu.CompilerParams(vmem_limit_bytes=17 << 20),
+    )(routes, edge, in_hbm(couplings))
 
 
 def block_of(source, q, width):
@@ -132,28 +133,30 @@
                 pair[slot - 1, q] = block
 
 
-def accumulate(dot, late, routes, edges, source_row, target_row, source, target, parts):
-    for part in range(PARTS):
-        c_high, c_low = parts[2 * part], parts[2 * part + 1]
-
-        def step(chunk, carry):
-            terms = []
-            for place in range(CHUNK):
-                i = chunk * CHUNK + place
-                k = routes[0, i]
-                terms.append((routes[target_row, i], times(dot, source[routes[source_row, i]], c_high[k], c_low[k])))
-            for row, term in terms:
-                target[row] += term
-            return carry
-
-        low, high = part_edges(routes.shape[1])[part:part + 2]
-        middle = edges[part] // CHUNK
-        first, last = (middle, high // CHUNK) if late else (low // CHUNK, middle)
-        lax.fori_loop(first, last, step, 0)
-
-
-def pull_near_body(routes, edges, qa, whole, cb, *refs):
-    parts, (table, strain) = refs[:2 * PARTS], refs[2 * PARTS:]
+def accumulate(dot, first, last, routes, source_row, target_row, source, target, c_high, c_low):
+    def step(size, start):
+        terms = []
+        for place in range(size):
+            i = start + place
+            k = routes[0, i]
+            terms.append((routes[target_row, i], times(dot, source[routes[source_row, i]], c_high[k], c_low[k])))
+        for row, term in terms:
+            target[row] += term
+
+    def whole(i, carry):
+        step(CHUNK, first * HALF + i * CHUNK)
+        return carry
+
+    def rest(i, carry):
+        step(HALF, (last - 1) * HALF)
+        return carry
+
+    lax.fori_loop(0, (last - first) // 2, whole, 0)
+    lax.fori_loop(0, (last - first) % 2, rest, 0)
+
+
+def pull_near_body(routes, edge, qa, whole, cb, *refs):
+    c_high, c_low, table, strain = refs
     blocks = strain.shape[0]
     for place, (source, slot) in enumerate(
             ((whole, 0), (whole, 1), (whole, 2), (qa, 0), (cb, None), (qa, 1), (qa, 2))):
@@ -161,18 +164,17 @@
             block = block_of(source, q, strain.shape[2]) if slot is None else source[slot, q]
             table[place * blocks + q] = stacked_split(block)
     strain[...] = jnp.zeros_like(strain)
-    accumulate(dot_nt, False, routes, edges, 1, 2, table, strain, parts)
-
-
-def pull_late_body(routes, edges, table_in, strain_in, db, *refs):
-    parts, refs = refs[:2 * PARTS], refs[2 * PARTS:]
-    *grams, table, strain_hl, g_out, strain = refs
+    accumulate(dot_nt, 0, edge[0], routes, 1, 2, table, strain, c_high, c_low)
+
+
+def pull_late_body(routes, edge, table_in, strain_in, db, *refs):
+    c_high, c_low, *grams, table, strain_hl, g_out, strain = refs
     blocks = strain.shape[0]
     for slot in range(2):
         for q in range(blocks):
             table[(NEAR_TABLES + slot) * blocks + q] = stacked_split(db[slot, q])
     strain[...] = strain_in[...]
-    accumulate(dot_nt, True, routes, edges, 1, 2, table, strain, parts)
+    accumulate(dot_nt, edge[0], routes.shape[1] // HALF, routes, 1, 2, table, strain, c_high, c_low)
     total = jnp.zeros((strain.shape[1],) * 2, F32)
     for q in range(blocks):
         both = stacked_split(strain[q])
@@ -187,37 +189,40 @@
             g_out[:, i * size:(i + 1) * size] = part
 
 
-def push_late_body(routes, edges, strain_hl, *refs):
-    parts, (pieces, *targets) = refs[:2 * PARTS], refs[2 * PARTS:]
+def push_late_body(routes, edge, strain_hl, c_high, c_low, pieces, *targets):
     blocks = strain_hl.shape[0]
     pieces[...] = jnp.zeros_like(pieces)
-    accumulate(dot_nn, True, routes, edges, 2, 1, strain_hl, pieces, parts)
+    accumulate(dot_nn, edge[0], routes.shape[1] // HALF, routes, 2, 1, strain_hl, pieces, c_high, c_low)
     for db in targets:
         for slot in range(2):
             for q in range(blocks):
                 db[slot, q] = pieces[(NEAR_TABLES + slot) * blocks + q]
 
 
-def push_near(routes, edges, strain_hl, parts, pieces_in, pieces, targets):
+def push_near_body(routes, edge, strain_hl, c_high, c_low, pieces_in, *refs):
+    *outs, pieces = refs
+    pieces[...] = pieces_in[:pieces.shape[0]]
+    accumulate(dot_nn, 0, edge[0], routes, 2, 1, strain_hl, pieces, c_high, c_low)
+    for place, target in enumerate(outs):
+        for q in range(target.shape[0]):
+            target[q] = pieces[place * target.shape[0] + q]
+
+
+def push_begin_body(routes, edge, strain_hl, c_high, c_low, pieces_in, pieces):
+    accumulate(dot_nn, 0, edge[0] // 2, routes, 2, 1, strain_hl, pieces, c_high, c_low)
+
+
+def push_end_body(routes, edge, strain_hl, c_high, c_low, pieces_in, own, ra, rb, qa, qb, pieces):
     blocks = strain_hl.shape[0]
-    pieces[...] = pieces_in[:pieces.shape[0]]
-    accumulate(dot_nn, False, routes, edges, 2, 1, strain_hl, pieces, parts)
-    for target, place in targets:
+    accumulate(dot_nn, edge[0] // 2, edge[0], routes, 2, 1, strain_hl, pieces, c_high, c_low)
+    outs = (own, ra, rb, qa.at[0], qa.at[1], qa.at[2], qb.at[0], qb.at[1], qb.at[2])
+    for target, place in zip(outs, (0, 1, 2, 3, 5, 6, 4, 7, 8)):
         for q in range(blocks):
             target[q] = pieces[place * blocks + q]
 
 
-def push_near_body(routes, edges, strain_hl, *refs):
-    parts, pieces_in, outs = refs[:2 * PARTS], refs[2 * PARTS], refs[2 * PARTS + 1:]
-    *outs, pieces = outs
-    push_near(routes, edges, strain_hl, parts, pieces_in, pieces, zip(outs, range(NEAR_TABLES)))
-
-
-def push_last_body(routes, edges, strain_hl, *refs):
-    parts, pieces_in, outs = refs[:2 * PARTS], refs[2 * PARTS], refs[2 * PARTS + 2:]
-    *outs, qa, qb, pieces = outs
-    outs += [qa.at[0], qa.at[1], qa.at[2], qb.at[0], qb.at[1], qb.at[2]]
-    push_near(routes, edges, strain_hl, parts, pieces_in, pieces, zip(outs, (0, 1, 2, 3, 5, 6, 4, 7, 8)))
+def add_body(grams, moved, after, total):
+    total[...] = grams[...] + moved[...]
 
 
 def diag_body(vector, diag, own, grams):
@@ -297,7 +302,7 @@
         r_out[:, lanes] = right[:, lanes] - full_tn(p[...], u[block]) + full_tn(q[...], w)
 
 
-MASKS = (2, 8, 24, 32, 96, 1, 6)
+MASKS = (2, 6, 8, 24, 32, 96, 1)
 
 
 def exchanged(value, mask):
@@ -310,25 +315,20 @@
     col_size = lax.axis_size("col")
     my_row, my_col = lax.axis_index("row"), lax.axis_index("col")
     local_row = pair_index[0] - (my_row * col_size + my_col) * blocks
-    owner = pair_index[1] // blocks
-    row_slot = slot_of(owner // col_size, my_row)
-    col_slot = slot_of(owner % col_size, my_col)
+    owner, in_owner = lax.div(pair_index[1], blocks), lax.rem(pair_index[1], blocks)
+    row_slot = slot_of(lax.div(owner, col_size), my_row)
+    col_slot = slot_of(lax.rem(owner, col_size), my_col)
     diagonal = (row_slot > 0) & (col_slot > 0)
     slot = jnp.where(diagonal, 2 + 2 * col_slot + row_slot, jnp.where(col_slot > 0, 2 + col_slot, row_slot))
-    table_row = slot * blocks + pair_index[1] % blocks
-    late = slot >= NEAR_TABLES
+    table_row = slot * blocks + in_owner
+    late = (slot >= NEAR_TABLES).astype(jnp.int32)
     number = jnp.arange(count, dtype=jnp.int32)
-    split_at = part_edges(count)[1]
-    part = (number >= split_at).astype(jnp.int32)
-    key = (2 * part + late.astype(jnp.int32)) * count + number
-    rank = jnp.sum((key[None, :] < key[:, None]).astype(jnp.int32), axis=1)
+    rank = jnp.sum(((late * count + number)[None, :] < (late * count + number)[:, None]).astype(jnp.int32), axis=1)
     placed = rank[None, :] == number[:, None]
-    columns = (number - part * split_at, table_row, local_row)
+    columns = (number, table_row, local_row)
     routes = jnp.stack([jnp.sum(jnp.where(placed, c[None, :], 0), axis=1) for c in columns])
-    starts = jnp.arange(PARTS, dtype=jnp.int32)
-    early = (part[None, :] == starts[:, None]) & ~late[None, :]
-    edges = starts * split_at + jnp.sum(early.astype(jnp.int32), axis=1)
-    return routes, edges
+    edge = (count - jnp.sum(late, keepdims=True)) >> (HALF.bit_length() - 1)
+    return routes, edge
 
 
 def per_device(right_sides, diag_blocks, couplings, pair_index):
@@ -348,28 +348,26 @@
     def spread(vector, *after):
         cb = swapped(vector, "col", 1)
         ra, rb = swapped(vector, "row", 0), swapped(vector, "row", 1)
-        whole, pair = call(stack_body, [stack_shape, pair_shape], 0, (after or (cb,)) + (vector, ra, rb))
+        whole, pair = call(stack_body, [stack_shape, pair_shape], 0, (*after, cb, vector, ra, rb))
         return (swapped(whole, "col", 0), whole, cb), swapped(pair, "col", 1)
 
     def pulled(near_tables, db, couplings, *grams):
-        table, strain = call(pull_near_body, [table_shape, block_shape], 2, (routes, edges, *near_tables, *couplings))
+        table, strain = call(pull_near_body, [table_shape, block_shape], 2, (routes, edge, *near_tables, *couplings))
         _, strain_hl, g = call(
             pull_late_body, [table_shape, split_shape, all_grams_shape if grams else gram_shape], 2,
-            (routes, edges, table, strain, db, *couplings, *grams), [block_shape], aliases={2: 0})
+            (routes, edge, table, strain, db, *couplings, *grams), [block_shape], aliases={2: 0})
         return strain_hl, g
 
-    routes, edges = routing(pair_index, blocks)
-    *larger, token = prepare(couplings, 0)
+    routes, edge = routing(pair_index, blocks)
+    *couplings, token = prepare(couplings, routes, edge)
     near_tables, db = spread(right_sides, token)
-    *smaller, _ = prepare(couplings, 1)
-    couplings = larger + smaller
     strain_hl, g1s = pulled(near_tables, db, couplings)
 
-    pieces, db = call(push_late_body, [pieces_shape, pair_shape], 2, (routes, edges, strain_hl, *couplings))
+    pieces, db = call(push_late_body, [pieces_shape, pair_shape], 2, (routes, edge, strain_hl, *couplings))
     db = swapped(db, "col", 1)
     own, ra, rb, ca, cb, qa_first, qa_second = call(
         push_near_body, [block_shape] * NEAR_TABLES, 2,
-        (routes, edges, strain_hl, *couplings, pieces), [near_pieces_shape])
+        (routes, edge, strain_hl, *couplings, pieces), [near_pieces_shape])
     ca, qa_first, qa_second = (swapped(a, "col", 0) for a in (ca, qa_first, qa_second))
     cb = swapped(cb, "col", 1)
     diag, g01 = call(diag_body, [block_shape, grams_shape], 0, (right_sides, diag_blocks))
@@ -380,18 +378,19 @@
     near_tables, db = spread(u)
     diag, g23 = call(diag_body, [block_shape, grams_shape], 0, (u, diag_blocks))
     strain_hl, grams = pulled(near_tables, db, couplings, g01, g1s, g23)
-    pieces, = call(push_late_body, [pieces_shape], 2, (routes, edges, strain_hl, *couplings))
-    grams = grams + exchanged(grams, MASKS[0])
-    own, ra, rb, qa, qb = call(
-        push_last_body, [block_shape] * 3 + [stack_shape] * 2, 2,
-        (routes, edges, strain_hl, *couplings, pieces, grams), [pieces_shape])
+    pieces, = call(push_late_body, [pieces_shape], 2, (routes, edge, strain_hl, *couplings))
+    grams = call(add_body, all_grams_shape, 0, (grams, exchanged(grams, MASKS[0]), pieces))
+    pieces, = call(push_begin_body, [pieces_shape], 2, (routes, edge, strain_hl, *couplings, pieces), aliases={5: 0})
+    grams = call(add_body, all_grams_shape, 0, (grams, exchanged(grams, MASKS[1]), pieces))
+    own, ra, rb, qa, qb, _ = call(
+        push_end_body, [block_shape] * 3 + [stack_shape] * 2 + [pieces_shape], 2,
+        (routes, edge, strain_hl, *couplings, pieces), aliases={5: 5})
+    grams = call(add_body, all_grams_shape, 0, (grams, exchanged(grams, MASKS[2]), own))
     qa, qb = swapped(qa, "col", 0), swapped(qb, "col", 1)
-    for mask in MASKS[1:4]:
+    for mask in MASKS[3:6]:
         grams = grams + exchanged(grams, mask)
     rest, ra, rb = call(middle_last_body, [block_shape] * 3, 0, (own, diag, ra, rb, qa, qb, grams))
     ra, rb = swapped(ra, "row", 0), swapped(rb, "row", 1)
-    for mask in MASKS[4:-1]:
-        grams = grams + exchanged(grams, mask)
     p, q = call(solve_body, [gram_shape] * 2, 0, (grams, exchanged(grams, MASKS[-1])))
     flat = jax.ShapeDtypeStruct(right_sides.shape, F32)
     return tuple(call(finish_body, [flat, flat], 0, (p, q, right_sides, u, rest, ra, rb)))

time: 127 us -> 120 us (0.945)
  waiting for transfers between devices: 51.6 us -> 43.9 us
  Pallas kernels: 49.6 us -> 44 us
  starting transfers between devices: 22.7 us -> 27.1 us
    ppermute x7, waiting for transfers between devices: 30.1 us -> 20.6 us  [exchanged(): lax.ppermute(value, ('row', 'col'), [(i, i ^ mask) for i in range(count)])]
    pallas_call x2 -> x1, Pallas kernels: 12.7 us -> 6.82 us  [prepare(): pl.pallas_call(prepare_body, in_specs=[SMEM_SPEC, SMEM_SPEC, pl.BlockSpec...]
    ppermute x7, starting transfers between devices: 0.32 us -> 3.55 us  [exchanged(): lax.ppermute(value, ('row', 'col'), [(i, i ^ mask) for i in range(count)])]
    ppermute x21, waiting for transfers between devices: 21.4 us -> 23.3 us  [swapped(): return lax.ppermute(value, axis, pairs_of(lax.axis_size(axis), shift))]
    pallas_call x17 -> x21, Pallas kernels: 36.9 us -> 37.2 us  [call(): pl.pallas_call(body, out_shape=out_shape, in_specs=[SMEM_SPEC] * n_smem +...]
  transfers between devices with their start and end apart: 28 -> 28, of which waited for: 14 -> 13; matrix products, arithmetic and copies ran while one was open for 2% -> 2% of each run, Pallas kernels for 32% -> 31%
where the time goes in v4:
time: 120 us; the launch traced here: 119 us
  Pallas kernels  44 us (37%)
  waiting for transfers between devices  43.9 us (37%)
  starting transfers between devices  27.1 us (23%)
  other arithmetic  2.46 us (2%)
  between operations  1.56 us (1%)
    pallas_call x21, Pallas kernels, call(): pl.pallas_call(body, out_shape=out_shape, in_specs=[SMEM_SPEC] * n_smem +...  37.2 us
    ppermute x21, starting transfers between devices, swapped(): return lax.ppermute(value, axis, pairs_of(lax.axis_size(axis), shift))  23.6 us
    ppermute x21, waiting for transfers between devices, swapped(): return lax.ppermute(value, axis, pairs_of(lax.axis_size(axis), shift))  23.3 us
    ppermute x7, waiting for transfers between devices, exchanged(): lax.ppermute(value, ('row', 'col'), [(i, i ^ mask) for i in range(count)])  20.6 us
    pallas_call x1, Pallas kernels, prepare(): pl.pallas_call(prepare_body, in_specs=[SMEM_SPEC, SMEM_SPEC, pl.BlockSpec...  6.82 us
    ppermute x7, starting transfers between devices, exchanged(): lax.ppermute(value, ('row', 'col'), [(i, i ^ mask) for i in range(count)])  3.55 us
  transfers between devices with their start and end apart: 28, of which 13 were waited for; matrix products, arithmetic and copies ran while one was open for 2% of the time, Pallas kernels for 31%

profile of v4, /device:TPU:0, one launch (start us, length us, event | category | flops | bytes accessed | tf_op | source)
XLA Modules:
  0.0 119.1 jit_solution(14886149440407628510)
XLA Ops:
  0.6 5.4 %collective-permute-start.2 = (f32[32,2048]{1,0:T(8,128)}, f32[32,2048]{1,0:T(8,128)S(1)}, u32[]{:S(2)}, u32[]{:S(2)}) collective-permute-start(f32[32,2048]{1,0:T(8,128)} %right.1), channel_id=1, source_target_pairs={{0,120},{8,16},{16,8},{24,32},{32,24},{40,48},{48,40},{56,64},{64,... | collective-permute-start | bytes 786440 | tf_op jit(solution)/shard_map/ppermute | solution.py:33
  6.0 3.2 %collective-permute-start = (f32[32,2048]{1,0:T(8,128)}, f32[32,2048]{1,0:T(8,128)S(1)}, u32[]{:S(2)}, u32[]{:S(2)}) collective-permute-start(f32[32,2048]{1,0:T(8,128)} %right.1), channel_id=1, source_target_pairs={{0,7},{1,2},{2,1},{3,4},{4,3},{5,6},{6,5},{7,0},{8,15},{9,10},{10,... | collective-permute-start | bytes 786440 | tf_op jit(solution)/shard_map/ppermute | solution.py:33
  12.3 6.8 %prepare.1 = (bf16[64,256,256]{2,1,0:T(8,128)(2,1)S(1)}, bf16[64,256,256]{2,1,0:T(8,128)(2,1)S(1)}, f32[8,128]{1,0:T(8,128)S(1)}) custom-call(s32[3,64]{1,0:T(4,128)S(1)} %pad_add_fusion.routes, s32[1]{0:T(128)} %bitcast.7.edge, f32[64,256,256]{2,1,0:T(8,128)} %couplings.1), custom_call_target="tpu_custom_call" | custom-call | tf_op jit(solution)/shard_map/prepare/pallas_call | solution.py:107
  21.7 6.7 %pull_near_body.2 = (bf16[72,64,256]{2,1,0:T(8,128)(2,1)S(1)}, f32[8,32,256]{2,1,0:T(8,128)S(1)}) custom-call(s32[3,64]{1,0:T(4,128)S(1)} %pad_add_fusion.routes, s32[1]{0:T(128)} %bitcast.7.edge, f32[3,8,32,256]{3,2,1,0:T(8,128)S(1)} %collective-permute-done.3.qa, f32[3,8,32,256]{3,2,1,0:T(8,128)S(1)} %get-tuple-element.43.whole, ...), custom_call_target="tpu_custom_call" | custom-call | tf_op jit(solution)/shard_map/pull_near_body/pallas_call | solution.py:78
  31.9 4.5 %push_near_body.1 = (f32[8,32,256]{2,1,0:T(8,128)S(1)}, f32[8,32,256]{2,1,0:T(8,128)S(1)}, f32[8,32,256]{2,1,0:T(8,128)S(1)}, f32[8,32,256]{2,1,0:T(8,128)S(1)},...) custom-call(s32[3,64]{1,0:T(4,128)S(1)} %pad_add_fusion.routes, s32[1]{0:T(128)} %bitcast.7.edge, ...), custom_call_target="tpu_custom_call" | custom-call | tf_op jit(solution)/shard_map/push_near_body/pallas_call | solution.py:78
  37.5 1.7 %collective-permute-start.6 = (f32[8,32,256]{2,1,0:T(8,128)S(1)}, f32[8,32,256]{2,1,0:T(8,128)S(1)}, u32[]{:S(2)}, u32[]{:S(2)}) collective-permute-start(f32[8,32,256]{2,1,0:T(8,128)S(1)} %get-tuple-element.54), channel_id=1, source_target_pairs={{0,7},{1,2},{2,1},{3,4},{4,3},{5,6},{6,5},{7,0},{8,15},{9,10},{10,... | collective-permute-start | bytes 786440 | tf_op jit(solution)/shard_map/ppermute | solution.py:33
  41.0 2.7 %collective-permute-start.10 = (f32[8,32,256]{2,1,0:T(8,128)S(1)}, f32[8,32,256]{2,1,0:T(8,128)S(1)}, u32[]{:S(2)}, u32[]{:S(2)}) collective-permute-start(f32[8,32,256]{2,1,0:T(8,128)S(1)} %get-tuple-element.60), channel_id=1, source_target_pairs={{0,8},{8,0},{16,24},{24,16},{32,40},{40,32},{48,56},{56,48},{64,72... | collective-permute-start | bytes 786440 | tf_op jit(solution)/shard_map/ppermute | solution.py:33
  45.5 4.0 %collective-permute-done.10.ra = f32[8,32,256]{2,1,0:T(8,128)S(1)} collective-permute-done((f32[8,32,256]{2,1,0:T(8,128)S(1)}, f32[8,32,256]{2,1,0:T(8,128)S(1)}, u32[]{:S(2)}, u32[]{:S(2)}) %collective-permute-start.10) | collective-permute-done | bytes 262176 | tf_op jit(solution)/shard_map/ppermute | solution.py:33
  49.5 4.8 %collective-permute-done.11.rb = f32[8,32,256]{2,1,0:T(8,128)S(1)} collective-permute-done((f32[8,32,256]{2,1,0:T(8,128)S(1)}, f32[8,32,256]{2,1,0:T(8,128)S(1)}, u32[]{:S(2)}, u32[]{:S(2)}) %collective-permute-start.11) | collective-permute-done | bytes 262176 | tf_op jit(solution)/shard_map/ppermute | solution.py:33
  54.8 9.3 %collective-permute-done.14.refs_3_ = f32[8,32,256]{2,1,0:T(8,128)S(1)} collective-permute-done((f32[8,32,256]{2,1,0:T(8,128)S(1)}, f32[8,32,256]{2,1,0:T(8,128)S(1)}, u32[]{:S(2)}, u32[]{:S(2)}) %collective-permute-start.14) | collective-permute-done | bytes 262176 | tf_op jit(solution)/shard_map/ppermute | solution.py:33
  64.3 2.2 %collective-permute-start.16 = (f32[2,8,32,256]{3,2,1,0:T(8,128)S(1)}, f32[2,8,32,256]{3,2,1,0:T(8,128)S(1)}, u32[]{:S(2)}, u32[]{:S(2)}) collective-permute-start(f32[2,8,32,256]{3,2,1,0:T(8,128)S(1)} %get-tuple-element.65), channel_id=1, source_target_pairs={{0,7},{1,2},{2,1},{3,4},{4,3},{5,6},{6,5},{7,0},{8,15},{9,10},{10,... | collective-permute-start | bytes 1572872 | tf_op jit(solution)/shard_map/ppermute | solution.py:33
  68.3 6.7 %pull_near_body.3 = (bf16[72,64,256]{2,1,0:T(8,128)(2,1)S(1)}, f32[8,32,256]{2,1,0:T(8,128)S(1)}) custom-call(s32[3,64]{1,0:T(4,128)S(1)} %pad_add_fusion.routes, s32[1]{0:T(128)} %bitcast.7.edge, f32[3,8,32,256]{3,2,1,0:T(8,128)S(1)} %collective-permute-done.15.qa, f32[3,8,32,256]{3,2,1,0:T(8,128)S(1)} %get-tuple-element.62.whole, ...), custom_call_target="tpu_custom_call" | custom-call | tf_op jit(solution)/shard_map/pull_near_body/pallas_call | solution.py:78
  77.7 2.1 %collective-permute-done.17.moved = f32[32,128]{1,0:T(8,128)S(1)} collective-permute-done((f32[32,128]{1,0:T(8,128)S(1)}, f32[32,128]{1,0:T(8,128)S(1)}, u32[]{:S(2)}, u32[]{:S(2)}) %collective-permute-start.17) | collective-permute-done | bytes 16416 | tf_op jit(solution)/shard_map/ppermute | solution.py:310
  79.8 2.5 %collective-permute-start.18 = (f32[32,128]{1,0:T(8,128)S(1)}, f32[32,128]{1,0:T(8,128)S(1)}, u32[]{:S(2)}, u32[]{:S(2)}) collective-permute-start(f32[32,128]{1,0:T(8,128)S(1)} %add_body.3.grams), channel_id=1, source_target_pairs={{0,6},{1,7},{2,4},{3,5},{4,2},{5,3},{6,0},{7,1},{8,14},{9,15},{10,... | collective-permute-start | bytes 49160 | tf_op jit(solution)/shard_map/ppermute | solution.py:310
  82.3 2.4 %push_begin_body.1.after.pieces_in = f32[72,32,256]{2,1,0:T(8,128)S(1)} custom-call(s32[3,64]{1,0:T(4,128)S(1)} %pad_add_fusion.routes, s32[1]{0:T(128)} %bitcast.7.edge, bf16[8,64,256]{2,1,0:T(8,128)(2,1)S(1)} %get-tuple-element.70.strain_hl, bf16[64,256,256]{2,1,0:T(8,128)(2,1)S(1)} %get-tuple-element.44.refs_0_.c_high, ...), custom_call_target="tpu_custom_call", output_to_operand_aliasing={{}: (5, {})} | custom-call | tf_op jit(solution)/shard_map/push_begin_body/pallas_call | solution.py:78
  84.8 2.6 %push_end_body.1 = (f32[8,32,256]{2,1,0:T(8,128)S(1)}, f32[8,32,256]{2,1,0:T(8,128)S(1)}, f32[8,32,256]{2,1,0:T(8,128)S(1)}, f32[3,8,32,256]{3,2,1,0:T(8,128)S(1...) custom-call(s32[3,64]{1,0:T(4,128)S(1)} %pad_add_fusion.routes, ...), custom_call_target="tpu_custom_call", output_to_operand_aliasing={{5}: (5, {})} | custom-call | tf_op jit(solution)/shard_map/push_end_body/pallas_call | solution.py:78
  87.4 2.4 %collective-permute-start.25 = (f32[3,8,32,256]{3,2,1,0:T(8,128)S(1)}, f32[3,8,32,256]{3,2,1,0:T(8,128)S(1)}, u32[]{:S(2)}, u32[]{:S(2)}) collective-permute-start(f32[3,8,32,256]{3,2,1,0:T(8,128)S(1)} %get-tuple-element.78), channel_id=1, source_target_pairs={{0,7},{1,2},{2,1},{3,4},{4,3},{5,6},{6,5},{7,0},{8,15},{9,10},{10,... | collective-permute-start | bytes 2359304 | tf_op jit(solution)/shard_map/ppermute | solution.py:33
  89.9 3.7 %collective-permute-done.19.moved = f32[32,128]{1,0:T(8,128)S(1)} collective-permute-done((f32[32,128]{1,0:T(8,128)S(1)}, f32[32,128]{1,0:T(8,128)S(1)}, u32[]{:S(2)}, u32[]{:S(2)}) %collective-permute-start.19) | collective-permute-done | bytes 16416 | tf_op jit(solution)/shard_map/ppermute | solution.py:310
  93.8 4.8 %collective-permute-done.20 = f32[32,128]{1,0:T(8,128)S(1)} collective-permute-done((f32[32,128]{1,0:T(8,128)S(1)}, f32[32,128]{1,0:T(8,128)S(1)}, u32[]{:S(2)}, u32[]{:S(2)}) %collective-permute-start.20) | collective-permute-done | bytes 16416 | tf_op jit(solution)/shard_map/ppermute | solution.py:310
  98.6 3.7 %collective-permute-done.21 = f32[32,128]{1,0:T(8,128)S(1)} collective-permute-done((f32[32,128]{1,0:T(8,128)S(1)}, f32[32,128]{1,0:T(8,128)S(1)}, u32[]{:S(2)}, u32[]{:S(2)}) %collective-permute-start.21) | collective-permute-done | bytes 16416 | tf_op jit(solution)/shard_map/ppermute | solution.py:310
  102.3 4.9 %collective-permute-done.22 = f32[32,128]{1,0:T(8,128)S(1)} collective-permute-done((f32[32,128]{1,0:T(8,128)S(1)}, f32[32,128]{1,0:T(8,128)S(1)}, u32[]{:S(2)}, u32[]{:S(2)}) %collective-permute-start.22) | collective-permute-done | bytes 16416 | tf_op jit(solution)/shard_map/ppermute | solution.py:310
  107.5 2.2 %collective-permute-start.27 = (f32[8,32,256]{2,1,0:T(8,128)S(1)}, f32[8,32,256]{2,1,0:T(8,128)S(1)}, u32[]{:S(2)}, u32[]{:S(2)}) collective-permute-start(f32[8,32,256]{2,1,0:T(8,128)S(1)} %get-tuple-element.81), channel_id=1, source_target_pairs={{0,120},{8,16},{16,8},{24,32},{32,24},{40,48},{48,40},{56,64},{64,... | collective-permute-start | bytes 786440 | tf_op jit(solution)/shard_map/ppermute | solution.py:33
  110.9 5.1 %solve_body.1 = (f32[32,32]{1,0:T(8,128)S(1)}, f32[32,32]{1,0:T(8,128)S(1)}) custom-call(f32[32,128]{1,0:T(8,128)S(1)} %add.72.grams, f32[32,128]{1,0:T(8,128)S(1)} %collective-permute-done.23.moved), custom_call_target="tpu_custom_call" | custom-call | tf_op jit(solution)/shard_map/solve_body/pallas_call | solution.py:78
  117.3 1.8 %finish_body.1 = (f32[32,2048]{1,0:T(8,128)}, f32[32,2048]{1,0:T(8,128)}) custom-call(f32[32,32]{1,0:T(8,128)S(1)} %get-tuple-element.72.p, f32[32,32]{1,0:T(8,128)S(1)} %get-tuple-element.73.q, f32[32,2048]{1,0:T(8,128)S(1)} %copy-done.1, f32[8,32,256]{2,1,0:T(8,128)S(1)} %sum_body.1.refs_1_.vector.u, f32[8,32,256]{2,1,0:T(8,128)S(1)} %get-tuple-element.79.rest, ...), custom_call_target="tpu_custom_call" | custom-call | tf_op jit(solution)/shard_map/finish_body/pallas_call | solution.py:78
  (68 shorter events, 21.1 us)
Async XLA Ops:
  0.6 18.5 %collective-permute-start.2 = (f32[32,2048]{1,0:T(8,128)}, f32[32,2048]{1,0:T(8,128)S(1)}, u32[]{:S(2)}, u32[]{:S(2)}) collective-permute-start(f32[32,2048]{1,0:T(8,128)} %right.1), channel_id=1, source_target_pairs={{0,120},{8,16},{16,8},{24,32},{32,24},{40,48},{48,40},{56,64},{64,... | collective-permute-start | bytes 786440 | tf_op jit(solution)/shard_map/ppermute | solution.py:33
  6.0 13.2 %collective-permute-start.1 = (f32[32,2048]{1,0:T(8,128)}, f32[32,2048]{1,0:T(8,128)S(1)}, u32[]{:S(2)}, u32[]{:S(2)}) collective-permute-start(f32[32,2048]{1,0:T(8,128)} %right.1), channel_id=1, source_target_pairs={{0,8},{8,0},{16,24},{24,16},{32,40},{40,32},{48,56},{56,48},{64,72... | collective-permute-start | bytes 786440 | tf_op jit(solution)/shard_map/ppermute | solution.py:33
  6.0 13.2 %collective-permute-start = (f32[32,2048]{1,0:T(8,128)}, f32[32,2048]{1,0:T(8,128)S(1)}, u32[]{:S(2)}, u32[]{:S(2)}) collective-permute-start(f32[32,2048]{1,0:T(8,128)} %right.1), channel_id=1, source_target_pairs={{0,7},{1,2},{2,1},{3,4},{4,3},{5,6},{6,5},{7,0},{8,15},{9,10},{10,... | collective-permute-start | bytes 786440 | tf_op jit(solution)/shard_map/ppermute | solution.py:33
  19.4 9.9 %collective-permute-start.4 = (f32[2,8,32,256]{3,2,1,0:T(8,128)S(1)}, f32[2,8,32,256]{3,2,1,0:T(8,128)S(1)}, u32[]{:S(2)}, u32[]{:S(2)}) collective-permute-start(f32[2,8,32,256]{3,2,1,0:T(8,128)S(1)} %get-tuple-element.48), channel_id=1, source_target_pairs={{0,7},{1,2},{2,1},{3,4},{4,3},{5,6},{6,5},{7,0},{8,15},{9,10},{10,... | collective-permute-start | bytes 1572872 | tf_op jit(solution)/shard_map/ppermute | solution.py:33
  31.0 9.9 %collective-permute-start.9 = (f32[2,8,32,256]{3,2,1,0:T(8,128)S(1)}, f32[2,8,32,256]{3,2,1,0:T(8,128)S(1)}, u32[]{:S(2)}, u32[]{:S(2)}) collective-permute-start(f32[2,8,32,256]{3,2,1,0:T(8,128)S(1)} %get-tuple-element.59), channel_id=1, source_target_pairs={{0,7},{1,2},{2,1},{3,4},{4,3},{5,6},{6,5},{7,0},{8,15},{9,10},{10,... | collective-permute-start | bytes 1572872 | tf_op jit(solution)/shard_map/ppermute | solution.py:33
  37.0 8.4 %collective-permute-start.5 = (f32[8,32,256]{2,1,0:T(8,128)S(1)}, f32[8,32,256]{2,1,0:T(8,128)S(1)}, u32[]{:S(2)}, u32[]{:S(2)}) collective-permute-start(f32[8,32,256]{2,1,0:T(8,128)S(1)} %get-tuple-element.53), channel_id=1, source_target_pairs={{0,1},{1,0},{2,3},{3,2},{4,5},{5,4},{6,7},{7,6},{8,9},{9,8},{10,11... | collective-permute-start | bytes 786440 | tf_op jit(solution)/shard_map/ppermute | solution.py:33
  37.5 8.0 %collective-permute-start.6 = (f32[8,32,256]{2,1,0:T(8,128)S(1)}, f32[8,32,256]{2,1,0:T(8,128)S(1)}, u32[]{:S(2)}, u32[]{:S(2)}) collective-permute-start(f32[8,32,256]{2,1,0:T(8,128)S(1)} %get-tuple-element.54), channel_id=1, source_target_pairs={{0,7},{1,2},{2,1},{3,4},{4,3},{5,6},{6,5},{7,0},{8,15},{9,10},{10,... | collective-permute-start | bytes 786440 | tf_op jit(solution)/shard_map/ppermute | solution.py:33
  41.0 8.5 %collective-permute-start.10 = (f32[8,32,256]{2,1,0:T(8,128)S(1)}, f32[8,32,256]{2,1,0:T(8,128)S(1)}, u32[]{:S(2)}, u32[]{:S(2)}) collective-permute-start(f32[8,32,256]{2,1,0:T(8,128)S(1)} %get-tuple-element.60), channel_id=1, source_target_pairs={{0,8},{8,0},{16,24},{24,16},{32,40},{40,32},{48,56},{56,48},{64,72... | collective-permute-start | bytes 786440 | tf_op jit(solution)/shard_map/ppermute | solution.py:33
  43.7 10.5 %collective-permute-start.11 = (f32[8,32,256]{2,1,0:T(8,128)S(1)}, f32[8,32,256]{2,1,0:T(8,128)S(1)}, u32[]{:S(2)}, u32[]{:S(2)}) collective-permute-start(f32[8,32,256]{2,1,0:T(8,128)S(1)} %get-tuple-element.61), channel_id=1, source_target_pairs={{0,120},{8,16},{16,8},{24,32},{32,24},{40,48},{48,40},{56,64},{64,... | collective-permute-start | bytes 786440 | tf_op jit(solution)/shard_map/ppermute | solution.py:33
  54.4 9.8 %collective-permute-start.14 = (f32[8,32,256]{2,1,0:T(8,128)S(1)}, f32[8,32,256]{2,1,0:T(8,128)S(1)}, u32[]{:S(2)}, u32[]{:S(2)}) collective-permute-start(f32[8,32,256]{2,1,0:T(8,128)S(1)} %sum_body.1.refs_1_.vector.u), channel_id=1, source_target_pairs={{0,120},{8,16},{16,8},{24,32},{32,24},{40,48},{48,40},{56,64},{64,... | collective-permute-start | bytes 786440 | tf_op jit(solution)/shard_map/ppermute | solution.py:33
  54.8 9.3 %collective-permute-start.13 = (f32[8,32,256]{2,1,0:T(8,128)S(1)}, f32[8,32,256]{2,1,0:T(8,128)S(1)}, u32[]{:S(2)}, u32[]{:S(2)}) collective-permute-start(f32[8,32,256]{2,1,0:T(8,128)S(1)} %sum_body.1.refs_1_.vector.u), channel_id=1, source_target_pairs={{0,8},{8,0},{16,24},{24,16},{32,40},{40,32},{48,56},{56,48},{64,72... | collective-permute-start | bytes 786440 | tf_op jit(solution)/shard_map/ppermute | solution.py:33
  54.8 9.3 %collective-permute-start.12 = (f32[8,32,256]{2,1,0:T(8,128)S(1)}, f32[8,32,256]{2,1,0:T(8,128)S(1)}, u32[]{:S(2)}, u32[]{:S(2)}) collective-permute-start(f32[8,32,256]{2,1,0:T(8,128)S(1)} %sum_body.1.refs_1_.vector.u), channel_id=1, source_target_pairs={{0,7},{1,2},{2,1},{3,4},{4,3},{5,6},{6,5},{7,0},{8,15},{9,10},{10,... | collective-permute-start | bytes 786440 | tf_op jit(solution)/shard_map/ppermute | solution.py:33
  64.3 4.0 %collective-permute-start.15 = (f32[3,8,32,256]{3,2,1,0:T(8,128)S(1)}, f32[3,8,32,256]{3,2,1,0:T(8,128)S(1)}, u32[]{:S(2)}, u32[]{:S(2)}) collective-permute-start(f32[3,8,32,256]{3,2,1,0:T(8,128)S(1)} %get-tuple-element.62.whole), channel_id=1, source_target_pairs={{0,1},{1,0},{2,3},{3,2},{4,5},{5,4},{6,7},{7,6},{8,9},{9,8},{10,11... | collective-permute-start | bytes 2359304 | tf_op jit(solution)/shard_map/ppermute | solution.py:33
  64.3 10.7 %collective-permute-start.16 = (f32[2,8,32,256]{3,2,1,0:T(8,128)S(1)}, f32[2,8,32,256]{3,2,1,0:T(8,128)S(1)}, u32[]{:S(2)}, u32[]{:S(2)}) collective-permute-start(f32[2,8,32,256]{3,2,1,0:T(8,128)S(1)} %get-tuple-element.65), channel_id=1, source_target_pairs={{0,7},{1,2},{2,1},{3,4},{4,3},{5,6},{6,5},{7,0},{8,15},{9,10},{10,... | collective-permute-start | bytes 1572872 | tf_op jit(solution)/shard_map/ppermute | solution.py:33
  76.0 3.8 %collective-permute-start.17 = (f32[32,128]{1,0:T(8,128)S(1)}, f32[32,128]{1,0:T(8,128)S(1)}, u32[]{:S(2)}, u32[]{:S(2)}) collective-permute-start(f32[32,128]{1,0:T(8,128)S(1)} %get-tuple-element.69.grams), channel_id=1, source_target_pairs={{0,2},{1,3},{2,0},{3,1},{4,6},{5,7},{6,4},{7,5},{8,10},{9,11},{10,... | collective-permute-start | bytes 49160 | tf_op jit(solution)/shard_map/ppermute | solution.py:310
  79.8 4.9 %collective-permute-start.18 = (f32[32,128]{1,0:T(8,128)S(1)}, f32[32,128]{1,0:T(8,128)S(1)}, u32[]{:S(2)}, u32[]{:S(2)}) collective-permute-start(f32[32,128]{1,0:T(8,128)S(1)} %add_body.3.grams), channel_id=1, source_target_pairs={{0,6},{1,7},{2,4},{3,5},{4,2},{5,3},{6,0},{7,1},{8,14},{9,15},{10,... | collective-permute-start | bytes 49160 | tf_op jit(solution)/shard_map/ppermute | solution.py:310
  87.4 19.9 %collective-permute-start.24 = (f32[3,8,32,256]{3,2,1,0:T(8,128)S(1)}, f32[3,8,32,256]{3,2,1,0:T(8,128)S(1)}, u32[]{:S(2)}, u32[]{:S(2)}) collective-permute-start(f32[3,8,32,256]{3,2,1,0:T(8,128)S(1)} %get-tuple-element.77), channel_id=1, source_target_pairs={{0,1},{1,0},{2,3},{3,2},{4,5},{5,4},{6,7},{7,6},{8,9},{9,8},{10,11... | collective-permute-start | bytes 2359304 | tf_op jit(solution)/shard_map/ppermute | solution.py:33
  87.4 19.8 %collective-permute-start.25 = (f32[3,8,32,256]{3,2,1,0:T(8,128)S(1)}, f32[3,8,32,256]{3,2,1,0:T(8,128)S(1)}, u32[]{:S(2)}, u32[]{:S(2)}) collective-permute-start(f32[3,8,32,256]{3,2,1,0:T(8,128)S(1)} %get-tuple-element.78), channel_id=1, source_target_pairs={{0,7},{1,2},{2,1},{3,4},{4,3},{5,6},{6,5},{7,0},{8,15},{9,10},{10,... | collective-permute-start | bytes 2359304 | tf_op jit(solution)/shard_map/ppermute | solution.py:33
  89.9 3.7 %collective-permute-start.19 = (f32[32,128]{1,0:T(8,128)S(1)}, f32[32,128]{1,0:T(8,128)S(1)}, u32[]{:S(2)}, u32[]{:S(2)}) collective-permute-start(f32[32,128]{1,0:T(8,128)S(1)} %add_body.4.grams), channel_id=1, source_target_pairs={{0,8},{1,9},{2,10},{3,11},{4,12},{5,13},{6,14},{7,15},{8,0},{9,1},... | collective-permute-start | bytes 49160 | tf_op jit(solution)/shard_map/ppermute | solution.py:310
  93.6 4.9 %collective-permute-start.20 = (f32[32,128]{1,0:T(8,128)S(1)}, f32[32,128]{1,0:T(8,128)S(1)}, u32[]{:S(2)}, u32[]{:S(2)}) collective-permute-start(f32[32,128]{1,0:T(8,128)S(1)} %add_body.5), channel_id=1, source_target_pairs={{0,24},{1,25},{2,26},{3,27},{4,28},{5,29},{6,30},{7,31},{8,16},{9,... | collective-permute-start | bytes 49160 | tf_op jit(solution)/shard_map/ppermute | solution.py:310
  98.6 3.7 %collective-permute-start.21 = (f32[32,128]{1,0:T(8,128)S(1)}, f32[32,128]{1,0:T(8,128)S(1)}, u32[]{:S(2)}, u32[]{:S(2)}) collective-permute-start(f32[32,128]{1,0:T(8,128)S(1)} %add.70), channel_id=1, source_target_pairs={{0,32},{1,33},{2,34},{3,35},{4,36},{5,37},{6,38},{7,39},{8,40},{9,... | collective-permute-start | bytes 49160 | tf_op jit(solution)/shard_map/ppermute | solution.py:310
  102.3 4.9 %collective-permute-start.22 = (f32[32,128]{1,0:T(8,128)S(1)}, f32[32,128]{1,0:T(8,128)S(1)}, u32[]{:S(2)}, u32[]{:S(2)}) collective-permute-start(f32[32,128]{1,0:T(8,128)S(1)} %add.71), channel_id=1, source_target_pairs={{0,96},{1,97},{2,98},{3,99},{4,100},{5,101},{6,102},{7,103},{8,104... | collective-permute-start | bytes 49160 | tf_op jit(solution)/shard_map/ppermute | solution.py:310
  107.4 8.6 %collective-permute-start.26 = (f32[8,32,256]{2,1,0:T(8,128)S(1)}, f32[8,32,256]{2,1,0:T(8,128)S(1)}, u32[]{:S(2)}, u32[]{:S(2)}) collective-permute-start(f32[8,32,256]{2,1,0:T(8,128)S(1)} %get-tuple-element.80), channel_id=1, source_target_pairs={{0,8},{8,0},{16,24},{24,16},{32,40},{40,32},{48,56},{56,48},{64,72... | collective-permute-start | bytes 786440 | tf_op jit(solution)/shard_map/ppermute | solution.py:33
  107.5 9.8 %collective-permute-start.27 = (f32[8,32,256]{2,1,0:T(8,128)S(1)}, f32[8,32,256]{2,1,0:T(8,128)S(1)}, u32[]{:S(2)}, u32[]{:S(2)}) collective-permute-start(f32[8,32,256]{2,1,0:T(8,128)S(1)} %get-tuple-element.81), channel_id=1, source_target_pairs={{0,120},{8,16},{16,8},{24,32},{32,24},{40,48},{48,40},{56,64},{64,... | collective-permute-start | bytes 786440 | tf_op jit(solution)/shard_map/ppermute | solution.py:33
  (6 other events, 27.2 us)

commit v5 on v4

--- a/solution.py
+++ b/solution.py
@@ -1,3 +1,5 @@
+import functools
+
 import jax
 import jax.numpy as jnp
 from jax import lax
@@ -14,7 +16,6 @@
 HALF = 4
 PREPARED = 8
 NEAR_TABLES = 7
-TOKEN = pltpu.VMEM((8, 128), F32)
 
 
 def in_vmem(value):
@@ -87,35 +88,64 @@
     )(*args[:n_smem], *[in_vmem(a) for a in args[n_smem:]])
 
 
-def prepare_body(routes, edge, couplings, c_high, c_low, token, buffer, arrived):
+def route(pair, routes, blocks):
+    count = pair.shape[1]
+    block_bits, col_bits = blocks.bit_length() - 1, lax.axis_size("col").bit_length() - 1
+    my_row, my_col = lax.axis_index("row"), lax.axis_index("col")
+    row_of, col_of = pair[0:1, :], pair[1:2, :]
+    owner = col_of >> block_bits
+    row_slot = slot_of(owner >> col_bits, my_row)
+    col_slot = slot_of(owner & (lax.axis_size("col") - 1), my_col)
+    diagonal = (row_slot > 0) & (col_slot > 0)
+    slot = jnp.where(diagonal, 2 + 2 * col_slot + row_slot, jnp.where(col_slot > 0, 2 + col_slot, row_slot))
+    table_row = slot * blocks + (col_of & (blocks - 1))
+    local_row = row_of & (blocks - 1)
+    number = lax.broadcasted_iota(jnp.int32, (1, count), 1)
+    late = jnp.where(slot >= NEAR_TABLES, 1, 0)
+    key = (late * count + number).astype(F32)
+    square = (count, count)
+    down, across = (lax.broadcasted_iota(jnp.int32, square, axis) for axis in (0, 1))
+
+    def upright(value):
+        return jnp.sum(jnp.where(down == across, value.astype(F32), 0.0), axis=1, keepdims=True)
+
+    rank = jnp.sum(jnp.where(key < upright(key), 1.0, 0.0), axis=1, keepdims=True)
+    placed = rank == across.astype(F32)
+    for i, value in enumerate((number, table_row, local_row)):
+        routes[i:i + 1, :] = jnp.sum(jnp.where(placed, upright(value), 0.0), axis=0, keepdims=True).astype(jnp.int32)
+    near = count - jnp.sum(late.astype(F32), axis=1, keepdims=True).astype(jnp.int32)
+    routes[3:4, :] = jnp.broadcast_to(near >> (HALF.bit_length() - 1), (1, count))
+
+
+def prepare_body(blocks, pair, couplings, c_high, c_low, routes, buffer, arrived):
     count = couplings.shape[0]
-    token[...] = jnp.zeros_like(token)
     copies = []
     for i in range(count // PREPARED):
         part = pl.ds(i * PREPARED, PREPARED)
         copies.append(pltpu.make_async_copy(couplings.at[part], buffer.at[part], arrived.at[i]))
     for copy in copies:
         copy.start()
+    route(pair, routes, blocks)
     for i, copy in enumerate(copies):
         copy.wait()
         for k in range(i * PREPARED, (i + 1) * PREPARED):
             c_high[k], c_low[k] = split(buffer[k])
 
 
-def prepare(couplings, routes, edge):
+def prepare(pair_index, couplings, blocks):
     shape = pltpu.VMEM(couplings.shape, BF16)
     return pl.pallas_call(
-        prepare_body,
-        in_specs=[SMEM_SPEC, SMEM_SPEC, pl.BlockSpec(memory_space=pltpu.HBM)],
+        functools.partial(prepare_body, blocks),
+        in_specs=[VMEM_SPEC, pl.BlockSpec(memory_space=pltpu.HBM)],
         out_specs=[VMEM_SPEC] * 3,
-        out_shape=[shape, shape, TOKEN],
+        out_shape=[shape, shape, pltpu.VMEM((4, pair_index.shape[1]), jnp.int32)],
         scratch_shapes=[
             pltpu.VMEM(couplings.shape, F32),
             pltpu.SemaphoreType.DMA((couplings.shape[0] // PREPARED,)),
         ],
         name="prepare",
-        compiler_params=pltpu.CompilerParams(vmem_limit_bytes=17 << 20),
-    )(routes, edge, in_hbm(couplings))
+        compiler_params=pltpu.CompilerParams(vmem_limit_bytes=18 << 20),
+    )(in_vmem(pair_index), in_hbm(couplings))
 
 
 def block_of(source, q, width):
@@ -155,7 +185,7 @@
     lax.fori_loop(0, (last - first) % 2, rest, 0)
 
 
-def pull_near_body(routes, edge, qa, whole, cb, *refs):
+def pull_near_body(routes, qa, whole, cb, *refs):
     c_high, c_low, table, strain = refs
     blocks = strain.shape[0]
     for place, (source, slot) in enumerate(
@@ -164,17 +194,17 @@
             block = block_of(source, q, strain.shape[2]) if slot is None else source[slot, q]
             table[place * blocks + q] = stacked_split(block)
     strain[...] = jnp.zeros_like(strain)
-    accumulate(dot_nt, 0, edge[0], routes, 1, 2, table, strain, c_high, c_low)
-
-
-def pull_late_body(routes, edge, table_in, strain_in, db, *refs):
+    accumulate(dot_nt, 0, routes[3, 0], routes, 1, 2, table, strain, c_high, c_low)
+
+
+def pull_late_body(routes, table_in, strain_in, db, *refs):
     c_high, c_low, *grams, table, strain_hl, g_out, strain = refs
     blocks = strain.shape[0]
     for slot in range(2):
         for q in range(blocks):
             table[(NEAR_TABLES + slot) * blocks + q] = stacked_split(db[slot, q])
     strain[...] = strain_in[...]
-    accumulate(dot_nt, edge[0], routes.shape[1] // HALF, routes, 1, 2, table, strain, c_high, c_low)
+    accumulate(dot_nt, routes[3, 0], routes.shape[1] // HALF, routes, 1, 2, table, strain, c_high, c_low)
     total = jnp.zeros((strain.shape[1],) * 2, F32)
     for q in range(blocks):
         both = stacked_split(strain[q])
@@ -189,32 +219,36 @@
             g_out[:, i * size:(i + 1) * size] = part
 
 
-def push_late_body(routes, edge, strain_hl, c_high, c_low, pieces, *targets):
+def push_late_body(routes, strain_hl, c_high, c_low, pieces, *targets):
     blocks = strain_hl.shape[0]
     pieces[...] = jnp.zeros_like(pieces)
-    accumulate(dot_nn, edge[0], routes.shape[1] // HALF, routes, 2, 1, strain_hl, pieces, c_high, c_low)
+    accumulate(dot_nn, routes[3, 0], routes.shape[1] // HALF, routes, 2, 1, strain_hl, pieces, c_high, c_low)
     for db in targets:
         for slot in range(2):
             for q in range(blocks):
                 db[slot, q] = pieces[(NEAR_TABLES + slot) * blocks + q]
 
 
-def push_near_body(routes, edge, strain_hl, c_high, c_low, pieces_in, *refs):
+def push_near_body(routes, strain_hl, c_high, c_low, pieces_in, *refs):
     *outs, pieces = refs
     pieces[...] = pieces_in[:pieces.shape[0]]
-    accumulate(dot_nn, 0, edge[0], routes, 2, 1, strain_hl, pieces, c_high, c_low)
+    accumulate(dot_nn, 0, routes[3, 0], routes, 2, 1, strain_hl, pieces, c_high, c_low)
     for place, target in enumerate(outs):
         for q in range(target.shape[0]):
             target[q] = pieces[place * target.shape[0] + q]
 
 
-def push_begin_body(routes, edge, strain_hl, c_high, c_low, pieces_in, pieces):
-    accumulate(dot_nn, 0, edge[0] // 2, routes, 2, 1, strain_hl, pieces, c_high, c_low)
-
-
-def push_end_body(routes, edge, strain_hl, c_high, c_low, pieces_in, own, ra, rb, qa, qb, pieces):
-    blocks = strain_hl.shape[0]
-    accumulate(dot_nn, edge[0] // 2, edge[0], routes, 2, 1, strain_hl, pieces, c_high, c_low)
+def push_begin_body(routes, strain_hl, c_high, c_low, pieces_in, pieces):
+    accumulate(dot_nn, 0, routes[3, 0] // 2, routes, 2, 1, strain_hl, pieces, c_high, c_low)
+
+
+def push_end_body(routes, strain_hl, c_high, c_low, pieces_in, pieces):
+    accumulate(dot_nn, routes[3, 0] // 2, routes[3, 0], routes, 2, 1, strain_hl, pieces, c_high, c_low)
+
+
+def pack_body(pieces, grams, moved, own, ra, rb, qa, qb, total):
+    total[...] = grams[...] + moved[...]
+    blocks = own.shape[0]
     outs = (own, ra, rb, qa.at[0], qa.at[1], qa.at[2], qb.at[0], qb.at[1], qb.at[2])
     for target, place in zip(outs, (0, 1, 2, 3, 5, 6, 4, 7, 8)):
         for q in range(blocks):
@@ -302,33 +336,13 @@
         r_out[:, lanes] = right[:, lanes] - full_tn(p[...], u[block]) + full_tn(q[...], w)
 
 
-MASKS = (2, 6, 8, 24, 32, 96, 1)
+MASKS = (2, 6, 8, 24, 1)
+RING = (32, 96, 64)
 
 
 def exchanged(value, mask):
     count = lax.axis_size("row") * lax.axis_size("col")
     return lax.ppermute(value, ("row", "col"), [(i, i ^ mask) for i in range(count)])
-
-
-def routing(pair_index, blocks):
-    count = pair_index.shape[1]
-    col_size = lax.axis_size("col")
-    my_row, my_col = lax.axis_index("row"), lax.axis_index("col")
-    local_row = pair_index[0] - (my_row * col_size + my_col) * blocks
-    owner, in_owner = lax.div(pair_index[1], blocks), lax.rem(pair_index[1], blocks)
-    row_slot = slot_of(lax.div(owner, col_size), my_row)
-    col_slot = slot_of(lax.rem(owner, col_size), my_col)
-    diagonal = (row_slot > 0) & (col_slot > 0)
-    slot = jnp.where(diagonal, 2 + 2 * col_slot + row_slot, jnp.where(col_slot > 0, 2 + col_slot, row_slot))
-    table_row = slot * blocks + in_owner
-    late = (slot >= NEAR_TABLES).astype(jnp.int32)
-    number = jnp.arange(count, dtype=jnp.int32)
-    rank = jnp.sum(((late * count + number)[None, :] < (late * count + number)[:, None]).astype(jnp.int32), axis=1)
-    placed = rank[None, :] == number[:, None]
-    columns = (number, table_row, local_row)
-    routes = jnp.stack([jnp.sum(jnp.where(placed, c[None, :], 0), axis=1) for c in columns])
-    edge = (count - jnp.sum(late, keepdims=True)) >> (HALF.bit_length() - 1)
-    return routes, edge
 
 
 def per_device(right_sides, diag_blocks, couplings, pair_index):
@@ -352,22 +366,21 @@
         return (swapped(whole, "col", 0), whole, cb), swapped(pair, "col", 1)
 
     def pulled(near_tables, db, couplings, *grams):
-        table, strain = call(pull_near_body, [table_shape, block_shape], 2, (routes, edge, *near_tables, *couplings))
+        table, strain = call(pull_near_body, [table_shape, block_shape], 1, (routes, *near_tables, *couplings))
         _, strain_hl, g = call(
-            pull_late_body, [table_shape, split_shape, all_grams_shape if grams else gram_shape], 2,
-            (routes, edge, table, strain, db, *couplings, *grams), [block_shape], aliases={2: 0})
+            pull_late_body, [table_shape, split_shape, all_grams_shape if grams else gram_shape], 1,
+            (routes, table, strain, db, *couplings, *grams), [block_shape], aliases={1: 0})
         return strain_hl, g
 
-    routes, edge = routing(pair_index, blocks)
-    *couplings, token = prepare(couplings, routes, edge)
-    near_tables, db = spread(right_sides, token)
+    *couplings, routes = prepare(pair_index, couplings, blocks)
+    near_tables, db = spread(right_sides, routes)
     strain_hl, g1s = pulled(near_tables, db, couplings)
 
-    pieces, db = call(push_late_body, [pieces_shape, pair_shape], 2, (routes, edge, strain_hl, *couplings))
+    pieces, db = call(push_late_body, [pieces_shape, pair_shape], 1, (routes, strain_hl, *couplings))
     db = swapped(db, "col", 1)
     own, ra, rb, ca, cb, qa_first, qa_second = call(
-        push_near_body, [block_shape] * NEAR_TABLES, 2,
-        (routes, edge, strain_hl, *couplings, pieces), [near_pieces_shape])
+        push_near_body, [block_shape] * NEAR_TABLES, 1,
+        (routes, strain_hl, *couplings, pieces), [near_pieces_shape])
     ca, qa_first, qa_second = (swapped(a, "col", 0) for a in (ca, qa_first, qa_second))
     cb = swapped(cb, "col", 1)
     diag, g01 = call(diag_body, [block_shape, grams_shape], 0, (right_sides, diag_blocks))
@@ -375,20 +388,21 @@
     ra, rb = swapped(ra, "row", 0), swapped(rb, "row", 1)
     u = call(sum_body, block_shape, 0, (own, diag, ca, cb, ra, rb))
 
-    near_tables, db = spread(u)
     diag, g23 = call(diag_body, [block_shape, grams_shape], 0, (u, diag_blocks))
+    near_tables, db = spread(u, g23)
     strain_hl, grams = pulled(near_tables, db, couplings, g01, g1s, g23)
-    pieces, = call(push_late_body, [pieces_shape], 2, (routes, edge, strain_hl, *couplings))
+    pieces, = call(push_late_body, [pieces_shape], 1, (routes, strain_hl, *couplings))
     grams = call(add_body, all_grams_shape, 0, (grams, exchanged(grams, MASKS[0]), pieces))
-    pieces, = call(push_begin_body, [pieces_shape], 2, (routes, edge, strain_hl, *couplings, pieces), aliases={5: 0})
+    pieces, = call(push_begin_body, [pieces_shape], 1, (routes, strain_hl, *couplings, pieces), aliases={4: 0})
     grams = call(add_body, all_grams_shape, 0, (grams, exchanged(grams, MASKS[1]), pieces))
-    own, ra, rb, qa, qb, _ = call(
-        push_end_body, [block_shape] * 3 + [stack_shape] * 2 + [pieces_shape], 2,
-        (routes, edge, strain_hl, *couplings, pieces), aliases={5: 5})
-    grams = call(add_body, all_grams_shape, 0, (grams, exchanged(grams, MASKS[2]), own))
+    pieces, = call(push_end_body, [pieces_shape], 1, (routes, strain_hl, *couplings, pieces), aliases={4: 0})
+    own, ra, rb, qa, qb, grams = call(
+        pack_body, [block_shape] * 3 + [stack_shape] * 2 + [all_grams_shape], 0,
+        (pieces, grams, exchanged(grams, MASKS[2])))
     qa, qb = swapped(qa, "col", 0), swapped(qb, "col", 1)
-    for mask in MASKS[3:6]:
-        grams = grams + exchanged(grams, mask)
+    grams = grams + exchanged(grams, MASKS[3])
+    first, second, third = (exchanged(grams, mask) for mask in RING)
+    grams = (grams + first) + (second + third)
     rest, ra, rb = call(middle_last_body, [block_shape] * 3, 0, (own, diag, ra, rb, qa, qb, grams))
     ra, rb = swapped(ra, "row", 0), swapped(rb, "row", 1)
     p, q = call(solve_body, [gram_shape] * 2, 0, (grams, exchanged(grams, MASKS[-1])))

time: 120 us -> 113 us (0.942)
  waiting for transfers between devices: 43.9 us -> 29.6 us
  starting transfers between devices: 27.1 us -> 38.1 us
  other arithmetic: 2.46 us -> 0.01 us
    ppermute x7 -> x8, waiting for transfers between devices: 20.6 us -> 9.74 us  [exchanged(): lax.ppermute(value, ('row', 'col'), [(i, i ^ mask) for i in range(count)])]
    ppermute x21, starting transfers between devices: 23.6 us -> 29.4 us  [swapped(): return lax.ppermute(value, axis, pairs_of(lax.axis_size(axis), shift))]
    ppermute x7 -> x8, starting transfers between devices: 3.55 us -> 8.64 us  [exchanged(): lax.ppermute(value, ('row', 'col'), [(i, i ^ mask) for i in range(count)])]
    ppermute x21, waiting for transfers between devices: 23.3 us -> 19.9 us  [swapped(): return lax.ppermute(value, axis, pairs_of(lax.axis_size(axis), shift))]
    reduce_sum x3 -> x0, other arithmetic: 1.65 us -> none  [the longest x1 1.33 us: routing(): edge = count - jnp.sum(late, keepdims=True) >> HALF.bit_length() - 1]
  transfers between devices with their start and end apart: 28 -> 29, of which waited for: 13 -> 15; matrix products, arithmetic and copies ran while one was open for 2% -> 0% of each run, Pallas kernels for 31% -> 34%
where the time goes in v5:
time: 113 us
  Pallas kernels  43.4 us (38%)
  starting transfers between devices  38.1 us (34%)
  waiting for transfers between devices  29.6 us (26%)
    pallas_call x21, Pallas kernels, call(): pl.pallas_call(body, out_shape=out_shape, in_specs=[SMEM_SPEC] * n_smem +...  37.1 us
    ppermute x21, starting transfers between devices, swapped(): return lax.ppermute(value, axis, pairs_of(lax.axis_size(axis), shift))  29.4 us
    ppermute x21, waiting for transfers between devices, swapped(): return lax.ppermute(value, axis, pairs_of(lax.axis_size(axis), shift))  19.9 us
    ppermute x8, waiting for transfers between devices, exchanged(): lax.ppermute(value, ('row', 'col'), [(i, i ^ mask) for i in range(count)])  9.74 us
    ppermute x8, starting transfers between devices, exchanged(): lax.ppermute(value, ('row', 'col'), [(i, i ^ mask) for i in range(count)])  8.64 us
    pallas_call x1, Pallas kernels, prepare(): pl.pallas_call(functools.partial(prepare_body, blocks), in_specs=[VMEM_SP...  6.25 us
  transfers between devices with their start and end apart: 29, of which 15 were waited for; matrix products, arithmetic and copies ran while one was open for 0% of the time, Pallas kernels for 34%

profile of v5, /device:TPU:0, one launch (start us, length us, event | category | flops | bytes accessed | tf_op | source)
XLA Modules:
  0.0 112.6 jit_solution(4176038028474546690)
XLA Ops:
  0.6 5.4 %collective-permute-start.2 = (f32[32,2048]{1,0:T(8,128)}, f32[32,2048]{1,0:T(8,128)S(1)}, u32[]{:S(2)}, u32[]{:S(2)}) collective-permute-start(f32[32,2048]{1,0:T(8,128)} %right.1), channel_id=1, source_target_pairs={{0,120},{8,16},{16,8},{24,32},{32,24},{40,48},{48,40},{56,64},{64,... | collective-permute-start | bytes 786440 | tf_op jit(solution)/shard_map/ppermute | solution.py:34
  6.0 3.2 %collective-permute-start = (f32[32,2048]{1,0:T(8,128)}, f32[32,2048]{1,0:T(8,128)S(1)}, u32[]{:S(2)}, u32[]{:S(2)}) collective-permute-start(f32[32,2048]{1,0:T(8,128)} %right.1), channel_id=1, source_target_pairs={{0,7},{1,2},{2,1},{3,4},{4,3},{5,6},{6,5},{7,0},{8,15},{9,10},{10,... | collective-permute-start | bytes 786440 | tf_op jit(solution)/shard_map/ppermute | solution.py:34
  9.9 6.3 %prepare.1 = (bf16[64,256,256]{2,1,0:T(8,128)(2,1)S(1)}, bf16[64,256,256]{2,1,0:T(8,128)(2,1)S(1)}, s32[4,64]{1,0:T(4,128)S(1)}) custom-call(s32[2,64]{1,0:T(2,128)S(1)} %copy-done.2, f32[64,256,256]{2,1,0:T(8,128)} %couplings.1), custom_call_target="tpu_custom_call" | custom-call | tf_op jit(solution)/shard_map/prepare/pallas_call | solution.py:137
  16.4 1.9 %collective-permute-start.4 = (f32[2,8,32,256]{3,2,1,0:T(8,128)S(1)}, f32[2,8,32,256]{3,2,1,0:T(8,128)S(1)}, u32[]{:S(2)}, u32[]{:S(2)}) collective-permute-start(f32[2,8,32,256]{3,2,1,0:T(8,128)S(1)} %get-tuple-element.49), channel_id=1, source_target_pairs={{0,7},{1,2},{2,1},{3,4},{4,3},{5,6},{6,5},{7,0},{8,15},{9,10},{10,... | collective-permute-start | bytes 1572872 | tf_op jit(solution)/shard_map/ppermute | solution.py:34
  18.7 6.7 %pull_near_body.2 = (bf16[72,64,256]{2,1,0:T(8,128)(2,1)S(1)}, f32[8,32,256]{2,1,0:T(8,128)S(1)}) custom-call(s32[4,64]{1,0:T(4,128)S(1)} %get-tuple-element.43.refs_0_.routes, f32[3,8,32,256]{3,2,1,0:T(8,128)S(1)} %collective-permute-done.3.qa, f32[3,8,32,256]{3,2,1,0:T(8,128)S(1)} %get-tuple-element.44.whole, ...), custom_call_target="tpu_custom_call" | custom-call | tf_op jit(solution)/shard_map/pull_near_body/pallas_call | solution.py:79
  28.0 1.9 %collective-permute-start.9 = (f32[2,8,32,256]{3,2,1,0:T(8,128)S(1)}, f32[2,8,32,256]{3,2,1,0:T(8,128)S(1)}, u32[]{:S(2)}, u32[]{:S(2)}) collective-permute-start(f32[2,8,32,256]{3,2,1,0:T(8,128)S(1)} %get-tuple-element.60), channel_id=1, source_target_pairs={{0,7},{1,2},{2,1},{3,4},{4,3},{5,6},{6,5},{7,0},{8,15},{9,10},{10,... | collective-permute-start | bytes 1572872 | tf_op jit(solution)/shard_map/ppermute | solution.py:34
  29.9 4.5 %push_near_body.1 = (f32[8,32,256]{2,1,0:T(8,128)S(1)}, f32[8,32,256]{2,1,0:T(8,128)S(1)}, f32[8,32,256]{2,1,0:T(8,128)S(1)}, f32[8,32,256]{2,1,0:T(8,128)S(1)},...) custom-call(s32[4,64]{1,0:T(4,128)S(1)} %get-tuple-element.43.refs_0_.routes, ...), custom_call_target="tpu_custom_call" | custom-call | tf_op jit(solution)/shard_map/push_near_body/pallas_call | solution.py:79
  38.0 1.8 %collective-permute-start.10 = (f32[8,32,256]{2,1,0:T(8,128)S(1)}, f32[8,32,256]{2,1,0:T(8,128)S(1)}, u32[]{:S(2)}, u32[]{:S(2)}) collective-permute-start(f32[8,32,256]{2,1,0:T(8,128)S(1)} %get-tuple-element.61), channel_id=1, source_target_pairs={{0,8},{8,0},{16,24},{24,16},{32,40},{40,32},{48,56},{56,48},{64,72... | collective-permute-start | bytes 786440 | tf_op jit(solution)/shard_map/ppermute | solution.py:34
  42.4 2.3 %collective-permute-done.10.ra = f32[8,32,256]{2,1,0:T(8,128)S(1)} collective-permute-done((f32[8,32,256]{2,1,0:T(8,128)S(1)}, f32[8,32,256]{2,1,0:T(8,128)S(1)}, u32[]{:S(2)}, u32[]{:S(2)}) %collective-permute-start.10) | collective-permute-done | bytes 262176 | tf_op jit(solution)/shard_map/ppermute | solution.py:34
  44.8 5.3 %collective-permute-done.11.rb = f32[8,32,256]{2,1,0:T(8,128)S(1)} collective-permute-done((f32[8,32,256]{2,1,0:T(8,128)S(1)}, f32[8,32,256]{2,1,0:T(8,128)S(1)}, u32[]{:S(2)}, u32[]{:S(2)}) %collective-permute-start.11) | collective-permute-done | bytes 262176 | tf_op jit(solution)/shard_map/ppermute | solution.py:34
  51.7 3.2 %collective-permute-start.12 = (f32[8,32,256]{2,1,0:T(8,128)S(1)}, f32[8,32,256]{2,1,0:T(8,128)S(1)}, u32[]{:S(2)}, u32[]{:S(2)}) collective-permute-start(f32[8,32,256]{2,1,0:T(8,128)S(1)} %sum_body.1.vector.refs_2_.u), channel_id=1, source_target_pairs={{0,7},{1,2},{2,1},{3,4},{4,3},{5,6},{6,5},{7,0},{8,15},{9,10},{10,... | collective-permute-start | bytes 786440 | tf_op jit(solution)/shard_map/ppermute | solution.py:34
  56.6 5.1 %collective-permute-done.14.refs_4_ = f32[8,32,256]{2,1,0:T(8,128)S(1)} collective-permute-done((f32[8,32,256]{2,1,0:T(8,128)S(1)}, f32[8,32,256]{2,1,0:T(8,128)S(1)}, u32[]{:S(2)}, u32[]{:S(2)}) %collective-permute-start.14) | collective-permute-done | bytes 262176 | tf_op jit(solution)/shard_map/ppermute | solution.py:34
  64.7 6.7 %pull_near_body.3 = (bf16[72,64,256]{2,1,0:T(8,128)(2,1)S(1)}, f32[8,32,256]{2,1,0:T(8,128)S(1)}) custom-call(s32[4,64]{1,0:T(4,128)S(1)} %get-tuple-element.43.refs_0_.routes, f32[3,8,32,256]{3,2,1,0:T(8,128)S(1)} %collective-permute-done.15.qa, f32[3,8,32,256]{3,2,1,0:T(8,128)S(1)} %get-tuple-element.64.whole, ...), custom_call_target="tpu_custom_call" | custom-call | tf_op jit(solution)/shard_map/pull_near_body/pallas_call | solution.py:79
  73.6 1.9 %collective-permute-start.17 = (f32[32,128]{1,0:T(8,128)S(1)}, f32[32,128]{1,0:T(8,128)S(1)}, u32[]{:S(2)}, u32[]{:S(2)}) collective-permute-start(f32[32,128]{1,0:T(8,128)S(1)} %get-tuple-element.71.grams), channel_id=1, source_target_pairs={{0,2},{1,3},{2,0},{3,1},{4,6},{5,7},{6,4},{7,5},{8,10},{9,11},{10,... | collective-permute-start | bytes 49160 | tf_op jit(solution)/shard_map/ppermute | solution.py:345
  77.4 2.6 %collective-permute-start.18 = (f32[32,128]{1,0:T(8,128)S(1)}, f32[32,128]{1,0:T(8,128)S(1)}, u32[]{:S(2)}, u32[]{:S(2)}) collective-permute-start(f32[32,128]{1,0:T(8,128)S(1)} %add_body.2.grams), channel_id=1, source_target_pairs={{0,6},{1,7},{2,4},{3,5},{4,2},{5,3},{6,0},{7,1},{8,14},{9,15},{10,... | collective-permute-start | bytes 49160 | tf_op jit(solution)/shard_map/ppermute | solution.py:345
  79.9 2.4 %push_begin_body.1.pieces_in.after = f32[72,32,256]{2,1,0:T(8,128)S(1)} custom-call(s32[4,64]{1,0:T(4,128)S(1)} %get-tuple-element.43.refs_0_.routes, bf16[8,64,256]{2,1,0:T(8,128)(2,1)S(1)} %get-tuple-element.70.strain_hl, bf16[64,256,256]{2,1,0:T(8,128)(2,1)S(1)} %get-tuple-element.45.refs_0_.c_high, ...), custom_call_target="tpu_custom_call", output_to_operand_aliasing={{}: (4, {})} | custom-call | tf_op jit(solution)/shard_map/push_begin_body/pallas_call | solution.py:79
  83.1 2.4 %push_end_body.1.pieces = f32[72,32,256]{2,1,0:T(8,128)S(1)} custom-call(s32[4,64]{1,0:T(4,128)S(1)} %get-tuple-element.43.refs_0_.routes, bf16[8,64,256]{2,1,0:T(8,128)(2,1)S(1)} %get-tuple-element.70.strain_hl, bf16[64,256,256]{2,1,0:T(8,128)(2,1)S(1)} %get-tuple-element.45.refs_0_.c_high, ...), custom_call_target="tpu_custom_call", output_to_operand_aliasing={{}: (4, {})} | custom-call | tf_op jit(solution)/shard_map/push_end_body/pallas_call | solution.py:79
  86.5 2.5 %collective-permute-start.26 = (f32[3,8,32,256]{3,2,1,0:T(8,128)S(1)}, f32[3,8,32,256]{3,2,1,0:T(8,128)S(1)}, u32[]{:S(2)}, u32[]{:S(2)}) collective-permute-start(f32[3,8,32,256]{3,2,1,0:T(8,128)S(1)} %get-tuple-element.80), channel_id=1, source_target_pairs={{0,7},{1,2},{2,1},{3,4},{4,3},{5,6},{6,5},{7,0},{8,15},{9,10},{10,... | collective-permute-start | bytes 2359304 | tf_op jit(solution)/shard_map/ppermute | solution.py:34
  89.0 4.9 %collective-permute-done.20 = f32[32,128]{1,0:T(8,128)S(1)} collective-permute-done((f32[32,128]{1,0:T(8,128)S(1)}, f32[32,128]{1,0:T(8,128)S(1)}, u32[]{:S(2)}, u32[]{:S(2)}) %collective-permute-start.20) | collective-permute-done | bytes 16416 | tf_op jit(solution)/shard_map/ppermute | solution.py:345
  94.6 2.8 %collective-permute-start.21 = (f32[32,128]{1,0:T(8,128)S(1)}, f32[32,128]{1,0:T(8,128)S(1)}, u32[]{:S(2)}, u32[]{:S(2)}) collective-permute-start(f32[32,128]{1,0:T(8,128)S(1)} %add.12), channel_id=1, source_target_pairs={{0,32},{1,33},{2,34},{3,35},{4,36},{5,37},{6,38},{7,39},{8,40},{9,... | collective-permute-start | bytes 49160 | tf_op jit(solution)/shard_map/ppermute | solution.py:345
  100.1 2.4 %collective-permute-start.28 = (f32[8,32,256]{2,1,0:T(8,128)S(1)}, f32[8,32,256]{2,1,0:T(8,128)S(1)}, u32[]{:S(2)}, u32[]{:S(2)}) collective-permute-start(f32[8,32,256]{2,1,0:T(8,128)S(1)} %get-tuple-element.83), channel_id=1, source_target_pairs={{0,120},{8,16},{16,8},{24,32},{32,24},{40,48},{48,40},{56,64},{64,... | collective-permute-start | bytes 786440 | tf_op jit(solution)/shard_map/ppermute | solution.py:34
  103.7 5.1 %solve_body.1 = (f32[32,32]{1,0:T(8,128)S(1)}, f32[32,32]{1,0:T(8,128)S(1)}) custom-call(f32[32,128]{1,0:T(8,128)S(1)} %add_add_fusion.grams, f32[32,128]{1,0:T(8,128)S(1)} %collective-permute-done.24.moved), custom_call_target="tpu_custom_call" | custom-call | tf_op jit(solution)/shard_map/solve_body/pallas_call | solution.py:79
  108.8 2.1 %collective-permute-done.28.rb = f32[8,32,256]{2,1,0:T(8,128)S(1)} collective-permute-done((f32[8,32,256]{2,1,0:T(8,128)S(1)}, f32[8,32,256]{2,1,0:T(8,128)S(1)}, u32[]{:S(2)}, u32[]{:S(2)}) %collective-permute-start.28) | collective-permute-done | bytes 262176 | tf_op jit(solution)/shard_map/ppermute | solution.py:34
  110.9 1.8 %finish_body.1 = (f32[32,2048]{1,0:T(8,128)}, f32[32,2048]{1,0:T(8,128)}) custom-call(f32[32,32]{1,0:T(8,128)S(1)} %get-tuple-element.73.p, f32[32,32]{1,0:T(8,128)S(1)} %get-tuple-element.74.q, f32[32,2048]{1,0:T(8,128)S(1)} %copy-done.1, f32[8,32,256]{2,1,0:T(8,128)S(1)} %sum_body.1.vector.refs_2_.u, f32[8,32,256]{2,1,0:T(8,128)S(1)} %get-tuple-element.81.rest, ...), custom_call_target="tpu_custom_call" | custom-call | tf_op jit(solution)/shard_map/finish_body/pallas_call | solution.py:79
  (64 shorter events, 26.6 us)
Async XLA Ops:
  0.6 15.5 %collective-permute-start.2 = (f32[32,2048]{1,0:T(8,128)}, f32[32,2048]{1,0:T(8,128)S(1)}, u32[]{:S(2)}, u32[]{:S(2)}) collective-permute-start(f32[32,2048]{1,0:T(8,128)} %right.1), channel_id=1, source_target_pairs={{0,120},{8,16},{16,8},{24,32},{32,24},{40,48},{48,40},{56,64},{64,... | collective-permute-start | bytes 786440 | tf_op jit(solution)/shard_map/ppermute | solution.py:34
  6.0 10.2 %collective-permute-start.1 = (f32[32,2048]{1,0:T(8,128)}, f32[32,2048]{1,0:T(8,128)S(1)}, u32[]{:S(2)}, u32[]{:S(2)}) collective-permute-start(f32[32,2048]{1,0:T(8,128)} %right.1), channel_id=1, source_target_pairs={{0,8},{8,0},{16,24},{24,16},{32,40},{40,32},{48,56},{56,48},{64,72... | collective-permute-start | bytes 786440 | tf_op jit(solution)/shard_map/ppermute | solution.py:34
  6.0 10.2 %collective-permute-start = (f32[32,2048]{1,0:T(8,128)}, f32[32,2048]{1,0:T(8,128)S(1)}, u32[]{:S(2)}, u32[]{:S(2)}) collective-permute-start(f32[32,2048]{1,0:T(8,128)} %right.1), channel_id=1, source_target_pairs={{0,7},{1,2},{2,1},{3,4},{4,3},{5,6},{6,5},{7,0},{8,15},{9,10},{10,... | collective-permute-start | bytes 786440 | tf_op jit(solution)/shard_map/ppermute | solution.py:34
  16.4 9.9 %collective-permute-start.4 = (f32[2,8,32,256]{3,2,1,0:T(8,128)S(1)}, f32[2,8,32,256]{3,2,1,0:T(8,128)S(1)}, u32[]{:S(2)}, u32[]{:S(2)}) collective-permute-start(f32[2,8,32,256]{3,2,1,0:T(8,128)S(1)} %get-tuple-element.49), channel_id=1, source_target_pairs={{0,7},{1,2},{2,1},{3,4},{4,3},{5,6},{6,5},{7,0},{8,15},{9,10},{10,... | collective-permute-start | bytes 1572872 | tf_op jit(solution)/shard_map/ppermute | solution.py:34
  28.0 9.9 %collective-permute-start.9 = (f32[2,8,32,256]{3,2,1,0:T(8,128)S(1)}, f32[2,8,32,256]{3,2,1,0:T(8,128)S(1)}, u32[]{:S(2)}, u32[]{:S(2)}) collective-permute-start(f32[2,8,32,256]{3,2,1,0:T(8,128)S(1)} %get-tuple-element.60), channel_id=1, source_target_pairs={{0,7},{1,2},{2,1},{3,4},{4,3},{5,6},{6,5},{7,0},{8,15},{9,10},{10,... | collective-permute-start | bytes 1572872 | tf_op jit(solution)/shard_map/ppermute | solution.py:34
  35.0 7.4 %collective-permute-start.5 = (f32[8,32,256]{2,1,0:T(8,128)S(1)}, f32[8,32,256]{2,1,0:T(8,128)S(1)}, u32[]{:S(2)}, u32[]{:S(2)}) collective-permute-start(f32[8,32,256]{2,1,0:T(8,128)S(1)} %get-tuple-element.54), channel_id=1, source_target_pairs={{0,1},{1,0},{2,3},{3,2},{4,5},{5,4},{6,7},{7,6},{8,9},{9,8},{10,11... | collective-permute-start | bytes 786440 | tf_op jit(solution)/shard_map/ppermute | solution.py:34
  35.1 7.4 %collective-permute-start.6 = (f32[8,32,256]{2,1,0:T(8,128)S(1)}, f32[8,32,256]{2,1,0:T(8,128)S(1)}, u32[]{:S(2)}, u32[]{:S(2)}) collective-permute-start(f32[8,32,256]{2,1,0:T(8,128)S(1)} %get-tuple-element.55), channel_id=1, source_target_pairs={{0,7},{1,2},{2,1},{3,4},{4,3},{5,6},{6,5},{7,0},{8,15},{9,10},{10,... | collective-permute-start | bytes 786440 | tf_op jit(solution)/shard_map/ppermute | solution.py:34
  38.0 6.8 %collective-permute-start.10 = (f32[8,32,256]{2,1,0:T(8,128)S(1)}, f32[8,32,256]{2,1,0:T(8,128)S(1)}, u32[]{:S(2)}, u32[]{:S(2)}) collective-permute-start(f32[8,32,256]{2,1,0:T(8,128)S(1)} %get-tuple-element.61), channel_id=1, source_target_pairs={{0,8},{8,0},{16,24},{24,16},{32,40},{40,32},{48,56},{56,48},{64,72... | collective-permute-start | bytes 786440 | tf_op jit(solution)/shard_map/ppermute | solution.py:34
  39.8 10.3 %collective-permute-start.11 = (f32[8,32,256]{2,1,0:T(8,128)S(1)}, f32[8,32,256]{2,1,0:T(8,128)S(1)}, u32[]{:S(2)}, u32[]{:S(2)}) collective-permute-start(f32[8,32,256]{2,1,0:T(8,128)S(1)} %get-tuple-element.62), channel_id=1, source_target_pairs={{0,120},{8,16},{16,8},{24,32},{32,24},{40,48},{48,40},{56,64},{64,... | collective-permute-start | bytes 786440 | tf_op jit(solution)/shard_map/ppermute | solution.py:34
  50.2 11.5 %collective-permute-start.14 = (f32[8,32,256]{2,1,0:T(8,128)S(1)}, f32[8,32,256]{2,1,0:T(8,128)S(1)}, u32[]{:S(2)}, u32[]{:S(2)}) collective-permute-start(f32[8,32,256]{2,1,0:T(8,128)S(1)} %sum_body.1.vector.refs_2_.u), channel_id=1, source_target_pairs={{0,120},{8,16},{16,8},{24,32},{32,24},{40,48},{48,40},{56,64},{64,... | collective-permute-start | bytes 786440 | tf_op jit(solution)/shard_map/ppermute | solution.py:34
  51.7 10.0 %collective-permute-start.13 = (f32[8,32,256]{2,1,0:T(8,128)S(1)}, f32[8,32,256]{2,1,0:T(8,128)S(1)}, u32[]{:S(2)}, u32[]{:S(2)}) collective-permute-start(f32[8,32,256]{2,1,0:T(8,128)S(1)} %sum_body.1.vector.refs_2_.u), channel_id=1, source_target_pairs={{0,8},{8,0},{16,24},{24,16},{32,40},{40,32},{48,56},{56,48},{64,72... | collective-permute-start | bytes 786440 | tf_op jit(solution)/shard_map/ppermute | solution.py:34
  51.7 10.0 %collective-permute-start.12 = (f32[8,32,256]{2,1,0:T(8,128)S(1)}, f32[8,32,256]{2,1,0:T(8,128)S(1)}, u32[]{:S(2)}, u32[]{:S(2)}) collective-permute-start(f32[8,32,256]{2,1,0:T(8,128)S(1)} %sum_body.1.vector.refs_2_.u), channel_id=1, source_target_pairs={{0,7},{1,2},{2,1},{3,4},{4,3},{5,6},{6,5},{7,0},{8,15},{9,10},{10,... | collective-permute-start | bytes 786440 | tf_op jit(solution)/shard_map/ppermute | solution.py:34
  62.8 9.8 %collective-permute-start.16 = (f32[2,8,32,256]{3,2,1,0:T(8,128)S(1)}, f32[2,8,32,256]{3,2,1,0:T(8,128)S(1)}, u32[]{:S(2)}, u32[]{:S(2)}) collective-permute-start(f32[2,8,32,256]{3,2,1,0:T(8,128)S(1)} %get-tuple-element.67), channel_id=1, source_target_pairs={{0,7},{1,2},{2,1},{3,4},{4,3},{5,6},{6,5},{7,0},{8,15},{9,10},{10,... | collective-permute-start | bytes 1572872 | tf_op jit(solution)/shard_map/ppermute | solution.py:34
  73.6 3.8 %collective-permute-start.17 = (f32[32,128]{1,0:T(8,128)S(1)}, f32[32,128]{1,0:T(8,128)S(1)}, u32[]{:S(2)}, u32[]{:S(2)}) collective-permute-start(f32[32,128]{1,0:T(8,128)S(1)} %get-tuple-element.71.grams), channel_id=1, source_target_pairs={{0,2},{1,3},{2,0},{3,1},{4,6},{5,7},{6,4},{7,5},{8,10},{9,11},{10,... | collective-permute-start | bytes 49160 | tf_op jit(solution)/shard_map/ppermute | solution.py:345
  77.4 5.0 %collective-permute-start.18 = (f32[32,128]{1,0:T(8,128)S(1)}, f32[32,128]{1,0:T(8,128)S(1)}, u32[]{:S(2)}, u32[]{:S(2)}) collective-permute-start(f32[32,128]{1,0:T(8,128)S(1)} %add_body.2.grams), channel_id=1, source_target_pairs={{0,6},{1,7},{2,4},{3,5},{4,2},{5,3},{6,0},{7,1},{8,14},{9,15},{10,... | collective-permute-start | bytes 49160 | tf_op jit(solution)/shard_map/ppermute | solution.py:345
  82.4 3.8 %collective-permute-start.19 = (f32[32,128]{1,0:T(8,128)S(1)}, f32[32,128]{1,0:T(8,128)S(1)}, u32[]{:S(2)}, u32[]{:S(2)}) collective-permute-start(f32[32,128]{1,0:T(8,128)S(1)} %add_body.3.grams), channel_id=1, source_target_pairs={{0,8},{1,9},{2,10},{3,11},{4,12},{5,13},{6,14},{7,15},{8,0},{9,1},... | collective-permute-start | bytes 49160 | tf_op jit(solution)/shard_map/ppermute | solution.py:345
  86.4 12.8 %collective-permute-start.25 = (f32[3,8,32,256]{3,2,1,0:T(8,128)S(1)}, f32[3,8,32,256]{3,2,1,0:T(8,128)S(1)}, u32[]{:S(2)}, u32[]{:S(2)}) collective-permute-start(f32[3,8,32,256]{3,2,1,0:T(8,128)S(1)} %get-tuple-element.79), channel_id=1, source_target_pairs={{0,1},{1,0},{2,3},{3,2},{4,5},{5,4},{6,7},{7,6},{8,9},{9,8},{10,11... | collective-permute-start | bytes 2359304 | tf_op jit(solution)/shard_map/ppermute | solution.py:34
  86.5 12.7 %collective-permute-start.26 = (f32[3,8,32,256]{3,2,1,0:T(8,128)S(1)}, f32[3,8,32,256]{3,2,1,0:T(8,128)S(1)}, u32[]{:S(2)}, u32[]{:S(2)}) collective-permute-start(f32[3,8,32,256]{3,2,1,0:T(8,128)S(1)} %get-tuple-element.80), channel_id=1, source_target_pairs={{0,7},{1,2},{2,1},{3,4},{4,3},{5,6},{6,5},{7,0},{8,15},{9,10},{10,... | collective-permute-start | bytes 2359304 | tf_op jit(solution)/shard_map/ppermute | solution.py:34
  89.0 4.9 %collective-permute-start.20 = (f32[32,128]{1,0:T(8,128)S(1)}, f32[32,128]{1,0:T(8,128)S(1)}, u32[]{:S(2)}, u32[]{:S(2)}) collective-permute-start(f32[32,128]{1,0:T(8,128)S(1)} %get-tuple-element.72), channel_id=1, source_target_pairs={{0,24},{1,25},{2,26},{3,27},{4,28},{5,29},{6,30},{7,31},{8,16},{9,... | collective-permute-start | bytes 49160 | tf_op jit(solution)/shard_map/ppermute | solution.py:345
  93.9 5.2 %collective-permute-start.23 = (f32[32,128]{1,0:T(8,128)S(1)}, f32[32,128]{1,0:T(8,128)S(1)}, u32[]{:S(2)}, u32[]{:S(2)}) collective-permute-start(f32[32,128]{1,0:T(8,128)S(1)} %add.12), channel_id=1, source_target_pairs={{0,64},{1,65},{2,66},{3,67},{4,68},{5,69},{6,70},{7,71},{8,72},{9,... | collective-permute-start | bytes 49160 | tf_op jit(solution)/shard_map/ppermute | solution.py:345
  93.9 5.2 %collective-permute-start.22 = (f32[32,128]{1,0:T(8,128)S(1)}, f32[32,128]{1,0:T(8,128)S(1)}, u32[]{:S(2)}, u32[]{:S(2)}) collective-permute-start(f32[32,128]{1,0:T(8,128)S(1)} %add.12), channel_id=1, source_target_pairs={{0,96},{1,97},{2,98},{3,99},{4,100},{5,101},{6,102},{7,103},{8,104... | collective-permute-start | bytes 49160 | tf_op jit(solution)/shard_map/ppermute | solution.py:345
  94.6 4.6 %collective-permute-start.21 = (f32[32,128]{1,0:T(8,128)S(1)}, f32[32,128]{1,0:T(8,128)S(1)}, u32[]{:S(2)}, u32[]{:S(2)}) collective-permute-start(f32[32,128]{1,0:T(8,128)S(1)} %add.12), channel_id=1, source_target_pairs={{0,32},{1,33},{2,34},{3,35},{4,36},{5,37},{6,38},{7,39},{8,40},{9,... | collective-permute-start | bytes 49160 | tf_op jit(solution)/shard_map/ppermute | solution.py:345
  99.4 9.5 %collective-permute-start.27 = (f32[8,32,256]{2,1,0:T(8,128)S(1)}, f32[8,32,256]{2,1,0:T(8,128)S(1)}, u32[]{:S(2)}, u32[]{:S(2)}) collective-permute-start(f32[8,32,256]{2,1,0:T(8,128)S(1)} %get-tuple-element.82), channel_id=1, source_target_pairs={{0,8},{8,0},{16,24},{24,16},{32,40},{40,32},{48,56},{56,48},{64,72... | collective-permute-start | bytes 786440 | tf_op jit(solution)/shard_map/ppermute | solution.py:34
  100.1 10.8 %collective-permute-start.28 = (f32[8,32,256]{2,1,0:T(8,128)S(1)}, f32[8,32,256]{2,1,0:T(8,128)S(1)}, u32[]{:S(2)}, u32[]{:S(2)}) collective-permute-start(f32[8,32,256]{2,1,0:T(8,128)S(1)} %get-tuple-element.83), channel_id=1, source_target_pairs={{0,120},{8,16},{16,8},{24,32},{32,24},{40,48},{48,40},{56,64},{64,... | collective-permute-start | bytes 786440 | tf_op jit(solution)/shard_map/ppermute | solution.py:34
  (8 other events, 37.1 us)

commit v6 on v5

--- a/solution.py
+++ b/solution.py
@@ -15,6 +15,7 @@
 CHUNK = 8
 HALF = 4
 PREPARED = 8
+SLOTS = 3
 NEAR_TABLES = 7
 
 
@@ -65,17 +66,17 @@
     return both[:half, :half] + both[:half, half:] + both[half:, :half] + both[half:, half:]
 
 
-def times(dot, stacked, high, low):
+def times(stacked, high, low):
     half = stacked.shape[0] // 2
-    first = dot(stacked, high)
-    return first[:half] + first[half:] + dot(stacked[:half], low)
+    first = dot_nn(stacked, high)
+    return first[:half] + first[half:] + dot_nn(stacked[:half], low)
 
 
 def stacked_split(value):
     return jnp.concatenate(split(value), axis=0)
 
 
-def call(body, out_shape, n_smem, args, scratch=(), aliases=None, limit=8 << 20):
+def call(body, out_shape, n_smem, args, scratch=(), aliases=None, limit=4 << 20):
     return pl.pallas_call(
         body,
         out_shape=out_shape,
@@ -117,34 +118,41 @@
     routes[3:4, :] = jnp.broadcast_to(near >> (HALF.bit_length() - 1), (1, count))
 
 
-def prepare_body(blocks, pair, couplings, c_high, c_low, routes, buffer, arrived):
-    count = couplings.shape[0]
-    copies = []
-    for i in range(count // PREPARED):
-        part = pl.ds(i * PREPARED, PREPARED)
-        copies.append(pltpu.make_async_copy(couplings.at[part], buffer.at[part], arrived.at[i]))
-    for copy in copies:
+def prepare_body(blocks, pair, couplings, c_high, c_low, t_high, t_low, routes, buffer, arrived):
+    groups = couplings.shape[0] // PREPARED
+    copies = [
+        pltpu.make_async_copy(
+            couplings.at[pl.ds(i * PREPARED, PREPARED)], buffer.at[i % SLOTS], arrived.at[i])
+        for i in range(groups)
+    ]
+    for copy in copies[:SLOTS]:
         copy.start()
     route(pair, routes, blocks)
     for i, copy in enumerate(copies):
         copy.wait()
-        for k in range(i * PREPARED, (i + 1) * PREPARED):
-            c_high[k], c_low[k] = split(buffer[k])
+        for place in range(PREPARED):
+            k = i * PREPARED + place
+            high, low = split(buffer[i % SLOTS, place])
+            c_high[k], c_low[k] = high, low
+            t_high[k], t_low[k] = high.T, low.T
+        if i + SLOTS < groups:
+            copies[i + SLOTS].start()
 
 
 def prepare(pair_index, couplings, blocks):
+    count, width = couplings.shape[:2]
     shape = pltpu.VMEM(couplings.shape, BF16)
     return pl.pallas_call(
         functools.partial(prepare_body, blocks),
         in_specs=[VMEM_SPEC, pl.BlockSpec(memory_space=pltpu.HBM)],
-        out_specs=[VMEM_SPEC] * 3,
-        out_shape=[shape, shape, pltpu.VMEM((4, pair_index.shape[1]), jnp.int32)],
+        out_specs=[VMEM_SPEC] * 5,
+        out_shape=[shape] * 4 + [pltpu.VMEM((4, count), jnp.int32)],
         scratch_shapes=[
-            pltpu.VMEM(couplings.shape, F32),
-            pltpu.SemaphoreType.DMA((couplings.shape[0] // PREPARED,)),
+            pltpu.VMEM((SLOTS, PREPARED, width, width), F32),
+            pltpu.SemaphoreType.DMA((count // PREPARED,)),
         ],
         name="prepare",
-        compiler_params=pltpu.CompilerParams(vmem_limit_bytes=18 << 20),
+        compiler_params=pltpu.CompilerParams(vmem_limit_bytes=7 << 20),
     )(in_vmem(pair_index), in_hbm(couplings))
 
 
@@ -163,13 +171,13 @@
                 pair[slot - 1, q] = block
 
 
-def accumulate(dot, first, last, routes, source_row, target_row, source, target, c_high, c_low):
+def accumulate(first, last, routes, source_row, target_row, source, target, c_high, c_low):
     def step(size, start):
         terms = []
         for place in range(size):
             i = start + place
             k = routes[0, i]
-            terms.append((routes[target_row, i], times(dot, source[routes[source_row, i]], c_high[k], c_low[k])))
+            terms.append((routes[target_row, i], times(source[routes[source_row, i]], c_high[k], c_low[k])))
         for row, term in terms:
             target[row] += term
 
@@ -194,7 +202,7 @@
             block = block_of(source, q, strain.shape[2]) if slot is None else source[slot, q]
             table[place * blocks + q] = stacked_split(block)
     strain[...] = jnp.zeros_like(strain)
-    accumulate(dot_nt, 0, routes[3, 0], routes, 1, 2, table, strain, c_high, c_low)
+    accumulate(0, routes[3, 0], routes, 1, 2, table, strain, c_high, c_low)
 
 
 def pull_late_body(routes, table_in, strain_in, db, *refs):
@@ -204,7 +212,7 @@
         for q in range(blocks):
             table[(NEAR_TABLES + slot) * blocks + q] = stacked_split(db[slot, q])
     strain[...] = strain_in[...]
-    accumulate(dot_nt, routes[3, 0], routes.shape[1] // HALF, routes, 1, 2, table, strain, c_high, c_low)
+    accumulate(routes[3, 0], routes.shape[1] // HALF, routes, 1, 2, table, strain, c_high, c_low)
     total = jnp.zeros((strain.shape[1],) * 2, F32)
     for q in range(blocks):
         both = stacked_split(strain[q])
@@ -222,7 +230,7 @@
 def push_late_body(routes, strain_hl, c_high, c_low, pieces, *targets):
     blocks = strain_hl.shape[0]
     pieces[...] = jnp.zeros_like(pieces)
-    accumulate(dot_nn, routes[3, 0], routes.shape[1] // HALF, routes, 2, 1, strain_hl, pieces, c_high, c_low)
+    accumulate(routes[3, 0], routes.shape[1] // HALF, routes, 2, 1, strain_hl, pieces, c_high, c_low)
     for db in targets:
         for slot in range(2):
             for q in range(blocks):
@@ -232,22 +240,21 @@
 def push_near_body(routes, strain_hl, c_high, c_low, pieces_in, *refs):
     *outs, pieces = refs
     pieces[...] = pieces_in[:pieces.shape[0]]
-    accumulate(dot_nn, 0, routes[3, 0], routes, 2, 1, strain_hl, pieces, c_high, c_low)
+    accumulate(0, routes[3, 0], routes, 2, 1, strain_hl, pieces, c_high, c_low)
     for place, target in enumerate(outs):
         for q in range(target.shape[0]):
             target[q] = pieces[place * target.shape[0] + q]
 
 
 def push_begin_body(routes, strain_hl, c_high, c_low, pieces_in, pieces):
-    accumulate(dot_nn, 0, routes[3, 0] // 2, routes, 2, 1, strain_hl, pieces, c_high, c_low)
+    accumulate(0, routes[3, 0] // 2, routes, 2, 1, strain_hl, pieces, c_high, c_low)
 
 
 def push_end_body(routes, strain_hl, c_high, c_low, pieces_in, pieces):
-    accumulate(dot_nn, routes[3, 0] // 2, routes[3, 0], routes, 2, 1, strain_hl, pieces, c_high, c_low)
-
-
-def pack_body(pieces, grams, moved, own, ra, rb, qa, qb, total):
-    total[...] = grams[...] + moved[...]
+    accumulate(routes[3, 0] // 2, routes[3, 0], routes, 2, 1, strain_hl, pieces, c_high, c_low)
+
+
+def pack_body(pieces, grams, own, ra, rb, qa, qb):
     blocks = own.shape[0]
     outs = (own, ra, rb, qa.at[0], qa.at[1], qa.at[2], qb.at[0], qb.at[1], qb.at[2])
     for target, place in zip(outs, (0, 1, 2, 3, 5, 6, 4, 7, 8)):
@@ -266,7 +273,7 @@
     width = diag.shape[1]
     for q in range(diag.shape[0]):
         both = stacked_split(block_of(vector, q, width))
-        term = times(dot_nn, both, *split(diag[q]))
+        term = times(both, *split(diag[q]))
         own[q] = term
         first += gram(both, both)
         second += gram(stacked_split(term), both)
@@ -327,13 +334,19 @@
     q[...] = full_nn(alpha, second)
 
 
-def finish_body(p, q, right, u, rest, ra, rb, x_out, r_out):
+def finish_body(p, q, right, u, rest, x_out, r_part):
     width = u.shape[2]
     for block in range(u.shape[0]):
         lanes = slice(block * width, (block + 1) * width)
-        w = rest[block] + ra[block] + rb[block]
         x_out[:, lanes] = full_tn(p[...], right[:, lanes]) - full_tn(q[...], u[block])
-        r_out[:, lanes] = right[:, lanes] - full_tn(p[...], u[block]) + full_tn(q[...], w)
+        r_part[block] = right[:, lanes] - full_tn(p[...], u[block]) + full_tn(q[...], rest[block])
+
+
+def finish_last_body(q, r_part, ra, rb, r_out):
+    width = ra.shape[2]
+    for block in range(ra.shape[0]):
+        lanes = slice(block * width, (block + 1) * width)
+        r_out[:, lanes] = r_part[block] + full_tn(q[...], ra[block] + rb[block])
 
 
 MASKS = (2, 6, 8, 24, 1)
@@ -365,16 +378,17 @@
         whole, pair = call(stack_body, [stack_shape, pair_shape], 0, (*after, cb, vector, ra, rb))
         return (swapped(whole, "col", 0), whole, cb), swapped(pair, "col", 1)
 
-    def pulled(near_tables, db, couplings, *grams):
-        table, strain = call(pull_near_body, [table_shape, block_shape], 1, (routes, *near_tables, *couplings))
+    def pulled(near_tables, db, *grams):
+        table, strain = call(pull_near_body, [table_shape, block_shape], 1, (routes, *near_tables, *transposes))
         _, strain_hl, g = call(
             pull_late_body, [table_shape, split_shape, all_grams_shape if grams else gram_shape], 1,
-            (routes, table, strain, db, *couplings, *grams), [block_shape], aliases={1: 0})
+            (routes, table, strain, db, *transposes, *grams), [block_shape], aliases={1: 0})
         return strain_hl, g
 
-    *couplings, routes = prepare(pair_index, couplings, blocks)
+    *halves, routes = prepare(pair_index, couplings, blocks)
+    couplings, transposes = halves[:2], halves[2:]
     near_tables, db = spread(right_sides, routes)
-    strain_hl, g1s = pulled(near_tables, db, couplings)
+    strain_hl, g1s = pulled(near_tables, db)
 
     pieces, db = call(push_late_body, [pieces_shape, pair_shape], 1, (routes, strain_hl, *couplings))
     db = swapped(db, "col", 1)
@@ -390,15 +404,14 @@
 
     diag, g23 = call(diag_body, [block_shape, grams_shape], 0, (u, diag_blocks))
     near_tables, db = spread(u, g23)
-    strain_hl, grams = pulled(near_tables, db, couplings, g01, g1s, g23)
+    strain_hl, grams = pulled(near_tables, db, g01, g1s, g23)
     pieces, = call(push_late_body, [pieces_shape], 1, (routes, strain_hl, *couplings))
     grams = call(add_body, all_grams_shape, 0, (grams, exchanged(grams, MASKS[0]), pieces))
     pieces, = call(push_begin_body, [pieces_shape], 1, (routes, strain_hl, *couplings, pieces), aliases={4: 0})
     grams = call(add_body, all_grams_shape, 0, (grams, exchanged(grams, MASKS[1]), pieces))
     pieces, = call(push_end_body, [pieces_shape], 1, (routes, strain_hl, *couplings, pieces), aliases={4: 0})
-    own, ra, rb, qa, qb, grams = call(
-        pack_body, [block_shape] * 3 + [stack_shape] * 2 + [all_grams_shape], 0,
-        (pieces, grams, exchanged(grams, MASKS[2])))
+    grams = call(add_body, all_grams_shape, 0, (grams, exchanged(grams, MASKS[2]), pieces))
+    own, ra, rb, qa, qb = call(pack_body, [block_shape] * 3 + [stack_shape] * 2, 0, (pieces, grams))
     qa, qb = swapped(qa, "col", 0), swapped(qb, "col", 1)
     grams = grams + exchanged(grams, MASKS[3])
     first, second, third = (exchanged(grams, mask) for mask in RING)
@@ -407,7 +420,8 @@
     ra, rb = swapped(ra, "row", 0), swapped(rb, "row", 1)
     p, q = call(solve_body, [gram_shape] * 2, 0, (grams, exchanged(grams, MASKS[-1])))
     flat = jax.ShapeDtypeStruct(right_sides.shape, F32)
-    return tuple(call(finish_body, [flat, flat], 0, (p, q, right_sides, u, rest, ra, rb)))
+    x_out, r_part = call(finish_body, [flat, block_shape], 0, (p, q, right_sides, u, rest))
+    return x_out, call(finish_last_body, flat, 0, (q, r_part, ra, rb))
 
 
 def solution(mesh):

time: 113 us -> 114 us (level)
  waiting for transfers between devices: 29.6 us -> 43.1 us
  starting transfers between devices: 38.1 us -> 27.5 us
  Pallas kernels: 43.4 us -> 41.2 us
    ppermute x21, waiting for transfers between devices: 19.9 us -> 28.6 us  [swapped(): return lax.ppermute(value, axis, pairs_of(lax.axis_size(axis), shift))]
    ppermute x21, starting transfers between devices: 29.4 us -> 23.7 us  [swapped(): return lax.ppermute(value, axis, pairs_of(lax.axis_size(axis), shift))]
    ppermute x8, starting transfers between devices: 8.64 us -> 3.71 us  [exchanged(): lax.ppermute(value, ('row', 'col'), [(i, i ^ mask) for i in range(count)])]
    ppermute x8, waiting for transfers between devices: 9.74 us -> 14.5 us  [exchanged(): lax.ppermute(value, ('row', 'col'), [(i, i ^ mask) for i in range(count)])]
    pallas_call x21 -> x23, Pallas kernels: 37.1 us -> 33.7 us  [call(): pl.pallas_call(body, out_shape=out_shape, in_specs=[SMEM_SPEC] * n_smem +...]
    pallas_call x1, Pallas kernels: 6.25 us -> 7.53 us  [prepare(): pl.pallas_call(functools.partial(prepare_body, blocks), in_specs=[VMEM_SP...]
  transfers between devices with their start and end apart: 29 -> 29, of which waited for: 15 -> 16; matrix products, arithmetic and copies ran while one was open for 0% -> 0% of each run, Pallas kernels for 34% -> 33%
where the time goes in v6:
time: 114 us; the launch traced here: 113 us
  waiting for transfers between devices  43.1 us (38%)
  Pallas kernels  41.2 us (36%)
  starting transfers between devices  27.5 us (24%)
    pallas_call x23, Pallas kernels, call(): pl.pallas_call(body, out_shape=out_shape, in_specs=[SMEM_SPEC] * n_smem +...  33.7 us
    ppermute x21, waiting for transfers between devices, swapped(): return lax.ppermute(value, axis, pairs_of(lax.axis_size(axis), shift))  28.6 us
    ppermute x21, starting transfers between devices, swapped(): return lax.ppermute(value, axis, pairs_of(lax.axis_size(axis), shift))  23.7 us
    ppermute x8, waiting for transfers between devices, exchanged(): lax.ppermute(value, ('row', 'col'), [(i, i ^ mask) for i in range(count)])  14.5 us
    pallas_call x1, Pallas kernels, prepare(): pl.pallas_call(functools.partial(prepare_body, blocks), in_specs=[VMEM_SP...  7.53 us
    ppermute x8, starting transfers between devices, exchanged(): lax.ppermute(value, ('row', 'col'), [(i, i ^ mask) for i in range(count)])  3.71 us
  transfers between devices with their start and end apart: 29, of which 16 were waited for; matrix products, arithmetic and copies ran while one was open for 0% of the time, Pallas kernels for 33%

profile of v6, /device:TPU:0, one launch (start us, length us, event | category | flops | bytes accessed | tf_op | source)
XLA Modules:
  0.0 113.3 jit_solution(3186175988907229292)
XLA Ops:
  0.6 5.4 %collective-permute-start.2 = (f32[32,2048]{1,0:T(8,128)}, f32[32,2048]{1,0:T(8,128)S(1)}, u32[]{:S(2)}, u32[]{:S(2)}) collective-permute-start(f32[32,2048]{1,0:T(8,128)} %right.1), channel_id=1, source_target_pairs={{0,120},{8,16},{16,8},{24,32},{32,24},{40,48},{48,40},{56,64},{64,... | collective-permute-start | bytes 786440 | tf_op jit(solution)/shard_map/ppermute | solution.py:35
  6.0 3.2 %collective-permute-start = (f32[32,2048]{1,0:T(8,128)}, f32[32,2048]{1,0:T(8,128)S(1)}, u32[]{:S(2)}, u32[]{:S(2)}) collective-permute-start(f32[32,2048]{1,0:T(8,128)} %right.1), channel_id=1, source_target_pairs={{0,7},{1,2},{2,1},{3,4},{4,3},{5,6},{6,5},{7,0},{8,15},{9,10},{10,... | collective-permute-start | bytes 786440 | tf_op jit(solution)/shard_map/ppermute | solution.py:35
  9.9 7.5 %prepare.1 = (bf16[64,256,256]{2,1,0:T(8,128)(2,1)S(1)}, bf16[64,256,256]{2,1,0:T(8,128)(2,1)S(1)}, bf16[64,256,256]{2,1,0:T(8,128)(2,1)S(1)}, bf16[64,256,256]{2,1,0:T(8,128)(2,1)S(1)}, s32[4,64]{1,0:T(4,128)S(1)}) custom-call(s32[2,64]{1,0:T(2,128)S(1)} %copy-done.2, f32[64,256,256]{2,1,0:T(8,128)} %couplings.1), custom_call_target="tpu_custom_call" | custom-call | tf_op jit(solution)/shard_map/prepare/pallas_call | solution.py:145
  19.9 4.5 %pull_near_body.2 = (bf16[72,64,256]{2,1,0:T(8,128)(2,1)S(1)}, f32[8,32,256]{2,1,0:T(8,128)S(1)}) custom-call(s32[4,64]{1,0:T(4,128)S(1)} %get-tuple-element.46.refs_0_.routes, f32[3,8,32,256]{3,2,1,0:T(8,128)S(1)} %collective-permute-done.3.qa, f32[3,8,32,256]{3,2,1,0:T(8,128)S(1)} %get-tuple-element.47.whole, ...), custom_call_target="tpu_custom_call" | custom-call | tf_op jit(solution)/shard_map/pull_near_body/pallas_call | solution.py:80
  24.4 3.2 %collective-permute-done.4.db = f32[2,8,32,256]{3,2,1,0:T(8,128)S(1)} collective-permute-done((f32[2,8,32,256]{3,2,1,0:T(8,128)S(1)}, f32[2,8,32,256]{3,2,1,0:T(8,128)S(1)}, u32[]{:S(2)}, u32[]{:S(2)}) %collective-permute-start.4) | collective-permute-done | bytes 524320 | tf_op jit(solution)/shard_map/ppermute | solution.py:35
  30.2 4.5 %push_near_body.1 = (f32[8,32,256]{2,1,0:T(8,128)S(1)}, f32[8,32,256]{2,1,0:T(8,128)S(1)}, f32[8,32,256]{2,1,0:T(8,128)S(1)}, f32[8,32,256]{2,1,0:T(8,128)S(1)},...) custom-call(s32[4,64]{1,0:T(4,128)S(1)} %get-tuple-element.46.refs_0_.routes, ...), custom_call_target="tpu_custom_call" | custom-call | tf_op jit(solution)/shard_map/push_near_body/pallas_call | solution.py:80
  35.4 2.1 %collective-permute-start.6 = (f32[8,32,256]{2,1,0:T(8,128)S(1)}, f32[8,32,256]{2,1,0:T(8,128)S(1)}, u32[]{:S(2)}, u32[]{:S(2)}) collective-permute-start(f32[8,32,256]{2,1,0:T(8,128)S(1)} %get-tuple-element.60), channel_id=1, source_target_pairs={{0,7},{1,2},{2,1},{3,4},{4,3},{5,6},{6,5},{7,0},{8,15},{9,10},{10,... | collective-permute-start | bytes 786440 | tf_op jit(solution)/shard_map/ppermute | solution.py:35
  39.3 1.8 %collective-permute-start.10 = (f32[8,32,256]{2,1,0:T(8,128)S(1)}, f32[8,32,256]{2,1,0:T(8,128)S(1)}, u32[]{:S(2)}, u32[]{:S(2)}) collective-permute-start(f32[8,32,256]{2,1,0:T(8,128)S(1)} %get-tuple-element.66), channel_id=1, source_target_pairs={{0,8},{8,0},{16,24},{24,16},{32,40},{40,32},{48,56},{56,48},{64,72... | collective-permute-start | bytes 786440 | tf_op jit(solution)/shard_map/ppermute | solution.py:35
  41.5 1.7 %diag_body.2 = (f32[8,32,256]{2,1,0:T(8,128)S(1)}, f32[2,32,32]{2,1,0:T(8,128)S(1)}) custom-call(f32[32,2048]{1,0:T(8,128)S(1)} %copy-done.1, f32[8,256,256]{2,1,0:T(8,128)S(1)} %copy-done), custom_call_target="tpu_custom_call" | custom-call | tf_op jit(solution)/shard_map/diag_body/pallas_call | solution.py:80
  43.2 3.0 %collective-permute-done.10.ra = f32[8,32,256]{2,1,0:T(8,128)S(1)} collective-permute-done((f32[8,32,256]{2,1,0:T(8,128)S(1)}, f32[8,32,256]{2,1,0:T(8,128)S(1)}, u32[]{:S(2)}, u32[]{:S(2)}) %collective-permute-start.10) | collective-permute-done | bytes 262176 | tf_op jit(solution)/shard_map/ppermute | solution.py:35
  46.2 5.3 %collective-permute-done.11.rb = f32[8,32,256]{2,1,0:T(8,128)S(1)} collective-permute-done((f32[8,32,256]{2,1,0:T(8,128)S(1)}, f32[8,32,256]{2,1,0:T(8,128)S(1)}, u32[]{:S(2)}, u32[]{:S(2)}) %collective-permute-start.11) | collective-permute-done | bytes 262176 | tf_op jit(solution)/shard_map/ppermute | solution.py:35
  52.2 2.3 %collective-permute-start.12 = (f32[8,32,256]{2,1,0:T(8,128)S(1)}, f32[8,32,256]{2,1,0:T(8,128)S(1)}, u32[]{:S(2)}, u32[]{:S(2)}) collective-permute-start(f32[8,32,256]{2,1,0:T(8,128)S(1)} %sum_body.1.vector.refs_2_.u), channel_id=1, source_target_pairs={{0,7},{1,2},{2,1},{3,4},{4,3},{5,6},{6,5},{7,0},{8,15},{9,10},{10,... | collective-permute-start | bytes 786440 | tf_op jit(solution)/shard_map/ppermute | solution.py:35
  56.3 7.2 %collective-permute-done.14.refs_4_ = f32[8,32,256]{2,1,0:T(8,128)S(1)} collective-permute-done((f32[8,32,256]{2,1,0:T(8,128)S(1)}, f32[8,32,256]{2,1,0:T(8,128)S(1)}, u32[]{:S(2)}, u32[]{:S(2)}) %collective-permute-start.14) | collective-permute-done | bytes 262176 | tf_op jit(solution)/shard_map/ppermute | solution.py:35
  66.2 4.4 %pull_near_body.3 = (bf16[72,64,256]{2,1,0:T(8,128)(2,1)S(1)}, f32[8,32,256]{2,1,0:T(8,128)S(1)}) custom-call(s32[4,64]{1,0:T(4,128)S(1)} %get-tuple-element.46.refs_0_.routes, f32[3,8,32,256]{3,2,1,0:T(8,128)S(1)} %collective-permute-done.15.qa, f32[3,8,32,256]{3,2,1,0:T(8,128)S(1)} %get-tuple-element.69.whole, ...), custom_call_target="tpu_custom_call" | custom-call | tf_op jit(solution)/shard_map/pull_near_body/pallas_call | solution.py:80
  70.6 3.4 %collective-permute-done.16.db = f32[2,8,32,256]{3,2,1,0:T(8,128)S(1)} collective-permute-done((f32[2,8,32,256]{3,2,1,0:T(8,128)S(1)}, f32[2,8,32,256]{3,2,1,0:T(8,128)S(1)}, u32[]{:S(2)}, u32[]{:S(2)}) %collective-permute-start.16) | collective-permute-done | bytes 524320 | tf_op jit(solution)/shard_map/ppermute | solution.py:35
  75.8 3.0 %collective-permute-done.17.moved = f32[32,128]{1,0:T(8,128)S(1)} collective-permute-done((f32[32,128]{1,0:T(8,128)S(1)}, f32[32,128]{1,0:T(8,128)S(1)}, u32[]{:S(2)}, u32[]{:S(2)}) %collective-permute-start.17) | collective-permute-done | bytes 16416 | tf_op jit(solution)/shard_map/ppermute | solution.py:358
  79.0 2.4 %push_begin_body.1.after.pieces_in = f32[72,32,256]{2,1,0:T(8,128)S(1)} custom-call(s32[4,64]{1,0:T(4,128)S(1)} %get-tuple-element.46.refs_0_.routes, bf16[8,64,256]{2,1,0:T(8,128)(2,1)S(1)} %get-tuple-element.76.strain_hl, bf16[64,256,256]{2,1,0:T(8,128)(2,1)S(1)} %get-tuple-element.54.c_high, ...), custom_call_target="tpu_custom_call", output_to_operand_aliasing={{}: (4, {})} | custom-call | tf_op jit(solution)/shard_map/push_begin_body/pallas_call | solution.py:80
  81.5 2.3 %collective-permute-done.18.moved = f32[32,128]{1,0:T(8,128)S(1)} collective-permute-done((f32[32,128]{1,0:T(8,128)S(1)}, f32[32,128]{1,0:T(8,128)S(1)}, u32[]{:S(2)}, u32[]{:S(2)}) %collective-permute-start.18) | collective-permute-done | bytes 16416 | tf_op jit(solution)/shard_map/ppermute | solution.py:358
  83.8 2.4 %push_end_body.1.after.pieces = f32[72,32,256]{2,1,0:T(8,128)S(1)} custom-call(s32[4,64]{1,0:T(4,128)S(1)} %get-tuple-element.46.refs_0_.routes, bf16[8,64,256]{2,1,0:T(8,128)(2,1)S(1)} %get-tuple-element.76.strain_hl, bf16[64,256,256]{2,1,0:T(8,128)(2,1)S(1)} %get-tuple-element.54.c_high, ...), custom_call_target="tpu_custom_call", output_to_operand_aliasing={{}: (4, {})} | custom-call | tf_op jit(solution)/shard_map/push_end_body/pallas_call | solution.py:80
  88.5 4.9 %collective-permute-done.20 = f32[32,128]{1,0:T(8,128)S(1)} collective-permute-done((f32[32,128]{1,0:T(8,128)S(1)}, f32[32,128]{1,0:T(8,128)S(1)}, u32[]{:S(2)}, u32[]{:S(2)}) %collective-permute-start.20) | collective-permute-done | bytes 16416 | tf_op jit(solution)/shard_map/ppermute | solution.py:358
  93.6 3.4 %collective-permute-start.21 = (f32[32,128]{1,0:T(8,128)S(1)}, f32[32,128]{1,0:T(8,128)S(1)}, u32[]{:S(2)}, u32[]{:S(2)}) collective-permute-start(f32[32,128]{1,0:T(8,128)S(1)} %add.12), channel_id=1, source_target_pairs={{0,32},{1,33},{2,34},{3,35},{4,36},{5,37},{6,38},{7,39},{8,40},{9,... | collective-permute-start | bytes 49160 | tf_op jit(solution)/shard_map/ppermute | solution.py:358
  97.0 1.8 %collective-permute-done.23 = f32[32,128]{1,0:T(8,128)S(1)} collective-permute-done((f32[32,128]{1,0:T(8,128)S(1)}, f32[32,128]{1,0:T(8,128)S(1)}, u32[]{:S(2)}, u32[]{:S(2)}) %collective-permute-start.23) | collective-permute-done | bytes 16416 | tf_op jit(solution)/shard_map/ppermute | solution.py:358
  101.5 2.0 %collective-permute-start.28 = (f32[8,32,256]{2,1,0:T(8,128)S(1)}, f32[8,32,256]{2,1,0:T(8,128)S(1)}, u32[]{:S(2)}, u32[]{:S(2)}) collective-permute-start(f32[8,32,256]{2,1,0:T(8,128)S(1)} %get-tuple-element.89), channel_id=1, source_target_pairs={{0,120},{8,16},{16,8},{24,32},{32,24},{40,48},{48,40},{56,64},{64,... | collective-permute-start | bytes 786440 | tf_op jit(solution)/shard_map/ppermute | solution.py:35
  104.7 5.1 %solve_body.1 = (f32[32,32]{1,0:T(8,128)S(1)}, f32[32,32]{1,0:T(8,128)S(1)}) custom-call(f32[32,128]{1,0:T(8,128)S(1)} %add_add_fusion.grams, f32[32,128]{1,0:T(8,128)S(1)} %collective-permute-done.24.moved), custom_call_target="tpu_custom_call" | custom-call | tf_op jit(solution)/shard_map/solve_body/pallas_call | solution.py:80
  (66 shorter events, 25.5 us)
Async XLA Ops:
  0.6 16.8 %collective-permute-start.2 = (f32[32,2048]{1,0:T(8,128)}, f32[32,2048]{1,0:T(8,128)S(1)}, u32[]{:S(2)}, u32[]{:S(2)}) collective-permute-start(f32[32,2048]{1,0:T(8,128)} %right.1), channel_id=1, source_target_pairs={{0,120},{8,16},{16,8},{24,32},{32,24},{40,48},{48,40},{56,64},{64,... | collective-permute-start | bytes 786440 | tf_op jit(solution)/shard_map/ppermute | solution.py:35
  6.0 11.4 %collective-permute-start.1 = (f32[32,2048]{1,0:T(8,128)}, f32[32,2048]{1,0:T(8,128)S(1)}, u32[]{:S(2)}, u32[]{:S(2)}) collective-permute-start(f32[32,2048]{1,0:T(8,128)} %right.1), channel_id=1, source_target_pairs={{0,8},{8,0},{16,24},{24,16},{32,40},{40,32},{48,56},{56,48},{64,72... | collective-permute-start | bytes 786440 | tf_op jit(solution)/shard_map/ppermute | solution.py:35
  6.0 11.4 %collective-permute-start = (f32[32,2048]{1,0:T(8,128)}, f32[32,2048]{1,0:T(8,128)S(1)}, u32[]{:S(2)}, u32[]{:S(2)}) collective-permute-start(f32[32,2048]{1,0:T(8,128)} %right.1), channel_id=1, source_target_pairs={{0,7},{1,2},{2,1},{3,4},{4,3},{5,6},{6,5},{7,0},{8,15},{9,10},{10,... | collective-permute-start | bytes 786440 | tf_op jit(solution)/shard_map/ppermute | solution.py:35
  17.7 9.9 %collective-permute-start.4 = (f32[2,8,32,256]{3,2,1,0:T(8,128)S(1)}, f32[2,8,32,256]{3,2,1,0:T(8,128)S(1)}, u32[]{:S(2)}, u32[]{:S(2)}) collective-permute-start(f32[2,8,32,256]{3,2,1,0:T(8,128)S(1)} %get-tuple-element.52), channel_id=1, source_target_pairs={{0,7},{1,2},{2,1},{3,4},{4,3},{5,6},{6,5},{7,0},{8,15},{9,10},{10,... | collective-permute-start | bytes 1572872 | tf_op jit(solution)/shard_map/ppermute | solution.py:35
  29.3 9.9 %collective-permute-start.9 = (f32[2,8,32,256]{3,2,1,0:T(8,128)S(1)}, f32[2,8,32,256]{3,2,1,0:T(8,128)S(1)}, u32[]{:S(2)}, u32[]{:S(2)}) collective-permute-start(f32[2,8,32,256]{3,2,1,0:T(8,128)S(1)} %get-tuple-element.65), channel_id=1, source_target_pairs={{0,7},{1,2},{2,1},{3,4},{4,3},{5,6},{6,5},{7,0},{8,15},{9,10},{10,... | collective-permute-start | bytes 1572872 | tf_op jit(solution)/shard_map/ppermute | solution.py:35
  35.3 7.9 %collective-permute-start.5 = (f32[8,32,256]{2,1,0:T(8,128)S(1)}, f32[8,32,256]{2,1,0:T(8,128)S(1)}, u32[]{:S(2)}, u32[]{:S(2)}) collective-permute-start(f32[8,32,256]{2,1,0:T(8,128)S(1)} %get-tuple-element.59), channel_id=1, source_target_pairs={{0,1},{1,0},{2,3},{3,2},{4,5},{5,4},{6,7},{7,6},{8,9},{9,8},{10,11... | collective-permute-start | bytes 786440 | tf_op jit(solution)/shard_map/ppermute | solution.py:35
  35.4 7.8 %collective-permute-start.6 = (f32[8,32,256]{2,1,0:T(8,128)S(1)}, f32[8,32,256]{2,1,0:T(8,128)S(1)}, u32[]{:S(2)}, u32[]{:S(2)}) collective-permute-start(f32[8,32,256]{2,1,0:T(8,128)S(1)} %get-tuple-element.60), channel_id=1, source_target_pairs={{0,7},{1,2},{2,1},{3,4},{4,3},{5,6},{6,5},{7,0},{8,15},{9,10},{10,... | collective-permute-start | bytes 786440 | tf_op jit(solution)/shard_map/ppermute | solution.py:35
  39.3 7.0 %collective-permute-start.10 = (f32[8,32,256]{2,1,0:T(8,128)S(1)}, f32[8,32,256]{2,1,0:T(8,128)S(1)}, u32[]{:S(2)}, u32[]{:S(2)}) collective-permute-start(f32[8,32,256]{2,1,0:T(8,128)S(1)} %get-tuple-element.66), channel_id=1, source_target_pairs={{0,8},{8,0},{16,24},{24,16},{32,40},{40,32},{48,56},{56,48},{64,72... | collective-permute-start | bytes 786440 | tf_op jit(solution)/shard_map/ppermute | solution.py:35
  41.1 10.5 %collective-permute-start.11 = (f32[8,32,256]{2,1,0:T(8,128)S(1)}, f32[8,32,256]{2,1,0:T(8,128)S(1)}, u32[]{:S(2)}, u32[]{:S(2)}) collective-permute-start(f32[8,32,256]{2,1,0:T(8,128)S(1)} %get-tuple-element.67), channel_id=1, source_target_pairs={{0,120},{8,16},{16,8},{24,32},{32,24},{40,48},{48,40},{56,64},{64,... | collective-permute-start | bytes 786440 | tf_op jit(solution)/shard_map/ppermute | solution.py:35
  51.7 11.8 %collective-permute-start.14 = (f32[8,32,256]{2,1,0:T(8,128)S(1)}, f32[8,32,256]{2,1,0:T(8,128)S(1)}, u32[]{:S(2)}, u32[]{:S(2)}) collective-permute-start(f32[8,32,256]{2,1,0:T(8,128)S(1)} %sum_body.1.vector.refs_2_.u), channel_id=1, source_target_pairs={{0,120},{8,16},{16,8},{24,32},{32,24},{40,48},{48,40},{56,64},{64,... | collective-permute-start | bytes 786440 | tf_op jit(solution)/shard_map/ppermute | solution.py:35
  52.2 11.2 %collective-permute-start.13 = (f32[8,32,256]{2,1,0:T(8,128)S(1)}, f32[8,32,256]{2,1,0:T(8,128)S(1)}, u32[]{:S(2)}, u32[]{:S(2)}) collective-permute-start(f32[8,32,256]{2,1,0:T(8,128)S(1)} %sum_body.1.vector.refs_2_.u), channel_id=1, source_target_pairs={{0,8},{8,0},{16,24},{24,16},{32,40},{40,32},{48,56},{56,48},{64,72... | collective-permute-start | bytes 786440 | tf_op jit(solution)/shard_map/ppermute | solution.py:35
  52.2 11.2 %collective-permute-start.12 = (f32[8,32,256]{2,1,0:T(8,128)S(1)}, f32[8,32,256]{2,1,0:T(8,128)S(1)}, u32[]{:S(2)}, u32[]{:S(2)}) collective-permute-start(f32[8,32,256]{2,1,0:T(8,128)S(1)} %sum_body.1.vector.refs_2_.u), channel_id=1, source_target_pairs={{0,7},{1,2},{2,1},{3,4},{4,3},{5,6},{6,5},{7,0},{8,15},{9,10},{10,... | collective-permute-start | bytes 786440 | tf_op jit(solution)/shard_map/ppermute | solution.py:35
  64.3 9.8 %collective-permute-start.16 = (f32[2,8,32,256]{3,2,1,0:T(8,128)S(1)}, f32[2,8,32,256]{3,2,1,0:T(8,128)S(1)}, u32[]{:S(2)}, u32[]{:S(2)}) collective-permute-start(f32[2,8,32,256]{3,2,1,0:T(8,128)S(1)} %get-tuple-element.72), channel_id=1, source_target_pairs={{0,7},{1,2},{2,1},{3,4},{4,3},{5,6},{6,5},{7,0},{8,15},{9,10},{10,... | collective-permute-start | bytes 1572872 | tf_op jit(solution)/shard_map/ppermute | solution.py:35
  75.1 3.8 %collective-permute-start.17 = (f32[32,128]{1,0:T(8,128)S(1)}, f32[32,128]{1,0:T(8,128)S(1)}, u32[]{:S(2)}, u32[]{:S(2)}) collective-permute-start(f32[32,128]{1,0:T(8,128)S(1)} %get-tuple-element.75.grams), channel_id=1, source_target_pairs={{0,2},{1,3},{2,0},{3,1},{4,6},{5,7},{6,4},{7,5},{8,10},{9,11},{10,... | collective-permute-start | bytes 49160 | tf_op jit(solution)/shard_map/ppermute | solution.py:358
  78.8 4.9 %collective-permute-start.18 = (f32[32,128]{1,0:T(8,128)S(1)}, f32[32,128]{1,0:T(8,128)S(1)}, u32[]{:S(2)}, u32[]{:S(2)}) collective-permute-start(f32[32,128]{1,0:T(8,128)S(1)} %add_body.3.grams), channel_id=1, source_target_pairs={{0,6},{1,7},{2,4},{3,5},{4,2},{5,3},{6,0},{7,1},{8,14},{9,15},{10,... | collective-permute-start | bytes 49160 | tf_op jit(solution)/shard_map/ppermute | solution.py:358
  83.8 3.7 %collective-permute-start.19 = (f32[32,128]{1,0:T(8,128)S(1)}, f32[32,128]{1,0:T(8,128)S(1)}, u32[]{:S(2)}, u32[]{:S(2)}) collective-permute-start(f32[32,128]{1,0:T(8,128)S(1)} %add_body.4.grams), channel_id=1, source_target_pairs={{0,8},{1,9},{2,10},{3,11},{4,12},{5,13},{6,14},{7,15},{8,0},{9,1},... | collective-permute-start | bytes 49160 | tf_op jit(solution)/shard_map/ppermute | solution.py:358
  87.7 11.1 %collective-permute-start.25 = (f32[3,8,32,256]{3,2,1,0:T(8,128)S(1)}, f32[3,8,32,256]{3,2,1,0:T(8,128)S(1)}, u32[]{:S(2)}, u32[]{:S(2)}) collective-permute-start(f32[3,8,32,256]{3,2,1,0:T(8,128)S(1)} %get-tuple-element.83), channel_id=1, source_target_pairs={{0,1},{1,0},{2,3},{3,2},{4,5},{5,4},{6,7},{7,6},{8,9},{9,8},{10,11... | collective-permute-start | bytes 2359304 | tf_op jit(solution)/shard_map/ppermute | solution.py:35
  87.8 12.7 %collective-permute-start.26 = (f32[3,8,32,256]{3,2,1,0:T(8,128)S(1)}, f32[3,8,32,256]{3,2,1,0:T(8,128)S(1)}, u32[]{:S(2)}, u32[]{:S(2)}) collective-permute-start(f32[3,8,32,256]{3,2,1,0:T(8,128)S(1)} %get-tuple-element.84), channel_id=1, source_target_pairs={{0,7},{1,2},{2,1},{3,4},{4,3},{5,6},{6,5},{7,0},{8,15},{9,10},{10,... | collective-permute-start | bytes 2359304 | tf_op jit(solution)/shard_map/ppermute | solution.py:35
  88.5 4.9 %collective-permute-start.20 = (f32[32,128]{1,0:T(8,128)S(1)}, f32[32,128]{1,0:T(8,128)S(1)}, u32[]{:S(2)}, u32[]{:S(2)}) collective-permute-start(f32[32,128]{1,0:T(8,128)S(1)} %add_body.5.grams), channel_id=1, source_target_pairs={{0,24},{1,25},{2,26},{3,27},{4,28},{5,29},{6,30},{7,31},{8,16},{9,... | collective-permute-start | bytes 49160 | tf_op jit(solution)/shard_map/ppermute | solution.py:358
  93.5 5.2 %collective-permute-start.23 = (f32[32,128]{1,0:T(8,128)S(1)}, f32[32,128]{1,0:T(8,128)S(1)}, u32[]{:S(2)}, u32[]{:S(2)}) collective-permute-start(f32[32,128]{1,0:T(8,128)S(1)} %add.12), channel_id=1, source_target_pairs={{0,64},{1,65},{2,66},{3,67},{4,68},{5,69},{6,70},{7,71},{8,72},{9,... | collective-permute-start | bytes 49160 | tf_op jit(solution)/shard_map/ppermute | solution.py:358
  93.5 5.2 %collective-permute-start.22 = (f32[32,128]{1,0:T(8,128)S(1)}, f32[32,128]{1,0:T(8,128)S(1)}, u32[]{:S(2)}, u32[]{:S(2)}) collective-permute-start(f32[32,128]{1,0:T(8,128)S(1)} %add.12), channel_id=1, source_target_pairs={{0,96},{1,97},{2,98},{3,99},{4,100},{5,101},{6,102},{7,103},{8,104... | collective-permute-start | bytes 49160 | tf_op jit(solution)/shard_map/ppermute | solution.py:358
  93.6 5.2 %collective-permute-start.21 = (f32[32,128]{1,0:T(8,128)S(1)}, f32[32,128]{1,0:T(8,128)S(1)}, u32[]{:S(2)}, u32[]{:S(2)}) collective-permute-start(f32[32,128]{1,0:T(8,128)S(1)} %add.12), channel_id=1, source_target_pairs={{0,32},{1,33},{2,34},{3,35},{4,36},{5,37},{6,38},{7,39},{8,40},{9,... | collective-permute-start | bytes 49160 | tf_op jit(solution)/shard_map/ppermute | solution.py:358
  100.6 10.9 %collective-permute-start.27 = (f32[8,32,256]{2,1,0:T(8,128)S(1)}, f32[8,32,256]{2,1,0:T(8,128)S(1)}, u32[]{:S(2)}, u32[]{:S(2)}) collective-permute-start(f32[8,32,256]{2,1,0:T(8,128)S(1)} %get-tuple-element.88), channel_id=1, source_target_pairs={{0,8},{8,0},{16,24},{24,16},{32,40},{40,32},{48,56},{56,48},{64,72... | collective-permute-start | bytes 786440 | tf_op jit(solution)/shard_map/ppermute | solution.py:35
  101.5 10.8 %collective-permute-start.28 = (f32[8,32,256]{2,1,0:T(8,128)S(1)}, f32[8,32,256]{2,1,0:T(8,128)S(1)}, u32[]{:S(2)}, u32[]{:S(2)}) collective-permute-start(f32[8,32,256]{2,1,0:T(8,128)S(1)} %get-tuple-element.89), channel_id=1, source_target_pairs={{0,120},{8,16},{16,8},{24,32},{32,24},{40,48},{48,40},{56,64},{64,... | collective-permute-start | bytes 786440 | tf_op jit(solution)/shard_map/ppermute | solution.py:35
  (8 other events, 40.4 us)

commit v7 on v6

--- a/solution.py
+++ b/solution.py
@@ -292,7 +292,7 @@
     mb[...] = rb[...] + qa[2] + qb[2]
 
 
-def sum_body(own, diag, ca, cb, ra, rb, out):
+def sum_body(own, diag, ca, cb, rb, ra, out):
     out[...] = (own[...] + diag[...]) + (ca[...] + cb[...]) + (ra[...] + rb[...])
 
 
@@ -334,23 +334,16 @@
     q[...] = full_nn(alpha, second)
 
 
-def finish_body(p, q, right, u, rest, x_out, r_part):
+def finish_body(p, q, right, u, rest, rb, ra, x_out, r_out):
     width = u.shape[2]
     for block in range(u.shape[0]):
         lanes = slice(block * width, (block + 1) * width)
+        w = rest[block] + (ra[block] + rb[block])
         x_out[:, lanes] = full_tn(p[...], right[:, lanes]) - full_tn(q[...], u[block])
-        r_part[block] = right[:, lanes] - full_tn(p[...], u[block]) + full_tn(q[...], rest[block])
-
-
-def finish_last_body(q, r_part, ra, rb, r_out):
-    width = ra.shape[2]
-    for block in range(ra.shape[0]):
-        lanes = slice(block * width, (block + 1) * width)
-        r_out[:, lanes] = r_part[block] + full_tn(q[...], ra[block] + rb[block])
-
-
-MASKS = (2, 6, 8, 24, 1)
-RING = (32, 96, 64)
+        r_out[:, lanes] = right[:, lanes] - full_tn(p[...], u[block]) + full_tn(q[...], w)
+
+
+MASKS = (2, 6, 32, 96, 8, 1, 24)
 
 
 def exchanged(value, mask):
@@ -399,8 +392,8 @@
     cb = swapped(cb, "col", 1)
     diag, g01 = call(diag_body, [block_shape, grams_shape], 0, (right_sides, diag_blocks))
     ra, rb = call(middle_early_body, [block_shape] * 2, 0, (ra, rb, qa_first, qa_second, db))
-    ra, rb = swapped(ra, "row", 0), swapped(rb, "row", 1)
-    u = call(sum_body, block_shape, 0, (own, diag, ca, cb, ra, rb))
+    rb, ra = swapped(rb, "row", 1), swapped(ra, "row", 0)
+    u = call(sum_body, block_shape, 0, (own, diag, ca, cb, rb, ra))
 
     diag, g23 = call(diag_body, [block_shape, grams_shape], 0, (u, diag_blocks))
     near_tables, db = spread(u, g23)
@@ -413,15 +406,14 @@
     grams = call(add_body, all_grams_shape, 0, (grams, exchanged(grams, MASKS[2]), pieces))
     own, ra, rb, qa, qb = call(pack_body, [block_shape] * 3 + [stack_shape] * 2, 0, (pieces, grams))
     qa, qb = swapped(qa, "col", 0), swapped(qb, "col", 1)
-    grams = grams + exchanged(grams, MASKS[3])
-    first, second, third = (exchanged(grams, mask) for mask in RING)
-    grams = (grams + first) + (second + third)
-    rest, ra, rb = call(middle_last_body, [block_shape] * 3, 0, (own, diag, ra, rb, qa, qb, grams))
-    ra, rb = swapped(ra, "row", 0), swapped(rb, "row", 1)
-    p, q = call(solve_body, [gram_shape] * 2, 0, (grams, exchanged(grams, MASKS[-1])))
+    for mask in MASKS[3:-1]:
+        grams = grams + exchanged(grams, mask)
+    moved = exchanged(grams, MASKS[-1])
+    rest, ra, rb = call(middle_last_body, [block_shape] * 3, 0, (own, diag, ra, rb, qa, qb, moved))
+    rb, ra = swapped(rb, "row", 1), swapped(ra, "row", 0)
+    p, q = call(solve_body, [gram_shape] * 2, 0, (grams, moved))
     flat = jax.ShapeDtypeStruct(right_sides.shape, F32)
-    x_out, r_part = call(finish_body, [flat, block_shape], 0, (p, q, right_sides, u, rest))
-    return x_out, call(finish_last_body, flat, 0, (q, r_part, ra, rb))
+    return tuple(call(finish_body, [flat, flat], 0, (p, q, right_sides, u, rest, rb, ra)))
 
 
 def solution(mesh):

time: 114 us -> 114 us (level)
  waiting for transfers between devices: 43.1 us -> 47.6 us
  starting transfers between devices: 27.5 us -> 24.2 us
    ppermute x8 -> x7, waiting for transfers between devices: 14.5 us -> 20.9 us  [exchanged(): lax.ppermute(value, ('row', 'col'), [(i, i ^ mask) for i in range(count)])]
    ppermute x8 -> x7, starting transfers between devices: 3.71 us -> 0.71 us  [exchanged(): lax.ppermute(value, ('row', 'col'), [(i, i ^ mask) for i in range(count)])]
    ppermute x21, waiting for transfers between devices: 28.6 us -> 26.6 us  [swapped(): return lax.ppermute(value, axis, pairs_of(lax.axis_size(axis), shift))]
    pallas_call x23 -> x22, Pallas kernels: 33.7 us -> 32.6 us  [call(): pl.pallas_call(body, out_shape=out_shape, in_specs=[SMEM_SPEC] * n_smem +...]
  transfers between devices with their start and end apart: 29 -> 28, of which waited for: 16 -> 15; matrix products, arithmetic and copies ran while one was open for 0% -> 0% of each run, Pallas kernels for 33% -> 31%
where the time goes in v7:
time: 114 us
  waiting for transfers between devices  47.6 us (42%)
  Pallas kernels  40.2 us (35%)
  starting transfers between devices  24.2 us (21%)
    pallas_call x22, Pallas kernels, call(): pl.pallas_call(body, out_shape=out_shape, in_specs=[SMEM_SPEC] * n_smem +...  32.6 us
    ppermute x21, waiting for transfers between devices, swapped(): return lax.ppermute(value, axis, pairs_of(lax.axis_size(axis), shift))  26.6 us
    ppermute x21, starting transfers between devices, swapped(): return lax.ppermute(value, axis, pairs_of(lax.axis_size(axis), shift))  23.5 us
    ppermute x7, waiting for transfers between devices, exchanged(): lax.ppermute(value, ('row', 'col'), [(i, i ^ mask) for i in range(count)])  20.9 us
    pallas_call x1, Pallas kernels, prepare(): pl.pallas_call(functools.partial(prepare_body, blocks), in_specs=[VMEM_SP...  7.53 us
  transfers between devices with their start and end apart: 28, of which 15 were waited for; matrix products, arithmetic and copies ran while one was open for 0% of the time, Pallas kernels for 31%

profile of v7, /device:TPU:0, one launch (start us, length us, event | category | flops | bytes accessed | tf_op | source)
XLA Modules:
  0.0 113.5 jit_solution(13446616086227987909)
XLA Ops:
  0.6 5.4 %collective-permute-start.2 = (f32[32,2048]{1,0:T(8,128)}, f32[32,2048]{1,0:T(8,128)S(1)}, u32[]{:S(2)}, u32[]{:S(2)}) collective-permute-start(f32[32,2048]{1,0:T(8,128)} %right.1), channel_id=1, source_target_pairs={{0,120},{8,16},{16,8},{24,32},{32,24},{40,48},{48,40},{56,64},{64,... | collective-permute-start | bytes 786440 | tf_op jit(solution)/shard_map/ppermute | solution.py:35
  6.0 3.2 %collective-permute-start = (f32[32,2048]{1,0:T(8,128)}, f32[32,2048]{1,0:T(8,128)S(1)}, u32[]{:S(2)}, u32[]{:S(2)}) collective-permute-start(f32[32,2048]{1,0:T(8,128)} %right.1), channel_id=1, source_target_pairs={{0,7},{1,2},{2,1},{3,4},{4,3},{5,6},{6,5},{7,0},{8,15},{9,10},{10,... | collective-permute-start | bytes 786440 | tf_op jit(solution)/shard_map/ppermute | solution.py:35
  9.9 7.5 %prepare.1 = (bf16[64,256,256]{2,1,0:T(8,128)(2,1)S(1)}, bf16[64,256,256]{2,1,0:T(8,128)(2,1)S(1)}, bf16[64,256,256]{2,1,0:T(8,128)(2,1)S(1)}, bf16[64,256,256]{2,1,0:T(8,128)(2,1)S(1)}, s32[4,64]{1,0:T(4,128)S(1)}) custom-call(s32[2,64]{1,0:T(2,128)S(1)} %copy-done.2, f32[64,256,256]{2,1,0:T(8,128)} %couplings.1), custom_call_target="tpu_custom_call" | custom-call | tf_op jit(solution)/shard_map/prepare/pallas_call | solution.py:145
  19.9 4.4 %pull_near_body.2 = (bf16[72,64,256]{2,1,0:T(8,128)(2,1)S(1)}, f32[8,32,256]{2,1,0:T(8,128)S(1)}) custom-call(s32[4,64]{1,0:T(4,128)S(1)} %get-tuple-element.44.refs_0_.routes, f32[3,8,32,256]{3,2,1,0:T(8,128)S(1)} %collective-permute-done.3.qa, f32[3,8,32,256]{3,2,1,0:T(8,128)S(1)} %get-tuple-element.45.whole, ...), custom_call_target="tpu_custom_call" | custom-call | tf_op jit(solution)/shard_map/pull_near_body/pallas_call | solution.py:80
  24.4 3.2 %collective-permute-done.4.db = f32[2,8,32,256]{3,2,1,0:T(8,128)S(1)} collective-permute-done((f32[2,8,32,256]{3,2,1,0:T(8,128)S(1)}, f32[2,8,32,256]{3,2,1,0:T(8,128)S(1)}, u32[]{:S(2)}, u32[]{:S(2)}) %collective-permute-start.4) | collective-permute-done | bytes 524320 | tf_op jit(solution)/shard_map/ppermute | solution.py:35
  30.2 4.5 %push_near_body.1 = (f32[8,32,256]{2,1,0:T(8,128)S(1)}, f32[8,32,256]{2,1,0:T(8,128)S(1)}, f32[8,32,256]{2,1,0:T(8,128)S(1)}, f32[8,32,256]{2,1,0:T(8,128)S(1)},...) custom-call(s32[4,64]{1,0:T(4,128)S(1)} %get-tuple-element.44.refs_0_.routes, ...), custom_call_target="tpu_custom_call" | custom-call | tf_op jit(solution)/shard_map/push_near_body/pallas_call | solution.py:80
  35.4 2.1 %collective-permute-start.6 = (f32[8,32,256]{2,1,0:T(8,128)S(1)}, f32[8,32,256]{2,1,0:T(8,128)S(1)}, u32[]{:S(2)}, u32[]{:S(2)}) collective-permute-start(f32[8,32,256]{2,1,0:T(8,128)S(1)} %get-tuple-element.58), channel_id=1, source_target_pairs={{0,7},{1,2},{2,1},{3,4},{4,3},{5,6},{6,5},{7,0},{8,15},{9,10},{10,... | collective-permute-start | bytes 786440 | tf_op jit(solution)/shard_map/ppermute | solution.py:35
  41.4 1.7 %diag_body.2 = (f32[8,32,256]{2,1,0:T(8,128)S(1)}, f32[2,32,32]{2,1,0:T(8,128)S(1)}) custom-call(f32[32,2048]{1,0:T(8,128)S(1)} %copy-done.1, f32[8,256,256]{2,1,0:T(8,128)S(1)} %copy-done), custom_call_target="tpu_custom_call" | custom-call | tf_op jit(solution)/shard_map/diag_body/pallas_call | solution.py:80
  43.1 7.3 %collective-permute-done.10.rb = f32[8,32,256]{2,1,0:T(8,128)S(1)} collective-permute-done((f32[8,32,256]{2,1,0:T(8,128)S(1)}, f32[8,32,256]{2,1,0:T(8,128)S(1)}, u32[]{:S(2)}, u32[]{:S(2)}) %collective-permute-start.10) | collective-permute-done | bytes 262176 | tf_op jit(solution)/shard_map/ppermute | solution.py:35
  50.5 2.0 %collective-permute-start.14 = (f32[8,32,256]{2,1,0:T(8,128)S(1)}, f32[8,32,256]{2,1,0:T(8,128)S(1)}, u32[]{:S(2)}, u32[]{:S(2)}) collective-permute-start(f32[8,32,256]{2,1,0:T(8,128)S(1)} %sum_body.1.vector.refs_2_.u), channel_id=1, source_target_pairs={{0,120},{8,16},{16,8},{24,32},{32,24},{40,48},{48,40},{56,64},{64,... | collective-permute-start | bytes 786440 | tf_op jit(solution)/shard_map/ppermute | solution.py:35
  55.2 6.3 %collective-permute-done.14.refs_4_ = f32[8,32,256]{2,1,0:T(8,128)S(1)} collective-permute-done((f32[8,32,256]{2,1,0:T(8,128)S(1)}, f32[8,32,256]{2,1,0:T(8,128)S(1)}, u32[]{:S(2)}, u32[]{:S(2)}) %collective-permute-start.14) | collective-permute-done | bytes 262176 | tf_op jit(solution)/shard_map/ppermute | solution.py:35
  64.0 4.4 %pull_near_body.3 = (bf16[72,64,256]{2,1,0:T(8,128)(2,1)S(1)}, f32[8,32,256]{2,1,0:T(8,128)S(1)}) custom-call(s32[4,64]{1,0:T(4,128)S(1)} %get-tuple-element.44.refs_0_.routes, f32[3,8,32,256]{3,2,1,0:T(8,128)S(1)} %collective-permute-done.15.qa, f32[3,8,32,256]{3,2,1,0:T(8,128)S(1)} %get-tuple-element.67.whole, ...), custom_call_target="tpu_custom_call" | custom-call | tf_op jit(solution)/shard_map/pull_near_body/pallas_call | solution.py:80
  68.5 3.2 %collective-permute-done.16.db = f32[2,8,32,256]{3,2,1,0:T(8,128)S(1)} collective-permute-done((f32[2,8,32,256]{3,2,1,0:T(8,128)S(1)}, f32[2,8,32,256]{3,2,1,0:T(8,128)S(1)}, u32[]{:S(2)}, u32[]{:S(2)}) %collective-permute-start.16) | collective-permute-done | bytes 524320 | tf_op jit(solution)/shard_map/ppermute | solution.py:35
  73.4 3.0 %collective-permute-done.17.moved = f32[32,128]{1,0:T(8,128)S(1)} collective-permute-done((f32[32,128]{1,0:T(8,128)S(1)}, f32[32,128]{1,0:T(8,128)S(1)}, u32[]{:S(2)}, u32[]{:S(2)}) %collective-permute-start.17) | collective-permute-done | bytes 16416 | tf_op jit(solution)/shard_map/ppermute | solution.py:351
  77.1 2.4 %push_begin_body.1.after.pieces_in = f32[72,32,256]{2,1,0:T(8,128)S(1)} custom-call(s32[4,64]{1,0:T(4,128)S(1)} %get-tuple-element.44.refs_0_.routes, bf16[8,64,256]{2,1,0:T(8,128)(2,1)S(1)} %get-tuple-element.74.strain_hl, bf16[64,256,256]{2,1,0:T(8,128)(2,1)S(1)} %get-tuple-element.52.c_high, ...), custom_call_target="tpu_custom_call", output_to_operand_aliasing={{}: (4, {})} | custom-call | tf_op jit(solution)/shard_map/push_begin_body/pallas_call | solution.py:80
  79.5 1.9 %collective-permute-done.18.moved = f32[32,128]{1,0:T(8,128)S(1)} collective-permute-done((f32[32,128]{1,0:T(8,128)S(1)}, f32[32,128]{1,0:T(8,128)S(1)}, u32[]{:S(2)}, u32[]{:S(2)}) %collective-permute-start.18) | collective-permute-done | bytes 16416 | tf_op jit(solution)/shard_map/ppermute | solution.py:351
  81.4 2.4 %push_end_body.1.after.pieces = f32[72,32,256]{2,1,0:T(8,128)S(1)} custom-call(s32[4,64]{1,0:T(4,128)S(1)} %get-tuple-element.44.refs_0_.routes, bf16[8,64,256]{2,1,0:T(8,128)(2,1)S(1)} %get-tuple-element.74.strain_hl, bf16[64,256,256]{2,1,0:T(8,128)(2,1)S(1)} %get-tuple-element.52.c_high, ...), custom_call_target="tpu_custom_call", output_to_operand_aliasing={{}: (4, {})} | custom-call | tf_op jit(solution)/shard_map/push_end_body/pallas_call | solution.py:80
  86.1 4.9 %collective-permute-done.20 = f32[32,128]{1,0:T(8,128)S(1)} collective-permute-done((f32[32,128]{1,0:T(8,128)S(1)}, f32[32,128]{1,0:T(8,128)S(1)}, u32[]{:S(2)}, u32[]{:S(2)}) %collective-permute-start.20) | collective-permute-done | bytes 16416 | tf_op jit(solution)/shard_map/ppermute | solution.py:351
  91.1 3.7 %collective-permute-done.21 = f32[32,128]{1,0:T(8,128)S(1)} collective-permute-done((f32[32,128]{1,0:T(8,128)S(1)}, f32[32,128]{1,0:T(8,128)S(1)}, u32[]{:S(2)}, u32[]{:S(2)}) %collective-permute-start.21) | collective-permute-done | bytes 16416 | tf_op jit(solution)/shard_map/ppermute | solution.py:351
  96.0 4.9 %collective-permute-done.23.moved.grams = f32[32,128]{1,0:T(8,128)S(1)} collective-permute-done((f32[32,128]{1,0:T(8,128)S(1)}, f32[32,128]{1,0:T(8,128)S(1)}, u32[]{:S(2)}, u32[]{:S(2)}) %collective-permute-start.23) | collective-permute-done | bytes 16416 | tf_op jit(solution)/shard_map/ppermute | solution.py:351
  101.1 2.6 %collective-permute-start.26 = (f32[8,32,256]{2,1,0:T(8,128)S(1)}, f32[8,32,256]{2,1,0:T(8,128)S(1)}, u32[]{:S(2)}, u32[]{:S(2)}) collective-permute-start(f32[8,32,256]{2,1,0:T(8,128)S(1)} %get-tuple-element.84), channel_id=1, source_target_pairs={{0,120},{8,16},{16,8},{24,32},{32,24},{40,48},{48,40},{56,64},{64,... | collective-permute-start | bytes 786440 | tf_op jit(solution)/shard_map/ppermute | solution.py:35
  103.7 5.1 %solve_body.1 = (f32[32,32]{1,0:T(8,128)S(1)}, f32[32,32]{1,0:T(8,128)S(1)}) custom-call(f32[32,128]{1,0:T(8,128)S(1)} %add.11.grams, f32[32,128]{1,0:T(8,128)S(1)} %collective-permute-done.23.moved.grams), custom_call_target="tpu_custom_call" | custom-call | tf_op jit(solution)/shard_map/solve_body/pallas_call | solution.py:80
  108.9 2.9 %collective-permute-done.26.rb = f32[8,32,256]{2,1,0:T(8,128)S(1)} collective-permute-done((f32[8,32,256]{2,1,0:T(8,128)S(1)}, f32[8,32,256]{2,1,0:T(8,128)S(1)}, u32[]{:S(2)}, u32[]{:S(2)}) %collective-permute-start.26) | collective-permute-done | bytes 262176 | tf_op jit(solution)/shard_map/ppermute | solution.py:35
  111.8 1.8 %finish_body.1 = (f32[32,2048]{1,0:T(8,128)}, f32[32,2048]{1,0:T(8,128)}) custom-call(f32[32,32]{1,0:T(8,128)S(1)} %get-tuple-element.75.p, f32[32,32]{1,0:T(8,128)S(1)} %get-tuple-element.76.q, f32[32,2048]{1,0:T(8,128)S(1)} %copy-done.1, f32[8,32,256]{2,1,0:T(8,128)S(1)} %sum_body.1.vector.refs_2_.u, f32[8,32,256]{2,1,0:T(8,128)S(1)} %get-tuple-element.83.rest, ...), custom_call_target="tpu_custom_call" | custom-call | tf_op jit(solution)/shard_map/finish_body/pallas_call | solution.py:80
  (64 shorter events, 21.7 us)
Async XLA Ops:
  0.6 16.8 %collective-permute-start.2 = (f32[32,2048]{1,0:T(8,128)}, f32[32,2048]{1,0:T(8,128)S(1)}, u32[]{:S(2)}, u32[]{:S(2)}) collective-permute-start(f32[32,2048]{1,0:T(8,128)} %right.1), channel_id=1, source_target_pairs={{0,120},{8,16},{16,8},{24,32},{32,24},{40,48},{48,40},{56,64},{64,... | collective-permute-start | bytes 786440 | tf_op jit(solution)/shard_map/ppermute | solution.py:35
  6.0 11.4 %collective-permute-start.1 = (f32[32,2048]{1,0:T(8,128)}, f32[32,2048]{1,0:T(8,128)S(1)}, u32[]{:S(2)}, u32[]{:S(2)}) collective-permute-start(f32[32,2048]{1,0:T(8,128)} %right.1), channel_id=1, source_target_pairs={{0,8},{8,0},{16,24},{24,16},{32,40},{40,32},{48,56},{56,48},{64,72... | collective-permute-start | bytes 786440 | tf_op jit(solution)/shard_map/ppermute | solution.py:35
  6.0 11.4 %collective-permute-start = (f32[32,2048]{1,0:T(8,128)}, f32[32,2048]{1,0:T(8,128)S(1)}, u32[]{:S(2)}, u32[]{:S(2)}) collective-permute-start(f32[32,2048]{1,0:T(8,128)} %right.1), channel_id=1, source_target_pairs={{0,7},{1,2},{2,1},{3,4},{4,3},{5,6},{6,5},{7,0},{8,15},{9,10},{10,... | collective-permute-start | bytes 786440 | tf_op jit(solution)/shard_map/ppermute | solution.py:35
  17.7 9.9 %collective-permute-start.4 = (f32[2,8,32,256]{3,2,1,0:T(8,128)S(1)}, f32[2,8,32,256]{3,2,1,0:T(8,128)S(1)}, u32[]{:S(2)}, u32[]{:S(2)}) collective-permute-start(f32[2,8,32,256]{3,2,1,0:T(8,128)S(1)} %get-tuple-element.50), channel_id=1, source_target_pairs={{0,7},{1,2},{2,1},{3,4},{4,3},{5,6},{6,5},{7,0},{8,15},{9,10},{10,... | collective-permute-start | bytes 1572872 | tf_op jit(solution)/shard_map/ppermute | solution.py:35
  29.3 9.9 %collective-permute-start.9 = (f32[2,8,32,256]{3,2,1,0:T(8,128)S(1)}, f32[2,8,32,256]{3,2,1,0:T(8,128)S(1)}, u32[]{:S(2)}, u32[]{:S(2)}) collective-permute-start(f32[2,8,32,256]{3,2,1,0:T(8,128)S(1)} %get-tuple-element.63), channel_id=1, source_target_pairs={{0,7},{1,2},{2,1},{3,4},{4,3},{5,6},{6,5},{7,0},{8,15},{9,10},{10,... | collective-permute-start | bytes 1572872 | tf_op jit(solution)/shard_map/ppermute | solution.py:35
  34.7 2.8 %collective-permute-start.7 = (f32[8,32,256]{2,1,0:T(8,128)S(1)}, f32[8,32,256]{2,1,0:T(8,128)S(1)}, u32[]{:S(2)}, u32[]{:S(2)}) collective-permute-start(f32[8,32,256]{2,1,0:T(8,128)S(1)} %get-tuple-element.61), channel_id=1, source_target_pairs={{0,1},{1,0},{2,3},{3,2},{4,5},{5,4},{6,7},{7,6},{8,9},{9,8},{10,11... | collective-permute-start | bytes 786440 | tf_op jit(solution)/shard_map/ppermute | solution.py:35
  35.3 7.8 %collective-permute-start.5 = (f32[8,32,256]{2,1,0:T(8,128)S(1)}, f32[8,32,256]{2,1,0:T(8,128)S(1)}, u32[]{:S(2)}, u32[]{:S(2)}) collective-permute-start(f32[8,32,256]{2,1,0:T(8,128)S(1)} %get-tuple-element.57), channel_id=1, source_target_pairs={{0,1},{1,0},{2,3},{3,2},{4,5},{5,4},{6,7},{7,6},{8,9},{9,8},{10,11... | collective-permute-start | bytes 786440 | tf_op jit(solution)/shard_map/ppermute | solution.py:35
  35.4 7.7 %collective-permute-start.6 = (f32[8,32,256]{2,1,0:T(8,128)S(1)}, f32[8,32,256]{2,1,0:T(8,128)S(1)}, u32[]{:S(2)}, u32[]{:S(2)}) collective-permute-start(f32[8,32,256]{2,1,0:T(8,128)S(1)} %get-tuple-element.58), channel_id=1, source_target_pairs={{0,7},{1,2},{2,1},{3,4},{4,3},{5,6},{6,5},{7,0},{8,15},{9,10},{10,... | collective-permute-start | bytes 786440 | tf_op jit(solution)/shard_map/ppermute | solution.py:35
  39.3 11.1 %collective-permute-start.10 = (f32[8,32,256]{2,1,0:T(8,128)S(1)}, f32[8,32,256]{2,1,0:T(8,128)S(1)}, u32[]{:S(2)}, u32[]{:S(2)}) collective-permute-start(f32[8,32,256]{2,1,0:T(8,128)S(1)} %get-tuple-element.64), channel_id=1, source_target_pairs={{0,120},{8,16},{16,8},{24,32},{32,24},{40,48},{48,40},{56,64},{64,... | collective-permute-start | bytes 786440 | tf_op jit(solution)/shard_map/ppermute | solution.py:35
  40.6 9.8 %collective-permute-start.11 = (f32[8,32,256]{2,1,0:T(8,128)S(1)}, f32[8,32,256]{2,1,0:T(8,128)S(1)}, u32[]{:S(2)}, u32[]{:S(2)}) collective-permute-start(f32[8,32,256]{2,1,0:T(8,128)S(1)} %get-tuple-element.65), channel_id=1, source_target_pairs={{0,8},{8,0},{16,24},{24,16},{32,40},{40,32},{48,56},{56,48},{64,72... | collective-permute-start | bytes 786440 | tf_op jit(solution)/shard_map/ppermute | solution.py:35
  50.5 11.1 %collective-permute-start.14 = (f32[8,32,256]{2,1,0:T(8,128)S(1)}, f32[8,32,256]{2,1,0:T(8,128)S(1)}, u32[]{:S(2)}, u32[]{:S(2)}) collective-permute-start(f32[8,32,256]{2,1,0:T(8,128)S(1)} %sum_body.1.vector.refs_2_.u), channel_id=1, source_target_pairs={{0,120},{8,16},{16,8},{24,32},{32,24},{40,48},{48,40},{56,64},{64,... | collective-permute-start | bytes 786440 | tf_op jit(solution)/shard_map/ppermute | solution.py:35
  52.5 9.1 %collective-permute-start.13 = (f32[8,32,256]{2,1,0:T(8,128)S(1)}, f32[8,32,256]{2,1,0:T(8,128)S(1)}, u32[]{:S(2)}, u32[]{:S(2)}) collective-permute-start(f32[8,32,256]{2,1,0:T(8,128)S(1)} %sum_body.1.vector.refs_2_.u), channel_id=1, source_target_pairs={{0,8},{8,0},{16,24},{24,16},{32,40},{40,32},{48,56},{56,48},{64,72... | collective-permute-start | bytes 786440 | tf_op jit(solution)/shard_map/ppermute | solution.py:35
  52.5 9.1 %collective-permute-start.12 = (f32[8,32,256]{2,1,0:T(8,128)S(1)}, f32[8,32,256]{2,1,0:T(8,128)S(1)}, u32[]{:S(2)}, u32[]{:S(2)}) collective-permute-start(f32[8,32,256]{2,1,0:T(8,128)S(1)} %sum_body.1.vector.refs_2_.u), channel_id=1, source_target_pairs={{0,7},{1,2},{2,1},{3,4},{4,3},{5,6},{6,5},{7,0},{8,15},{9,10},{10,... | collective-permute-start | bytes 786440 | tf_op jit(solution)/shard_map/ppermute | solution.py:35
  61.8 9.9 %collective-permute-start.16 = (f32[2,8,32,256]{3,2,1,0:T(8,128)S(1)}, f32[2,8,32,256]{3,2,1,0:T(8,128)S(1)}, u32[]{:S(2)}, u32[]{:S(2)}) collective-permute-start(f32[2,8,32,256]{3,2,1,0:T(8,128)S(1)} %get-tuple-element.70), channel_id=1, source_target_pairs={{0,7},{1,2},{2,1},{3,4},{4,3},{5,6},{6,5},{7,0},{8,15},{9,10},{10,... | collective-permute-start | bytes 1572872 | tf_op jit(solution)/shard_map/ppermute | solution.py:35
  72.7 3.8 %collective-permute-start.17 = (f32[32,128]{1,0:T(8,128)S(1)}, f32[32,128]{1,0:T(8,128)S(1)}, u32[]{:S(2)}, u32[]{:S(2)}) collective-permute-start(f32[32,128]{1,0:T(8,128)S(1)} %get-tuple-element.73.grams), channel_id=1, source_target_pairs={{0,2},{1,3},{2,0},{3,1},{4,6},{5,7},{6,4},{7,5},{8,10},{9,11},{10,... | collective-permute-start | bytes 49160 | tf_op jit(solution)/shard_map/ppermute | solution.py:351
  76.4 4.9 %collective-permute-start.18 = (f32[32,128]{1,0:T(8,128)S(1)}, f32[32,128]{1,0:T(8,128)S(1)}, u32[]{:S(2)}, u32[]{:S(2)}) collective-permute-start(f32[32,128]{1,0:T(8,128)S(1)} %add_body.3.grams), channel_id=1, source_target_pairs={{0,6},{1,7},{2,4},{3,5},{4,2},{5,3},{6,0},{7,1},{8,14},{9,15},{10,... | collective-permute-start | bytes 49160 | tf_op jit(solution)/shard_map/ppermute | solution.py:351
  81.4 3.7 %collective-permute-start.19 = (f32[32,128]{1,0:T(8,128)S(1)}, f32[32,128]{1,0:T(8,128)S(1)}, u32[]{:S(2)}, u32[]{:S(2)}) collective-permute-start(f32[32,128]{1,0:T(8,128)S(1)} %add_body.4.grams), channel_id=1, source_target_pairs={{0,32},{1,33},{2,34},{3,35},{4,36},{5,37},{6,38},{7,39},{8,40},{9,... | collective-permute-start | bytes 49160 | tf_op jit(solution)/shard_map/ppermute | solution.py:351
  85.3 15.7 %collective-permute-start.24 = (f32[3,8,32,256]{3,2,1,0:T(8,128)S(1)}, f32[3,8,32,256]{3,2,1,0:T(8,128)S(1)}, u32[]{:S(2)}, u32[]{:S(2)}) collective-permute-start(f32[3,8,32,256]{3,2,1,0:T(8,128)S(1)} %get-tuple-element.81), channel_id=1, source_target_pairs={{0,1},{1,0},{2,3},{3,2},{4,5},{5,4},{6,7},{7,6},{8,9},{9,8},{10,11... | collective-permute-start | bytes 2359304 | tf_op jit(solution)/shard_map/ppermute | solution.py:35
  85.4 15.6 %collective-permute-start.25 = (f32[3,8,32,256]{3,2,1,0:T(8,128)S(1)}, f32[3,8,32,256]{3,2,1,0:T(8,128)S(1)}, u32[]{:S(2)}, u32[]{:S(2)}) collective-permute-start(f32[3,8,32,256]{3,2,1,0:T(8,128)S(1)} %get-tuple-element.82), channel_id=1, source_target_pairs={{0,7},{1,2},{2,1},{3,4},{4,3},{5,6},{6,5},{7,0},{8,15},{9,10},{10,... | collective-permute-start | bytes 2359304 | tf_op jit(solution)/shard_map/ppermute | solution.py:35
  86.1 4.9 %collective-permute-start.20 = (f32[32,128]{1,0:T(8,128)S(1)}, f32[32,128]{1,0:T(8,128)S(1)}, u32[]{:S(2)}, u32[]{:S(2)}) collective-permute-start(f32[32,128]{1,0:T(8,128)S(1)} %add_body.5.grams), channel_id=1, source_target_pairs={{0,96},{1,97},{2,98},{3,99},{4,100},{5,101},{6,102},{7,103},{8,104... | collective-permute-start | bytes 49160 | tf_op jit(solution)/shard_map/ppermute | solution.py:351
  91.1 3.7 %collective-permute-start.21 = (f32[32,128]{1,0:T(8,128)S(1)}, f32[32,128]{1,0:T(8,128)S(1)}, u32[]{:S(2)}, u32[]{:S(2)}) collective-permute-start(f32[32,128]{1,0:T(8,128)S(1)} %add.9), channel_id=1, source_target_pairs={{0,8},{1,9},{2,10},{3,11},{4,12},{5,13},{6,14},{7,15},{8,0},{9,1},... | collective-permute-start | bytes 49160 | tf_op jit(solution)/shard_map/ppermute | solution.py:351
  96.0 4.9 %collective-permute-start.23 = (f32[32,128]{1,0:T(8,128)S(1)}, f32[32,128]{1,0:T(8,128)S(1)}, u32[]{:S(2)}, u32[]{:S(2)}) collective-permute-start(f32[32,128]{1,0:T(8,128)S(1)} %add.11.grams), channel_id=1, source_target_pairs={{0,24},{1,25},{2,26},{3,27},{4,28},{5,29},{6,30},{7,31},{8,16},{9,... | collective-permute-start | bytes 49160 | tf_op jit(solution)/shard_map/ppermute | solution.py:351
  101.1 10.6 %collective-permute-start.26 = (f32[8,32,256]{2,1,0:T(8,128)S(1)}, f32[8,32,256]{2,1,0:T(8,128)S(1)}, u32[]{:S(2)}, u32[]{:S(2)}) collective-permute-start(f32[8,32,256]{2,1,0:T(8,128)S(1)} %get-tuple-element.84), channel_id=1, source_target_pairs={{0,120},{8,16},{16,8},{24,32},{32,24},{40,48},{48,40},{56,64},{64,... | collective-permute-start | bytes 786440 | tf_op jit(solution)/shard_map/ppermute | solution.py:35
  103.7 8.0 %collective-permute-start.27 = (f32[8,32,256]{2,1,0:T(8,128)S(1)}, f32[8,32,256]{2,1,0:T(8,128)S(1)}, u32[]{:S(2)}, u32[]{:S(2)}) collective-permute-start(f32[8,32,256]{2,1,0:T(8,128)S(1)} %get-tuple-element.85), channel_id=1, source_target_pairs={{0,8},{8,0},{16,24},{24,16},{32,40},{40,32},{48,56},{56,48},{64,72... | collective-permute-start | bytes 786440 | tf_op jit(solution)/shard_map/ppermute | solution.py:35
  (7 other events, 37.3 us)

commit v8 on v7

--- a/solution.py
+++ b/solution.py
@@ -15,7 +15,7 @@
 CHUNK = 8
 HALF = 4
 PREPARED = 8
-SLOTS = 3
+SLOTS = 8
 NEAR_TABLES = 7
 
 
@@ -118,15 +118,18 @@
     routes[3:4, :] = jnp.broadcast_to(near >> (HALF.bit_length() - 1), (1, count))
 
 
-def prepare_body(blocks, pair, couplings, c_high, c_low, t_high, t_low, routes, buffer, arrived):
+def prepare_body(blocks, pairs, couplings, c_high, c_low, t_high, t_low, routes, pair, buffer, arrived, pair_arrived):
     groups = couplings.shape[0] // PREPARED
     copies = [
         pltpu.make_async_copy(
             couplings.at[pl.ds(i * PREPARED, PREPARED)], buffer.at[i % SLOTS], arrived.at[i])
         for i in range(groups)
     ]
+    pair_copy = pltpu.make_async_copy(pairs, pair, pair_arrived)
+    pair_copy.start()
     for copy in copies[:SLOTS]:
         copy.start()
+    pair_copy.wait()
     route(pair, routes, blocks)
     for i, copy in enumerate(copies):
         copy.wait()
@@ -144,16 +147,18 @@
     shape = pltpu.VMEM(couplings.shape, BF16)
     return pl.pallas_call(
         functools.partial(prepare_body, blocks),
-        in_specs=[VMEM_SPEC, pl.BlockSpec(memory_space=pltpu.HBM)],
+        in_specs=[pl.BlockSpec(memory_space=pltpu.HBM)] * 2,
         out_specs=[VMEM_SPEC] * 5,
         out_shape=[shape] * 4 + [pltpu.VMEM((4, count), jnp.int32)],
         scratch_shapes=[
+            pltpu.VMEM(pair_index.shape, jnp.int32),
             pltpu.VMEM((SLOTS, PREPARED, width, width), F32),
             pltpu.SemaphoreType.DMA((count // PREPARED,)),
+            pltpu.SemaphoreType.DMA,
         ],
         name="prepare",
-        compiler_params=pltpu.CompilerParams(vmem_limit_bytes=7 << 20),
-    )(in_vmem(pair_index), in_hbm(couplings))
+        compiler_params=pltpu.CompilerParams(vmem_limit_bytes=17 << 20),
+    )(in_hbm(pair_index), in_hbm(couplings))
 
 
 def block_of(source, q, width):
@@ -343,7 +348,8 @@
         r_out[:, lanes] = right[:, lanes] - full_tn(p[...], u[block]) + full_tn(q[...], w)
 
 
-MASKS = (2, 6, 32, 96, 8, 1, 24)
+MASKS = (2, 6, 8, 24, 1)
+RING = (32, 96, 64)
 
 
 def exchanged(value, mask):
@@ -406,12 +412,12 @@
     grams = call(add_body, all_grams_shape, 0, (grams, exchanged(grams, MASKS[2]), pieces))
     own, ra, rb, qa, qb = call(pack_body, [block_shape] * 3 + [stack_shape] * 2, 0, (pieces, grams))
     qa, qb = swapped(qa, "col", 0), swapped(qb, "col", 1)
-    for mask in MASKS[3:-1]:
-        grams = grams + exchanged(grams, mask)
-    moved = exchanged(grams, MASKS[-1])
-    rest, ra, rb = call(middle_last_body, [block_shape] * 3, 0, (own, diag, ra, rb, qa, qb, moved))
+    grams = grams + exchanged(grams, MASKS[3])
+    first, second, third = (exchanged(grams, mask) for mask in RING)
+    grams = (grams + first) + (second + third)
+    rest, ra, rb = call(middle_last_body, [block_shape] * 3, 0, (own, diag, ra, rb, qa, qb, grams))
     rb, ra = swapped(rb, "row", 1), swapped(ra, "row", 0)
-    p, q = call(solve_body, [gram_shape] * 2, 0, (grams, moved))
+    p, q = call(solve_body, [gram_shape] * 2, 0, (grams, exchanged(grams, MASKS[4])))
     flat = jax.ShapeDtypeStruct(right_sides.shape, F32)
     return tuple(call(finish_body, [flat, flat], 0, (p, q, right_sides, u, rest, rb, ra)))
 

time: 114 us -> 113 us (level)
  waiting for transfers between devices: 47.6 us -> 42.5 us
  Pallas kernels: 40.2 us -> 43.1 us
  starting transfers between devices: 24.2 us -> 26.7 us
    ppermute x7 -> x8, waiting for transfers between devices: 20.9 us -> 14.2 us  [exchanged(): lax.ppermute(value, ('row', 'col'), [(i, i ^ mask) for i in range(count)])]
    ppermute x7 -> x8, starting transfers between devices: 0.71 us -> 4.16 us  [exchanged(): lax.ppermute(value, ('row', 'col'), [(i, i ^ mask) for i in range(count)])]
    pallas_call x1, Pallas kernels: 7.53 us -> 10.5 us  [prepare(): pl.pallas_call(functools.partial(prepare_body, blocks), in_specs=[pl.Bloc...]
    ppermute x21, waiting for transfers between devices: 26.6 us -> 28.3 us  [swapped(): return lax.ppermute(value, axis, pairs_of(lax.axis_size(axis), shift))]
  transfers between devices with their start and end apart: 28 -> 29, of which waited for: 15 -> 16; matrix products, arithmetic and copies ran while one was open for 0% -> 0% of each run, Pallas kernels for 31% -> 34%
where the time goes in v8:
time: 113 us
  Pallas kernels  43.1 us (38%)
  waiting for transfers between devices  42.5 us (38%)
  starting transfers between devices  26.7 us (24%)
    pallas_call x22, Pallas kernels, call(): pl.pallas_call(body, out_shape=out_shape, in_specs=[SMEM_SPEC] * n_smem +...  32.6 us
    ppermute x21, waiting for transfers between devices, swapped(): return lax.ppermute(value, axis, pairs_of(lax.axis_size(axis), shift))  28.3 us
    ppermute x21, starting transfers between devices, swapped(): return lax.ppermute(value, axis, pairs_of(lax.axis_size(axis), shift))  22.6 us
    ppermute x8, waiting for transfers between devices, exchanged(): lax.ppermute(value, ('row', 'col'), [(i, i ^ mask) for i in range(count)])  14.2 us
    pallas_call x1, Pallas kernels, prepare(): pl.pallas_call(functools.partial(prepare_body, blocks), in_specs=[pl.Bloc...  10.5 us
    ppermute x8, starting transfers between devices, exchanged(): lax.ppermute(value, ('row', 'col'), [(i, i ^ mask) for i in range(count)])  4.16 us
  transfers between devices with their start and end apart: 29, of which 16 were waited for; matrix products, arithmetic and copies ran while one was open for 0% of the time, Pallas kernels for 34%

profile of v8, /device:TPU:0, one launch (start us, length us, event | category | flops | bytes accessed | tf_op | source)
XLA Modules:
  0.0 113.2 jit_solution(3131260583964727832)
XLA Ops:
  0.6 5.4 %collective-permute-start.2 = (f32[32,2048]{1,0:T(8,128)}, f32[32,2048]{1,0:T(8,128)S(1)}, u32[]{:S(2)}, u32[]{:S(2)}) collective-permute-start(f32[32,2048]{1,0:T(8,128)} %right.1), channel_id=1, source_target_pairs={{0,120},{8,16},{16,8},{24,32},{32,24},{40,48},{48,40},{56,64},{64,... | collective-permute-start | bytes 786440 | tf_op jit(solution)/shard_map/ppermute | solution.py:35
  6.0 3.2 %collective-permute-start = (f32[32,2048]{1,0:T(8,128)}, f32[32,2048]{1,0:T(8,128)S(1)}, u32[]{:S(2)}, u32[]{:S(2)}) collective-permute-start(f32[32,2048]{1,0:T(8,128)} %right.1), channel_id=1, source_target_pairs={{0,7},{1,2},{2,1},{3,4},{4,3},{5,6},{6,5},{7,0},{8,15},{9,10},{10,... | collective-permute-start | bytes 786440 | tf_op jit(solution)/shard_map/ppermute | solution.py:35
  9.2 10.5 %prepare.1 = (bf16[64,256,256]{2,1,0:T(8,128)(2,1)S(1)}, bf16[64,256,256]{2,1,0:T(8,128)(2,1)S(1)}, bf16[64,256,256]{2,1,0:T(8,128)(2,1)S(1)}, bf16[64,256,256]{2,1,0:T(8,128)(2,1)S(1)}, s32[4,64]{1,0:T(4,128)S(1)}) custom-call(s32[2,64]{1,0:T(2,128)} %pairs.1, f32[64,256,256]{2,1,0:T(8,128)} %couplings.1), custom_call_target="tpu_custom_call" | custom-call | tf_op jit(solution)/shard_map/prepare/pallas_call | solution.py:148
  22.2 4.5 %pull_near_body.2 = (bf16[72,64,256]{2,1,0:T(8,128)(2,1)S(1)}, f32[8,32,256]{2,1,0:T(8,128)S(1)}) custom-call(s32[4,64]{1,0:T(4,128)S(1)} %get-tuple-element.44.refs_0_.routes, f32[3,8,32,256]{3,2,1,0:T(8,128)S(1)} %collective-permute-done.3.qa, f32[3,8,32,256]{3,2,1,0:T(8,128)S(1)} %get-tuple-element.45.whole, ...), custom_call_target="tpu_custom_call" | custom-call | tf_op jit(solution)/shard_map/pull_near_body/pallas_call | solution.py:80
  26.7 3.1 %collective-permute-done.4.db = f32[2,8,32,256]{3,2,1,0:T(8,128)S(1)} collective-permute-done((f32[2,8,32,256]{3,2,1,0:T(8,128)S(1)}, f32[2,8,32,256]{3,2,1,0:T(8,128)S(1)}, u32[]{:S(2)}, u32[]{:S(2)}) %collective-permute-start.4) | collective-permute-done | bytes 524320 | tf_op jit(solution)/shard_map/ppermute | solution.py:35
  32.5 4.4 %push_near_body.1 = (f32[8,32,256]{2,1,0:T(8,128)S(1)}, f32[8,32,256]{2,1,0:T(8,128)S(1)}, f32[8,32,256]{2,1,0:T(8,128)S(1)}, f32[8,32,256]{2,1,0:T(8,128)S(1)},...) custom-call(s32[4,64]{1,0:T(4,128)S(1)} %get-tuple-element.44.refs_0_.routes, ...), custom_call_target="tpu_custom_call" | custom-call | tf_op jit(solution)/shard_map/push_near_body/pallas_call | solution.py:80
  37.6 2.1 %collective-permute-start.6 = (f32[8,32,256]{2,1,0:T(8,128)S(1)}, f32[8,32,256]{2,1,0:T(8,128)S(1)}, u32[]{:S(2)}, u32[]{:S(2)}) collective-permute-start(f32[8,32,256]{2,1,0:T(8,128)S(1)} %get-tuple-element.58), channel_id=1, source_target_pairs={{0,7},{1,2},{2,1},{3,4},{4,3},{5,6},{6,5},{7,0},{8,15},{9,10},{10,... | collective-permute-start | bytes 786440 | tf_op jit(solution)/shard_map/ppermute | solution.py:35
  43.7 1.7 %diag_body.2 = (f32[8,32,256]{2,1,0:T(8,128)S(1)}, f32[2,32,32]{2,1,0:T(8,128)S(1)}) custom-call(f32[32,2048]{1,0:T(8,128)S(1)} %copy-done.1, f32[8,256,256]{2,1,0:T(8,128)S(1)} %copy-done), custom_call_target="tpu_custom_call" | custom-call | tf_op jit(solution)/shard_map/diag_body/pallas_call | solution.py:80
  45.4 6.9 %collective-permute-done.10.rb = f32[8,32,256]{2,1,0:T(8,128)S(1)} collective-permute-done((f32[8,32,256]{2,1,0:T(8,128)S(1)}, f32[8,32,256]{2,1,0:T(8,128)S(1)}, u32[]{:S(2)}, u32[]{:S(2)}) %collective-permute-start.10) | collective-permute-done | bytes 262176 | tf_op jit(solution)/shard_map/ppermute | solution.py:35
  52.4 1.8 %collective-permute-start.14 = (f32[8,32,256]{2,1,0:T(8,128)S(1)}, f32[8,32,256]{2,1,0:T(8,128)S(1)}, u32[]{:S(2)}, u32[]{:S(2)}) collective-permute-start(f32[8,32,256]{2,1,0:T(8,128)S(1)} %sum_body.1.vector.refs_2_.u), channel_id=1, source_target_pairs={{0,120},{8,16},{16,8},{24,32},{32,24},{40,48},{48,40},{56,64},{64,... | collective-permute-start | bytes 786440 | tf_op jit(solution)/shard_map/ppermute | solution.py:35
  56.8 6.9 %collective-permute-done.14.refs_4_ = f32[8,32,256]{2,1,0:T(8,128)S(1)} collective-permute-done((f32[8,32,256]{2,1,0:T(8,128)S(1)}, f32[8,32,256]{2,1,0:T(8,128)S(1)}, u32[]{:S(2)}, u32[]{:S(2)}) %collective-permute-start.14) | collective-permute-done | bytes 262176 | tf_op jit(solution)/shard_map/ppermute | solution.py:35
  66.2 4.5 %pull_near_body.3 = (bf16[72,64,256]{2,1,0:T(8,128)(2,1)S(1)}, f32[8,32,256]{2,1,0:T(8,128)S(1)}) custom-call(s32[4,64]{1,0:T(4,128)S(1)} %get-tuple-element.44.refs_0_.routes, f32[3,8,32,256]{3,2,1,0:T(8,128)S(1)} %collective-permute-done.15.qa, f32[3,8,32,256]{3,2,1,0:T(8,128)S(1)} %get-tuple-element.67.whole, ...), custom_call_target="tpu_custom_call" | custom-call | tf_op jit(solution)/shard_map/pull_near_body/pallas_call | solution.py:80
  70.7 3.1 %collective-permute-done.16.db = f32[2,8,32,256]{3,2,1,0:T(8,128)S(1)} collective-permute-done((f32[2,8,32,256]{3,2,1,0:T(8,128)S(1)}, f32[2,8,32,256]{3,2,1,0:T(8,128)S(1)}, u32[]{:S(2)}, u32[]{:S(2)}) %collective-permute-start.16) | collective-permute-done | bytes 524320 | tf_op jit(solution)/shard_map/ppermute | solution.py:35
  75.6 3.0 %collective-permute-done.17.moved = f32[32,128]{1,0:T(8,128)S(1)} collective-permute-done((f32[32,128]{1,0:T(8,128)S(1)}, f32[32,128]{1,0:T(8,128)S(1)}, u32[]{:S(2)}, u32[]{:S(2)}) %collective-permute-start.17) | collective-permute-done | bytes 16416 | tf_op jit(solution)/shard_map/ppermute | solution.py:357
  79.2 2.4 %push_begin_body.1.after.pieces_in = f32[72,32,256]{2,1,0:T(8,128)S(1)} custom-call(s32[4,64]{1,0:T(4,128)S(1)} %get-tuple-element.44.refs_0_.routes, bf16[8,64,256]{2,1,0:T(8,128)(2,1)S(1)} %get-tuple-element.74.strain_hl, bf16[64,256,256]{2,1,0:T(8,128)(2,1)S(1)} %get-tuple-element.52.c_high, ...), custom_call_target="tpu_custom_call", output_to_operand_aliasing={{}: (4, {})} | custom-call | tf_op jit(solution)/shard_map/push_begin_body/pallas_call | solution.py:80
  81.6 1.9 %collective-permute-done.18.moved = f32[32,128]{1,0:T(8,128)S(1)} collective-permute-done((f32[32,128]{1,0:T(8,128)S(1)}, f32[32,128]{1,0:T(8,128)S(1)}, u32[]{:S(2)}, u32[]{:S(2)}) %collective-permute-start.18) | collective-permute-done | bytes 16416 | tf_op jit(solution)/shard_map/ppermute | solution.py:357
  83.5 2.4 %push_end_body.1.after.pieces = f32[72,32,256]{2,1,0:T(8,128)S(1)} custom-call(s32[4,64]{1,0:T(4,128)S(1)} %get-tuple-element.44.refs_0_.routes, bf16[8,64,256]{2,1,0:T(8,128)(2,1)S(1)} %get-tuple-element.74.strain_hl, bf16[64,256,256]{2,1,0:T(8,128)(2,1)S(1)} %get-tuple-element.52.c_high, ...), custom_call_target="tpu_custom_call", output_to_operand_aliasing={{}: (4, {})} | custom-call | tf_op jit(solution)/shard_map/push_end_body/pallas_call | solution.py:80
  88.3 4.9 %collective-permute-done.20 = f32[32,128]{1,0:T(8,128)S(1)} collective-permute-done((f32[32,128]{1,0:T(8,128)S(1)}, f32[32,128]{1,0:T(8,128)S(1)}, u32[]{:S(2)}, u32[]{:S(2)}) %collective-permute-start.20) | collective-permute-done | bytes 16416 | tf_op jit(solution)/shard_map/ppermute | solution.py:357
  94.8 1.9 %collective-permute-start.21 = (f32[32,128]{1,0:T(8,128)S(1)}, f32[32,128]{1,0:T(8,128)S(1)}, u32[]{:S(2)}, u32[]{:S(2)}) collective-permute-start(f32[32,128]{1,0:T(8,128)S(1)} %add.12), channel_id=1, source_target_pairs={{0,32},{1,33},{2,34},{3,35},{4,36},{5,37},{6,38},{7,39},{8,40},{9,... | collective-permute-start | bytes 49160 | tf_op jit(solution)/shard_map/ppermute | solution.py:357
  96.7 1.8 %collective-permute-done.23 = f32[32,128]{1,0:T(8,128)S(1)} collective-permute-done((f32[32,128]{1,0:T(8,128)S(1)}, f32[32,128]{1,0:T(8,128)S(1)}, u32[]{:S(2)}, u32[]{:S(2)}) %collective-permute-start.23) | collective-permute-done | bytes 16416 | tf_op jit(solution)/shard_map/ppermute | solution.py:357
  100.4 1.9 %collective-permute-start.27 = (f32[8,32,256]{2,1,0:T(8,128)S(1)}, f32[8,32,256]{2,1,0:T(8,128)S(1)}, u32[]{:S(2)}, u32[]{:S(2)}) collective-permute-start(f32[8,32,256]{2,1,0:T(8,128)S(1)} %get-tuple-element.84), channel_id=1, source_target_pairs={{0,120},{8,16},{16,8},{24,32},{32,24},{40,48},{48,40},{56,64},{64,... | collective-permute-start | bytes 786440 | tf_op jit(solution)/shard_map/ppermute | solution.py:35
  103.5 5.1 %solve_body.1 = (f32[32,32]{1,0:T(8,128)S(1)}, f32[32,32]{1,0:T(8,128)S(1)}) custom-call(f32[32,128]{1,0:T(8,128)S(1)} %add_add_fusion.grams, f32[32,128]{1,0:T(8,128)S(1)} %collective-permute-done.24.moved), custom_call_target="tpu_custom_call" | custom-call | tf_op jit(solution)/shard_map/solve_body/pallas_call | solution.py:80
  108.6 2.9 %collective-permute-done.27.rb = f32[8,32,256]{2,1,0:T(8,128)S(1)} collective-permute-done((f32[8,32,256]{2,1,0:T(8,128)S(1)}, f32[8,32,256]{2,1,0:T(8,128)S(1)}, u32[]{:S(2)}, u32[]{:S(2)}) %collective-permute-start.27) | collective-permute-done | bytes 262176 | tf_op jit(solution)/shard_map/ppermute | solution.py:35
  111.5 1.8 %finish_body.1 = (f32[32,2048]{1,0:T(8,128)}, f32[32,2048]{1,0:T(8,128)}) custom-call(f32[32,32]{1,0:T(8,128)S(1)} %get-tuple-element.75.p, f32[32,32]{1,0:T(8,128)S(1)} %get-tuple-element.76.q, f32[32,2048]{1,0:T(8,128)S(1)} %copy-done.1, f32[8,32,256]{2,1,0:T(8,128)S(1)} %sum_body.1.vector.refs_2_.u, f32[8,32,256]{2,1,0:T(8,128)S(1)} %get-tuple-element.83.rest, ...), custom_call_target="tpu_custom_call" | custom-call | tf_op jit(solution)/shard_map/finish_body/pallas_call | solution.py:80
  (63 shorter events, 24.2 us)
Async XLA Ops:
  0.6 19.1 %collective-permute-start.2 = (f32[32,2048]{1,0:T(8,128)}, f32[32,2048]{1,0:T(8,128)S(1)}, u32[]{:S(2)}, u32[]{:S(2)}) collective-permute-start(f32[32,2048]{1,0:T(8,128)} %right.1), channel_id=1, source_target_pairs={{0,120},{8,16},{16,8},{24,32},{32,24},{40,48},{48,40},{56,64},{64,... | collective-permute-start | bytes 786440 | tf_op jit(solution)/shard_map/ppermute | solution.py:35
  6.0 13.7 %collective-permute-start.1 = (f32[32,2048]{1,0:T(8,128)}, f32[32,2048]{1,0:T(8,128)S(1)}, u32[]{:S(2)}, u32[]{:S(2)}) collective-permute-start(f32[32,2048]{1,0:T(8,128)} %right.1), channel_id=1, source_target_pairs={{0,8},{8,0},{16,24},{24,16},{32,40},{40,32},{48,56},{56,48},{64,72... | collective-permute-start | bytes 786440 | tf_op jit(solution)/shard_map/ppermute | solution.py:35
  6.0 13.8 %collective-permute-start = (f32[32,2048]{1,0:T(8,128)}, f32[32,2048]{1,0:T(8,128)S(1)}, u32[]{:S(2)}, u32[]{:S(2)}) collective-permute-start(f32[32,2048]{1,0:T(8,128)} %right.1), channel_id=1, source_target_pairs={{0,7},{1,2},{2,1},{3,4},{4,3},{5,6},{6,5},{7,0},{8,15},{9,10},{10,... | collective-permute-start | bytes 786440 | tf_op jit(solution)/shard_map/ppermute | solution.py:35
  20.0 9.9 %collective-permute-start.4 = (f32[2,8,32,256]{3,2,1,0:T(8,128)S(1)}, f32[2,8,32,256]{3,2,1,0:T(8,128)S(1)}, u32[]{:S(2)}, u32[]{:S(2)}) collective-permute-start(f32[2,8,32,256]{3,2,1,0:T(8,128)S(1)} %get-tuple-element.50), channel_id=1, source_target_pairs={{0,7},{1,2},{2,1},{3,4},{4,3},{5,6},{6,5},{7,0},{8,15},{9,10},{10,... | collective-permute-start | bytes 1572872 | tf_op jit(solution)/shard_map/ppermute | solution.py:35
  31.6 9.9 %collective-permute-start.9 = (f32[2,8,32,256]{3,2,1,0:T(8,128)S(1)}, f32[2,8,32,256]{3,2,1,0:T(8,128)S(1)}, u32[]{:S(2)}, u32[]{:S(2)}) collective-permute-start(f32[2,8,32,256]{3,2,1,0:T(8,128)S(1)} %get-tuple-element.63), channel_id=1, source_target_pairs={{0,7},{1,2},{2,1},{3,4},{4,3},{5,6},{6,5},{7,0},{8,15},{9,10},{10,... | collective-permute-start | bytes 1572872 | tf_op jit(solution)/shard_map/ppermute | solution.py:35
  37.6 7.8 %collective-permute-start.5 = (f32[8,32,256]{2,1,0:T(8,128)S(1)}, f32[8,32,256]{2,1,0:T(8,128)S(1)}, u32[]{:S(2)}, u32[]{:S(2)}) collective-permute-start(f32[8,32,256]{2,1,0:T(8,128)S(1)} %get-tuple-element.57), channel_id=1, source_target_pairs={{0,1},{1,0},{2,3},{3,2},{4,5},{5,4},{6,7},{7,6},{8,9},{9,8},{10,11... | collective-permute-start | bytes 786440 | tf_op jit(solution)/shard_map/ppermute | solution.py:35
  37.6 7.8 %collective-permute-start.6 = (f32[8,32,256]{2,1,0:T(8,128)S(1)}, f32[8,32,256]{2,1,0:T(8,128)S(1)}, u32[]{:S(2)}, u32[]{:S(2)}) collective-permute-start(f32[8,32,256]{2,1,0:T(8,128)S(1)} %get-tuple-element.58), channel_id=1, source_target_pairs={{0,7},{1,2},{2,1},{3,4},{4,3},{5,6},{6,5},{7,0},{8,15},{9,10},{10,... | collective-permute-start | bytes 786440 | tf_op jit(solution)/shard_map/ppermute | solution.py:35
  41.6 10.8 %collective-permute-start.10 = (f32[8,32,256]{2,1,0:T(8,128)S(1)}, f32[8,32,256]{2,1,0:T(8,128)S(1)}, u32[]{:S(2)}, u32[]{:S(2)}) collective-permute-start(f32[8,32,256]{2,1,0:T(8,128)S(1)} %get-tuple-element.64), channel_id=1, source_target_pairs={{0,120},{8,16},{16,8},{24,32},{32,24},{40,48},{48,40},{56,64},{64,... | collective-permute-start | bytes 786440 | tf_op jit(solution)/shard_map/ppermute | solution.py:35
  42.7 9.6 %collective-permute-start.11 = (f32[8,32,256]{2,1,0:T(8,128)S(1)}, f32[8,32,256]{2,1,0:T(8,128)S(1)}, u32[]{:S(2)}, u32[]{:S(2)}) collective-permute-start(f32[8,32,256]{2,1,0:T(8,128)S(1)} %get-tuple-element.65), channel_id=1, source_target_pairs={{0,8},{8,0},{16,24},{24,16},{32,40},{40,32},{48,56},{56,48},{64,72... | collective-permute-start | bytes 786440 | tf_op jit(solution)/shard_map/ppermute | solution.py:35
  52.4 11.3 %collective-permute-start.14 = (f32[8,32,256]{2,1,0:T(8,128)S(1)}, f32[8,32,256]{2,1,0:T(8,128)S(1)}, u32[]{:S(2)}, u32[]{:S(2)}) collective-permute-start(f32[8,32,256]{2,1,0:T(8,128)S(1)} %sum_body.1.vector.refs_2_.u), channel_id=1, source_target_pairs={{0,120},{8,16},{16,8},{24,32},{32,24},{40,48},{48,40},{56,64},{64,... | collective-permute-start | bytes 786440 | tf_op jit(solution)/shard_map/ppermute | solution.py:35
  54.2 9.5 %collective-permute-start.13 = (f32[8,32,256]{2,1,0:T(8,128)S(1)}, f32[8,32,256]{2,1,0:T(8,128)S(1)}, u32[]{:S(2)}, u32[]{:S(2)}) collective-permute-start(f32[8,32,256]{2,1,0:T(8,128)S(1)} %sum_body.1.vector.refs_2_.u), channel_id=1, source_target_pairs={{0,8},{8,0},{16,24},{24,16},{32,40},{40,32},{48,56},{56,48},{64,72... | collective-permute-start | bytes 786440 | tf_op jit(solution)/shard_map/ppermute | solution.py:35
  54.2 9.5 %collective-permute-start.12 = (f32[8,32,256]{2,1,0:T(8,128)S(1)}, f32[8,32,256]{2,1,0:T(8,128)S(1)}, u32[]{:S(2)}, u32[]{:S(2)}) collective-permute-start(f32[8,32,256]{2,1,0:T(8,128)S(1)} %sum_body.1.vector.refs_2_.u), channel_id=1, source_target_pairs={{0,7},{1,2},{2,1},{3,4},{4,3},{5,6},{6,5},{7,0},{8,15},{9,10},{10,... | collective-permute-start | bytes 786440 | tf_op jit(solution)/shard_map/ppermute | solution.py:35
  63.9 9.9 %collective-permute-start.16 = (f32[2,8,32,256]{3,2,1,0:T(8,128)S(1)}, f32[2,8,32,256]{3,2,1,0:T(8,128)S(1)}, u32[]{:S(2)}, u32[]{:S(2)}) collective-permute-start(f32[2,8,32,256]{3,2,1,0:T(8,128)S(1)} %get-tuple-element.70), channel_id=1, source_target_pairs={{0,7},{1,2},{2,1},{3,4},{4,3},{5,6},{6,5},{7,0},{8,15},{9,10},{10,... | collective-permute-start | bytes 1572872 | tf_op jit(solution)/shard_map/ppermute | solution.py:35
  74.8 3.8 %collective-permute-start.17 = (f32[32,128]{1,0:T(8,128)S(1)}, f32[32,128]{1,0:T(8,128)S(1)}, u32[]{:S(2)}, u32[]{:S(2)}) collective-permute-start(f32[32,128]{1,0:T(8,128)S(1)} %get-tuple-element.73.grams), channel_id=1, source_target_pairs={{0,2},{1,3},{2,0},{3,1},{4,6},{5,7},{6,4},{7,5},{8,10},{9,11},{10,... | collective-permute-start | bytes 49160 | tf_op jit(solution)/shard_map/ppermute | solution.py:357
  78.6 4.9 %collective-permute-start.18 = (f32[32,128]{1,0:T(8,128)S(1)}, f32[32,128]{1,0:T(8,128)S(1)}, u32[]{:S(2)}, u32[]{:S(2)}) collective-permute-start(f32[32,128]{1,0:T(8,128)S(1)} %add_body.3.grams), channel_id=1, source_target_pairs={{0,6},{1,7},{2,4},{3,5},{4,2},{5,3},{6,0},{7,1},{8,14},{9,15},{10,... | collective-permute-start | bytes 49160 | tf_op jit(solution)/shard_map/ppermute | solution.py:357
  83.5 3.7 %collective-permute-start.19 = (f32[32,128]{1,0:T(8,128)S(1)}, f32[32,128]{1,0:T(8,128)S(1)}, u32[]{:S(2)}, u32[]{:S(2)}) collective-permute-start(f32[32,128]{1,0:T(8,128)S(1)} %add_body.4.grams), channel_id=1, source_target_pairs={{0,8},{1,9},{2,10},{3,11},{4,12},{5,13},{6,14},{7,15},{8,0},{9,1},... | collective-permute-start | bytes 49160 | tf_op jit(solution)/shard_map/ppermute | solution.py:357
  87.4 11.2 %collective-permute-start.25 = (f32[3,8,32,256]{3,2,1,0:T(8,128)S(1)}, f32[3,8,32,256]{3,2,1,0:T(8,128)S(1)}, u32[]{:S(2)}, u32[]{:S(2)}) collective-permute-start(f32[3,8,32,256]{3,2,1,0:T(8,128)S(1)} %get-tuple-element.81), channel_id=1, source_target_pairs={{0,1},{1,0},{2,3},{3,2},{4,5},{5,4},{6,7},{7,6},{8,9},{9,8},{10,11... | collective-permute-start | bytes 2359304 | tf_op jit(solution)/shard_map/ppermute | solution.py:35
  87.5 12.7 %collective-permute-start.26 = (f32[3,8,32,256]{3,2,1,0:T(8,128)S(1)}, f32[3,8,32,256]{3,2,1,0:T(8,128)S(1)}, u32[]{:S(2)}, u32[]{:S(2)}) collective-permute-start(f32[3,8,32,256]{3,2,1,0:T(8,128)S(1)} %get-tuple-element.82), channel_id=1, source_target_pairs={{0,7},{1,2},{2,1},{3,4},{4,3},{5,6},{6,5},{7,0},{8,15},{9,10},{10,... | collective-permute-start | bytes 2359304 | tf_op jit(solution)/shard_map/ppermute | solution.py:35
  88.3 4.9 %collective-permute-start.20 = (f32[32,128]{1,0:T(8,128)S(1)}, f32[32,128]{1,0:T(8,128)S(1)}, u32[]{:S(2)}, u32[]{:S(2)}) collective-permute-start(f32[32,128]{1,0:T(8,128)S(1)} %add_body.5.grams), channel_id=1, source_target_pairs={{0,24},{1,25},{2,26},{3,27},{4,28},{5,29},{6,30},{7,31},{8,16},{9,... | collective-permute-start | bytes 49160 | tf_op jit(solution)/shard_map/ppermute | solution.py:357
  93.2 5.2 %collective-permute-start.23 = (f32[32,128]{1,0:T(8,128)S(1)}, f32[32,128]{1,0:T(8,128)S(1)}, u32[]{:S(2)}, u32[]{:S(2)}) collective-permute-start(f32[32,128]{1,0:T(8,128)S(1)} %add.12), channel_id=1, source_target_pairs={{0,64},{1,65},{2,66},{3,67},{4,68},{5,69},{6,70},{7,71},{8,72},{9,... | collective-permute-start | bytes 49160 | tf_op jit(solution)/shard_map/ppermute | solution.py:357
  93.2 5.2 %collective-permute-start.22 = (f32[32,128]{1,0:T(8,128)S(1)}, f32[32,128]{1,0:T(8,128)S(1)}, u32[]{:S(2)}, u32[]{:S(2)}) collective-permute-start(f32[32,128]{1,0:T(8,128)S(1)} %add.12), channel_id=1, source_target_pairs={{0,96},{1,97},{2,98},{3,99},{4,100},{5,101},{6,102},{7,103},{8,104... | collective-permute-start | bytes 49160 | tf_op jit(solution)/shard_map/ppermute | solution.py:357
  94.8 3.7 %collective-permute-start.21 = (f32[32,128]{1,0:T(8,128)S(1)}, f32[32,128]{1,0:T(8,128)S(1)}, u32[]{:S(2)}, u32[]{:S(2)}) collective-permute-start(f32[32,128]{1,0:T(8,128)S(1)} %add.12), channel_id=1, source_target_pairs={{0,32},{1,33},{2,34},{3,35},{4,36},{5,37},{6,38},{7,39},{8,40},{9,... | collective-permute-start | bytes 49160 | tf_op jit(solution)/shard_map/ppermute | solution.py:357
  100.4 11.1 %collective-permute-start.27 = (f32[8,32,256]{2,1,0:T(8,128)S(1)}, f32[8,32,256]{2,1,0:T(8,128)S(1)}, u32[]{:S(2)}, u32[]{:S(2)}) collective-permute-start(f32[8,32,256]{2,1,0:T(8,128)S(1)} %get-tuple-element.84), channel_id=1, source_target_pairs={{0,120},{8,16},{16,8},{24,32},{32,24},{40,48},{48,40},{56,64},{64,... | collective-permute-start | bytes 786440 | tf_op jit(solution)/shard_map/ppermute | solution.py:35
  102.3 9.2 %collective-permute-start.28 = (f32[8,32,256]{2,1,0:T(8,128)S(1)}, f32[8,32,256]{2,1,0:T(8,128)S(1)}, u32[]{:S(2)}, u32[]{:S(2)}) collective-permute-start(f32[8,32,256]{2,1,0:T(8,128)S(1)} %get-tuple-element.85), channel_id=1, source_target_pairs={{0,8},{8,0},{16,24},{24,16},{32,40},{40,32},{48,56},{56,48},{64,72... | collective-permute-start | bytes 786440 | tf_op jit(solution)/shard_map/ppermute | solution.py:35
  (7 other events, 41.7 us)

commit v9 on v8

--- a/solution.py
+++ b/solution.py
@@ -129,9 +129,10 @@
     pair_copy.start()
     for copy in copies[:SLOTS]:
         copy.start()
-    pair_copy.wait()
-    route(pair, routes, blocks)
     for i, copy in enumerate(copies):
+        if i == groups - 1:
+            pair_copy.wait()
+            route(pair, routes, blocks)
         copy.wait()
         for place in range(PREPARED):
             k = i * PREPARED + place

time: 113 us -> 110 us (0.973)
  starting transfers between devices: 26.7 us -> 36.6 us
  waiting for transfers between devices: 42.5 us -> 32.7 us
  Pallas kernels: 43.1 us -> 39.8 us
    ppermute x21, waiting for transfers between devices: 28.3 us -> 22.7 us  [swapped(): return lax.ppermute(value, axis, pairs_of(lax.axis_size(axis), shift))]
    ppermute x21, starting transfers between devices: 22.6 us -> 27.9 us  [swapped(): return lax.ppermute(value, axis, pairs_of(lax.axis_size(axis), shift))]
    ppermute x8, starting transfers between devices: 4.16 us -> 8.63 us  [exchanged(): lax.ppermute(value, ('row', 'col'), [(i, i ^ mask) for i in range(count)])]
    ppermute x8, waiting for transfers between devices: 14.2 us -> 10 us  [exchanged(): lax.ppermute(value, ('row', 'col'), [(i, i ^ mask) for i in range(count)])]
    pallas_call x1, Pallas kernels: 10.5 us -> 7.19 us  [prepare(): pl.pallas_call(functools.partial(prepare_body, blocks), in_specs=[pl.Bloc...]
  transfers between devices with their start and end apart: 29 -> 29, of which waited for: 16 -> 14; matrix products, arithmetic and copies ran while one was open for 0% -> 0% of each run, Pallas kernels for 34% -> 32%
where the time goes in v9:
time: 110 us
  Pallas kernels  39.8 us (36%)
  starting transfers between devices  36.6 us (33%)
  waiting for transfers between devices  32.7 us (30%)
    pallas_call x22, Pallas kernels, call(): pl.pallas_call(body, out_shape=out_shape, in_specs=[SMEM_SPEC] * n_smem +...  32.6 us
    ppermute x21, starting transfers between devices, swapped(): return lax.ppermute(value, axis, pairs_of(lax.axis_size(axis), shift))  27.9 us
    ppermute x21, waiting for transfers between devices, swapped(): return lax.ppermute(value, axis, pairs_of(lax.axis_size(axis), shift))  22.7 us
    ppermute x8, waiting for transfers between devices, exchanged(): lax.ppermute(value, ('row', 'col'), [(i, i ^ mask) for i in range(count)])  10 us
    ppermute x8, starting transfers between devices, exchanged(): lax.ppermute(value, ('row', 'col'), [(i, i ^ mask) for i in range(count)])  8.63 us
    pallas_call x1, Pallas kernels, prepare(): pl.pallas_call(functools.partial(prepare_body, blocks), in_specs=[pl.Bloc...  7.19 us
  transfers between devices with their start and end apart: 29, of which 14 were waited for; matrix products, arithmetic and copies ran while one was open for 0% of the time, Pallas kernels for 32%

profile of v9, /device:TPU:0, one launch (start us, length us, event | category | flops | bytes accessed | tf_op | source)
XLA Modules:
  0.0 110.0 jit_solution(351620012561383961)
XLA Ops:
  0.6 5.4 %collective-permute-start.2 = (f32[32,2048]{1,0:T(8,128)}, f32[32,2048]{1,0:T(8,128)S(1)}, u32[]{:S(2)}, u32[]{:S(2)}) collective-permute-start(f32[32,2048]{1,0:T(8,128)} %right.1), channel_id=1, source_target_pairs={{0,120},{8,16},{16,8},{24,32},{32,24},{40,48},{48,40},{56,64},{64,... | collective-permute-start | bytes 786440 | tf_op jit(solution)/shard_map/ppermute | solution.py:35
  6.0 3.2 %collective-permute-start = (f32[32,2048]{1,0:T(8,128)}, f32[32,2048]{1,0:T(8,128)S(1)}, u32[]{:S(2)}, u32[]{:S(2)}) collective-permute-start(f32[32,2048]{1,0:T(8,128)} %right.1), channel_id=1, source_target_pairs={{0,7},{1,2},{2,1},{3,4},{4,3},{5,6},{6,5},{7,0},{8,15},{9,10},{10,... | collective-permute-start | bytes 786440 | tf_op jit(solution)/shard_map/ppermute | solution.py:35
  9.2 7.2 %prepare.1 = (bf16[64,256,256]{2,1,0:T(8,128)(2,1)S(1)}, bf16[64,256,256]{2,1,0:T(8,128)(2,1)S(1)}, bf16[64,256,256]{2,1,0:T(8,128)(2,1)S(1)}, bf16[64,256,256]{2,1,0:T(8,128)(2,1)S(1)}, s32[4,64]{1,0:T(4,128)S(1)}) custom-call(s32[2,64]{1,0:T(2,128)} %pairs.1, f32[64,256,256]{2,1,0:T(8,128)} %couplings.1), custom_call_target="tpu_custom_call" | custom-call | tf_op jit(solution)/shard_map/prepare/pallas_call | solution.py:149
  18.9 4.5 %pull_near_body.2 = (bf16[72,64,256]{2,1,0:T(8,128)(2,1)S(1)}, f32[8,32,256]{2,1,0:T(8,128)S(1)}) custom-call(s32[4,64]{1,0:T(4,128)S(1)} %get-tuple-element.44.refs_0_.routes, f32[3,8,32,256]{3,2,1,0:T(8,128)S(1)} %collective-permute-done.3.qa, f32[3,8,32,256]{3,2,1,0:T(8,128)S(1)} %get-tuple-element.45.whole, ...), custom_call_target="tpu_custom_call" | custom-call | tf_op jit(solution)/shard_map/pull_near_body/pallas_call | solution.py:80
  23.4 3.2 %collective-permute-done.4.db = f32[2,8,32,256]{3,2,1,0:T(8,128)S(1)} collective-permute-done((f32[2,8,32,256]{3,2,1,0:T(8,128)S(1)}, f32[2,8,32,256]{3,2,1,0:T(8,128)S(1)}, u32[]{:S(2)}, u32[]{:S(2)}) %collective-permute-start.4) | collective-permute-done | bytes 524320 | tf_op jit(solution)/shard_map/ppermute | solution.py:35
  29.9 4.4 %push_near_body.1 = (f32[8,32,256]{2,1,0:T(8,128)S(1)}, f32[8,32,256]{2,1,0:T(8,128)S(1)}, f32[8,32,256]{2,1,0:T(8,128)S(1)}, f32[8,32,256]{2,1,0:T(8,128)S(1)},...) custom-call(s32[4,64]{1,0:T(4,128)S(1)} %get-tuple-element.44.refs_0_.routes, ...), custom_call_target="tpu_custom_call" | custom-call | tf_op jit(solution)/shard_map/push_near_body/pallas_call | solution.py:80
  38.2 2.3 %collective-permute-start.10 = (f32[8,32,256]{2,1,0:T(8,128)S(1)}, f32[8,32,256]{2,1,0:T(8,128)S(1)}, u32[]{:S(2)}, u32[]{:S(2)}) collective-permute-start(f32[8,32,256]{2,1,0:T(8,128)S(1)} %get-tuple-element.64), channel_id=1, source_target_pairs={{0,120},{8,16},{16,8},{24,32},{32,24},{40,48},{48,40},{56,64},{64,... | collective-permute-start | bytes 786440 | tf_op jit(solution)/shard_map/ppermute | solution.py:35
  42.3 7.2 %collective-permute-done.10.rb = f32[8,32,256]{2,1,0:T(8,128)S(1)} collective-permute-done((f32[8,32,256]{2,1,0:T(8,128)S(1)}, f32[8,32,256]{2,1,0:T(8,128)S(1)}, u32[]{:S(2)}, u32[]{:S(2)}) %collective-permute-start.10) | collective-permute-done | bytes 262176 | tf_op jit(solution)/shard_map/ppermute | solution.py:35
  49.6 2.4 %collective-permute-start.14 = (f32[8,32,256]{2,1,0:T(8,128)S(1)}, f32[8,32,256]{2,1,0:T(8,128)S(1)}, u32[]{:S(2)}, u32[]{:S(2)}) collective-permute-start(f32[8,32,256]{2,1,0:T(8,128)S(1)} %sum_body.1.vector.refs_2_.u), channel_id=1, source_target_pairs={{0,120},{8,16},{16,8},{24,32},{32,24},{40,48},{48,40},{56,64},{64,... | collective-permute-start | bytes 786440 | tf_op jit(solution)/shard_map/ppermute | solution.py:35
  55.2 4.8 %collective-permute-done.14.refs_4_ = f32[8,32,256]{2,1,0:T(8,128)S(1)} collective-permute-done((f32[8,32,256]{2,1,0:T(8,128)S(1)}, f32[8,32,256]{2,1,0:T(8,128)S(1)}, u32[]{:S(2)}, u32[]{:S(2)}) %collective-permute-start.14) | collective-permute-done | bytes 262176 | tf_op jit(solution)/shard_map/ppermute | solution.py:35
  60.2 2.4 %collective-permute-start.16 = (f32[2,8,32,256]{3,2,1,0:T(8,128)S(1)}, f32[2,8,32,256]{3,2,1,0:T(8,128)S(1)}, u32[]{:S(2)}, u32[]{:S(2)}) collective-permute-start(f32[2,8,32,256]{3,2,1,0:T(8,128)S(1)} %get-tuple-element.70), channel_id=1, source_target_pairs={{0,7},{1,2},{2,1},{3,4},{4,3},{5,6},{6,5},{7,0},{8,15},{9,10},{10,... | collective-permute-start | bytes 1572872 | tf_op jit(solution)/shard_map/ppermute | solution.py:35
  62.6 4.5 %pull_near_body.3 = (bf16[72,64,256]{2,1,0:T(8,128)(2,1)S(1)}, f32[8,32,256]{2,1,0:T(8,128)S(1)}) custom-call(s32[4,64]{1,0:T(4,128)S(1)} %get-tuple-element.44.refs_0_.routes, f32[3,8,32,256]{3,2,1,0:T(8,128)S(1)} %collective-permute-done.15.qa, f32[3,8,32,256]{3,2,1,0:T(8,128)S(1)} %get-tuple-element.67.whole, ...), custom_call_target="tpu_custom_call" | custom-call | tf_op jit(solution)/shard_map/pull_near_body/pallas_call | solution.py:80
  67.1 3.0 %collective-permute-done.16.db = f32[2,8,32,256]{3,2,1,0:T(8,128)S(1)} collective-permute-done((f32[2,8,32,256]{3,2,1,0:T(8,128)S(1)}, f32[2,8,32,256]{3,2,1,0:T(8,128)S(1)}, u32[]{:S(2)}, u32[]{:S(2)}) %collective-permute-start.16) | collective-permute-done | bytes 524320 | tf_op jit(solution)/shard_map/ppermute | solution.py:35
  71.1 2.5 %collective-permute-start.17 = (f32[32,128]{1,0:T(8,128)S(1)}, f32[32,128]{1,0:T(8,128)S(1)}, u32[]{:S(2)}, u32[]{:S(2)}) collective-permute-start(f32[32,128]{1,0:T(8,128)S(1)} %get-tuple-element.73.grams), channel_id=1, source_target_pairs={{0,2},{1,3},{2,0},{3,1},{4,6},{5,7},{6,4},{7,5},{8,10},{9,11},{10,... | collective-permute-start | bytes 49160 | tf_op jit(solution)/shard_map/ppermute | solution.py:358
  75.3 2.1 %collective-permute-start.18 = (f32[32,128]{1,0:T(8,128)S(1)}, f32[32,128]{1,0:T(8,128)S(1)}, u32[]{:S(2)}, u32[]{:S(2)}) collective-permute-start(f32[32,128]{1,0:T(8,128)S(1)} %add_body.3.grams), channel_id=1, source_target_pairs={{0,6},{1,7},{2,4},{3,5},{4,2},{5,3},{6,0},{7,1},{8,14},{9,15},{10,... | collective-permute-start | bytes 49160 | tf_op jit(solution)/shard_map/ppermute | solution.py:358
  77.4 2.4 %push_begin_body.1.after.pieces_in = f32[72,32,256]{2,1,0:T(8,128)S(1)} custom-call(s32[4,64]{1,0:T(4,128)S(1)} %get-tuple-element.44.refs_0_.routes, bf16[8,64,256]{2,1,0:T(8,128)(2,1)S(1)} %get-tuple-element.74.strain_hl, bf16[64,256,256]{2,1,0:T(8,128)(2,1)S(1)} %get-tuple-element.52.c_high, ...), custom_call_target="tpu_custom_call", output_to_operand_aliasing={{}: (4, {})} | custom-call | tf_op jit(solution)/shard_map/push_begin_body/pallas_call | solution.py:80
  80.8 2.4 %push_end_body.1.after.pieces = f32[72,32,256]{2,1,0:T(8,128)S(1)} custom-call(s32[4,64]{1,0:T(4,128)S(1)} %get-tuple-element.44.refs_0_.routes, bf16[8,64,256]{2,1,0:T(8,128)(2,1)S(1)} %get-tuple-element.74.strain_hl, bf16[64,256,256]{2,1,0:T(8,128)(2,1)S(1)} %get-tuple-element.52.c_high, ...), custom_call_target="tpu_custom_call", output_to_operand_aliasing={{}: (4, {})} | custom-call | tf_op jit(solution)/shard_map/push_end_body/pallas_call | solution.py:80
  84.2 2.2 %collective-permute-start.26 = (f32[3,8,32,256]{3,2,1,0:T(8,128)S(1)}, f32[3,8,32,256]{3,2,1,0:T(8,128)S(1)}, u32[]{:S(2)}, u32[]{:S(2)}) collective-permute-start(f32[3,8,32,256]{3,2,1,0:T(8,128)S(1)} %get-tuple-element.82), channel_id=1, source_target_pairs={{0,7},{1,2},{2,1},{3,4},{4,3},{5,6},{6,5},{7,0},{8,15},{9,10},{10,... | collective-permute-start | bytes 2359304 | tf_op jit(solution)/shard_map/ppermute | solution.py:35
  86.5 4.9 %collective-permute-done.20 = f32[32,128]{1,0:T(8,128)S(1)} collective-permute-done((f32[32,128]{1,0:T(8,128)S(1)}, f32[32,128]{1,0:T(8,128)S(1)}, u32[]{:S(2)}, u32[]{:S(2)}) %collective-permute-start.20) | collective-permute-done | bytes 16416 | tf_op jit(solution)/shard_map/ppermute | solution.py:358
  91.5 3.4 %collective-permute-start.21 = (f32[32,128]{1,0:T(8,128)S(1)}, f32[32,128]{1,0:T(8,128)S(1)}, u32[]{:S(2)}, u32[]{:S(2)}) collective-permute-start(f32[32,128]{1,0:T(8,128)S(1)} %add.12), channel_id=1, source_target_pairs={{0,32},{1,33},{2,34},{3,35},{4,36},{5,37},{6,38},{7,39},{8,40},{9,... | collective-permute-start | bytes 49160 | tf_op jit(solution)/shard_map/ppermute | solution.py:358
  97.1 2.9 %collective-permute-start.27 = (f32[8,32,256]{2,1,0:T(8,128)S(1)}, f32[8,32,256]{2,1,0:T(8,128)S(1)}, u32[]{:S(2)}, u32[]{:S(2)}) collective-permute-start(f32[8,32,256]{2,1,0:T(8,128)S(1)} %get-tuple-element.84), channel_id=1, source_target_pairs={{0,120},{8,16},{16,8},{24,32},{32,24},{40,48},{48,40},{56,64},{64,... | collective-permute-start | bytes 786440 | tf_op jit(solution)/shard_map/ppermute | solution.py:35
  101.1 5.1 %solve_body.1 = (f32[32,32]{1,0:T(8,128)S(1)}, f32[32,32]{1,0:T(8,128)S(1)}) custom-call(f32[32,128]{1,0:T(8,128)S(1)} %add_add_fusion.grams, f32[32,128]{1,0:T(8,128)S(1)} %collective-permute-done.24.moved), custom_call_target="tpu_custom_call" | custom-call | tf_op jit(solution)/shard_map/solve_body/pallas_call | solution.py:80
  106.2 1.9 %collective-permute-done.27.rb = f32[8,32,256]{2,1,0:T(8,128)S(1)} collective-permute-done((f32[8,32,256]{2,1,0:T(8,128)S(1)}, f32[8,32,256]{2,1,0:T(8,128)S(1)}, u32[]{:S(2)}, u32[]{:S(2)}) %collective-permute-start.27) | collective-permute-done | bytes 262176 | tf_op jit(solution)/shard_map/ppermute | solution.py:35
  108.2 1.8 %finish_body.1 = (f32[32,2048]{1,0:T(8,128)}, f32[32,2048]{1,0:T(8,128)}) custom-call(f32[32,32]{1,0:T(8,128)S(1)} %get-tuple-element.75.p, f32[32,32]{1,0:T(8,128)S(1)} %get-tuple-element.76.q, f32[32,2048]{1,0:T(8,128)S(1)} %copy-done.1, f32[8,32,256]{2,1,0:T(8,128)S(1)} %sum_body.1.vector.refs_2_.u, f32[8,32,256]{2,1,0:T(8,128)S(1)} %get-tuple-element.83.rest, ...), custom_call_target="tpu_custom_call" | custom-call | tf_op jit(solution)/shard_map/finish_body/pallas_call | solution.py:80
  (63 shorter events, 23.0 us)
Async XLA Ops:
  0.6 15.8 %collective-permute-start.2 = (f32[32,2048]{1,0:T(8,128)}, f32[32,2048]{1,0:T(8,128)S(1)}, u32[]{:S(2)}, u32[]{:S(2)}) collective-permute-start(f32[32,2048]{1,0:T(8,128)} %right.1), channel_id=1, source_target_pairs={{0,120},{8,16},{16,8},{24,32},{32,24},{40,48},{48,40},{56,64},{64,... | collective-permute-start | bytes 786440 | tf_op jit(solution)/shard_map/ppermute | solution.py:35
  6.0 10.4 %collective-permute-start.1 = (f32[32,2048]{1,0:T(8,128)}, f32[32,2048]{1,0:T(8,128)S(1)}, u32[]{:S(2)}, u32[]{:S(2)}) collective-permute-start(f32[32,2048]{1,0:T(8,128)} %right.1), channel_id=1, source_target_pairs={{0,8},{8,0},{16,24},{24,16},{32,40},{40,32},{48,56},{56,48},{64,72... | collective-permute-start | bytes 786440 | tf_op jit(solution)/shard_map/ppermute | solution.py:35
  6.0 10.4 %collective-permute-start = (f32[32,2048]{1,0:T(8,128)}, f32[32,2048]{1,0:T(8,128)S(1)}, u32[]{:S(2)}, u32[]{:S(2)}) collective-permute-start(f32[32,2048]{1,0:T(8,128)} %right.1), channel_id=1, source_target_pairs={{0,7},{1,2},{2,1},{3,4},{4,3},{5,6},{6,5},{7,0},{8,15},{9,10},{10,... | collective-permute-start | bytes 786440 | tf_op jit(solution)/shard_map/ppermute | solution.py:35
  16.6 9.9 %collective-permute-start.4 = (f32[2,8,32,256]{3,2,1,0:T(8,128)S(1)}, f32[2,8,32,256]{3,2,1,0:T(8,128)S(1)}, u32[]{:S(2)}, u32[]{:S(2)}) collective-permute-start(f32[2,8,32,256]{3,2,1,0:T(8,128)S(1)} %get-tuple-element.50), channel_id=1, source_target_pairs={{0,7},{1,2},{2,1},{3,4},{4,3},{5,6},{6,5},{7,0},{8,15},{9,10},{10,... | collective-permute-start | bytes 1572872 | tf_op jit(solution)/shard_map/ppermute | solution.py:35
  28.2 9.9 %collective-permute-start.9 = (f32[2,8,32,256]{3,2,1,0:T(8,128)S(1)}, f32[2,8,32,256]{3,2,1,0:T(8,128)S(1)}, u32[]{:S(2)}, u32[]{:S(2)}) collective-permute-start(f32[2,8,32,256]{3,2,1,0:T(8,128)S(1)} %get-tuple-element.63), channel_id=1, source_target_pairs={{0,7},{1,2},{2,1},{3,4},{4,3},{5,6},{6,5},{7,0},{8,15},{9,10},{10,... | collective-permute-start | bytes 1572872 | tf_op jit(solution)/shard_map/ppermute | solution.py:35
  34.9 7.4 %collective-permute-start.5 = (f32[8,32,256]{2,1,0:T(8,128)S(1)}, f32[8,32,256]{2,1,0:T(8,128)S(1)}, u32[]{:S(2)}, u32[]{:S(2)}) collective-permute-start(f32[8,32,256]{2,1,0:T(8,128)S(1)} %get-tuple-element.57), channel_id=1, source_target_pairs={{0,1},{1,0},{2,3},{3,2},{4,5},{5,4},{6,7},{7,6},{8,9},{9,8},{10,11... | collective-permute-start | bytes 786440 | tf_op jit(solution)/shard_map/ppermute | solution.py:35
  35.0 7.3 %collective-permute-start.6 = (f32[8,32,256]{2,1,0:T(8,128)S(1)}, f32[8,32,256]{2,1,0:T(8,128)S(1)}, u32[]{:S(2)}, u32[]{:S(2)}) collective-permute-start(f32[8,32,256]{2,1,0:T(8,128)S(1)} %get-tuple-element.58), channel_id=1, source_target_pairs={{0,7},{1,2},{2,1},{3,4},{4,3},{5,6},{6,5},{7,0},{8,15},{9,10},{10,... | collective-permute-start | bytes 786440 | tf_op jit(solution)/shard_map/ppermute | solution.py:35
  38.2 11.3 %collective-permute-start.10 = (f32[8,32,256]{2,1,0:T(8,128)S(1)}, f32[8,32,256]{2,1,0:T(8,128)S(1)}, u32[]{:S(2)}, u32[]{:S(2)}) collective-permute-start(f32[8,32,256]{2,1,0:T(8,128)S(1)} %get-tuple-element.64), channel_id=1, source_target_pairs={{0,120},{8,16},{16,8},{24,32},{32,24},{40,48},{48,40},{56,64},{64,... | collective-permute-start | bytes 786440 | tf_op jit(solution)/shard_map/ppermute | solution.py:35
  40.6 9.0 %collective-permute-start.11 = (f32[8,32,256]{2,1,0:T(8,128)S(1)}, f32[8,32,256]{2,1,0:T(8,128)S(1)}, u32[]{:S(2)}, u32[]{:S(2)}) collective-permute-start(f32[8,32,256]{2,1,0:T(8,128)S(1)} %get-tuple-element.65), channel_id=1, source_target_pairs={{0,8},{8,0},{16,24},{24,16},{32,40},{40,32},{48,56},{56,48},{64,72... | collective-permute-start | bytes 786440 | tf_op jit(solution)/shard_map/ppermute | solution.py:35
  49.6 10.4 %collective-permute-start.14 = (f32[8,32,256]{2,1,0:T(8,128)S(1)}, f32[8,32,256]{2,1,0:T(8,128)S(1)}, u32[]{:S(2)}, u32[]{:S(2)}) collective-permute-start(f32[8,32,256]{2,1,0:T(8,128)S(1)} %sum_body.1.vector.refs_2_.u), channel_id=1, source_target_pairs={{0,120},{8,16},{16,8},{24,32},{32,24},{40,48},{48,40},{56,64},{64,... | collective-permute-start | bytes 786440 | tf_op jit(solution)/shard_map/ppermute | solution.py:35
  52.0 8.0 %collective-permute-start.13 = (f32[8,32,256]{2,1,0:T(8,128)S(1)}, f32[8,32,256]{2,1,0:T(8,128)S(1)}, u32[]{:S(2)}, u32[]{:S(2)}) collective-permute-start(f32[8,32,256]{2,1,0:T(8,128)S(1)} %sum_body.1.vector.refs_2_.u), channel_id=1, source_target_pairs={{0,8},{8,0},{16,24},{24,16},{32,40},{40,32},{48,56},{56,48},{64,72... | collective-permute-start | bytes 786440 | tf_op jit(solution)/shard_map/ppermute | solution.py:35
  52.0 8.0 %collective-permute-start.12 = (f32[8,32,256]{2,1,0:T(8,128)S(1)}, f32[8,32,256]{2,1,0:T(8,128)S(1)}, u32[]{:S(2)}, u32[]{:S(2)}) collective-permute-start(f32[8,32,256]{2,1,0:T(8,128)S(1)} %sum_body.1.vector.refs_2_.u), channel_id=1, source_target_pairs={{0,7},{1,2},{2,1},{3,4},{4,3},{5,6},{6,5},{7,0},{8,15},{9,10},{10,... | collective-permute-start | bytes 786440 | tf_op jit(solution)/shard_map/ppermute | solution.py:35
  60.2 9.9 %collective-permute-start.16 = (f32[2,8,32,256]{3,2,1,0:T(8,128)S(1)}, f32[2,8,32,256]{3,2,1,0:T(8,128)S(1)}, u32[]{:S(2)}, u32[]{:S(2)}) collective-permute-start(f32[2,8,32,256]{3,2,1,0:T(8,128)S(1)} %get-tuple-element.70), channel_id=1, source_target_pairs={{0,7},{1,2},{2,1},{3,4},{4,3},{5,6},{6,5},{7,0},{8,15},{9,10},{10,... | collective-permute-start | bytes 1572872 | tf_op jit(solution)/shard_map/ppermute | solution.py:35
  71.1 4.2 %collective-permute-start.17 = (f32[32,128]{1,0:T(8,128)S(1)}, f32[32,128]{1,0:T(8,128)S(1)}, u32[]{:S(2)}, u32[]{:S(2)}) collective-permute-start(f32[32,128]{1,0:T(8,128)S(1)} %get-tuple-element.73.grams), channel_id=1, source_target_pairs={{0,2},{1,3},{2,0},{3,1},{4,6},{5,7},{6,4},{7,5},{8,10},{9,11},{10,... | collective-permute-start | bytes 49160 | tf_op jit(solution)/shard_map/ppermute | solution.py:358
  75.3 4.9 %collective-permute-start.18 = (f32[32,128]{1,0:T(8,128)S(1)}, f32[32,128]{1,0:T(8,128)S(1)}, u32[]{:S(2)}, u32[]{:S(2)}) collective-permute-start(f32[32,128]{1,0:T(8,128)S(1)} %add_body.3.grams), channel_id=1, source_target_pairs={{0,6},{1,7},{2,4},{3,5},{4,2},{5,3},{6,0},{7,1},{8,14},{9,15},{10,... | collective-permute-start | bytes 49160 | tf_op jit(solution)/shard_map/ppermute | solution.py:358
  80.2 3.7 %collective-permute-start.19 = (f32[32,128]{1,0:T(8,128)S(1)}, f32[32,128]{1,0:T(8,128)S(1)}, u32[]{:S(2)}, u32[]{:S(2)}) collective-permute-start(f32[32,128]{1,0:T(8,128)S(1)} %add_body.4.grams), channel_id=1, source_target_pairs={{0,8},{1,9},{2,10},{3,11},{4,12},{5,13},{6,14},{7,15},{8,0},{9,1},... | collective-permute-start | bytes 49160 | tf_op jit(solution)/shard_map/ppermute | solution.py:358
  84.1 12.5 %collective-permute-start.25 = (f32[3,8,32,256]{3,2,1,0:T(8,128)S(1)}, f32[3,8,32,256]{3,2,1,0:T(8,128)S(1)}, u32[]{:S(2)}, u32[]{:S(2)}) collective-permute-start(f32[3,8,32,256]{3,2,1,0:T(8,128)S(1)} %get-tuple-element.81), channel_id=1, source_target_pairs={{0,1},{1,0},{2,3},{3,2},{4,5},{5,4},{6,7},{7,6},{8,9},{9,8},{10,11... | collective-permute-start | bytes 2359304 | tf_op jit(solution)/shard_map/ppermute | solution.py:35
  84.2 12.7 %collective-permute-start.26 = (f32[3,8,32,256]{3,2,1,0:T(8,128)S(1)}, f32[3,8,32,256]{3,2,1,0:T(8,128)S(1)}, u32[]{:S(2)}, u32[]{:S(2)}) collective-permute-start(f32[3,8,32,256]{3,2,1,0:T(8,128)S(1)} %get-tuple-element.82), channel_id=1, source_target_pairs={{0,7},{1,2},{2,1},{3,4},{4,3},{5,6},{6,5},{7,0},{8,15},{9,10},{10,... | collective-permute-start | bytes 2359304 | tf_op jit(solution)/shard_map/ppermute | solution.py:35
  86.5 4.9 %collective-permute-start.20 = (f32[32,128]{1,0:T(8,128)S(1)}, f32[32,128]{1,0:T(8,128)S(1)}, u32[]{:S(2)}, u32[]{:S(2)}) collective-permute-start(f32[32,128]{1,0:T(8,128)S(1)} %add_body.5.grams), channel_id=1, source_target_pairs={{0,24},{1,25},{2,26},{3,27},{4,28},{5,29},{6,30},{7,31},{8,16},{9,... | collective-permute-start | bytes 49160 | tf_op jit(solution)/shard_map/ppermute | solution.py:358
  91.4 5.2 %collective-permute-start.23 = (f32[32,128]{1,0:T(8,128)S(1)}, f32[32,128]{1,0:T(8,128)S(1)}, u32[]{:S(2)}, u32[]{:S(2)}) collective-permute-start(f32[32,128]{1,0:T(8,128)S(1)} %add.12), channel_id=1, source_target_pairs={{0,64},{1,65},{2,66},{3,67},{4,68},{5,69},{6,70},{7,71},{8,72},{9,... | collective-permute-start | bytes 49160 | tf_op jit(solution)/shard_map/ppermute | solution.py:358
  91.4 5.2 %collective-permute-start.22 = (f32[32,128]{1,0:T(8,128)S(1)}, f32[32,128]{1,0:T(8,128)S(1)}, u32[]{:S(2)}, u32[]{:S(2)}) collective-permute-start(f32[32,128]{1,0:T(8,128)S(1)} %add.12), channel_id=1, source_target_pairs={{0,96},{1,97},{2,98},{3,99},{4,100},{5,101},{6,102},{7,103},{8,104... | collective-permute-start | bytes 49160 | tf_op jit(solution)/shard_map/ppermute | solution.py:358
  91.5 5.2 %collective-permute-start.21 = (f32[32,128]{1,0:T(8,128)S(1)}, f32[32,128]{1,0:T(8,128)S(1)}, u32[]{:S(2)}, u32[]{:S(2)}) collective-permute-start(f32[32,128]{1,0:T(8,128)S(1)} %add.12), channel_id=1, source_target_pairs={{0,32},{1,33},{2,34},{3,35},{4,36},{5,37},{6,38},{7,39},{8,40},{9,... | collective-permute-start | bytes 49160 | tf_op jit(solution)/shard_map/ppermute | solution.py:358
  97.1 11.1 %collective-permute-start.27 = (f32[8,32,256]{2,1,0:T(8,128)S(1)}, f32[8,32,256]{2,1,0:T(8,128)S(1)}, u32[]{:S(2)}, u32[]{:S(2)}) collective-permute-start(f32[8,32,256]{2,1,0:T(8,128)S(1)} %get-tuple-element.84), channel_id=1, source_target_pairs={{0,120},{8,16},{16,8},{24,32},{32,24},{40,48},{48,40},{56,64},{64,... | collective-permute-start | bytes 786440 | tf_op jit(solution)/shard_map/ppermute | solution.py:35
  99.9 8.3 %collective-permute-start.28 = (f32[8,32,256]{2,1,0:T(8,128)S(1)}, f32[8,32,256]{2,1,0:T(8,128)S(1)}, u32[]{:S(2)}, u32[]{:S(2)}) collective-permute-start(f32[8,32,256]{2,1,0:T(8,128)S(1)} %get-tuple-element.85), channel_id=1, source_target_pairs={{0,8},{8,0},{16,24},{24,16},{32,40},{40,32},{48,56},{56,48},{64,72... | collective-permute-start | bytes 786440 | tf_op jit(solution)/shard_map/ppermute | solution.py:35
  (7 other events, 36.5 us)

commit v10 on v9

--- a/solution.py
+++ b/solution.py
@@ -14,8 +14,8 @@
 SMEM_SPEC = pl.BlockSpec(memory_space=pltpu.SMEM)
 CHUNK = 8
 HALF = 4
-PREPARED = 8
-SLOTS = 8
+PREPARED = 4
+SLOTS = 16
 NEAR_TABLES = 7
 
 

time: 110 us -> 112 us (1.018)
  waiting for transfers between devices: 32.7 us -> 40.6 us
  starting transfers between devices: 36.6 us -> 29.8 us
    ppermute x21, waiting for transfers between devices: 22.7 us -> 26.8 us  [swapped(): return lax.ppermute(value, axis, pairs_of(lax.axis_size(axis), shift))]
    ppermute x8, waiting for transfers between devices: 10 us -> 13.7 us  [exchanged(): lax.ppermute(value, ('row', 'col'), [(i, i ^ mask) for i in range(count)])]
    ppermute x8, starting transfers between devices: 8.63 us -> 5.1 us  [exchanged(): lax.ppermute(value, ('row', 'col'), [(i, i ^ mask) for i in range(count)])]
    ppermute x21, starting transfers between devices: 27.9 us -> 24.7 us  [swapped(): return lax.ppermute(value, axis, pairs_of(lax.axis_size(axis), shift))]
  transfers between devices with their start and end apart: 29 -> 29, of which waited for: 14 -> 19; matrix products, arithmetic and copies ran while one was open for 0% -> 0% of each run, Pallas kernels for 32% -> 32%
where the time goes in v10:
time: 112 us; the launch traced here: 111 us
  waiting for transfers between devices  40.6 us (36%)
  Pallas kernels  40 us (36%)
  starting transfers between devices  29.8 us (27%)
    pallas_call x22, Pallas kernels, call(): pl.pallas_call(body, out_shape=out_shape, in_specs=[SMEM_SPEC] * n_smem +...  32.6 us
    ppermute x21, waiting for transfers between devices, swapped(): return lax.ppermute(value, axis, pairs_of(lax.axis_size(axis), shift))  26.8 us
    ppermute x21, starting transfers between devices, swapped(): return lax.ppermute(value, axis, pairs_of(lax.axis_size(axis), shift))  24.7 us
    ppermute x8, waiting for transfers between devices, exchanged(): lax.ppermute(value, ('row', 'col'), [(i, i ^ mask) for i in range(count)])  13.7 us
    pallas_call x1, Pallas kernels, prepare(): pl.pallas_call(functools.partial(prepare_body, blocks), in_specs=[pl.Bloc...  7.47 us
    ppermute x8, starting transfers between devices, exchanged(): lax.ppermute(value, ('row', 'col'), [(i, i ^ mask) for i in range(count)])  5.1 us
  transfers between devices with their start and end apart: 29, of which 19 were waited for; matrix products, arithmetic and copies ran while one was open for 0% of the time, Pallas kernels for 32%

profile of v10, /device:TPU:0, one launch (start us, length us, event | category | flops | bytes accessed | tf_op | source)
XLA Modules:
  0.0 111.2 jit_solution(399329585027497942)
XLA Ops:
  0.6 5.4 %collective-permute-start.2 = (f32[32,2048]{1,0:T(8,128)}, f32[32,2048]{1,0:T(8,128)S(1)}, u32[]{:S(2)}, u32[]{:S(2)}) collective-permute-start(f32[32,2048]{1,0:T(8,128)} %right.1), channel_id=1, source_target_pairs={{0,120},{8,16},{16,8},{24,32},{32,24},{40,48},{48,40},{56,64},{64,... | collective-permute-start | bytes 786440 | tf_op jit(solution)/shard_map/ppermute | solution.py:35
  6.0 3.2 %collective-permute-start = (f32[32,2048]{1,0:T(8,128)}, f32[32,2048]{1,0:T(8,128)S(1)}, u32[]{:S(2)}, u32[]{:S(2)}) collective-permute-start(f32[32,2048]{1,0:T(8,128)} %right.1), channel_id=1, source_target_pairs={{0,7},{1,2},{2,1},{3,4},{4,3},{5,6},{6,5},{7,0},{8,15},{9,10},{10,... | collective-permute-start | bytes 786440 | tf_op jit(solution)/shard_map/ppermute | solution.py:35
  9.2 7.5 %prepare.1 = (bf16[64,256,256]{2,1,0:T(8,128)(2,1)S(1)}, bf16[64,256,256]{2,1,0:T(8,128)(2,1)S(1)}, bf16[64,256,256]{2,1,0:T(8,128)(2,1)S(1)}, bf16[64,256,256]{2,1,0:T(8,128)(2,1)S(1)}, s32[4,64]{1,0:T(4,128)S(1)}) custom-call(s32[2,64]{1,0:T(2,128)} %pairs.1, f32[64,256,256]{2,1,0:T(8,128)} %couplings.1), custom_call_target="tpu_custom_call" | custom-call | tf_op jit(solution)/shard_map/prepare/pallas_call | solution.py:149
  19.2 4.5 %pull_near_body.2 = (bf16[72,64,256]{2,1,0:T(8,128)(2,1)S(1)}, f32[8,32,256]{2,1,0:T(8,128)S(1)}) custom-call(s32[4,64]{1,0:T(4,128)S(1)} %get-tuple-element.44.refs_0_.routes, f32[3,8,32,256]{3,2,1,0:T(8,128)S(1)} %collective-permute-done.3.qa, f32[3,8,32,256]{3,2,1,0:T(8,128)S(1)} %get-tuple-element.45.whole, ...), custom_call_target="tpu_custom_call" | custom-call | tf_op jit(solution)/shard_map/pull_near_body/pallas_call | solution.py:80
  23.7 3.2 %collective-permute-done.4.db = f32[2,8,32,256]{3,2,1,0:T(8,128)S(1)} collective-permute-done((f32[2,8,32,256]{3,2,1,0:T(8,128)S(1)}, f32[2,8,32,256]{3,2,1,0:T(8,128)S(1)}, u32[]{:S(2)}, u32[]{:S(2)}) %collective-permute-start.4) | collective-permute-done | bytes 524320 | tf_op jit(solution)/shard_map/ppermute | solution.py:35
  29.9 4.4 %push_near_body.1 = (f32[8,32,256]{2,1,0:T(8,128)S(1)}, f32[8,32,256]{2,1,0:T(8,128)S(1)}, f32[8,32,256]{2,1,0:T(8,128)S(1)}, f32[8,32,256]{2,1,0:T(8,128)S(1)},...) custom-call(s32[4,64]{1,0:T(4,128)S(1)} %get-tuple-element.44.refs_0_.routes, ...), custom_call_target="tpu_custom_call" | custom-call | tf_op jit(solution)/shard_map/push_near_body/pallas_call | solution.py:80
  38.5 2.2 %collective-permute-start.10 = (f32[8,32,256]{2,1,0:T(8,128)S(1)}, f32[8,32,256]{2,1,0:T(8,128)S(1)}, u32[]{:S(2)}, u32[]{:S(2)}) collective-permute-start(f32[8,32,256]{2,1,0:T(8,128)S(1)} %get-tuple-element.64), channel_id=1, source_target_pairs={{0,120},{8,16},{16,8},{24,32},{32,24},{40,48},{48,40},{56,64},{64,... | collective-permute-start | bytes 786440 | tf_op jit(solution)/shard_map/ppermute | solution.py:35
  40.7 1.7 %diag_body.2 = (f32[8,32,256]{2,1,0:T(8,128)S(1)}, f32[2,32,32]{2,1,0:T(8,128)S(1)}) custom-call(f32[32,2048]{1,0:T(8,128)S(1)} %copy-done.1, f32[8,256,256]{2,1,0:T(8,128)S(1)} %copy-done), custom_call_target="tpu_custom_call" | custom-call | tf_op jit(solution)/shard_map/diag_body/pallas_call | solution.py:80
  43.4 7.2 %collective-permute-done.10.rb = f32[8,32,256]{2,1,0:T(8,128)S(1)} collective-permute-done((f32[8,32,256]{2,1,0:T(8,128)S(1)}, f32[8,32,256]{2,1,0:T(8,128)S(1)}, u32[]{:S(2)}, u32[]{:S(2)}) %collective-permute-start.10) | collective-permute-done | bytes 262176 | tf_op jit(solution)/shard_map/ppermute | solution.py:35
  50.7 1.8 %collective-permute-start.14 = (f32[8,32,256]{2,1,0:T(8,128)S(1)}, f32[8,32,256]{2,1,0:T(8,128)S(1)}, u32[]{:S(2)}, u32[]{:S(2)}) collective-permute-start(f32[8,32,256]{2,1,0:T(8,128)S(1)} %sum_body.1.vector.refs_2_.u), channel_id=1, source_target_pairs={{0,120},{8,16},{16,8},{24,32},{32,24},{40,48},{48,40},{56,64},{64,... | collective-permute-start | bytes 786440 | tf_op jit(solution)/shard_map/ppermute | solution.py:35
  55.5 6.3 %collective-permute-done.14.refs_4_ = f32[8,32,256]{2,1,0:T(8,128)S(1)} collective-permute-done((f32[8,32,256]{2,1,0:T(8,128)S(1)}, f32[8,32,256]{2,1,0:T(8,128)S(1)}, u32[]{:S(2)}, u32[]{:S(2)}) %collective-permute-start.14) | collective-permute-done | bytes 262176 | tf_op jit(solution)/shard_map/ppermute | solution.py:35
  64.2 4.5 %pull_near_body.3 = (bf16[72,64,256]{2,1,0:T(8,128)(2,1)S(1)}, f32[8,32,256]{2,1,0:T(8,128)S(1)}) custom-call(s32[4,64]{1,0:T(4,128)S(1)} %get-tuple-element.44.refs_0_.routes, f32[3,8,32,256]{3,2,1,0:T(8,128)S(1)} %collective-permute-done.15.qa, f32[3,8,32,256]{3,2,1,0:T(8,128)S(1)} %get-tuple-element.67.whole, ...), custom_call_target="tpu_custom_call" | custom-call | tf_op jit(solution)/shard_map/pull_near_body/pallas_call | solution.py:80
  68.7 3.2 %collective-permute-done.16.db = f32[2,8,32,256]{3,2,1,0:T(8,128)S(1)} collective-permute-done((f32[2,8,32,256]{3,2,1,0:T(8,128)S(1)}, f32[2,8,32,256]{3,2,1,0:T(8,128)S(1)}, u32[]{:S(2)}, u32[]{:S(2)}) %collective-permute-start.16) | collective-permute-done | bytes 524320 | tf_op jit(solution)/shard_map/ppermute | solution.py:35
  74.5 2.0 %collective-permute-done.17.moved = f32[32,128]{1,0:T(8,128)S(1)} collective-permute-done((f32[32,128]{1,0:T(8,128)S(1)}, f32[32,128]{1,0:T(8,128)S(1)}, u32[]{:S(2)}, u32[]{:S(2)}) %collective-permute-start.17) | collective-permute-done | bytes 16416 | tf_op jit(solution)/shard_map/ppermute | solution.py:358
  77.2 2.4 %push_begin_body.1.after.pieces_in = f32[72,32,256]{2,1,0:T(8,128)S(1)} custom-call(s32[4,64]{1,0:T(4,128)S(1)} %get-tuple-element.44.refs_0_.routes, bf16[8,64,256]{2,1,0:T(8,128)(2,1)S(1)} %get-tuple-element.74.strain_hl, bf16[64,256,256]{2,1,0:T(8,128)(2,1)S(1)} %get-tuple-element.52.c_high, ...), custom_call_target="tpu_custom_call", output_to_operand_aliasing={{}: (4, {})} | custom-call | tf_op jit(solution)/shard_map/push_begin_body/pallas_call | solution.py:80
  79.6 1.9 %collective-permute-done.18.moved = f32[32,128]{1,0:T(8,128)S(1)} collective-permute-done((f32[32,128]{1,0:T(8,128)S(1)}, f32[32,128]{1,0:T(8,128)S(1)}, u32[]{:S(2)}, u32[]{:S(2)}) %collective-permute-start.18) | collective-permute-done | bytes 16416 | tf_op jit(solution)/shard_map/ppermute | solution.py:358
  81.5 2.4 %push_end_body.1.after.pieces = f32[72,32,256]{2,1,0:T(8,128)S(1)} custom-call(s32[4,64]{1,0:T(4,128)S(1)} %get-tuple-element.44.refs_0_.routes, bf16[8,64,256]{2,1,0:T(8,128)(2,1)S(1)} %get-tuple-element.74.strain_hl, bf16[64,256,256]{2,1,0:T(8,128)(2,1)S(1)} %get-tuple-element.52.c_high, ...), custom_call_target="tpu_custom_call", output_to_operand_aliasing={{}: (4, {})} | custom-call | tf_op jit(solution)/shard_map/push_end_body/pallas_call | solution.py:80
  86.3 4.9 %collective-permute-done.20 = f32[32,128]{1,0:T(8,128)S(1)} collective-permute-done((f32[32,128]{1,0:T(8,128)S(1)}, f32[32,128]{1,0:T(8,128)S(1)}, u32[]{:S(2)}, u32[]{:S(2)}) %collective-permute-start.20) | collective-permute-done | bytes 16416 | tf_op jit(solution)/shard_map/ppermute | solution.py:358
  91.2 2.1 %collective-permute-start.22 = (f32[32,128]{1,0:T(8,128)S(1)}, f32[32,128]{1,0:T(8,128)S(1)}, u32[]{:S(2)}, u32[]{:S(2)}) collective-permute-start(f32[32,128]{1,0:T(8,128)S(1)} %add.12), channel_id=1, source_target_pairs={{0,96},{1,97},{2,98},{3,99},{4,100},{5,101},{6,102},{7,103},{8,104... | collective-permute-start | bytes 49160 | tf_op jit(solution)/shard_map/ppermute | solution.py:358
  94.7 1.8 %collective-permute-done.23 = f32[32,128]{1,0:T(8,128)S(1)} collective-permute-done((f32[32,128]{1,0:T(8,128)S(1)}, f32[32,128]{1,0:T(8,128)S(1)}, u32[]{:S(2)}, u32[]{:S(2)}) %collective-permute-start.23) | collective-permute-done | bytes 16416 | tf_op jit(solution)/shard_map/ppermute | solution.py:358
  98.4 3.1 %collective-permute-start.27 = (f32[8,32,256]{2,1,0:T(8,128)S(1)}, f32[8,32,256]{2,1,0:T(8,128)S(1)}, u32[]{:S(2)}, u32[]{:S(2)}) collective-permute-start(f32[8,32,256]{2,1,0:T(8,128)S(1)} %get-tuple-element.84), channel_id=1, source_target_pairs={{0,120},{8,16},{16,8},{24,32},{32,24},{40,48},{48,40},{56,64},{64,... | collective-permute-start | bytes 786440 | tf_op jit(solution)/shard_map/ppermute | solution.py:35
  102.6 5.1 %solve_body.1 = (f32[32,32]{1,0:T(8,128)S(1)}, f32[32,32]{1,0:T(8,128)S(1)}) custom-call(f32[32,128]{1,0:T(8,128)S(1)} %add_add_fusion.grams, f32[32,128]{1,0:T(8,128)S(1)} %collective-permute-done.24.moved), custom_call_target="tpu_custom_call" | custom-call | tf_op jit(solution)/shard_map/solve_body/pallas_call | solution.py:80
  107.7 1.8 %collective-permute-done.27.rb = f32[8,32,256]{2,1,0:T(8,128)S(1)} collective-permute-done((f32[8,32,256]{2,1,0:T(8,128)S(1)}, f32[8,32,256]{2,1,0:T(8,128)S(1)}, u32[]{:S(2)}, u32[]{:S(2)}) %collective-permute-start.27) | collective-permute-done | bytes 262176 | tf_op jit(solution)/shard_map/ppermute | solution.py:35
  109.5 1.8 %finish_body.1 = (f32[32,2048]{1,0:T(8,128)}, f32[32,2048]{1,0:T(8,128)}) custom-call(f32[32,32]{1,0:T(8,128)S(1)} %get-tuple-element.75.p, f32[32,32]{1,0:T(8,128)S(1)} %get-tuple-element.76.q, f32[32,2048]{1,0:T(8,128)S(1)} %copy-done.1, f32[8,32,256]{2,1,0:T(8,128)S(1)} %sum_body.1.vector.refs_2_.u, f32[8,32,256]{2,1,0:T(8,128)S(1)} %get-tuple-element.83.rest, ...), custom_call_target="tpu_custom_call" | custom-call | tf_op jit(solution)/shard_map/finish_body/pallas_call | solution.py:80
  (63 shorter events, 26.2 us)
Async XLA Ops:
  0.6 16.1 %collective-permute-start.2 = (f32[32,2048]{1,0:T(8,128)}, f32[32,2048]{1,0:T(8,128)S(1)}, u32[]{:S(2)}, u32[]{:S(2)}) collective-permute-start(f32[32,2048]{1,0:T(8,128)} %right.1), channel_id=1, source_target_pairs={{0,120},{8,16},{16,8},{24,32},{32,24},{40,48},{48,40},{56,64},{64,... | collective-permute-start | bytes 786440 | tf_op jit(solution)/shard_map/ppermute | solution.py:35
  6.0 10.7 %collective-permute-start.1 = (f32[32,2048]{1,0:T(8,128)}, f32[32,2048]{1,0:T(8,128)S(1)}, u32[]{:S(2)}, u32[]{:S(2)}) collective-permute-start(f32[32,2048]{1,0:T(8,128)} %right.1), channel_id=1, source_target_pairs={{0,8},{8,0},{16,24},{24,16},{32,40},{40,32},{48,56},{56,48},{64,72... | collective-permute-start | bytes 786440 | tf_op jit(solution)/shard_map/ppermute | solution.py:35
  6.0 10.7 %collective-permute-start = (f32[32,2048]{1,0:T(8,128)}, f32[32,2048]{1,0:T(8,128)S(1)}, u32[]{:S(2)}, u32[]{:S(2)}) collective-permute-start(f32[32,2048]{1,0:T(8,128)} %right.1), channel_id=1, source_target_pairs={{0,7},{1,2},{2,1},{3,4},{4,3},{5,6},{6,5},{7,0},{8,15},{9,10},{10,... | collective-permute-start | bytes 786440 | tf_op jit(solution)/shard_map/ppermute | solution.py:35
  16.9 9.9 %collective-permute-start.4 = (f32[2,8,32,256]{3,2,1,0:T(8,128)S(1)}, f32[2,8,32,256]{3,2,1,0:T(8,128)S(1)}, u32[]{:S(2)}, u32[]{:S(2)}) collective-permute-start(f32[2,8,32,256]{3,2,1,0:T(8,128)S(1)} %get-tuple-element.50), channel_id=1, source_target_pairs={{0,7},{1,2},{2,1},{3,4},{4,3},{5,6},{6,5},{7,0},{8,15},{9,10},{10,... | collective-permute-start | bytes 1572872 | tf_op jit(solution)/shard_map/ppermute | solution.py:35
  28.5 9.9 %collective-permute-start.9 = (f32[2,8,32,256]{3,2,1,0:T(8,128)S(1)}, f32[2,8,32,256]{3,2,1,0:T(8,128)S(1)}, u32[]{:S(2)}, u32[]{:S(2)}) collective-permute-start(f32[2,8,32,256]{3,2,1,0:T(8,128)S(1)} %get-tuple-element.63), channel_id=1, source_target_pairs={{0,7},{1,2},{2,1},{3,4},{4,3},{5,6},{6,5},{7,0},{8,15},{9,10},{10,... | collective-permute-start | bytes 1572872 | tf_op jit(solution)/shard_map/ppermute | solution.py:35
  36.0 6.5 %collective-permute-start.5 = (f32[8,32,256]{2,1,0:T(8,128)S(1)}, f32[8,32,256]{2,1,0:T(8,128)S(1)}, u32[]{:S(2)}, u32[]{:S(2)}) collective-permute-start(f32[8,32,256]{2,1,0:T(8,128)S(1)} %get-tuple-element.57), channel_id=1, source_target_pairs={{0,1},{1,0},{2,3},{3,2},{4,5},{5,4},{6,7},{7,6},{8,9},{9,8},{10,11... | collective-permute-start | bytes 786440 | tf_op jit(solution)/shard_map/ppermute | solution.py:35
  36.4 7.0 %collective-permute-start.6 = (f32[8,32,256]{2,1,0:T(8,128)S(1)}, f32[8,32,256]{2,1,0:T(8,128)S(1)}, u32[]{:S(2)}, u32[]{:S(2)}) collective-permute-start(f32[8,32,256]{2,1,0:T(8,128)S(1)} %get-tuple-element.58), channel_id=1, source_target_pairs={{0,7},{1,2},{2,1},{3,4},{4,3},{5,6},{6,5},{7,0},{8,15},{9,10},{10,... | collective-permute-start | bytes 786440 | tf_op jit(solution)/shard_map/ppermute | solution.py:35
  38.5 12.1 %collective-permute-start.10 = (f32[8,32,256]{2,1,0:T(8,128)S(1)}, f32[8,32,256]{2,1,0:T(8,128)S(1)}, u32[]{:S(2)}, u32[]{:S(2)}) collective-permute-start(f32[8,32,256]{2,1,0:T(8,128)S(1)} %get-tuple-element.64), channel_id=1, source_target_pairs={{0,120},{8,16},{16,8},{24,32},{32,24},{40,48},{48,40},{56,64},{64,... | collective-permute-start | bytes 786440 | tf_op jit(solution)/shard_map/ppermute | solution.py:35
  40.7 9.8 %collective-permute-start.11 = (f32[8,32,256]{2,1,0:T(8,128)S(1)}, f32[8,32,256]{2,1,0:T(8,128)S(1)}, u32[]{:S(2)}, u32[]{:S(2)}) collective-permute-start(f32[8,32,256]{2,1,0:T(8,128)S(1)} %get-tuple-element.65), channel_id=1, source_target_pairs={{0,8},{8,0},{16,24},{24,16},{32,40},{40,32},{48,56},{56,48},{64,72... | collective-permute-start | bytes 786440 | tf_op jit(solution)/shard_map/ppermute | solution.py:35
  50.7 11.1 %collective-permute-start.14 = (f32[8,32,256]{2,1,0:T(8,128)S(1)}, f32[8,32,256]{2,1,0:T(8,128)S(1)}, u32[]{:S(2)}, u32[]{:S(2)}) collective-permute-start(f32[8,32,256]{2,1,0:T(8,128)S(1)} %sum_body.1.vector.refs_2_.u), channel_id=1, source_target_pairs={{0,120},{8,16},{16,8},{24,32},{32,24},{40,48},{48,40},{56,64},{64,... | collective-permute-start | bytes 786440 | tf_op jit(solution)/shard_map/ppermute | solution.py:35
  52.5 9.2 %collective-permute-start.13 = (f32[8,32,256]{2,1,0:T(8,128)S(1)}, f32[8,32,256]{2,1,0:T(8,128)S(1)}, u32[]{:S(2)}, u32[]{:S(2)}) collective-permute-start(f32[8,32,256]{2,1,0:T(8,128)S(1)} %sum_body.1.vector.refs_2_.u), channel_id=1, source_target_pairs={{0,8},{8,0},{16,24},{24,16},{32,40},{40,32},{48,56},{56,48},{64,72... | collective-permute-start | bytes 786440 | tf_op jit(solution)/shard_map/ppermute | solution.py:35
  52.5 9.2 %collective-permute-start.12 = (f32[8,32,256]{2,1,0:T(8,128)S(1)}, f32[8,32,256]{2,1,0:T(8,128)S(1)}, u32[]{:S(2)}, u32[]{:S(2)}) collective-permute-start(f32[8,32,256]{2,1,0:T(8,128)S(1)} %sum_body.1.vector.refs_2_.u), channel_id=1, source_target_pairs={{0,7},{1,2},{2,1},{3,4},{4,3},{5,6},{6,5},{7,0},{8,15},{9,10},{10,... | collective-permute-start | bytes 786440 | tf_op jit(solution)/shard_map/ppermute | solution.py:35
  61.9 9.9 %collective-permute-start.16 = (f32[2,8,32,256]{3,2,1,0:T(8,128)S(1)}, f32[2,8,32,256]{3,2,1,0:T(8,128)S(1)}, u32[]{:S(2)}, u32[]{:S(2)}) collective-permute-start(f32[2,8,32,256]{3,2,1,0:T(8,128)S(1)} %get-tuple-element.70), channel_id=1, source_target_pairs={{0,7},{1,2},{2,1},{3,4},{4,3},{5,6},{6,5},{7,0},{8,15},{9,10},{10,... | collective-permute-start | bytes 1572872 | tf_op jit(solution)/shard_map/ppermute | solution.py:35
  72.8 3.8 %collective-permute-start.17 = (f32[32,128]{1,0:T(8,128)S(1)}, f32[32,128]{1,0:T(8,128)S(1)}, u32[]{:S(2)}, u32[]{:S(2)}) collective-permute-start(f32[32,128]{1,0:T(8,128)S(1)} %get-tuple-element.73.grams), channel_id=1, source_target_pairs={{0,2},{1,3},{2,0},{3,1},{4,6},{5,7},{6,4},{7,5},{8,10},{9,11},{10,... | collective-permute-start | bytes 49160 | tf_op jit(solution)/shard_map/ppermute | solution.py:358
  76.6 4.9 %collective-permute-start.18 = (f32[32,128]{1,0:T(8,128)S(1)}, f32[32,128]{1,0:T(8,128)S(1)}, u32[]{:S(2)}, u32[]{:S(2)}) collective-permute-start(f32[32,128]{1,0:T(8,128)S(1)} %add_body.3.grams), channel_id=1, source_target_pairs={{0,6},{1,7},{2,4},{3,5},{4,2},{5,3},{6,0},{7,1},{8,14},{9,15},{10,... | collective-permute-start | bytes 49160 | tf_op jit(solution)/shard_map/ppermute | solution.py:358
  81.5 3.7 %collective-permute-start.19 = (f32[32,128]{1,0:T(8,128)S(1)}, f32[32,128]{1,0:T(8,128)S(1)}, u32[]{:S(2)}, u32[]{:S(2)}) collective-permute-start(f32[32,128]{1,0:T(8,128)S(1)} %add_body.4.grams), channel_id=1, source_target_pairs={{0,8},{1,9},{2,10},{3,11},{4,12},{5,13},{6,14},{7,15},{8,0},{9,1},... | collective-permute-start | bytes 49160 | tf_op jit(solution)/shard_map/ppermute | solution.py:358
  85.4 11.6 %collective-permute-start.25 = (f32[3,8,32,256]{3,2,1,0:T(8,128)S(1)}, f32[3,8,32,256]{3,2,1,0:T(8,128)S(1)}, u32[]{:S(2)}, u32[]{:S(2)}) collective-permute-start(f32[3,8,32,256]{3,2,1,0:T(8,128)S(1)} %get-tuple-element.81), channel_id=1, source_target_pairs={{0,1},{1,0},{2,3},{3,2},{4,5},{5,4},{6,7},{7,6},{8,9},{9,8},{10,11... | collective-permute-start | bytes 2359304 | tf_op jit(solution)/shard_map/ppermute | solution.py:35
  85.5 12.7 %collective-permute-start.26 = (f32[3,8,32,256]{3,2,1,0:T(8,128)S(1)}, f32[3,8,32,256]{3,2,1,0:T(8,128)S(1)}, u32[]{:S(2)}, u32[]{:S(2)}) collective-permute-start(f32[3,8,32,256]{3,2,1,0:T(8,128)S(1)} %get-tuple-element.82), channel_id=1, source_target_pairs={{0,7},{1,2},{2,1},{3,4},{4,3},{5,6},{6,5},{7,0},{8,15},{9,10},{10,... | collective-permute-start | bytes 2359304 | tf_op jit(solution)/shard_map/ppermute | solution.py:35
  86.3 4.9 %collective-permute-start.20 = (f32[32,128]{1,0:T(8,128)S(1)}, f32[32,128]{1,0:T(8,128)S(1)}, u32[]{:S(2)}, u32[]{:S(2)}) collective-permute-start(f32[32,128]{1,0:T(8,128)S(1)} %add_body.5.grams), channel_id=1, source_target_pairs={{0,24},{1,25},{2,26},{3,27},{4,28},{5,29},{6,30},{7,31},{8,16},{9,... | collective-permute-start | bytes 49160 | tf_op jit(solution)/shard_map/ppermute | solution.py:358
  91.2 5.2 %collective-permute-start.23 = (f32[32,128]{1,0:T(8,128)S(1)}, f32[32,128]{1,0:T(8,128)S(1)}, u32[]{:S(2)}, u32[]{:S(2)}) collective-permute-start(f32[32,128]{1,0:T(8,128)S(1)} %add.12), channel_id=1, source_target_pairs={{0,64},{1,65},{2,66},{3,67},{4,68},{5,69},{6,70},{7,71},{8,72},{9,... | collective-permute-start | bytes 49160 | tf_op jit(solution)/shard_map/ppermute | solution.py:358
  91.2 5.2 %collective-permute-start.22 = (f32[32,128]{1,0:T(8,128)S(1)}, f32[32,128]{1,0:T(8,128)S(1)}, u32[]{:S(2)}, u32[]{:S(2)}) collective-permute-start(f32[32,128]{1,0:T(8,128)S(1)} %add.12), channel_id=1, source_target_pairs={{0,96},{1,97},{2,98},{3,99},{4,100},{5,101},{6,102},{7,103},{8,104... | collective-permute-start | bytes 49160 | tf_op jit(solution)/shard_map/ppermute | solution.py:358
  93.3 3.7 %collective-permute-start.21 = (f32[32,128]{1,0:T(8,128)S(1)}, f32[32,128]{1,0:T(8,128)S(1)}, u32[]{:S(2)}, u32[]{:S(2)}) collective-permute-start(f32[32,128]{1,0:T(8,128)S(1)} %add.12), channel_id=1, source_target_pairs={{0,32},{1,33},{2,34},{3,35},{4,36},{5,37},{6,38},{7,39},{8,40},{9,... | collective-permute-start | bytes 49160 | tf_op jit(solution)/shard_map/ppermute | solution.py:358
  98.4 11.1 %collective-permute-start.27 = (f32[8,32,256]{2,1,0:T(8,128)S(1)}, f32[8,32,256]{2,1,0:T(8,128)S(1)}, u32[]{:S(2)}, u32[]{:S(2)}) collective-permute-start(f32[8,32,256]{2,1,0:T(8,128)S(1)} %get-tuple-element.84), channel_id=1, source_target_pairs={{0,120},{8,16},{16,8},{24,32},{32,24},{40,48},{48,40},{56,64},{64,... | collective-permute-start | bytes 786440 | tf_op jit(solution)/shard_map/ppermute | solution.py:35
  101.4 8.1 %collective-permute-start.28 = (f32[8,32,256]{2,1,0:T(8,128)S(1)}, f32[8,32,256]{2,1,0:T(8,128)S(1)}, u32[]{:S(2)}, u32[]{:S(2)}) collective-permute-start(f32[8,32,256]{2,1,0:T(8,128)S(1)} %get-tuple-element.85), channel_id=1, source_target_pairs={{0,8},{8,0},{16,24},{24,16},{32,40},{40,32},{48,56},{56,48},{64,72... | collective-permute-start | bytes 786440 | tf_op jit(solution)/shard_map/ppermute | solution.py:35
  (7 other events, 37.1 us)
